TPU v7x, 1024 devices: a whole 4x8x16 slice. The times are simulated.
1024 devices in a mesh: dp: 32 (over x, z_hi, core), pipe: 8 (over y), tensor: 4 (over z_lo).
Axes of the slice: x: 4, y: 8, z: 16 (z_hi: 4, z_lo: 4; z = z_hi * 4 + z_lo), core: 2. Of those that a mesh axis runs over, the one named last changes fastest.
Arguments:
- down_in: bfloat16 [64, 32, 2048], P('dp'), may hold values from -6 to 6
- up_in: bfloat16 [64, 32, 2048], P('dp'), may hold values from -6 to 6
- w_qkv: bfloat16 [8, 2048, 1536], P(None, 'dp', 'tensor'), may hold values from -0.125 to 0.125
- w_out: bfloat16 [8, 1024, 2048], P(None, 'tensor', 'dp'), may hold values from -0.1875 to 0.1875
- norm_gain: bfloat16 [8, 2048], P(None, 'dp'), may hold values from 0.099609375 to 1.8984375
- down_docs: int32 [64, 32], P('dp'), may hold values from 0 to 3, never falling along the last dimension, each value on 1 to 16 neighbouring positions
- up_docs: int32 [64, 32], P('dp'), may hold values from 0 to 3, never falling along the last dimension, each value on 1 to 16 neighbouring positions
Outputs:
- down_acts: bfloat16 [8, 64, 32, 2048], P('pipe', 'dp', 'tensor')
- up_acts: bfloat16 [8, 64, 32, 2048], P('pipe', 'dp', 'tensor')
Inputs may be any that keep to these rules, and one draw needn't show every extreme that they name: `down_docs`: in every micro-batch the document numbers never fall along the positions, every one of the 4 numbers occurs, and no document is longer than 16 positions. `up_docs`: in every micro-batch the document numbers never fall along the positions, every one of the 4 numbers occurs, and no document is longer than 16 positions.
All inputs are finite; a program needn't handle non-finite values.
Results may differ from a plain program's by a relative error of at most 0.034.
Values may be sent and summed in bfloat16 or wider, within the bound.
No kernel may reach another device: no remote copies, remote signals or barrier semaphores. Data moves between devices by JAX's collectives and lax.ppermute only.
A program may use at most 32 MiB of HBM per device.

v0:
```python
import jax
import jax.numpy as jnp
from jax import lax
from jax.sharding import PartitionSpec as P

HEADS = 16
KV_HEADS = 4
HEAD_DIM = 64
SEQ = 32


EPSILON = 1e-05
THETA = 500000.0


def shifted(value, axis, by):
    length = lax.axis_size(axis)
    pairs = [(i, i + by) for i in range(length) if 0 <= i + by < length]
    return lax.ppermute(value, axis, pairs)


def rotary_tables(length, width):
    half_width = width // 2
    frequency = THETA ** (-(jnp.arange(half_width, dtype=jnp.float32) * 2.0 / width))
    angles = jnp.arange(length, dtype=jnp.float32)[:, None] * frequency[None, :]
    return (jnp.cos(angles), jnp.sin(angles))


def rotate(values, cosine, sine):
    half_width = values.shape[-1] // 2
    first = values[..., :half_width]
    second = values[..., half_width:]
    cosine = cosine[:, None, :]
    sine = sine[:, None, :]
    return jnp.concatenate(
        [first * cosine - second * sine, second * cosine + first * sine], axis=-1
    )


def normalize(inputs, gain):
    values = inputs.astype(jnp.float32)
    scale = lax.rsqrt(jnp.mean(values * values, axis=-1, keepdims=True) + EPSILON)
    return (values * scale * gain.astype(jnp.float32)).astype(jnp.bfloat16)


def attend(inputs, gain, qkv_cols, out_rows, docs, cosine, sine, heads_here, kv_here):
    normed = normalize(inputs, gain)
    length = normed.shape[0]
    query_width = heads_here * HEAD_DIM
    key_width = kv_here * HEAD_DIM
    projected = jnp.dot(normed, qkv_cols, preferred_element_type=jnp.float32)
    query = rotate(
        projected[:, :query_width].reshape(length, heads_here, HEAD_DIM), cosine, sine
    ).astype(jnp.bfloat16)
    keys = rotate(
        projected[:, query_width : query_width + key_width].reshape(length, kv_here, HEAD_DIM),
        cosine,
        sine,
    ).astype(jnp.bfloat16)
    values = (
        projected[:, query_width + key_width :]
        .reshape(length, kv_here, HEAD_DIM)
        .astype(jnp.bfloat16)
    )
    query = query.reshape(length, kv_here, heads_here // kv_here, HEAD_DIM)
    scores = jnp.einsum(
        "qgrd,kgd->grqk", query, keys, preferred_element_type=jnp.float32
    ) * HEAD_DIM ** (-0.5)
    positions = jnp.arange(length)
    allowed = (positions[:, None] >= positions[None, :]) & (docs[:, None] == docs[None, :])
    scores = jnp.where(allowed, scores, -1e30)
    weights = jax.nn.softmax(scores, axis=-1).astype(jnp.bfloat16)
    context = jnp.einsum("grqk,kgd->qgrd", weights, values, preferred_element_type=jnp.float32)
    context = context.reshape(length, query_width).astype(jnp.bfloat16)
    partial_sum = jnp.dot(context, out_rows, preferred_element_type=jnp.float32)
    return partial_sum.astype(jnp.bfloat16).astype(jnp.float32)


def pick(array, index):
    return lax.dynamic_index_in_dim(array, index, 0, keepdims=False)


def on_device(down_in, up_in, w_qkv, w_out, norm_gain, down_docs, up_docs):
    sections = lax.axis_size("pipe")
    position = lax.axis_index("pipe")
    mirror = sections - 1 - position
    groups = lax.axis_size("tensor")
    member = lax.axis_index("tensor")
    heads_here = HEADS // groups
    kv_here = KV_HEADS // groups
    qkv_pair = jnp.stack([pick(w_qkv, position), pick(w_qkv, mirror)])
    out_pair = jnp.stack([pick(w_out, position), pick(w_out, mirror)])
    gain_pair = jnp.stack([pick(norm_gain, position), pick(norm_gain, mirror)])
    qkv_full, out_full, gain_full = (
        lax.all_gather(qkv_pair, "dp", axis=1, tiled=True),
        lax.all_gather(out_pair, "dp", axis=2, tiled=True),
        lax.all_gather(gain_pair, "dp", axis=1, tiled=True),
    )
    cosine, sine = rotary_tables(SEQ, HEAD_DIM)
    mb_count = down_in.shape[0]
    width = down_in.shape[2]
    rows_here = SEQ // groups
    row_start = member * rows_here
    last_batch = mb_count - 1

    def own_rows(block):
        return lax.dynamic_slice_in_dim(block, row_start, rows_here, 0)

    def store(outputs, result, index):
        valid = (index >= 0) & (index < mb_count)
        slot = jnp.clip(index, 0, last_batch)
        previous = pick(outputs, slot)
        return lax.dynamic_update_index_in_dim(outputs, jnp.where(valid, result, previous), slot, 0)

    buffer_rows = SEQ

    def advance(step, carry):
        down_buf, up_buf, down_out, up_out = carry
        down_index = step - position
        up_index = step - mirror
        inject = jnp.clip(step, 0, last_batch)
        fresh_down = pick(down_in, inject)
        fresh_up = pick(up_in, inject)
        down_doc = pick(down_docs, jnp.clip(down_index, 0, last_batch))
        up_doc = pick(up_docs, jnp.clip(up_index, 0, last_batch))
        down_whole = jnp.where(position == 0, fresh_down, down_buf)
        up_whole = jnp.where(mirror == 0, fresh_up, up_buf)
        down_own = own_rows(down_whole)
        up_own = own_rows(up_whole)
        down_part = attend(
            down_whole,
            gain_full[0],
            qkv_full[0],
            out_full[0],
            down_doc,
            cosine,
            sine,
            heads_here,
            kv_here,
        )
        up_part = attend(
            up_whole,
            gain_full[1],
            qkv_full[1],
            out_full[1],
            up_doc,
            cosine,
            sine,
            heads_here,
            kv_here,
        )
        down_sum, up_sum = (
            lax.psum_scatter(
                down_part.astype(jnp.bfloat16), "tensor", scatter_dimension=0, tiled=True
            ).astype(jnp.float32),
            lax.psum_scatter(
                up_part.astype(jnp.bfloat16), "tensor", scatter_dimension=0, tiled=True
            ).astype(jnp.float32),
        )
        down_y = (down_own.astype(jnp.float32) + down_sum).astype(jnp.bfloat16)
        up_y = (up_own.astype(jnp.float32) + up_sum).astype(jnp.bfloat16)
        down_send, up_send = (
            lax.all_gather(down_y, "tensor", axis=0, tiled=True),
            lax.all_gather(up_y, "tensor", axis=0, tiled=True),
        )
        down_out = store(down_out, down_y, down_index)
        up_out = store(up_out, up_y, up_index)
        down_buf = shifted(down_send, "pipe", 1)
        up_buf = shifted(up_send, "pipe", -1)
        return (down_buf, up_buf, down_out, up_out)

    start_buf = jnp.zeros((buffer_rows, width), jnp.bfloat16)
    start_out = jnp.zeros((mb_count, rows_here, width), jnp.bfloat16)
    carry = (start_buf, start_buf, start_out, start_out)
    carry = lax.fori_loop(0, mb_count + sections - 1, advance, carry)
    return (carry[2][None], carry[3][None])


def solution(mesh):
    placed = (
        P("dp", None, None),
        P("dp", None, None),
        P(None, "dp", "tensor"),
        P(None, "tensor", "dp"),
        P(None, "dp"),
        P("dp", None),
        P("dp", None),
    )
    return jax.shard_map(
        on_device,
        mesh=mesh,
        in_specs=placed,
        out_specs=(P("pipe", "dp", "tensor", None), P("pipe", "dp", "tensor", None)),
        check_vma=False,
    )
```

profile of v0, /device:TPU:6, one launch (start us, length us, event | category | flops | bytes accessed | tf_op | source)
XLA Modules:
  0.0 1060.6 jit_solution(15727634535686822693)
XLA Ops:
  11.3 58.8 %all-gather = bf16[32,64,2]{1,2,0:T(2,128)(2,1)S(1)} all-gather(bf16[1,64,2]{1,2,0:T(2,128)(2,1)S(1)} %maximum_bitcast_fusion.4), channel_id=1, replica_groups=mesh['dp'=32,'pipe'=8,'tensor'=4] {'dp'}, dimensions={0}, use_global_device_ids=true | all-gather | bytes 8448 | tf_op jit(solution)/shard_map/all_gather | solution.py:97
  70.3 37.8 %all-gather.6.cloned.1.call-done = bf16[2,256,2048]{1,0,2:T(2,128)(2,1)} async-done(((bf16[2,256,64]{1,0,2:T(2,128)(2,1)}), bf16[2,256,2048]{1,0,2:T(2,128)(2,1)}) %all-gather.6.cloned.1.call-update) | async-done | bytes 2097168 | tf_op jit(solution)/shard_map/all_gather | solution.py:96
  112.8 86.6 %all-gather.4.cloned.1.call-done = bf16[2,2048,384]{2,1,0:T(8,128)(2,1)} async-done(((bf16[2,64,384]{2,1,0:T(8,128)(2,1)}), bf16[2,2048,384]{2,1,0:T(8,128)(2,1)}) %all-gather.4.cloned.1.call-update) | async-done | bytes 3145744 | tf_op jit(solution)/shard_map/all_gather | solution.py:95
  199.6 853.6 %while.24 = (s32[]{:T(128)}, bf16[32,2048]{1,0:T(8,128)(2,1)S(1)}, bf16[32,2048]{1,0:T(8,128)(2,1)S(1)}, bf16[2,8,2048]{2,1,0:T(8,128)(2,1)S(1)}, bf16[2,8,2048]...) while((s32[]{:T(128)}, bf16[32,2048]{1,0:T(8,128)(2,1)S(1)}, ...), condition=%wide.region_9.10_spmd.clone.clone.clone, body=%wide.region_0.9_spmd.clone.clone.clone.sunk | while | flops 171470400 | bytes 10545707 | solution.py:175
  207.7 25.7 %reduce-scatter.5.cloned.1.call-done = bf16[8,2048]{1,0:T(8,128)(2,1)} async-done(((bf16[32,2048]{1,0:T(8,128)(2,1)}), bf16[8,2048]{1,0:T(8,128)(2,1)}) %reduce-scatter.5.cloned.1.call-update) | async-done | bytes 32784 | tf_op jit(solution)/shard_map/while/body/eval_jaxpr/reduce_scatter | solution.py:156
  248.9 19.7 %reduce-scatter.3.cloned.1.call-done = bf16[8,2048]{1,0:T(8,128)(2,1)} async-done(((bf16[32,2048]{1,0:T(8,128)(2,1)}), bf16[8,2048]{1,0:T(8,128)(2,1)}) %reduce-scatter.3.cloned.1.call-update) | async-done | bytes 32784 | tf_op jit(solution)/shard_map/while/body/eval_jaxpr/reduce_scatter | solution.py:153
  296.7 32.2 %reduce-scatter.5.cloned.1.call-done = bf16[8,2048]{1,0:T(8,128)(2,1)} async-done(((bf16[32,2048]{1,0:T(8,128)(2,1)}), bf16[8,2048]{1,0:T(8,128)(2,1)}) %reduce-scatter.5.cloned.1.call-update) | async-done | bytes 32784 | tf_op jit(solution)/shard_map/while/body/eval_jaxpr/reduce_scatter | solution.py:156
  344.3 19.8 %reduce-scatter.3.cloned.1.call-done = bf16[8,2048]{1,0:T(8,128)(2,1)} async-done(((bf16[32,2048]{1,0:T(8,128)(2,1)}), bf16[8,2048]{1,0:T(8,128)(2,1)}) %reduce-scatter.3.cloned.1.call-update) | async-done | bytes 32784 | tf_op jit(solution)/shard_map/while/body/eval_jaxpr/reduce_scatter | solution.py:153
  392.2 32.2 %reduce-scatter.5.cloned.1.call-done = bf16[8,2048]{1,0:T(8,128)(2,1)} async-done(((bf16[32,2048]{1,0:T(8,128)(2,1)}), bf16[8,2048]{1,0:T(8,128)(2,1)}) %reduce-scatter.5.cloned.1.call-update) | async-done | bytes 32784 | tf_op jit(solution)/shard_map/while/body/eval_jaxpr/reduce_scatter | solution.py:156
  439.9 19.9 %reduce-scatter.3.cloned.1.call-done = bf16[8,2048]{1,0:T(8,128)(2,1)} async-done(((bf16[32,2048]{1,0:T(8,128)(2,1)}), bf16[8,2048]{1,0:T(8,128)(2,1)}) %reduce-scatter.3.cloned.1.call-update) | async-done | bytes 32784 | tf_op jit(solution)/shard_map/while/body/eval_jaxpr/reduce_scatter | solution.py:153
  487.9 32.3 %reduce-scatter.5.cloned.1.call-done = bf16[8,2048]{1,0:T(8,128)(2,1)} async-done(((bf16[32,2048]{1,0:T(8,128)(2,1)}), bf16[8,2048]{1,0:T(8,128)(2,1)}) %reduce-scatter.5.cloned.1.call-update) | async-done | bytes 32784 | tf_op jit(solution)/shard_map/while/body/eval_jaxpr/reduce_scatter | solution.py:156
  535.6 19.8 %reduce-scatter.3.cloned.1.call-done = bf16[8,2048]{1,0:T(8,128)(2,1)} async-done(((bf16[32,2048]{1,0:T(8,128)(2,1)}), bf16[8,2048]{1,0:T(8,128)(2,1)}) %reduce-scatter.3.cloned.1.call-update) | async-done | bytes 32784 | tf_op jit(solution)/shard_map/while/body/eval_jaxpr/reduce_scatter | solution.py:153
  556.1 13.5 %all_gather.38 = bf16[32,2048]{1,0:T(8,128)(2,1)S(1)} all-gather(bf16[8,2048]{1,0:T(8,128)(2,1)S(1)} %get-tuple-element.831), channel_id=1, replica_groups=mesh['dp'=32,'pipe'=8,'tensor'=4] {'tensor'}, dimensions={0}, use_global_device_ids=true | all-gather | bytes 163840 | tf_op jit(solution)/shard_map/while/body/eval_jaxpr/all_gather | solution.py:163
  583.4 32.2 %reduce-scatter.5.cloned.1.call-done = bf16[8,2048]{1,0:T(8,128)(2,1)} async-done(((bf16[32,2048]{1,0:T(8,128)(2,1)}), bf16[8,2048]{1,0:T(8,128)(2,1)}) %reduce-scatter.5.cloned.1.call-update) | async-done | bytes 32784 | tf_op jit(solution)/shard_map/while/body/eval_jaxpr/reduce_scatter | solution.py:156
  631.2 19.7 %reduce-scatter.3.cloned.1.call-done = bf16[8,2048]{1,0:T(8,128)(2,1)} async-done(((bf16[32,2048]{1,0:T(8,128)(2,1)}), bf16[8,2048]{1,0:T(8,128)(2,1)}) %reduce-scatter.3.cloned.1.call-update) | async-done | bytes 32784 | tf_op jit(solution)/shard_map/while/body/eval_jaxpr/reduce_scatter | solution.py:153
  678.9 32.3 %reduce-scatter.5.cloned.1.call-done = bf16[8,2048]{1,0:T(8,128)(2,1)} async-done(((bf16[32,2048]{1,0:T(8,128)(2,1)}), bf16[8,2048]{1,0:T(8,128)(2,1)}) %reduce-scatter.5.cloned.1.call-update) | async-done | bytes 32784 | tf_op jit(solution)/shard_map/while/body/eval_jaxpr/reduce_scatter | solution.py:156
  726.7 19.8 %reduce-scatter.3.cloned.1.call-done = bf16[8,2048]{1,0:T(8,128)(2,1)} async-done(((bf16[32,2048]{1,0:T(8,128)(2,1)}), bf16[8,2048]{1,0:T(8,128)(2,1)}) %reduce-scatter.3.cloned.1.call-update) | async-done | bytes 32784 | tf_op jit(solution)/shard_map/while/body/eval_jaxpr/reduce_scatter | solution.py:153
  774.6 32.2 %reduce-scatter.5.cloned.1.call-done = bf16[8,2048]{1,0:T(8,128)(2,1)} async-done(((bf16[32,2048]{1,0:T(8,128)(2,1)}), bf16[8,2048]{1,0:T(8,128)(2,1)}) %reduce-scatter.5.cloned.1.call-update) | async-done | bytes 32784 | tf_op jit(solution)/shard_map/while/body/eval_jaxpr/reduce_scatter | solution.py:156
  822.3 19.7 %reduce-scatter.3.cloned.1.call-done = bf16[8,2048]{1,0:T(8,128)(2,1)} async-done(((bf16[32,2048]{1,0:T(8,128)(2,1)}), bf16[8,2048]{1,0:T(8,128)(2,1)}) %reduce-scatter.3.cloned.1.call-update) | async-done | bytes 32784 | tf_op jit(solution)/shard_map/while/body/eval_jaxpr/reduce_scatter | solution.py:153
  870.2 32.1 %reduce-scatter.5.cloned.1.call-done = bf16[8,2048]{1,0:T(8,128)(2,1)} async-done(((bf16[32,2048]{1,0:T(8,128)(2,1)}), bf16[8,2048]{1,0:T(8,128)(2,1)}) %reduce-scatter.5.cloned.1.call-update) | async-done | bytes 32784 | tf_op jit(solution)/shard_map/while/body/eval_jaxpr/reduce_scatter | solution.py:156
  917.8 19.7 %reduce-scatter.3.cloned.1.call-done = bf16[8,2048]{1,0:T(8,128)(2,1)} async-done(((bf16[32,2048]{1,0:T(8,128)(2,1)}), bf16[8,2048]{1,0:T(8,128)(2,1)}) %reduce-scatter.3.cloned.1.call-update) | async-done | bytes 32784 | tf_op jit(solution)/shard_map/while/body/eval_jaxpr/reduce_scatter | solution.py:153
  965.6 32.2 %reduce-scatter.5.cloned.1.call-done = bf16[8,2048]{1,0:T(8,128)(2,1)} async-done(((bf16[32,2048]{1,0:T(8,128)(2,1)}), bf16[8,2048]{1,0:T(8,128)(2,1)}) %reduce-scatter.5.cloned.1.call-update) | async-done | bytes 32784 | tf_op jit(solution)/shard_map/while/body/eval_jaxpr/reduce_scatter | solution.py:156
  998.6 13.5 %all_gather.39 = bf16[32,2048]{1,0:T(8,128)(2,1)S(1)} all-gather(bf16[8,2048]{1,0:T(8,128)(2,1)S(1)} %get-tuple-element.838), channel_id=1, replica_groups=mesh['dp'=32,'pipe'=8,'tensor'=4] {'tensor'}, dimensions={0}, use_global_device_ids=true | all-gather | bytes 163840 | tf_op jit(solution)/shard_map/while/body/eval_jaxpr/all_gather | solution.py:164
  1013.4 19.7 %reduce-scatter.3.cloned.1.call-done = bf16[8,2048]{1,0:T(8,128)(2,1)} async-done(((bf16[32,2048]{1,0:T(8,128)(2,1)}), bf16[8,2048]{1,0:T(8,128)(2,1)}) %reduce-scatter.3.cloned.1.call-update) | async-done | bytes 32784 | tf_op jit(solution)/shard_map/while/body/eval_jaxpr/reduce_scatter | solution.py:153
  (469 shorter events, 372.4 us)
Async XLA Ops:
  7.2 100.9 %all-gather.6.cloned.1.call-start = ((), (), s32[]{:S(2)}) async-start(), calls=%async_computation.3 | async-start | bytes 2162688 | tf_op jit(solution)/shard_map/all_gather | solution.py:96
  8.9 190.6 %all-gather.4.cloned.1.call-start = ((), (), s32[]{:S(2)}) async-start(), calls=%async_computation.2 | async-start | bytes 3244032 | tf_op jit(solution)/shard_map/all_gather | solution.py:95
  205.9 62.7 %reduce-scatter.3.cloned.1.call-start = ((), (), s32[]{:S(2)}) async-start(), calls=%async_computation.4 | async-start | bytes 163840 | tf_op jit(solution)/shard_map/while/body/eval_jaxpr/reduce_scatter | solution.py:153
  288.7 40.2 %reduce-scatter.5.cloned.1.call-start = ((), (), s32[]{:S(2)}) async-start(), calls=%async_computation.5 | async-start | bytes 163840 | tf_op jit(solution)/shard_map/while/body/eval_jaxpr/reduce_scatter | solution.py:156
  294.9 69.3 %reduce-scatter.3.cloned.1.call-start = ((), (), s32[]{:S(2)}) async-start(), calls=%async_computation.4 | async-start | bytes 163840 | tf_op jit(solution)/shard_map/while/body/eval_jaxpr/reduce_scatter | solution.py:153
  343.0 38.7 %collective-permute-start.1 = (bf16[32,2048]{1,0:T(8,128)(2,1)S(1)}, bf16[32,2048]{1,0:T(8,128)(2,1)S(1)}, u32[]{:S(2)}, u32[]{:S(2)}) collective-permute-start(bf16[32,2048]{1,0:T(8,128)(2,1)S(1)} %all_gather.39), channel_id=1, source_target_pairs={{4,0},{8,4},{12,8},{16,12},{20,16},{24,20},{28,24},{5,1},{9,5},{13... | collective-permute-start | bytes 393224 | tf_op jit(solution)/shard_map/while/body/eval_jaxpr/ppermute | solution.py:19
  384.2 40.2 %reduce-scatter.5.cloned.1.call-start = ((), (), s32[]{:S(2)}) async-start(), calls=%async_computation.5 | async-start | bytes 163840 | tf_op jit(solution)/shard_map/while/body/eval_jaxpr/reduce_scatter | solution.py:156
  390.4 69.4 %reduce-scatter.3.cloned.1.call-start = ((), (), s32[]{:S(2)}) async-start(), calls=%async_computation.4 | async-start | bytes 163840 | tf_op jit(solution)/shard_map/while/body/eval_jaxpr/reduce_scatter | solution.py:153
  438.6 38.7 %collective-permute-start.1 = (bf16[32,2048]{1,0:T(8,128)(2,1)S(1)}, bf16[32,2048]{1,0:T(8,128)(2,1)S(1)}, u32[]{:S(2)}, u32[]{:S(2)}) collective-permute-start(bf16[32,2048]{1,0:T(8,128)(2,1)S(1)} %all_gather.39), channel_id=1, source_target_pairs={{4,0},{8,4},{12,8},{16,12},{20,16},{24,20},{28,24},{5,1},{9,5},{13... | collective-permute-start | bytes 393224 | tf_op jit(solution)/shard_map/while/body/eval_jaxpr/ppermute | solution.py:19
  479.8 40.3 %reduce-scatter.5.cloned.1.call-start = ((), (), s32[]{:S(2)}) async-start(), calls=%async_computation.5 | async-start | bytes 163840 | tf_op jit(solution)/shard_map/while/body/eval_jaxpr/reduce_scatter | solution.py:156
  486.1 69.3 %reduce-scatter.3.cloned.1.call-start = ((), (), s32[]{:S(2)}) async-start(), calls=%async_computation.4 | async-start | bytes 163840 | tf_op jit(solution)/shard_map/while/body/eval_jaxpr/reduce_scatter | solution.py:153
  575.4 40.3 %reduce-scatter.5.cloned.1.call-start = ((), (), s32[]{:S(2)}) async-start(), calls=%async_computation.5 | async-start | bytes 163840 | tf_op jit(solution)/shard_map/while/body/eval_jaxpr/reduce_scatter | solution.py:156
  581.6 69.3 %reduce-scatter.3.cloned.1.call-start = ((), (), s32[]{:S(2)}) async-start(), calls=%async_computation.4 | async-start | bytes 163840 | tf_op jit(solution)/shard_map/while/body/eval_jaxpr/reduce_scatter | solution.py:153
  670.9 40.4 %reduce-scatter.5.cloned.1.call-start = ((), (), s32[]{:S(2)}) async-start(), calls=%async_computation.5 | async-start | bytes 163840 | tf_op jit(solution)/shard_map/while/body/eval_jaxpr/reduce_scatter | solution.py:156
  677.1 69.4 %reduce-scatter.3.cloned.1.call-start = ((), (), s32[]{:S(2)}) async-start(), calls=%async_computation.4 | async-start | bytes 163840 | tf_op jit(solution)/shard_map/while/body/eval_jaxpr/reduce_scatter | solution.py:153
  725.4 38.7 %collective-permute-start.1 = (bf16[32,2048]{1,0:T(8,128)(2,1)S(1)}, bf16[32,2048]{1,0:T(8,128)(2,1)S(1)}, u32[]{:S(2)}, u32[]{:S(2)}) collective-permute-start(bf16[32,2048]{1,0:T(8,128)(2,1)S(1)} %all_gather.39), channel_id=1, source_target_pairs={{4,0},{8,4},{12,8},{16,12},{20,16},{24,20},{28,24},{5,1},{9,5},{13... | collective-permute-start | bytes 393224 | tf_op jit(solution)/shard_map/while/body/eval_jaxpr/ppermute | solution.py:19
  766.6 40.3 %reduce-scatter.5.cloned.1.call-start = ((), (), s32[]{:S(2)}) async-start(), calls=%async_computation.5 | async-start | bytes 163840 | tf_op jit(solution)/shard_map/while/body/eval_jaxpr/reduce_scatter | solution.py:156
  772.8 69.3 %reduce-scatter.3.cloned.1.call-start = ((), (), s32[]{:S(2)}) async-start(), calls=%async_computation.4 | async-start | bytes 163840 | tf_op jit(solution)/shard_map/while/body/eval_jaxpr/reduce_scatter | solution.py:153
  821.0 38.7 %collective-permute-start.1 = (bf16[32,2048]{1,0:T(8,128)(2,1)S(1)}, bf16[32,2048]{1,0:T(8,128)(2,1)S(1)}, u32[]{:S(2)}, u32[]{:S(2)}) collective-permute-start(bf16[32,2048]{1,0:T(8,128)(2,1)S(1)} %all_gather.39), channel_id=1, source_target_pairs={{4,0},{8,4},{12,8},{16,12},{20,16},{24,20},{28,24},{5,1},{9,5},{13... | collective-permute-start | bytes 393224 | tf_op jit(solution)/shard_map/while/body/eval_jaxpr/ppermute | solution.py:19
  862.2 40.1 %reduce-scatter.5.cloned.1.call-start = ((), (), s32[]{:S(2)}) async-start(), calls=%async_computation.5 | async-start | bytes 163840 | tf_op jit(solution)/shard_map/while/body/eval_jaxpr/reduce_scatter | solution.py:156
  868.4 69.1 %reduce-scatter.3.cloned.1.call-start = ((), (), s32[]{:S(2)}) async-start(), calls=%async_computation.4 | async-start | bytes 163840 | tf_op jit(solution)/shard_map/while/body/eval_jaxpr/reduce_scatter | solution.py:153
  957.5 40.3 %reduce-scatter.5.cloned.1.call-start = ((), (), s32[]{:S(2)}) async-start(), calls=%async_computation.5 | async-start | bytes 163840 | tf_op jit(solution)/shard_map/while/body/eval_jaxpr/reduce_scatter | solution.py:156
  963.8 69.2 %reduce-scatter.3.cloned.1.call-start = ((), (), s32[]{:S(2)}) async-start(), calls=%async_computation.4 | async-start | bytes 163840 | tf_op jit(solution)/shard_map/while/body/eval_jaxpr/reduce_scatter | solution.py:153
  1012.1 38.6 %collective-permute-start.1 = (bf16[32,2048]{1,0:T(8,128)(2,1)S(1)}, bf16[32,2048]{1,0:T(8,128)(2,1)S(1)}, u32[]{:S(2)}, u32[]{:S(2)}) collective-permute-start(bf16[32,2048]{1,0:T(8,128)(2,1)S(1)} %all_gather.39), channel_id=1, source_target_pairs={{4,0},{8,4},{12,8},{16,12},{20,16},{24,20},{28,24},{5,1},{9,5},{13... | collective-permute-start | bytes 393224 | tf_op jit(solution)/shard_map/while/body/eval_jaxpr/ppermute | solution.py:19
  (28 other events, 651.3 us)
Sparse Core Ops, SparseCore 0:
  12.9 95.1 all-gather.5
  112.4 87.0 all-gather.3
  206.0 27.2 reduce-scatter.4
  237.0 31.5 reduce-scatter.2
  295.0 33.8 reduce-scatter.4
  332.5 31.6 reduce-scatter.2
  390.6 33.7 reduce-scatter.4
  428.1 31.6 reduce-scatter.2
  486.2 33.9 reduce-scatter.4
  523.7 31.5 reduce-scatter.2
  581.7 33.8 reduce-scatter.4
  619.3 31.5 reduce-scatter.2
  677.2 33.9 reduce-scatter.4
  714.9 31.5 reduce-scatter.2
  772.9 33.8 reduce-scatter.4
  810.4 31.5 reduce-scatter.2
  868.5 33.7 reduce-scatter.4
  905.9 31.5 reduce-scatter.2
  963.9 33.8 reduce-scatter.4
  1001.4 31.5 reduce-scatter.2
where the time goes:
time: 1070 us; the launch traced here: 1060 us
  waiting for transfers between devices  608 us (57%)
  blocking collectives  300 us (28%)
  matrix products  57.2 us (5%)
  starting transfers between devices  42.4 us (4%)
  other arithmetic  21.5 us (2%)
  local copies, waits for them, and re-layouts  14.2 us (1%)
  between operations  14.2 us (1%)
    reduce_scatter x9, waiting for transfers between devices, advance(): lax.psum_scatter(up_part.astype(jnp.bfloat16), 'tensor', scatter_dimensio...  283 us
    reduce_scatter x9, waiting for transfers between devices, advance(): lax.psum_scatter(down_part.astype(jnp.bfloat16), 'tensor', scatter_dimens...  178 us
    all_gather x9, blocking collectives, advance(): lax.all_gather(up_y, 'tensor', axis=0, tiled=True)  121 us
    all_gather x9, blocking collectives, advance(): lax.all_gather(down_y, 'tensor', axis=0, tiled=True)  121 us
    all_gather x1, waiting for transfers between devices, on_device(): lax.all_gather(qkv_pair, 'dp', axis=1, tiled=True)  86.6 us
    all_gather x1, blocking collectives, on_device(): lax.all_gather(gain_pair, 'dp', axis=1, tiled=True)  58.8 us
    ppermute x18, starting transfers between devices, shifted(): return lax.ppermute(value, axis, pairs)  41.9 us
    all_gather x1, waiting for transfers between devices, on_device(): lax.all_gather(out_pair, 'dp', axis=2, tiled=True)  37.8 us
  transfers between devices with their start and end apart: 38, of which 29 were waited for; matrix products, arithmetic and copies ran while one was open for 3% of the time, Pallas kernels for 0%

commit v1 on v0

v1 whole, which is shorter than its diff:
```python
import functools

import jax
import jax.numpy as jnp
import numpy as np
from jax import lax
from jax.experimental import pallas as pl
from jax.experimental.pallas import tpu as pltpu
from jax.sharding import Mesh, PartitionSpec as P

HEADS = 16
KV_HEADS = 4
HEAD_DIM = 64
SEQ = 32
D = 2048
EPSILON = 1e-05
THETA = 500000.0

GROUPS = 4
GROUP_HEADS = 4
QKV = 384
CTX = 256
X = 4
ZH = 4
ZL = 4
Z = ZH * ZL
STEPS = Z // 2
BLOCK = 512


def rotary_tables():
    half = HEAD_DIM // 2
    frequency = THETA ** (-(jnp.arange(half, dtype=jnp.float32) * 2.0 / HEAD_DIM))
    angles = jnp.arange(SEQ, dtype=jnp.float32)[:, None] * frequency[None, :]
    return jnp.cos(angles), jnp.sin(angles)


def block_class(kind, k):
    return k % ZL if kind == "ring" else (-k) % ZL


BLOCKS = [("ring", k) for k in range(STEPS + 1)] + [("swap", k) for k in range(1, STEPS)]


def section_kernel(step, info, x_ref, allowed_ref, rope_ref, held_ref, *refs):
    blocks, (out_ref, xs, total) = refs[:Z], refs[Z:]

    @pl.when(info[0] != step)
    def _():
        out_ref[...] = held_ref[...]

    @pl.when(info[0] == step)
    def _():
        f32, bf16 = jnp.float32, jnp.bfloat16
        squares = jnp.zeros((SEQ, 1), f32)
        for zh in range(ZH):
            for x in range(X):
                part = x_ref[:, pl.ds(x * 512 + zh * 128, 128)]
                xs[zh, :, pl.ds(x * 128, 128)] = part
                wide = part.astype(f32)
                total[zh, :, pl.ds(x * 128, 128)] = wide
                squares = squares + jnp.sum(wide * wide, axis=-1, keepdims=True)
        scale = lax.rsqrt(squares * (1.0 / D) + EPSILON)

        cos, sin = rope_ref[0], rope_ref[1]
        kcos, ksin_a, ksin_b = rope_ref[2], rope_ref[3], rope_ref[4]
        allowed = allowed_ref[...] > 0.5
        lane = lax.broadcasted_iota(jnp.int32, (SEQ, 128), 1)
        lane2 = lax.broadcasted_iota(jnp.int32, (SEQ, 256), 1)
        head_of = (lane2 % 128) // 32

        contexts = []
        for c in range(GROUPS):
            projected = jnp.zeros((SEQ, QKV), f32)
            for i, (kind, k) in enumerate(BLOCKS):
                if block_class(kind, k) == c:
                    projected = projected + jnp.dot(
                        xs[info[1 + i]], blocks[i][:, :QKV], preferred_element_type=f32
                    )
            projected = projected * scale
            first, second = projected[:, :128], projected[:, 128:256]
            query = jnp.concatenate(
                [first * cos - second * sin, second * cos + first * sin], axis=-1
            ).astype(bf16)
            kv = projected[:, 256:]
            kv = kv * kcos + pltpu.roll(kv, 96, 1) * ksin_a + pltpu.roll(kv, 32, 1) * ksin_b
            key_a = jnp.where(lane < 32, kv, 0.0)
            key_a = key_a + pltpu.roll(key_a, 32, 1)
            key_a = key_a + pltpu.roll(key_a, 64, 1)
            key_b = jnp.where((lane >= 32) & (lane < 64), kv, 0.0)
            key_b = key_b + pltpu.roll(key_b, 32, 1)
            key_b = key_b + pltpu.roll(key_b, 64, 1)
            keys = jnp.concatenate([key_a, key_b], axis=-1).astype(bf16)
            zero = jnp.zeros((), bf16)
            queries = jnp.concatenate(
                [jnp.where(head_of == h, query, zero) for h in range(GROUP_HEADS)], axis=0
            )
            scores = lax.dot_general(
                queries, keys, (((1,), (1,)), ((), ())), preferred_element_type=f32
            ) * HEAD_DIM ** (-0.5)
            scores = jnp.where(allowed, scores, -1e30)
            scores = jnp.exp(scores - jnp.max(scores, axis=-1, keepdims=True))
            weights = (scores / jnp.sum(scores, axis=-1, keepdims=True)).astype(bf16)
            mixed = jnp.dot(weights, kv.astype(bf16), preferred_element_type=f32)
            rows = [mixed[h * SEQ : (h + 1) * SEQ] for h in range(GROUP_HEADS)]
            context = jnp.concatenate(
                [
                    jnp.where(lane < 64, pltpu.roll(rows[0], 64, 1), rows[1]),
                    jnp.where(lane < 64, pltpu.roll(rows[2], 64, 1), rows[3]),
                ],
                axis=-1,
            )
            contexts.append(context.astype(bf16))

        for i, (kind, k) in enumerate(BLOCKS):
            zh = info[1 + i]
            total[zh] = total[zh] + lax.dot_general(
                contexts[block_class(kind, k)],
                blocks[i][:, QKV:],
                (((1,), (1,)), ((), ())),
                preferred_element_type=f32,
            )
        for zh in range(ZH):
            for x in range(X):
                out_ref[:, pl.ds(x * 512 + zh * 128, 128)] = total[
                    zh, :, pl.ds(x * 128, 128)
                ].astype(bf16)


def run_section(step, info, values, allowed, rope, held, blocks):
    vmem = pl.BlockSpec(memory_space=pltpu.VMEM)
    return pl.pallas_call(
        functools.partial(section_kernel, step),
        out_shape=jax.ShapeDtypeStruct((SEQ, D), jnp.bfloat16),
        in_specs=[pl.BlockSpec(memory_space=pltpu.SMEM)] + [vmem] * (4 + Z),
        out_specs=vmem,
        scratch_shapes=[
            pltpu.VMEM((ZH, SEQ, BLOCK), jnp.bfloat16),
            pltpu.VMEM((ZH, SEQ, BLOCK), jnp.float32),
        ],
        input_output_aliases={4: 0},
        compiler_params=pltpu.CompilerParams(vmem_limit_bytes=20 * 1024 * 1024),
        name="section",
    )(info, values, allowed, rope, held, *blocks)


def gather_section(shard):
    block = lax.all_to_all(
        jnp.broadcast_to(shard[None], (2 * X, *shard.shape)), ("x", "core"), 0, 0
    ).reshape(BLOCK, QKV + CTX)

    def index(z, core):
        return ((z // ZL) * 2 + core) * ZL + z % ZL

    around = [
        (index(z, core), index((z + (1 if core == 0 else -1)) % Z, core))
        for z in range(Z)
        for core in range(2)
    ]
    ring, swap = [block], []
    for k in range(1, STEPS + 1):
        ring.append(lax.ppermute(ring[-1], ("z_hi", "core", "tensor"), around))
        if k < STEPS:
            swap.append(lax.ppermute(ring[-1], "core", [(0, 1), (1, 0)]))
    return ring + swap


def on_device(down_in, up_in, w_qkv, w_out, norm_gain, down_docs, up_docs):
    position = lax.axis_index("pipe")
    member = lax.axis_index("tensor")
    core = lax.axis_index("core")
    z = lax.axis_index("z_hi") * ZL + member
    sections = lax.axis_size("pipe")

    def pick(array, index):
        return lax.dynamic_index_in_dim(array, index, 0, keepdims=False)

    qkv = pick(w_qkv, position).astype(jnp.float32)
    qkv = qkv * pick(norm_gain, position).astype(jnp.float32)[:, None]
    qkv = qkv.astype(jnp.bfloat16)
    rows = qkv.shape[0]
    query = qkv[:, :256].reshape(rows, GROUP_HEADS, 2, 32).transpose(0, 2, 1, 3).reshape(rows, 256)
    shard = jnp.concatenate([query, qkv[:, 256:], pick(w_out, position).T], axis=1)
    blocks = gather_section(shard)

    offsets = np.array([0] + [-k if kind == "ring" else k for kind, k in BLOCKS], np.int32)
    places = ((z + (1 - 2 * core) * offsets) & (Z - 1)) >> 2
    info = jnp.where(np.arange(1 + Z) == 0, position, places).astype(jnp.int32)

    cos, sin = rotary_tables()
    one, zero = jnp.ones((SEQ, 64), jnp.float32), jnp.zeros((SEQ, 32), jnp.float32)
    rope = jnp.stack(
        [
            jnp.tile(cos, (1, 4)),
            jnp.tile(sin, (1, 4)),
            jnp.concatenate([cos, cos, one], axis=1),
            jnp.concatenate([-sin, zero, zero, zero], axis=1),
            jnp.concatenate([zero, sin, zero, zero], axis=1),
        ]
    )
    docs = pick(jnp.concatenate([down_docs, up_docs]), member)
    spots = jnp.arange(SEQ)
    allowed = (spots[:, None] >= spots[None, :]) & (docs[:, None] == docs[None, :])
    allowed = jnp.tile(allowed.astype(jnp.float32), (GROUP_HEADS, 1))

    values = pick(jnp.concatenate([down_in, up_in]), member)
    held = jnp.zeros((SEQ, D), jnp.bfloat16)
    for step in range(sections):
        held = run_section(step, info, values, allowed, rope, held, blocks)
        if step + 1 < sections:
            values = lax.ppermute(held, "pipe", [(step, step + 1)])

    parts = lax.all_to_all(held.reshape(4, SEQ // 4, D), "tensor", 0, 0)
    down = parts[:2]
    up = lax.ppermute(parts[2:], "pipe", [(i, sections - 1 - i) for i in range(sections)])
    return down[None], up[None]


def solution(mesh):
    fine = Mesh(
        mesh.devices.reshape(X, ZH, 2, *mesh.devices.shape[1:]),
        ("x", "z_hi", "core", "pipe", "tensor"),
    )
    dp = ("x", "z_hi", "core")
    placed = (
        P(dp, None, None),
        P(dp, None, None),
        P(None, dp, "tensor"),
        P(None, "tensor", dp),
        P(None, dp),
        P(dp, None),
        P(dp, None),
    )
    return jax.shard_map(
        on_device,
        mesh=fine,
        in_specs=placed,
        out_specs=(P("pipe", dp, "tensor", None), P("pipe", dp, "tensor", None)),
        check_vma=False,
    )
```

time: 1070 us -> 247 us (0.23)
  waiting for transfers between devices: 608 us -> 87.7 us
  blocking collectives: 300 us -> 33.6 us
  matrix products: 57.2 us -> 0 us
  starting transfers between devices: 42.4 us -> 98 us
  other arithmetic: 21.5 us -> 1.19 us
  Pallas kernels: 0 us -> 16.8 us
  between operations: 14.2 us -> 1.17 us
    reduce_scatter x18 -> x0, waiting for transfers between devices: 461 us -> none  [the longest x9 283 us: advance(): lax.psum_scatter(up_part.astype(jnp.bfloat16), 'tensor', scatter_dimensio...]
    all_gather x19 -> x0, blocking collectives: 300 us -> none  [the longest x9 121 us: advance(): lax.all_gather(up_y, 'tensor', axis=0, tiled=True)]
    all_gather x2 -> x0, waiting for transfers between devices: 124 us -> none  [the longest x1 86.6 us: on_device(): lax.all_gather(qkv_pair, 'dp', axis=1, tiled=True)]
    ppermute x18 -> x23, waiting for transfers between devices: 22.4 us -> 87.7 us  [the longest x8 83 us: gather_section(): ring.append(lax.ppermute(ring[-1], ('z_hi', 'core', 'tensor'), around))]
    dot_general x72 -> x0, matrix products: 57.2 us -> none  [the longest x18 32.1 us: attend(): projected = jnp.dot(normed, qkv_cols, preferred_element_type=jnp.float32)]
    ppermute x18 -> x23, starting transfers between devices: 41.9 us -> 98 us  [the longest x1 63 us: on_device(): lax.ppermute(parts[2:], 'pipe', [(i, sections - 1 - i) for i in range(sec...]
    all_to_all x0 -> x2, blocking collectives: none -> 33.6 us  [the longest x1 25.2 us: gather_section(): lax.all_to_all(jnp.broadcast_to(shard[None], (2 * X, *shard.shape)), ('x'...]
    pallas_call x0 -> x8, Pallas kernels: none -> 16.8 us  [run_section(): pl.pallas_call(functools.partial(section_kernel, step), out_shape=jax.Sha...]
  transfers between devices with their start and end apart: 38 -> 23, of which waited for: 29 -> 10; matrix products, arithmetic and copies ran while one was open for 3% -> 0% of each run, Pallas kernels for 0% -> 0%
where the time goes in v1:
time: 247 us; the launch traced here: 244 us
  starting transfers between devices  98 us (40%)
  waiting for transfers between devices  87.7 us (36%)
  blocking collectives  33.6 us (14%)
  Pallas kernels  16.8 us (7%)
  local copies, waits for them, and re-layouts  5.95 us (2%)
    ppermute x8, waiting for transfers between devices, gather_section(): ring.append(lax.ppermute(ring[-1], ('z_hi', 'core', 'tensor'), around))  83 us
    ppermute x1, starting transfers between devices, on_device(): lax.ppermute(parts[2:], 'pipe', [(i, sections - 1 - i) for i in range(sec...  63 us
    all_to_all x1, blocking collectives, gather_section(): lax.all_to_all(jnp.broadcast_to(shard[None], (2 * X, *shard.shape)), ('x'...  25.2 us
    pallas_call x8, Pallas kernels, run_section(): pl.pallas_call(functools.partial(section_kernel, step), out_shape=jax.Sha...  16.8 us
    ppermute x8, starting transfers between devices, gather_section(): ring.append(lax.ppermute(ring[-1], ('z_hi', 'core', 'tensor'), around))  15.3 us
    ppermute x7, starting transfers between devices, gather_section(): swap.append(lax.ppermute(ring[-1], 'core', [(0, 1), (1, 0)]))  14.4 us
    all_to_all x1, blocking collectives, on_device(): parts = lax.all_to_all(held.reshape(4, SEQ // 4, D), 'tensor', 0, 0)  8.31 us
    ppermute x7, starting transfers between devices, on_device(): values = lax.ppermute(held, 'pipe', [(step, step + 1)])  5.31 us
  transfers between devices with their start and end apart: 23, of which 10 were waited for; matrix products, arithmetic and copies ran while one was open for 0% of the time, Pallas kernels for 0%

profile of v1, /device:TPU:6, one launch (start us, length us, event | category | flops | bytes accessed | tf_op | source)
XLA Modules:
  0.0 244.4 jit_solution(2757782843335244185)
XLA Ops:
  5.0 25.2 %all_to_all.10 = bf16[8,64,640]{2,1,0:T(8,128)(2,1)S(1)} all-to-all(bf16[8,64,640]{2,1,0:T(8,128)(2,1)S(1)} %broadcast_in_dim.36), channel_id=1, replica_groups=mesh['x'=4,'z_hi'=4,'core'=2,'pipe'=8,'tensor'=4] {'x','core'}, dimensions={0} | all-to-all | bytes 1310720 | tf_op jit(solution)/shard_map/all_to_all | solution.py:148
  30.3 1.9 collective-permute-start
  32.2 13.9 %collective-permute-done.refs_1_ = bf16[512,640]{1,0:T(8,128)(2,1)S(1)} collective-permute-done((bf16[512,640]{1,0:T(8,128)(2,1)S(1)}, bf16[512,640]{1,0:T(8,128)(2,1)S(1)}, u32[]{:S(2)}, u32[]{:S(2)}) %collective-permute-start) | collective-permute-done | bytes 655392 | tf_op jit(solution)/shard_map/ppermute | solution.py:162
  48.0 11.8 %collective-permute-done.1.refs_2_ = bf16[512,640]{1,0:T(8,128)(2,1)S(1)} collective-permute-done((bf16[512,640]{1,0:T(8,128)(2,1)S(1)}, bf16[512,640]{1,0:T(8,128)(2,1)S(1)}, u32[]{:S(2)}, u32[]{:S(2)}) %collective-permute-start.1) | collective-permute-done | bytes 655392 | tf_op jit(solution)/shard_map/ppermute | solution.py:162
  61.7 11.8 %collective-permute-done.2.refs_3_ = bf16[512,640]{1,0:T(8,128)(2,1)S(1)} collective-permute-done((bf16[512,640]{1,0:T(8,128)(2,1)S(1)}, bf16[512,640]{1,0:T(8,128)(2,1)S(1)}, u32[]{:S(2)}, u32[]{:S(2)}) %collective-permute-start.2) | collective-permute-done | bytes 655392 | tf_op jit(solution)/shard_map/ppermute | solution.py:162
  73.5 1.9 collective-permute-start.3
  75.4 11.9 %collective-permute-done.3.refs_4_ = bf16[512,640]{1,0:T(8,128)(2,1)} collective-permute-done((bf16[512,640]{1,0:T(8,128)(2,1)S(1)}, bf16[512,640]{1,0:T(8,128)(2,1)}, u32[]{:S(2)}, u32[]{:S(2)}) %collective-permute-start.3) | collective-permute-done | bytes 655392 | tf_op jit(solution)/shard_map/ppermute | solution.py:162
  87.3 1.9 collective-permute-start.4
  89.4 11.9 %collective-permute-done.4.refs_5_ = bf16[512,640]{1,0:T(8,128)(2,1)} collective-permute-done((bf16[512,640]{1,0:T(8,128)(2,1)}, bf16[512,640]{1,0:T(8,128)(2,1)}, u32[]{:S(2)}, u32[]{:S(2)}) %collective-permute-start.4) | collective-permute-done | bytes 655392 | tf_op jit(solution)/shard_map/ppermute | solution.py:162
  101.3 1.9 collective-permute-start.5
  104.2 1.9 collective-permute-start.8
  106.2 2.4 collective-permute-start.9
  108.6 1.9 collective-permute-start.10
  110.5 4.7 %collective-permute-done.5.refs_6_ = bf16[512,640]{1,0:T(8,128)(2,1)} collective-permute-done((bf16[512,640]{1,0:T(8,128)(2,1)}, bf16[512,640]{1,0:T(8,128)(2,1)}, u32[]{:S(2)}, u32[]{:S(2)}) %collective-permute-start.5) | collective-permute-done | bytes 655392 | tf_op jit(solution)/shard_map/ppermute | solution.py:162
  119.3 2.4 collective-permute-start.12
  121.7 1.9 collective-permute-start.13
  123.6 5.5 %collective-permute-done.6.refs_7_ = bf16[512,640]{1,0:T(8,128)(2,1)S(1)} collective-permute-done((bf16[512,640]{1,0:T(8,128)(2,1)}, bf16[512,640]{1,0:T(8,128)(2,1)S(1)}, u32[]{:S(2)}, u32[]{:S(2)}) %collective-permute-start.6) | collective-permute-done | bytes 655392 | tf_op jit(solution)/shard_map/ppermute | solution.py:162
  131.1 1.9 collective-permute-start.7
  133.2 11.5 %collective-permute-done.7.refs_8_ = bf16[512,640]{1,0:T(8,128)(2,1)S(1)} collective-permute-done((bf16[512,640]{1,0:T(8,128)(2,1)S(1)}, bf16[512,640]{1,0:T(8,128)(2,1)S(1)}, u32[]{:S(2)}, u32[]{:S(2)}) %collective-permute-start.7) | collective-permute-done | bytes 655392 | tf_op jit(solution)/shard_map/ppermute | solution.py:162
  144.8 5.9 %section.8.held_ref = bf16[32,2048]{1,0:T(8,128)(2,1)S(1)} custom-call(s32[17]{0:T(128)S(1)} %shift-right-arithmetic_select_fusion.info, bf16[32,2048]{1,0:T(8,128)(2,1)S(1)} %fusion.2.x_ref, f32[128,32]{1,0:T(8,128)S(1)} %bitcast.45, f32[5,32,128]{2,1,0:T(8,128)S(1)} %fusion.4.rope_ref, ...), custom_call_target="tpu_custom_call", output_to_operand_aliasing={{}: (4, {})} | custom-call | tf_op jit(solution)/shard_map/section/pallas_call | solution.py:132
  152.0 2.5 %collective-permute-done.15.x_ref = bf16[32,2048]{1,0:T(8,128)(2,1)S(1)} collective-permute-done((bf16[32,2048]{1,0:T(8,128)(2,1)S(1)}, bf16[32,2048]{1,0:T(8,128)(2,1)S(1)}, u32[]{:S(2)}, u32[]{:S(2)}) %collective-permute-start.15) | collective-permute-done | bytes 131104 | tf_op jit(solution)/shard_map/ppermute | solution.py:211
  169.5 8.3 %all_to_all.11 = bf16[4,8,2048]{2,1,0:T(8,128)(2,1)S(1)} all-to-all(bf16[4,8,2048]{2,1,0:T(8,128)(2,1)S(1)} %bitcast.44), channel_id=1, replica_groups=mesh['x'=4,'z_hi'=4,'core'=2,'pipe'=8,'tensor'=4] {'tensor'}, dimensions={0} | all-to-all | bytes 262144 | tf_op jit(solution)/shard_map/all_to_all | solution.py:213
  178.5 63.0 %collective-permute-start.22 = (bf16[2,8,2048]{2,1,0:T(8,128)(2,1)S(1)}, bf16[2,8,2048]{2,1,0:T(8,128)(2,1)S(1)}, u32[]{:S(2)}, u32[]{:S(2)}) collective-permute-start(bf16[2,8,2048]{2,1,0:T(8,128)(2,1)S(1)} %get-tuple-element.2), channel_id=1, source_target_pairs={{0,28},{4,24},{8,20},{12,16},{16,12},{20,8},{24,4},{28,0},{1,29},{... | collective-permute-start | bytes 196616 | tf_op jit(solution)/shard_map/ppermute | solution.py:215
  241.5 2.2 collective-permute-done.22
  (86 shorter events, 32.9 us)
Async XLA Ops:
  30.3 15.8 %collective-permute-start = (bf16[512,640]{1,0:T(8,128)(2,1)S(1)}, bf16[512,640]{1,0:T(8,128)(2,1)S(1)}, u32[]{:S(2)}, u32[]{:S(2)}) collective-permute-start(bf16[512,640]{1,0:T(8,128)(2,1)S(1)} %bitcast.35), channel_id=1, source_target_pairs={{0,1},{32,227},{1,2},{33,32},{2,3},{34,33},{3,64},{35,34},{64,65},... | collective-permute-start | bytes 1966088 | tf_op jit(solution)/shard_map/ppermute | solution.py:162
  46.1 13.7 %collective-permute-start.1 = (bf16[512,640]{1,0:T(8,128)(2,1)S(1)}, bf16[512,640]{1,0:T(8,128)(2,1)S(1)}, u32[]{:S(2)}, u32[]{:S(2)}) collective-permute-start(bf16[512,640]{1,0:T(8,128)(2,1)S(1)} %collective-permute-done.refs_1_), channel_id=1, source_target_pairs={{0,1},{32,227},{1,2},{33,32},{2,3},{34,33},{3,64},{35,34},{64,65},... | collective-permute-start | bytes 1966088 | tf_op jit(solution)/shard_map/ppermute | solution.py:162
  59.8 13.7 %collective-permute-start.2 = (bf16[512,640]{1,0:T(8,128)(2,1)S(1)}, bf16[512,640]{1,0:T(8,128)(2,1)S(1)}, u32[]{:S(2)}, u32[]{:S(2)}) collective-permute-start(bf16[512,640]{1,0:T(8,128)(2,1)S(1)} %collective-permute-done.1.refs_2_), channel_id=1, source_target_pairs={{0,1},{32,227},{1,2},{33,32},{2,3},{34,33},{3,64},{35,34},{64,65},... | collective-permute-start | bytes 1966088 | tf_op jit(solution)/shard_map/ppermute | solution.py:162
  73.5 13.8 %collective-permute-start.3 = (bf16[512,640]{1,0:T(8,128)(2,1)S(1)}, bf16[512,640]{1,0:T(8,128)(2,1)}, u32[]{:S(2)}, u32[]{:S(2)}) collective-permute-start(bf16[512,640]{1,0:T(8,128)(2,1)S(1)} %collective-permute-done.2.refs_3_), channel_id=1, source_target_pairs={{0,1},{32,227},{1,2},{33,32},{2,3},{34,33},{3,64},{35,34},{64,65},... | collective-permute-start | bytes 1966088 | tf_op jit(solution)/shard_map/ppermute | solution.py:162
  87.3 14.0 %collective-permute-start.4 = (bf16[512,640]{1,0:T(8,128)(2,1)}, bf16[512,640]{1,0:T(8,128)(2,1)}, u32[]{:S(2)}, u32[]{:S(2)}) collective-permute-start(bf16[512,640]{1,0:T(8,128)(2,1)} %collective-permute-done.3.refs_4_), channel_id=1, source_target_pairs={{0,1},{32,227},{1,2},{33,32},{2,3},{34,33},{3,64},{35,34},{64,65},... | collective-permute-start | bytes 1966088 | tf_op jit(solution)/shard_map/ppermute | solution.py:162
  101.3 14.0 %collective-permute-start.5 = (bf16[512,640]{1,0:T(8,128)(2,1)}, bf16[512,640]{1,0:T(8,128)(2,1)}, u32[]{:S(2)}, u32[]{:S(2)}) collective-permute-start(bf16[512,640]{1,0:T(8,128)(2,1)} %collective-permute-done.4.refs_5_), channel_id=1, source_target_pairs={{0,1},{32,227},{1,2},{33,32},{2,3},{34,33},{3,64},{35,34},{64,65},... | collective-permute-start | bytes 1966088 | tf_op jit(solution)/shard_map/ppermute | solution.py:162
  103.3 29.8 %copy-start.2 = (bf16[2,32,2048]{2,1,0:T(8,128)(2,1)S(1)}, bf16[2,32,2048]{2,1,0:T(8,128)(2,1)}, u32[]{:S(2)}) copy-start(bf16[2,32,2048]{2,1,0:T(8,128)(2,1)} %param.9) | copy-start | bytes 786436
  104.2 15.0 %collective-permute-start.8 = (bf16[512,640]{1,0:T(8,128)(2,1)S(1)}, bf16[512,640]{1,0:T(8,128)(2,1)S(1)}, u32[]{:S(2)}, u32[]{:S(2)}) collective-permute-start(bf16[512,640]{1,0:T(8,128)(2,1)S(1)} %collective-permute-done.refs_1_), channel_id=1, source_target_pairs={{0,32},{32,0},{1,33},{33,1},{2,34},{34,2},{3,35},{35,3},{4,36},{36... | collective-permute-start | bytes 1966088 | tf_op jit(solution)/shard_map/ppermute | solution.py:164
  106.2 15.5 %collective-permute-start.9 = (bf16[512,640]{1,0:T(8,128)(2,1)S(1)}, bf16[512,640]{1,0:T(8,128)(2,1)S(1)}, u32[]{:S(2)}, u32[]{:S(2)}) collective-permute-start(bf16[512,640]{1,0:T(8,128)(2,1)S(1)} %collective-permute-done.1.refs_2_), channel_id=1, source_target_pairs={{0,32},{32,0},{1,33},{33,1},{2,34},{34,2},{3,35},{35,3},{4,36},{36... | collective-permute-start | bytes 1966088 | tf_op jit(solution)/shard_map/ppermute | solution.py:164
  108.6 22.5 %collective-permute-start.10 = (bf16[512,640]{1,0:T(8,128)(2,1)S(1)}, bf16[512,640]{1,0:T(8,128)(2,1)S(1)}, u32[]{:S(2)}, u32[]{:S(2)}) collective-permute-start(bf16[512,640]{1,0:T(8,128)(2,1)S(1)} %collective-permute-done.2.refs_3_), channel_id=1, source_target_pairs={{0,32},{32,0},{1,33},{33,1},{2,34},{34,2},{3,35},{35,3},{4,36},{36... | collective-permute-start | bytes 1966088 | tf_op jit(solution)/shard_map/ppermute | solution.py:164
  115.3 13.9 %collective-permute-start.6 = (bf16[512,640]{1,0:T(8,128)(2,1)}, bf16[512,640]{1,0:T(8,128)(2,1)S(1)}, u32[]{:S(2)}, u32[]{:S(2)}) collective-permute-start(bf16[512,640]{1,0:T(8,128)(2,1)} %collective-permute-done.5.refs_6_), channel_id=1, source_target_pairs={{0,1},{32,227},{1,2},{33,32},{2,3},{34,33},{3,64},{35,34},{64,65},... | collective-permute-start | bytes 1966088 | tf_op jit(solution)/shard_map/ppermute | solution.py:162
  117.4 15.8 %collective-permute-start.11 = (bf16[512,640]{1,0:T(8,128)(2,1)}, bf16[512,640]{1,0:T(8,128)(2,1)S(1)}, u32[]{:S(2)}, u32[]{:S(2)}) collective-permute-start(bf16[512,640]{1,0:T(8,128)(2,1)} %collective-permute-done.3.refs_4_), channel_id=1, source_target_pairs={{0,32},{32,0},{1,33},{33,1},{2,34},{34,2},{3,35},{35,3},{4,36},{36... | collective-permute-start | bytes 1966088 | tf_op jit(solution)/shard_map/ppermute | solution.py:164
  119.3 13.9 %collective-permute-start.12 = (bf16[512,640]{1,0:T(8,128)(2,1)}, bf16[512,640]{1,0:T(8,128)(2,1)S(1)}, u32[]{:S(2)}, u32[]{:S(2)}) collective-permute-start(bf16[512,640]{1,0:T(8,128)(2,1)} %collective-permute-done.4.refs_5_), channel_id=1, source_target_pairs={{0,32},{32,0},{1,33},{33,1},{2,34},{34,2},{3,35},{35,3},{4,36},{36... | collective-permute-start | bytes 1966088 | tf_op jit(solution)/shard_map/ppermute | solution.py:164
  121.7 11.5 %collective-permute-start.13 = (bf16[512,640]{1,0:T(8,128)(2,1)}, bf16[512,640]{1,0:T(8,128)(2,1)S(1)}, u32[]{:S(2)}, u32[]{:S(2)}) collective-permute-start(bf16[512,640]{1,0:T(8,128)(2,1)} %collective-permute-done.5.refs_6_), channel_id=1, source_target_pairs={{0,32},{32,0},{1,33},{33,1},{2,34},{34,2},{3,35},{35,3},{4,36},{36... | collective-permute-start | bytes 1966088 | tf_op jit(solution)/shard_map/ppermute | solution.py:164
  129.1 4.1 %collective-permute-start.14 = (bf16[512,640]{1,0:T(8,128)(2,1)S(1)}, bf16[512,640]{1,0:T(8,128)(2,1)S(1)}, u32[]{:S(2)}, u32[]{:S(2)}) collective-permute-start(bf16[512,640]{1,0:T(8,128)(2,1)S(1)} %collective-permute-done.6.refs_7_), channel_id=1, source_target_pairs={{0,32},{32,0},{1,33},{33,1},{2,34},{34,2},{3,35},{35,3},{4,36},{36... | collective-permute-start | bytes 1966088 | tf_op jit(solution)/shard_map/ppermute | solution.py:164
  131.1 13.7 %collective-permute-start.7 = (bf16[512,640]{1,0:T(8,128)(2,1)S(1)}, bf16[512,640]{1,0:T(8,128)(2,1)S(1)}, u32[]{:S(2)}, u32[]{:S(2)}) collective-permute-start(bf16[512,640]{1,0:T(8,128)(2,1)S(1)} %collective-permute-done.6.refs_7_), channel_id=1, source_target_pairs={{0,1},{32,227},{1,2},{33,32},{2,3},{34,33},{3,64},{35,34},{64,65},... | collective-permute-start | bytes 1966088 | tf_op jit(solution)/shard_map/ppermute | solution.py:162
  150.7 3.8 %collective-permute-start.15 = (bf16[32,2048]{1,0:T(8,128)(2,1)S(1)}, bf16[32,2048]{1,0:T(8,128)(2,1)S(1)}, u32[]{:S(2)}, u32[]{:S(2)}) collective-permute-start(bf16[32,2048]{1,0:T(8,128)(2,1)S(1)} %section.8.held_ref), channel_id=1, source_target_pairs={{0,4},{1,5},{2,6},{3,7},{32,36},{33,37},{34,38},{35,39},{64,68},{6... | collective-permute-start | bytes 393224 | tf_op jit(solution)/shard_map/ppermute | solution.py:211
  156.0 0.7 collective-permute-start.16
  158.2 0.7 collective-permute-start.17
  160.6 0.7 collective-permute-start.18
  162.9 0.7 collective-permute-start.19
  165.1 0.7 collective-permute-start.20
  167.3 0.7 collective-permute-start.21
  178.5 65.3 %collective-permute-start.22 = (bf16[2,8,2048]{2,1,0:T(8,128)(2,1)S(1)}, bf16[2,8,2048]{2,1,0:T(8,128)(2,1)S(1)}, u32[]{:S(2)}, u32[]{:S(2)}) collective-permute-start(bf16[2,8,2048]{2,1,0:T(8,128)(2,1)S(1)} %get-tuple-element.2), channel_id=1, source_target_pairs={{0,28},{4,24},{8,20},{12,16},{16,12},{20,8},{24,4},{28,0},{1,29},{... | collective-permute-start | bytes 196616 | tf_op jit(solution)/shard_map/ppermute | solution.py:215
  (8 other events, 36.1 us)

commit v2 on v1

v2 whole, which is shorter than its diff:
```python
import functools

import jax
import jax.numpy as jnp
import numpy as np
from jax import lax
from jax.experimental import pallas as pl
from jax.experimental.pallas import tpu as pltpu
from jax.sharding import Mesh, PartitionSpec as P

HEAD_DIM = 64
SEQ = 32
D = 2048
EPSILON = 1e-05
THETA = 500000.0

GROUPS = 4
GROUP_HEADS = 4
QKV = 384
CTX = 256
X = 4
ZH = 4
ZL = 4
Z = ZH * ZL
STEPS = Z // 2
ROWS = 256

OFFSETS = [-k for k in range(STEPS + 1)] + list(range(1, STEPS))

F32, BF16 = jnp.float32, jnp.bfloat16


def rotary_tables():
    half = HEAD_DIM // 2
    frequency = THETA ** (-(jnp.arange(half, dtype=jnp.float32) * 2.0 / HEAD_DIM))
    angles = jnp.arange(SEQ, dtype=jnp.float32)[:, None] * frequency[None, :]
    return jnp.cos(angles), jnp.sin(angles)


def attention(projected, rope, allowed):
    lane = lax.broadcasted_iota(jnp.int32, (SEQ, 128), 1)
    lane2 = lax.broadcasted_iota(jnp.int32, (SEQ, 256), 1)
    head_of = (lane2 % 128) // 32
    zero = jnp.zeros((), BF16)
    cos, sin, kcos, ksin_a, ksin_b = rope
    queries, keys, values = [], [], []
    for part in projected:
        first, second = part[:, :128], part[:, 128:256]
        query = jnp.concatenate(
            [first * cos - second * sin, second * cos + first * sin], axis=-1
        ).astype(BF16)
        queries.append(
            jnp.concatenate([jnp.where(head_of == h, query, zero) for h in range(GROUP_HEADS)], axis=0)
        )
    for part in projected:
        kv = part[:, 256:]
        kv = kv * kcos + pltpu.roll(kv, 96, 1) * ksin_a + pltpu.roll(kv, 32, 1) * ksin_b
        key_a = jnp.where(lane < 32, kv, 0.0)
        key_a = key_a + pltpu.roll(key_a, 32, 1)
        key_a = key_a + pltpu.roll(key_a, 64, 1)
        key_b = jnp.where((lane >= 32) & (lane < 64), kv, 0.0)
        key_b = key_b + pltpu.roll(key_b, 32, 1)
        key_b = key_b + pltpu.roll(key_b, 64, 1)
        keys.append(jnp.concatenate([key_a, key_b], axis=-1).astype(BF16))
        values.append(kv.astype(BF16))
    scores = [
        lax.dot_general(q, k, (((1,), (1,)), ((), ())), preferred_element_type=F32)
        for q, k in zip(queries, keys)
    ]
    scores = [jnp.where(allowed, s * HEAD_DIM ** (-0.5), -1e30) for s in scores]
    scores = [jnp.exp(s - jnp.max(s, axis=-1, keepdims=True)) for s in scores]
    weights = [(s * (1.0 / jnp.sum(s, axis=-1, keepdims=True))).astype(BF16) for s in scores]
    contexts = []
    for weight, value in zip(weights, values):
        mixed = jnp.dot(weight, value, preferred_element_type=F32)
        rows = [mixed[h * SEQ : (h + 1) * SEQ] for h in range(GROUP_HEADS)]
        context = jnp.concatenate(
            [
                jnp.where(lane < 64, pltpu.roll(rows[0], 64, 1), rows[1]),
                jnp.where(lane < 64, pltpu.roll(rows[2], 64, 1), rows[3]),
            ],
            axis=-1,
        )
        contexts.append(context.astype(BF16))
    return contexts


def section_kernel(step, last, info, x_ref, allowed_ref, rope_ref, held_ref, *refs):
    blocks, refs = refs[: 2 * Z], refs[2 * Z :]
    out_ref, xs, total = refs[0], refs[-2], refs[-1]

    @pl.when(info[0] != step)
    def _():
        out_ref[...] = held_ref[...]

    @pl.when(info[0] == step)
    def _():
        squares = jnp.zeros((SEQ, 1), F32)
        for j in range(2 * ZH):
            part = x_ref[:, pl.ds(j * ROWS, ROWS)]
            xs[j] = part
            wide = part.astype(F32)
            total[j] = wide
            squares = squares + jnp.sum(wide * wide, axis=-1, keepdims=True)
        scale = lax.rsqrt(squares * (1.0 / D) + EPSILON)

        projected = []
        for c in range(GROUPS):
            terms = [
                jnp.dot(xs[info[1 + i]], blocks[i][:, :QKV], preferred_element_type=F32)
                for i in range(2 * Z)
                if OFFSETS[i % Z] % ZL == c
            ]
            projected.append(functools.reduce(jnp.add, terms) * scale)
        contexts = attention(projected, [rope_ref[i] for i in range(5)], allowed_ref[...] > 0.5)
        for i in range(2 * Z):
            j = info[1 + i]
            total[j] = total[j] + jnp.dot(
                contexts[OFFSETS[i % Z] % ZL], blocks[i][:, QKV:], preferred_element_type=F32
            )

        if not last:
            for j in range(2 * ZH):
                refs[1][:, pl.ds(j * ROWS, ROWS)] = total[j].astype(BF16)
        lane = lax.broadcasted_iota(jnp.int32, (SEQ, 128), 1)
        for zh in range(ZH):
            for pair in range(2):
                one = total[zh, :, pl.ds(pair * 128, 128)]
                two = total[ZH + zh, :, pl.ds(pair * 128, 128)]
                even = jnp.where(lane < 64, one, pltpu.roll(two, 64, 1))
                odd = jnp.where(lane < 64, pltpu.roll(one, 64, 1), two)
                out_ref[:, pl.ds(2 * pair * 512 + zh * 128, 128)] = even.astype(BF16)
                out_ref[:, pl.ds((2 * pair + 1) * 512 + zh * 128, 128)] = odd.astype(BF16)


def run_section(step, last, info, values, allowed, rope, held, blocks):
    vmem = pl.BlockSpec(memory_space=pltpu.VMEM)
    shape = jax.ShapeDtypeStruct((SEQ, D), BF16)
    return pl.pallas_call(
        functools.partial(section_kernel, step, last),
        out_shape=[shape] if last else [shape, shape],
        in_specs=[pl.BlockSpec(memory_space=pltpu.SMEM)] + [vmem] * (4 + 2 * Z),
        out_specs=[vmem] if last else [vmem, vmem],
        scratch_shapes=[
            pltpu.VMEM((2 * ZH, SEQ, ROWS), BF16),
            pltpu.VMEM((2 * ZH, SEQ, ROWS), F32),
        ],
        input_output_aliases={4: 0},
        compiler_params=pltpu.CompilerParams(vmem_limit_bytes=20 * 1024 * 1024),
        name="section",
    )(info, values, allowed, rope, held, *blocks)


def shard_kernel(where, qkv_ref, out_ref, gain_ref, shard_ref):
    rows = qkv_ref.shape[1]
    section = lax.broadcasted_iota(jnp.int32, gain_ref.shape, 0)
    gain = jnp.where(section == where[0], gain_ref[...].astype(F32), 0.0)
    gain = jnp.sum(gain, axis=0, keepdims=True)
    row = lax.broadcasted_iota(jnp.int32, (rows, rows), 0)
    column = lax.broadcasted_iota(jnp.int32, (rows, rows), 1)
    gain = jnp.sum(jnp.where(row == column, gain, 0.0), axis=1, keepdims=True)
    qkv = qkv_ref[0].astype(F32) * gain
    one, two = qkv[:, :128], qkv[:, 128:256]
    lane = lax.broadcasted_iota(jnp.int32, (rows, 128), 1)

    def lanes(parts):
        result = parts[3]
        for i in (2, 1, 0):
            result = jnp.where(lane < 32 * (i + 1), parts[i], result)
        return result

    first = lanes([one, pltpu.roll(one, 96, 1), pltpu.roll(two, 64, 1), pltpu.roll(two, 32, 1)])
    second = lanes([pltpu.roll(one, 96, 1), pltpu.roll(one, 64, 1), pltpu.roll(two, 32, 1), two])
    shard = jnp.concatenate([first, second, qkv[:, 256:]], axis=1).astype(BF16)
    for x in range(X):
        shard_ref[x, :, pl.ds(0, QKV)] = shard
        shard_ref[x, :, pl.ds(QKV, CTX)] = out_ref[0]


def block_kernel(parts_ref, block_ref):
    rows = parts_ref.shape[1]
    for x in range(X):
        block_ref[pl.ds(x * rows, rows), pl.ds(0, QKV)] = parts_ref[x, :, pl.ds(0, QKV)]
    columns = jnp.concatenate([parts_ref[x, :, pl.ds(QKV, CTX)] for x in range(X)], axis=0)
    block_ref[:, pl.ds(QKV, CTX)] = columns.astype(F32).T.astype(BF16)


def gather_section(position, w_qkv, w_out, norm_gain):
    rows = w_qkv.shape[1]
    vmem = pl.BlockSpec(memory_space=pltpu.VMEM)
    shard = pl.pallas_call(
        shard_kernel,
        out_shape=jax.ShapeDtypeStruct((X, rows, QKV + CTX), BF16),
        grid_spec=pltpu.PrefetchScalarGridSpec(
            num_scalar_prefetch=1,
            grid=(1,),
            in_specs=[
                pl.BlockSpec((1, rows, QKV), lambda i, where: (where[0], 0, 0)),
                pl.BlockSpec((1, rows, CTX), lambda i, where: (where[0], 0, 0)),
                pl.BlockSpec(norm_gain.shape, lambda i, where: (0, 0)),
            ],
            out_specs=pl.BlockSpec((X, rows, QKV + CTX), lambda i, where: (0, 0, 0)),
        ),
        name="shard",
    )(position.reshape(1), w_qkv, w_out.transpose(0, 2, 1), norm_gain)
    block = pl.pallas_call(
        block_kernel,
        out_shape=jax.ShapeDtypeStruct((ROWS, QKV + CTX), BF16),
        in_specs=[vmem],
        out_specs=vmem,
        name="block",
    )(lax.all_to_all(shard, "x", 0, 0))

    axes = ("z_hi", "tensor")
    forward = [(z, (z + 1) % Z) for z in range(Z)]
    backward = [(z, (z - 1) % Z) for z in range(Z)]

    def swapped(value):
        return lax.ppermute(value, "core", [(0, 1), (1, 0)])

    own = {0: block}
    other = {}
    for k in range(1, STEPS + 1):
        ahead, behind = own[1 - k], own[k - 1]
        if k >= 2:
            other[2 - k], ahead = lax.optimization_barrier((other[2 - k], ahead))
        if k >= 3:
            other[k - 2], behind = lax.optimization_barrier((other[k - 2], behind))
        own[-k] = lax.ppermute(ahead, axes, forward)
        if k < STEPS:
            own[k] = lax.ppermute(behind, axes, backward)
        for i in sorted({1 - k, k - 1}):
            other[i] = swapped(own[i])
    other[-STEPS] = swapped(own[-STEPS])
    return [own[i] for i in OFFSETS] + [other[i] for i in OFFSETS]


def order_kernel(member, *refs):
    *received, down_ref, up_ref = refs
    for k, part in enumerate(received):
        source = (member[0] + len(received) - k) % len(received)

        @pl.when(source < 2)
        def _():
            down_ref[0, source] = part[...]

        @pl.when(source >= 2)
        def _():
            up_ref[0, source - 2] = part[...]


def exchange(held, member):
    planes, members = lax.axis_size("pipe"), lax.axis_size("tensor")
    rows = SEQ // members
    received = []
    for k in range(members):
        chunk = lax.dynamic_slice_in_dim(held, ((member + k) % members) * rows, rows, 0)
        pairs = [
            (y * members + t, (y if t < 2 else planes - 1 - y) * members + (t + k) % members)
            for y in range(planes)
            for t in range(members)
        ]
        received.append(lax.ppermute(chunk, ("pipe", "tensor"), pairs))
    vmem = pl.BlockSpec(memory_space=pltpu.VMEM)
    shape = jax.ShapeDtypeStruct((1, members // 2, rows, D), BF16)
    return pl.pallas_call(
        order_kernel,
        out_shape=[shape, shape],
        in_specs=[pl.BlockSpec(memory_space=pltpu.SMEM)] + [vmem] * members,
        out_specs=[vmem, vmem],
        name="order",
    )(member.reshape(1), *received)


def on_device(down_in, up_in, w_qkv, w_out, norm_gain, down_docs, up_docs):
    position = lax.axis_index("pipe")
    member = lax.axis_index("tensor")
    core = lax.axis_index("core")
    z = lax.axis_index("z_hi") * ZL + member
    sections = lax.axis_size("pipe")

    def pick(array, index):
        return lax.dynamic_index_in_dim(array, index, 0, keepdims=False)

    blocks = gather_section(position, w_qkv, w_out, norm_gain)

    offsets = np.array([0] + OFFSETS + OFFSETS, np.int32)
    mine = np.arange(1 + 2 * Z) <= Z
    parts = jnp.where(mine, core, 1 - core) * ZH + (((z + offsets) & (Z - 1)) >> 2)
    info = jnp.where(np.arange(1 + 2 * Z) == 0, position, parts).astype(jnp.int32)

    cos, sin = rotary_tables()
    one, zero = jnp.ones((SEQ, 64), F32), jnp.zeros((SEQ, 32), F32)
    rope = jnp.stack(
        [
            jnp.tile(cos, (1, 4)),
            jnp.tile(sin, (1, 4)),
            jnp.concatenate([cos, cos, one], axis=1),
            jnp.concatenate([-sin, zero, zero, zero], axis=1),
            jnp.concatenate([zero, sin, zero, zero], axis=1),
        ]
    )
    docs = pick(jnp.concatenate([down_docs, up_docs]), member)
    spots = jnp.arange(SEQ)
    allowed = (spots[:, None] >= spots[None, :]) & (docs[:, None] == docs[None, :])
    allowed = jnp.tile(allowed.astype(F32), (GROUP_HEADS, 1))

    values = pick(jnp.concatenate([down_in, up_in]), member)
    values = values.reshape(SEQ, X, ZH, 2, 64).transpose(0, 3, 2, 1, 4).reshape(SEQ, D)
    held = jnp.zeros((SEQ, D), BF16)
    for step in range(sections):
        last = step + 1 == sections
        held, *following = run_section(step, last, info, values, allowed, rope, held, blocks)
        if not last:
            values = lax.ppermute(following[0], "pipe", [(step, step + 1)])
    return exchange(held, member)


def solution(mesh):
    fine = Mesh(
        mesh.devices.reshape(X, ZH, 2, *mesh.devices.shape[1:]),
        ("x", "z_hi", "core", "pipe", "tensor"),
    )
    dp = ("x", "z_hi", "core")
    placed = (
        P(dp, None, None),
        P(dp, None, None),
        P(None, dp, "tensor"),
        P(None, "tensor", dp),
        P(None, dp),
        P(dp, None),
        P(dp, None),
    )
    return jax.shard_map(
        on_device,
        mesh=fine,
        in_specs=placed,
        out_specs=(P("pipe", dp, "tensor", None), P("pipe", dp, "tensor", None)),
        check_vma=False,
    )
```

time: 247 us -> 246 us (level)
  the two profiles are of different devices: /device:TPU:6 before, /device:TPU:64 now
where the time goes in v2:
time: 246 us; the launch traced here: 244 us
  starting transfers between devices  157 us (64%)
  waiting for transfers between devices  27.6 us (11%)
  local copies, waits for them, and re-layouts  22.7 us (9%)
  Pallas kernels  21.4 us (9%)
  blocking collectives  11.8 us (5%)
    ppermute x4, starting transfers between devices, exchange(): received.append(lax.ppermute(chunk, ('pipe', 'tensor'), pairs))  58.1 us
    ppermute x7, starting transfers between devices, gather_section(): own[k] = lax.ppermute(behind, axes, backward)  43.3 us
    ppermute x16, starting transfers between devices, swapped(): return lax.ppermute(value, 'core', [(0, 1), (1, 0)])  32.2 us
    ppermute x8, starting transfers between devices, gather_section(): own[-k] = lax.ppermute(ahead, axes, forward)  17.7 us
    unnamed x91, local copies, waits for them, and re-layouts  17.7 us
    pallas_call x8, Pallas kernels, run_section(): pl.pallas_call(functools.partial(section_kernel, step, last), out_shape=[...  16.4 us
    ppermute x8, waiting for transfers between devices, gather_section(): own[-k] = lax.ppermute(ahead, axes, forward)  12.1 us
    all_to_all x1, blocking collectives, gather_section(): lax.all_to_all(shard, 'x', 0, 0)  11.8 us
  transfers between devices with their start and end apart: 42, of which 14 were waited for; matrix products, arithmetic and copies ran while one was open for 3% of the time, Pallas kernels for 0%

profile of v2, /device:TPU:64, one launch (start us, length us, event | category | flops | bytes accessed | tf_op | source)
XLA Modules:
  0.0 243.6 jit_solution(14281703732030923127)
XLA Ops:
  2.4 11.8 %all_to_all.5.parts_ref = bf16[4,64,640]{2,1,0:T(8,128)(2,1)} all-to-all(bf16[4,64,640]{2,1,0:T(8,128)(2,1)} %shard.1), channel_id=1, replica_groups=mesh['x'=4,'z_hi'=4,'core'=2,'pipe'=8,'tensor'=4] {'x'}, dimensions={0} | all-to-all | bytes 655360 | tf_op jit(solution)/shard_map/all_to_all | solution.py:212
  16.0 4.3 %collective-permute-start = (bf16[256,640]{1,0:T(8,128)(2,1)}, bf16[256,640]{1,0:T(8,128)(2,1)S(1)}, u32[]{:S(2)}, u32[]{:S(2)}) collective-permute-start(bf16[256,640]{1,0:T(8,128)(2,1)} %block.1.refs_0_), channel_id=1, source_target_pairs={{0,1},{1,2},{2,3},{3,64},{64,65},{65,66},{66,67},{67,128},{128,129... | collective-permute-start | bytes 983048 | tf_op jit(solution)/shard_map/ppermute | solution.py:229
  22.2 11.2 %collective-permute-start.15 = (bf16[256,640]{1,0:T(8,128)(2,1)}, bf16[256,640]{1,0:T(8,128)(2,1)S(1)}, u32[]{:S(2)}, u32[]{:S(2)}) collective-permute-start(bf16[256,640]{1,0:T(8,128)(2,1)} %block.1.refs_0_), channel_id=1, source_target_pairs={{0,195},{1,0},{2,1},{3,2},{64,3},{65,64},{66,65},{67,66},{128,67},... | collective-permute-start | bytes 983048 | tf_op jit(solution)/shard_map/ppermute | solution.py:231
  38.7 2.7 %collective-permute-done.15.refs_9_ = bf16[256,640]{1,0:T(8,128)(2,1)S(1)} collective-permute-done((bf16[256,640]{1,0:T(8,128)(2,1)}, bf16[256,640]{1,0:T(8,128)(2,1)S(1)}, u32[]{:S(2)}, u32[]{:S(2)}) %collective-permute-start.15) | collective-permute-done | bytes 327712 | tf_op jit(solution)/shard_map/ppermute | solution.py:231
  41.4 6.2 %collective-permute-start.16 = (bf16[256,640]{1,0:T(8,128)(2,1)S(1)}, bf16[256,640]{1,0:T(8,128)(2,1)S(1)}, u32[]{:S(2)}, u32[]{:S(2)}) collective-permute-start(bf16[256,640]{1,0:T(8,128)(2,1)S(1)} %collective-permute-done.15.refs_9_), channel_id=1, source_target_pairs={{0,195},{1,0},{2,1},{3,2},{64,3},{65,64},{66,65},{67,66},{128,67},... | collective-permute-start | bytes 983048 | tf_op jit(solution)/shard_map/ppermute | solution.py:231
  51.4 2.4 collective-permute-start.5
  54.4 5.5 %collective-permute-start.18 = (bf16[256,640]{1,0:T(8,128)(2,1)S(1)}, bf16[256,640]{1,0:T(8,128)(2,1)}, u32[]{:S(2)}, u32[]{:S(2)}) collective-permute-start(bf16[256,640]{1,0:T(8,128)(2,1)S(1)} %collective-permute-done.16.refs_10_), channel_id=1, source_target_pairs={{0,195},{1,0},{2,1},{3,2},{64,3},{65,64},{66,65},{67,66},{128,67},... | collective-permute-start | bytes 983048 | tf_op jit(solution)/shard_map/ppermute | solution.py:231
  65.3 1.9 collective-permute-start.7
  73.5 4.8 %collective-permute-start.20 = (bf16[256,640]{1,0:T(8,128)(2,1)}, bf16[256,640]{1,0:T(8,128)(2,1)}, u32[]{:S(2)}, u32[]{:S(2)}) collective-permute-start(bf16[256,640]{1,0:T(8,128)(2,1)} %collective-permute-done.18.refs_11_), channel_id=1, source_target_pairs={{0,195},{1,0},{2,1},{3,2},{64,3},{65,64},{66,65},{67,66},{128,67},... | collective-permute-start | bytes 983048 | tf_op jit(solution)/shard_map/ppermute | solution.py:231
  78.4 2.1 collective-permute-start.21
  80.5 1.9 collective-permute-start.8
  82.5 2.2 collective-permute-start.9
  86.3 5.1 %collective-permute-start.22 = (bf16[256,640]{1,0:T(8,128)(2,1)}, bf16[256,640]{1,0:T(8,128)(2,1)S(1)}, u32[]{:S(2)}, u32[]{:S(2)}) collective-permute-start(bf16[256,640]{1,0:T(8,128)(2,1)} %collective-permute-done.20.refs_12_), channel_id=1, source_target_pairs={{0,195},{1,0},{2,1},{3,2},{64,3},{65,64},{66,65},{67,66},{128,67},... | collective-permute-start | bytes 983048 | tf_op jit(solution)/shard_map/ppermute | solution.py:231
  98.6 5.6 %collective-permute-start.24 = (bf16[256,640]{1,0:T(8,128)(2,1)S(1)}, bf16[256,640]{1,0:T(8,128)(2,1)S(1)}, u32[]{:S(2)}, u32[]{:S(2)}) collective-permute-start(bf16[256,640]{1,0:T(8,128)(2,1)S(1)} %collective-permute-done.22.refs_13_), channel_id=1, source_target_pairs={{0,195},{1,0},{2,1},{3,2},{64,3},{65,64},{66,65},{67,66},{128,67},... | collective-permute-start | bytes 983048 | tf_op jit(solution)/shard_map/ppermute | solution.py:231
  111.5 4.9 %collective-permute-start.26 = (bf16[256,640]{1,0:T(8,128)(2,1)S(1)}, bf16[256,640]{1,0:T(8,128)(2,1)S(1)}, u32[]{:S(2)}, u32[]{:S(2)}) collective-permute-start(bf16[256,640]{1,0:T(8,128)(2,1)S(1)} %collective-permute-done.24.refs_14_), channel_id=1, source_target_pairs={{0,195},{1,0},{2,1},{3,2},{64,3},{65,64},{66,65},{67,66},{128,67},... | collective-permute-start | bytes 983048 | tf_op jit(solution)/shard_map/ppermute | solution.py:231
  116.4 3.6 %collective-permute-done.12.refs_7_ = bf16[256,640]{1,0:T(8,128)(2,1)S(1)} collective-permute-done((bf16[256,640]{1,0:T(8,128)(2,1)S(1)}, bf16[256,640]{1,0:T(8,128)(2,1)S(1)}, u32[]{:S(2)}, u32[]{:S(2)}) %collective-permute-start.12) | collective-permute-done | bytes 327712 | tf_op jit(solution)/shard_map/ppermute | solution.py:229
  124.0 2.4 collective-permute-start.27
  128.3 3.3 %collective-permute-done.14.refs_8_ = bf16[256,640]{1,0:T(8,128)(2,1)S(1)} collective-permute-done((bf16[256,640]{1,0:T(8,128)(2,1)S(1)}, bf16[256,640]{1,0:T(8,128)(2,1)S(1)}, u32[]{:S(2)}, u32[]{:S(2)}) %collective-permute-start.14) | collective-permute-done | bytes 327712 | tf_op jit(solution)/shard_map/ppermute | solution.py:229
  136.1 4.0 %section.8 = (bf16[32,2048]{1,0:T(8,128)(2,1)S(1)}, bf16[32,2048]{1,0:T(8,128)(2,1)S(1)}) custom-call(s32[33]{0:T(128)S(1)} %add_select_fusion.info, bf16[32,2048]{1,0:T(8,128)(2,1)S(1)} %copy-done.32, f32[128,32]{1,0:T(8,128)S(1)} %bitcast.17, f32[5,32,128]{2,1,0:T(8,128)S(1)} %fusion.2.rope_ref, ...), custom_call_target="tpu_custom_call", output_to_operand_aliasing={{0}: (4, {})} | custom-call | tf_op jit(solution)/shard_map/section/pallas_call | solution.py:139
  141.5 3.3 %collective-permute-done.31.x_ref = bf16[32,2048]{1,0:T(8,128)(2,1)S(1)} collective-permute-done((bf16[32,2048]{1,0:T(8,128)(2,1)S(1)}, bf16[32,2048]{1,0:T(8,128)(2,1)S(1)}, u32[]{:S(2)}, u32[]{:S(2)}) %collective-permute-start.31) | collective-permute-done | bytes 131104 | tf_op jit(solution)/shard_map/ppermute | solution.py:315
  156.8 2.3 section.14
  178.1 49.5 %collective-permute-start.39 = (bf16[8,2048]{1,0:T(8,128)(2,1)S(1)}, bf16[8,2048]{1,0:T(8,128)(2,1)S(1)}, u32[]{:S(2)}, u32[]{:S(2)}) collective-permute-start(bf16[8,2048]{1,0:T(8,128)(2,1)S(1)} %get-tuple-element.82), channel_id=1, source_target_pairs={{0,1},{1,2},{2,31},{3,28},{4,5},{5,6},{6,27},{7,24},{8,9},{9,10},{... | collective-permute-start | bytes 98312 | tf_op jit(solution)/shard_map/ppermute | solution.py:263
  227.6 6.0 %collective-permute-start.40 = (bf16[8,2048]{1,0:T(8,128)(2,1)S(1)}, bf16[8,2048]{1,0:T(8,128)(2,1)S(1)}, u32[]{:S(2)}, u32[]{:S(2)}) collective-permute-start(bf16[8,2048]{1,0:T(8,128)(2,1)S(1)} %get-tuple-element.81), channel_id=1, source_target_pairs={{0,2},{1,3},{2,28},{3,29},{4,6},{5,7},{6,24},{7,25},{8,10},{9,11},... | collective-permute-start | bytes 98312 | tf_op jit(solution)/shard_map/ppermute | solution.py:263
  236.4 5.1 %collective-permute-done.41.refs_3_ = bf16[8,2048]{1,0:T(8,128)(2,1)S(1)} collective-permute-done((bf16[8,2048]{1,0:T(8,128)(2,1)S(1)}, bf16[8,2048]{1,0:T(8,128)(2,1)S(1)}, u32[]{:S(2)}, u32[]{:S(2)}) %collective-permute-start.41) | collective-permute-done | bytes 32800 | tf_op jit(solution)/shard_map/ppermute | solution.py:263
  (188 shorter events, 89.9 us)
Async XLA Ops:
  16.0 18.8 %collective-permute-start = (bf16[256,640]{1,0:T(8,128)(2,1)}, bf16[256,640]{1,0:T(8,128)(2,1)S(1)}, u32[]{:S(2)}, u32[]{:S(2)}) collective-permute-start(bf16[256,640]{1,0:T(8,128)(2,1)} %block.1.refs_0_), channel_id=1, source_target_pairs={{0,1},{1,2},{2,3},{3,64},{64,65},{65,66},{66,67},{67,128},{128,129... | collective-permute-start | bytes 983048 | tf_op jit(solution)/shard_map/ppermute | solution.py:229
  20.3 14.6 %collective-permute-start.1 = (bf16[256,640]{1,0:T(8,128)(2,1)}, bf16[256,640]{1,0:T(8,128)(2,1)S(1)}, u32[]{:S(2)}, u32[]{:S(2)}) collective-permute-start(bf16[256,640]{1,0:T(8,128)(2,1)} %block.1.refs_0_), channel_id=1, source_target_pairs={{0,32},{32,0},{1,33},{33,1},{2,34},{34,2},{3,35},{35,3},{4,36},{36... | collective-permute-start | bytes 983048 | tf_op jit(solution)/shard_map/ppermute | solution.py:219
  22.2 19.2 %collective-permute-start.15 = (bf16[256,640]{1,0:T(8,128)(2,1)}, bf16[256,640]{1,0:T(8,128)(2,1)S(1)}, u32[]{:S(2)}, u32[]{:S(2)}) collective-permute-start(bf16[256,640]{1,0:T(8,128)(2,1)} %block.1.refs_0_), channel_id=1, source_target_pairs={{0,195},{1,0},{2,1},{3,2},{64,3},{65,64},{66,65},{67,66},{128,67},... | collective-permute-start | bytes 983048 | tf_op jit(solution)/shard_map/ppermute | solution.py:231
  34.8 14.7 %collective-permute-start.2 = (bf16[256,640]{1,0:T(8,128)(2,1)S(1)}, bf16[256,640]{1,0:T(8,128)(2,1)S(1)}, u32[]{:S(2)}, u32[]{:S(2)}) collective-permute-start(bf16[256,640]{1,0:T(8,128)(2,1)S(1)} %collective-permute-done.refs_1_), channel_id=1, source_target_pairs={{0,1},{1,2},{2,3},{3,64},{64,65},{65,66},{66,67},{67,128},{128,129... | collective-permute-start | bytes 983048 | tf_op jit(solution)/shard_map/ppermute | solution.py:229
  36.8 12.7 %collective-permute-start.3 = (bf16[256,640]{1,0:T(8,128)(2,1)S(1)}, bf16[256,640]{1,0:T(8,128)(2,1)S(1)}, u32[]{:S(2)}, u32[]{:S(2)}) collective-permute-start(bf16[256,640]{1,0:T(8,128)(2,1)S(1)} %collective-permute-done.refs_1_), channel_id=1, source_target_pairs={{0,32},{32,0},{1,33},{33,1},{2,34},{34,2},{3,35},{35,3},{4,36},{36... | collective-permute-start | bytes 983048 | tf_op jit(solution)/shard_map/ppermute | solution.py:219
  41.4 13.0 %collective-permute-start.16 = (bf16[256,640]{1,0:T(8,128)(2,1)S(1)}, bf16[256,640]{1,0:T(8,128)(2,1)S(1)}, u32[]{:S(2)}, u32[]{:S(2)}) collective-permute-start(bf16[256,640]{1,0:T(8,128)(2,1)S(1)} %collective-permute-done.15.refs_9_), channel_id=1, source_target_pairs={{0,195},{1,0},{2,1},{3,2},{64,3},{65,64},{66,65},{67,66},{128,67},... | collective-permute-start | bytes 983048 | tf_op jit(solution)/shard_map/ppermute | solution.py:231
  49.5 13.9 %collective-permute-start.4 = (bf16[256,640]{1,0:T(8,128)(2,1)S(1)}, bf16[256,640]{1,0:T(8,128)(2,1)S(1)}, u32[]{:S(2)}, u32[]{:S(2)}) collective-permute-start(bf16[256,640]{1,0:T(8,128)(2,1)S(1)} %collective-permute-done.2.refs_2_), channel_id=1, source_target_pairs={{0,1},{1,2},{2,3},{3,64},{64,65},{65,66},{66,67},{67,128},{128,129... | collective-permute-start | bytes 983048 | tf_op jit(solution)/shard_map/ppermute | solution.py:229
  51.4 11.9 %collective-permute-start.5 = (bf16[256,640]{1,0:T(8,128)(2,1)S(1)}, bf16[256,640]{1,0:T(8,128)(2,1)S(1)}, u32[]{:S(2)}, u32[]{:S(2)}) collective-permute-start(bf16[256,640]{1,0:T(8,128)(2,1)S(1)} %collective-permute-done.2.refs_2_), channel_id=1, source_target_pairs={{0,32},{32,0},{1,33},{33,1},{2,34},{34,2},{3,35},{35,3},{4,36},{36... | collective-permute-start | bytes 983048 | tf_op jit(solution)/shard_map/ppermute | solution.py:219
  54.4 18.4 %collective-permute-start.18 = (bf16[256,640]{1,0:T(8,128)(2,1)S(1)}, bf16[256,640]{1,0:T(8,128)(2,1)}, u32[]{:S(2)}, u32[]{:S(2)}) collective-permute-start(bf16[256,640]{1,0:T(8,128)(2,1)S(1)} %collective-permute-done.16.refs_10_), channel_id=1, source_target_pairs={{0,195},{1,0},{2,1},{3,2},{64,3},{65,64},{66,65},{67,66},{128,67},... | collective-permute-start | bytes 983048 | tf_op jit(solution)/shard_map/ppermute | solution.py:231
  59.9 12.9 %collective-permute-start.19 = (bf16[256,640]{1,0:T(8,128)(2,1)S(1)}, bf16[256,640]{1,0:T(8,128)(2,1)S(1)}, u32[]{:S(2)}, u32[]{:S(2)}) collective-permute-start(bf16[256,640]{1,0:T(8,128)(2,1)S(1)} %collective-permute-done.16.refs_10_), channel_id=1, source_target_pairs={{0,32},{32,0},{1,33},{33,1},{2,34},{34,2},{3,35},{35,3},{4,36},{36... | collective-permute-start | bytes 983048 | tf_op jit(solution)/shard_map/ppermute | solution.py:219
  63.4 17.1 %collective-permute-start.6 = (bf16[256,640]{1,0:T(8,128)(2,1)S(1)}, bf16[256,640]{1,0:T(8,128)(2,1)}, u32[]{:S(2)}, u32[]{:S(2)}) collective-permute-start(bf16[256,640]{1,0:T(8,128)(2,1)S(1)} %collective-permute-done.4.refs_3_), channel_id=1, source_target_pairs={{0,1},{1,2},{2,3},{3,64},{64,65},{65,66},{66,67},{67,128},{128,129... | collective-permute-start | bytes 983048 | tf_op jit(solution)/shard_map/ppermute | solution.py:229
  65.3 15.2 %collective-permute-start.7 = (bf16[256,640]{1,0:T(8,128)(2,1)S(1)}, bf16[256,640]{1,0:T(8,128)(2,1)}, u32[]{:S(2)}, u32[]{:S(2)}) collective-permute-start(bf16[256,640]{1,0:T(8,128)(2,1)S(1)} %collective-permute-done.4.refs_3_), channel_id=1, source_target_pairs={{0,32},{32,0},{1,33},{33,1},{2,34},{34,2},{3,35},{35,3},{4,36},{36... | collective-permute-start | bytes 983048 | tf_op jit(solution)/shard_map/ppermute | solution.py:219
  73.5 12.8 %collective-permute-start.20 = (bf16[256,640]{1,0:T(8,128)(2,1)}, bf16[256,640]{1,0:T(8,128)(2,1)}, u32[]{:S(2)}, u32[]{:S(2)}) collective-permute-start(bf16[256,640]{1,0:T(8,128)(2,1)} %collective-permute-done.18.refs_11_), channel_id=1, source_target_pairs={{0,195},{1,0},{2,1},{3,2},{64,3},{65,64},{66,65},{67,66},{128,67},... | collective-permute-start | bytes 983048 | tf_op jit(solution)/shard_map/ppermute | solution.py:231
  80.5 13.6 %collective-permute-start.8 = (bf16[256,640]{1,0:T(8,128)(2,1)}, bf16[256,640]{1,0:T(8,128)(2,1)}, u32[]{:S(2)}, u32[]{:S(2)}) collective-permute-start(bf16[256,640]{1,0:T(8,128)(2,1)} %collective-permute-done.6.refs_4_), channel_id=1, source_target_pairs={{0,1},{1,2},{2,3},{3,64},{64,65},{65,66},{66,67},{67,128},{128,129... | collective-permute-start | bytes 983048 | tf_op jit(solution)/shard_map/ppermute | solution.py:229
  82.5 11.7 %collective-permute-start.9 = (bf16[256,640]{1,0:T(8,128)(2,1)}, bf16[256,640]{1,0:T(8,128)(2,1)}, u32[]{:S(2)}, u32[]{:S(2)}) collective-permute-start(bf16[256,640]{1,0:T(8,128)(2,1)} %collective-permute-done.6.refs_4_), channel_id=1, source_target_pairs={{0,32},{32,0},{1,33},{33,1},{2,34},{34,2},{3,35},{35,3},{4,36},{36... | collective-permute-start | bytes 983048 | tf_op jit(solution)/shard_map/ppermute | solution.py:219
  86.3 12.3 %collective-permute-start.22 = (bf16[256,640]{1,0:T(8,128)(2,1)}, bf16[256,640]{1,0:T(8,128)(2,1)S(1)}, u32[]{:S(2)}, u32[]{:S(2)}) collective-permute-start(bf16[256,640]{1,0:T(8,128)(2,1)} %collective-permute-done.20.refs_12_), channel_id=1, source_target_pairs={{0,195},{1,0},{2,1},{3,2},{64,3},{65,64},{66,65},{67,66},{128,67},... | collective-permute-start | bytes 983048 | tf_op jit(solution)/shard_map/ppermute | solution.py:231
  94.1 13.4 %collective-permute-start.10 = (bf16[256,640]{1,0:T(8,128)(2,1)}, bf16[256,640]{1,0:T(8,128)(2,1)S(1)}, u32[]{:S(2)}, u32[]{:S(2)}) collective-permute-start(bf16[256,640]{1,0:T(8,128)(2,1)} %collective-permute-done.8.refs_5_), channel_id=1, source_target_pairs={{0,1},{1,2},{2,3},{3,64},{64,65},{65,66},{66,67},{67,128},{128,129... | collective-permute-start | bytes 983048 | tf_op jit(solution)/shard_map/ppermute | solution.py:229
  98.6 12.9 %collective-permute-start.24 = (bf16[256,640]{1,0:T(8,128)(2,1)S(1)}, bf16[256,640]{1,0:T(8,128)(2,1)S(1)}, u32[]{:S(2)}, u32[]{:S(2)}) collective-permute-start(bf16[256,640]{1,0:T(8,128)(2,1)S(1)} %collective-permute-done.22.refs_13_), channel_id=1, source_target_pairs={{0,195},{1,0},{2,1},{3,2},{64,3},{65,64},{66,65},{67,66},{128,67},... | collective-permute-start | bytes 983048 | tf_op jit(solution)/shard_map/ppermute | solution.py:231
  107.6 12.5 %collective-permute-start.12 = (bf16[256,640]{1,0:T(8,128)(2,1)S(1)}, bf16[256,640]{1,0:T(8,128)(2,1)S(1)}, u32[]{:S(2)}, u32[]{:S(2)}) collective-permute-start(bf16[256,640]{1,0:T(8,128)(2,1)S(1)} %collective-permute-done.10.refs_6_), channel_id=1, source_target_pairs={{0,1},{1,2},{2,3},{3,64},{64,65},{65,66},{66,67},{67,128},{128,129... | collective-permute-start | bytes 983048 | tf_op jit(solution)/shard_map/ppermute | solution.py:229
  111.5 14.8 %collective-permute-start.26 = (bf16[256,640]{1,0:T(8,128)(2,1)S(1)}, bf16[256,640]{1,0:T(8,128)(2,1)S(1)}, u32[]{:S(2)}, u32[]{:S(2)}) collective-permute-start(bf16[256,640]{1,0:T(8,128)(2,1)S(1)} %collective-permute-done.24.refs_14_), channel_id=1, source_target_pairs={{0,195},{1,0},{2,1},{3,2},{64,3},{65,64},{66,65},{67,66},{128,67},... | collective-permute-start | bytes 983048 | tf_op jit(solution)/shard_map/ppermute | solution.py:231
  120.0 11.6 %collective-permute-start.14 = (bf16[256,640]{1,0:T(8,128)(2,1)S(1)}, bf16[256,640]{1,0:T(8,128)(2,1)S(1)}, u32[]{:S(2)}, u32[]{:S(2)}) collective-permute-start(bf16[256,640]{1,0:T(8,128)(2,1)S(1)} %collective-permute-done.12.refs_7_), channel_id=1, source_target_pairs={{0,1},{1,2},{2,3},{3,64},{64,65},{65,66},{66,67},{67,128},{128,129... | collective-permute-start | bytes 983048 | tf_op jit(solution)/shard_map/ppermute | solution.py:229
  122.0 11.6 %collective-permute-start.29 = (bf16[256,640]{1,0:T(8,128)(2,1)S(1)}, bf16[256,640]{1,0:T(8,128)(2,1)S(1)}, u32[]{:S(2)}, u32[]{:S(2)}) collective-permute-start(bf16[256,640]{1,0:T(8,128)(2,1)S(1)} %collective-permute-done.24.refs_14_), channel_id=1, source_target_pairs={{0,32},{32,0},{1,33},{33,1},{2,34},{34,2},{3,35},{35,3},{4,36},{36... | collective-permute-start | bytes 983048 | tf_op jit(solution)/shard_map/ppermute | solution.py:219
  177.4 58.2 %collective-permute-start.38 = (bf16[8,2048]{1,0:T(8,128)(2,1)S(1)}, bf16[8,2048]{1,0:T(8,128)(2,1)S(1)}, u32[]{:S(2)}, u32[]{:S(2)}) collective-permute-start(bf16[8,2048]{1,0:T(8,128)(2,1)S(1)} %get-tuple-element.83), channel_id=1, source_target_pairs={{0,0},{1,1},{2,30},{3,31},{4,4},{5,5},{6,26},{7,27},{8,8},{9,9},{1... | collective-permute-start | bytes 98312 | tf_op jit(solution)/shard_map/ppermute | solution.py:263
  178.1 57.5 %collective-permute-start.39 = (bf16[8,2048]{1,0:T(8,128)(2,1)S(1)}, bf16[8,2048]{1,0:T(8,128)(2,1)S(1)}, u32[]{:S(2)}, u32[]{:S(2)}) collective-permute-start(bf16[8,2048]{1,0:T(8,128)(2,1)S(1)} %get-tuple-element.82), channel_id=1, source_target_pairs={{0,1},{1,2},{2,31},{3,28},{4,5},{5,6},{6,27},{7,24},{8,9},{9,10},{... | collective-permute-start | bytes 98312 | tf_op jit(solution)/shard_map/ppermute | solution.py:263
  (62 other events, 909.2 us)

commit v3 on v2

v3 whole, which is shorter than its diff:
```python
import functools

import jax
import jax.numpy as jnp
import numpy as np
from jax import lax
from jax.experimental import pallas as pl
from jax.experimental.pallas import tpu as pltpu
from jax.sharding import Mesh, PartitionSpec as P

HEAD_DIM = 64
SEQ = 32
D = 2048
EPSILON = 1e-05
THETA = 500000.0

GROUPS = 4
GROUP_HEADS = 4
QKV = 384
CTX = 256
X = 4
ZH = 4
ZL = 4
Z = ZH * ZL
ROWS = 256

F32, BF16 = jnp.float32, jnp.bfloat16

SMALL = pltpu.CompilerParams(vmem_limit_bytes=4 * 1024 * 1024)
MEDIUM = pltpu.CompilerParams(vmem_limit_bytes=20 * 1024 * 1024)


def rotary_tables():
    half = HEAD_DIM // 2
    lane = jnp.arange(4 * half)[None, :]
    frequency = THETA ** (-((lane % half).astype(F32) * 2.0 / HEAD_DIM))
    angles = jnp.arange(SEQ, dtype=F32)[:, None] * frequency
    cos, sin = jnp.cos(angles), jnp.sin(angles)
    return [
        cos,
        sin,
        jnp.where(lane < 2 * half, cos, 1.0),
        jnp.where(lane < half, -sin, 0.0),
        jnp.where((lane >= half) & (lane < 2 * half), sin, 0.0),
    ]


def attention(projected, rope, allowed):
    lane = lax.broadcasted_iota(jnp.int32, (SEQ, 128), 1)
    lane2 = lax.broadcasted_iota(jnp.int32, (SEQ, 256), 1)
    head_of = (lane2 % 128) // 32
    zero = jnp.zeros((), BF16)
    cos, sin, kcos, ksin_a, ksin_b = rope
    queries, keys, values = [], [], []
    for part in projected:
        first, second = part[:, :128], part[:, 128:256]
        query = jnp.concatenate(
            [first * cos - second * sin, second * cos + first * sin], axis=-1
        ).astype(BF16)
        queries.append(
            jnp.concatenate([jnp.where(head_of == h, query, zero) for h in range(GROUP_HEADS)], axis=0)
        )
    for part in projected:
        kv = part[:, 256:]
        kv = kv * kcos + pltpu.roll(kv, 96, 1) * ksin_a + pltpu.roll(kv, 32, 1) * ksin_b
        key_a = jnp.where(lane < 32, kv, 0.0)
        key_a = key_a + pltpu.roll(key_a, 32, 1)
        key_a = key_a + pltpu.roll(key_a, 64, 1)
        key_b = jnp.where((lane >= 32) & (lane < 64), kv, 0.0)
        key_b = key_b + pltpu.roll(key_b, 32, 1)
        key_b = key_b + pltpu.roll(key_b, 64, 1)
        keys.append(jnp.concatenate([key_a, key_b], axis=-1).astype(BF16))
        values.append(kv.astype(BF16))
    scores = [
        lax.dot_general(q, k, (((1,), (1,)), ((), ())), preferred_element_type=F32)
        for q, k in zip(queries, keys)
    ]
    scores = [jnp.where(allowed, s * HEAD_DIM ** (-0.5), -1e30) for s in scores]
    scores = [jnp.exp(s - jnp.max(s, axis=-1, keepdims=True)) for s in scores]
    weights = [(s * (1.0 / jnp.sum(s, axis=-1, keepdims=True))).astype(BF16) for s in scores]
    contexts = []
    for weight, value in zip(weights, values):
        mixed = jnp.dot(weight, value, preferred_element_type=F32)
        rows = [mixed[h * SEQ : (h + 1) * SEQ] for h in range(GROUP_HEADS)]
        context = jnp.concatenate(
            [
                jnp.where(lane < 64, pltpu.roll(rows[0], 64, 1), rows[1]),
                jnp.where(lane < 64, pltpu.roll(rows[2], 64, 1), rows[3]),
            ],
            axis=-1,
        )
        contexts.append(context.astype(BF16))
    return contexts


def section_kernel(step, last, where, x_ref, allowed_ref, held_ref, *refs):
    rope, weights, outputs = refs[:5], (refs[5:8], refs[8:11]), refs[11:]
    out_ref = outputs[-1]

    def rows_of(i, zh, t, columns):
        part, first = ((0, 0), (1, ZH), (2, 0), (1, 0))[t]
        return jnp.concatenate(
            [weights[i][part][x, first + zh, :, columns] for x in range(X)], axis=0
        )

    @pl.when(where[0] != step)
    def _():
        out_ref[...] = held_ref[...].astype(out_ref.dtype)

    @pl.when(where[0] == step)
    def _():
        places = [(i, zh) for i in range(2) for zh in range(ZH)]
        parts = [x_ref[:, pl.ds(j * ROWS, ROWS)] for j in range(2 * ZH)]
        squares = [jnp.sum(jnp.square(part.astype(F32)), axis=-1, keepdims=True) for part in parts]
        scale = lax.rsqrt(functools.reduce(jnp.add, squares) * (1.0 / D) + EPSILON)
        projected = []
        for t in range(GROUPS):
            terms = [
                jnp.dot(part, rows_of(i, zh, t, pl.ds(0, QKV)), preferred_element_type=F32)
                for part, (i, zh) in zip(parts, places)
            ]
            projected.append(functools.reduce(jnp.add, terms) * scale)
        contexts = attention(projected, [part[...] for part in rope], allowed_ref[...] > 0.5)
        for j, (i, zh) in enumerate(places):
            terms = [
                lax.dot_general(
                    contexts[t],
                    rows_of(i, zh, t, pl.ds(QKV, CTX)),
                    (((1,), (1,)), ((), ())),
                    preferred_element_type=F32,
                )
                for t in range(GROUPS)
            ]
            total = x_ref[:, pl.ds(j * ROWS, ROWS)].astype(F32) + functools.reduce(jnp.add, terms)
            out_ref[:, pl.ds(j * ROWS, ROWS)] = total.astype(out_ref.dtype)

    if last:
        rows = outputs[0].shape[0]
        for k, chunk_ref in enumerate(outputs[:-1]):
            place = (where[3] + k) % (SEQ // rows)
            chunk_ref[...] = out_ref[pl.ds(pl.multiple_of(place * rows, rows), rows), :].astype(BF16)


def run_section(step, last, where, values, allowed, held, rope, weights):
    vmem = pl.BlockSpec(memory_space=pltpu.VMEM)
    whole, chunk = (jax.ShapeDtypeStruct((rows, D), BF16) for rows in (SEQ, SEQ // 4))
    return pl.pallas_call(
        functools.partial(section_kernel, step, last),
        out_shape=[chunk] * 4 if last else whole,
        in_specs=[pl.BlockSpec(memory_space=pltpu.SMEM)] + [vmem] * 14,
        out_specs=[vmem] * 4 if last else vmem,
        scratch_shapes=[pltpu.VMEM((SEQ, D), F32)] if last else [],
        input_output_aliases={} if last else {3: 0},
        compiler_params=MEDIUM,
        name="section",
    )(where, values, allowed, held, *rope, *weights)


def shard_kernel(where, qkv_ref, out_ref, gain_ref, shard_ref):
    rows = qkv_ref.shape[1]
    section = lax.broadcasted_iota(jnp.int32, gain_ref.shape, 0)
    gain = jnp.where(section == where[0], gain_ref[...].astype(F32), 0.0)
    gain = jnp.sum(gain, axis=0, keepdims=True)
    row = lax.broadcasted_iota(jnp.int32, (rows, rows), 0)
    column = lax.broadcasted_iota(jnp.int32, (rows, rows), 1)
    gain = jnp.sum(jnp.where(row == column, gain, 0.0), axis=1, keepdims=True)
    qkv = qkv_ref[0].astype(F32) * gain
    one, two = qkv[:, :128], qkv[:, 128:256]
    lane = lax.broadcasted_iota(jnp.int32, (rows, 128), 1)

    def lanes(parts):
        result = parts[3]
        for i in (2, 1, 0):
            result = jnp.where(lane < 32 * (i + 1), parts[i], result)
        return result

    first = lanes([one, pltpu.roll(one, 96, 1), pltpu.roll(two, 64, 1), pltpu.roll(two, 32, 1)])
    second = lanes([pltpu.roll(one, 96, 1), pltpu.roll(one, 64, 1), pltpu.roll(two, 32, 1), two])
    shard = jnp.concatenate([first, second, qkv[:, 256:]], axis=1).astype(BF16)
    for z in range(shard_ref.shape[0]):
        shard_ref[z, :, pl.ds(0, QKV)] = shard
        shard_ref[z, :, pl.ds(QKV, CTX)] = out_ref[0]


def join_kernel(here_ref, after_ref, before_ref, half_ref, rest_ref, out_ref):
    half = half_ref.shape[0]
    out_ref[0] = here_ref[...]
    out_ref[1] = after_ref[...]
    out_ref[2, pl.ds(0, half)] = half_ref[...]
    out_ref[2, pl.ds(half, half)] = rest_ref[...]
    out_ref[3] = before_ref[...]


def gather_section(where, w_qkv, w_out, norm_gain):
    rows = w_qkv.shape[1]
    shape = (ZH, rows, QKV + CTX)
    vmem = pl.BlockSpec(memory_space=pltpu.VMEM)
    shards = pl.pallas_call(
        shard_kernel,
        out_shape=jax.ShapeDtypeStruct(shape, BF16),
        grid_spec=pltpu.PrefetchScalarGridSpec(
            num_scalar_prefetch=1,
            grid=(1,),
            in_specs=[
                pl.BlockSpec((1, rows, QKV), lambda i, where: (where[0], 0, 0)),
                pl.BlockSpec((1, rows, CTX), lambda i, where: (where[0], 0, 0)),
                pl.BlockSpec(norm_gain.shape, lambda i, where: (0, 0)),
            ],
            out_specs=pl.BlockSpec(shape, lambda i, where: (0, 0, 0)),
        ),
        compiler_params=SMALL,
        name="shard",
    )(where, w_qkv, w_out.transpose(0, 2, 1), norm_gain)

    one, other = [(x, (x + 1) % X) for x in range(X)], [(x, (x - 1) % X) for x in range(X)]

    def first_along_x(parts):
        return lax.ppermute(parts, "x", one), lax.ppermute(parts, "x", other)

    def rest_along_x(parts, before, after):
        half = parts.shape[0] // 2
        return pl.pallas_call(
            join_kernel,
            out_shape=jax.ShapeDtypeStruct((X, *parts.shape), BF16),
            in_specs=[vmem] * 5,
            out_specs=vmem,
            compiler_params=MEDIUM,
            name="join",
        )(
            parts,
            after,
            before,
            lax.ppermute(before[:half], "x", one),
            lax.ppermute(after[half:], "x", other),
        )

    def along_z(parts, by):
        return lax.ppermute(parts, ("z_hi", "tensor"), [(z, (z + by) % Z) for z in range(Z)])

    here = lax.all_to_all(shards, "z_hi", 0, 0)
    half = ZH // 2
    ahead, behind = along_z(here, 1), along_z(here, -1)
    here_x = first_along_x(here)
    near, *here_x = lax.optimization_barrier((jnp.concatenate([ahead, behind]), *here_x))
    near_x = first_along_x(near)
    across = jnp.concatenate([along_z(ahead[:half], 1), along_z(behind[half:], -1)])
    across, *here_x = lax.optimization_barrier((across, *here_x))
    across_x = first_along_x(across)
    _, *near_x = lax.optimization_barrier((across, *near_x))
    own = [
        rest_along_x(here, *here_x),
        rest_along_x(near, *near_x),
        rest_along_x(across, *across_x),
    ]
    return own + [lax.ppermute(part, "core", [(0, 1), (1, 0)]) for part in own]


def turned(values, by):
    result = values
    for count in range(1, X):
        result = jnp.where(by == count, pltpu.roll(values, 64 * count, 1), result)
    return result


def enter_kernel(where, down_ref, up_ref, down_docs_ref, up_docs_ref, out_ref, allowed_ref):
    member = where[3]
    x_ref = jnp.where(member < 2, down_ref[member % 2], up_ref[member % 2]).astype(F32)
    docs = [docs_ref[...] for docs_ref in (down_docs_ref, up_docs_ref)]
    docs = jnp.where(member < 2, docs[0], docs[1])
    docs = jnp.where(member % 2 == 0, docs[:1], docs[1:])
    row = lax.broadcasted_iota(jnp.int32, (SEQ, SEQ), 0)
    column = lax.broadcasted_iota(jnp.int32, (SEQ, SEQ), 1)
    own_docs = jnp.sum(jnp.where(row == column, docs, 0), axis=1, keepdims=True)
    allowed = jnp.where((row >= column) & (own_docs == docs), 1.0, 0.0)
    for h in range(GROUP_HEADS):
        allowed_ref[pl.ds(h * SEQ, SEQ), :] = allowed
    lane = lax.broadcasted_iota(jnp.int32, (SEQ, 128), 1)
    for zh in range(ZH):
        tiles = [x_ref[:, x * 512 + zh * 128 : x * 512 + zh * 128 + 128] for x in range(X)]
        cores = []
        for core in range(2):
            pairs = [
                jnp.where(lane < 64, a, pltpu.roll(b, 64, 1))
                if core == 0
                else jnp.where(lane < 64, pltpu.roll(a, 64, 1), b)
                for a, b in (tiles[:2], tiles[2:])
            ]
            cores.append(turned(jnp.concatenate(pairs, axis=1), (X - where[1]) % X))
        for i in range(2):
            part = jnp.where(where[2] == i, cores[0], cores[1])
            out_ref[:, pl.ds((i * ZH + zh) * ROWS, ROWS)] = part.astype(BF16)


def order_kernel(where, *refs):
    *received, down_ref, up_ref = refs
    rows = received[0].shape[0]
    values = jnp.concatenate([part[...] for part in received], axis=0).astype(F32)
    lane = lax.broadcasted_iota(jnp.int32, (values.shape[0], 128), 1)
    tiles = {}
    for zh in range(ZH):
        mine, other = (
            turned(values[:, (i * ZH + zh) * ROWS : (i * ZH + zh + 1) * ROWS], where[1])
            for i in range(2)
        )
        zero, one = jnp.where(where[2] == 0, mine, other), jnp.where(where[2] == 0, other, mine)
        for pair in range(2):
            a, b = (part[:, pair * 128 : (pair + 1) * 128] for part in (zero, one))
            tiles[2 * pair, zh] = jnp.where(lane < 64, a, pltpu.roll(b, 64, 1))
            tiles[2 * pair + 1, zh] = jnp.where(lane < 64, pltpu.roll(a, 64, 1), b)
    natural = jnp.concatenate(
        [tiles[x, zh] for x in range(X) for zh in range(ZH)], axis=1
    ).astype(BF16)
    for k in range(len(received)):
        source = (where[3] + len(received) - k) % len(received)
        part = natural[k * rows : (k + 1) * rows]

        @pl.when(source < 2)
        def _():
            down_ref[0, source] = part

        @pl.when(source >= 2)
        def _():
            up_ref[0, source - 2] = part


def exchange(chunks, where):
    planes, members = lax.axis_size("pipe"), lax.axis_size("tensor")
    rows = SEQ // members
    received = []
    for k, chunk in enumerate(chunks):
        pairs = [
            (y * members + t, (y if t < 2 else planes - 1 - y) * members + (t + k) % members)
            for y in range(planes)
            for t in range(members)
        ]
        received.append(lax.ppermute(chunk, ("pipe", "tensor"), pairs))
    vmem = pl.BlockSpec(memory_space=pltpu.VMEM)
    shape = jax.ShapeDtypeStruct((1, members // 2, rows, D), BF16)
    return pl.pallas_call(
        order_kernel,
        out_shape=[shape, shape],
        in_specs=[pl.BlockSpec(memory_space=pltpu.SMEM)] + [vmem] * members,
        out_specs=[vmem, vmem],
        compiler_params=SMALL,
        name="order",
    )(where, *received)


def on_device(down_in, up_in, w_qkv, w_out, norm_gain, down_docs, up_docs):
    where = jnp.stack([lax.axis_index(name) for name in ("pipe", "x", "core", "tensor")])
    sections = lax.axis_size("pipe")
    weights = gather_section(where, w_qkv, w_out, norm_gain)
    rope = rotary_tables()
    vmem = pl.BlockSpec(memory_space=pltpu.VMEM)
    values, allowed = pl.pallas_call(
        enter_kernel,
        out_shape=[
            jax.ShapeDtypeStruct((SEQ, D), BF16),
            jax.ShapeDtypeStruct((GROUP_HEADS * SEQ, SEQ), F32),
        ],
        in_specs=[pl.BlockSpec(memory_space=pltpu.SMEM)] + [vmem] * 4,
        out_specs=[vmem, vmem],
        compiler_params=SMALL,
        name="enter",
    )(where, down_in, up_in, down_docs, up_docs)
    held = jnp.zeros((SEQ, D), BF16)
    for step in range(sections - 1):
        held = run_section(step, False, where, values, allowed, held, rope, weights)
        values = lax.ppermute(held, "pipe", [(step, step + 1)])
    chunks = run_section(sections - 1, True, where, values, allowed, held, rope, weights)
    return exchange(chunks, where)


def solution(mesh):
    fine = Mesh(
        mesh.devices.reshape(X, ZH, 2, *mesh.devices.shape[1:]),
        ("x", "z_hi", "core", "pipe", "tensor"),
    )
    dp = ("x", "z_hi", "core")
    placed = (
        P(dp, None, None),
        P(dp, None, None),
        P(None, dp, "tensor"),
        P(None, "tensor", dp),
        P(None, dp),
        P(dp, None),
        P(dp, None),
    )
    return jax.shard_map(
        on_device,
        mesh=fine,
        in_specs=placed,
        out_specs=(P("pipe", dp, "tensor", None), P("pipe", dp, "tensor", None)),
        check_vma=False,
    )
```

time: 246 us -> 219 us (0.89)
  the two profiles are of different devices: /device:TPU:64 before, /device:TPU:6 now
where the time goes in v3:
time: 219 us; the launch traced here: 218 us
  starting transfers between devices  129 us (59%)
  blocking collectives  42.2 us (19%)
  waiting for transfers between devices  31.1 us (14%)
  Pallas kernels  11.2 us (5%)
  local copies, waits for them, and re-layouts  2.82 us (1%)
    ppermute x4, starting transfers between devices, exchange(): received.append(lax.ppermute(chunk, ('pipe', 'tensor'), pairs))  66.5 us
    all_to_all x1, blocking collectives, gather_section(): here = lax.all_to_all(shards, 'z_hi', 0, 0)  42.2 us
    ppermute x6, starting transfers between devices, first_along_x(): return (lax.ppermute(parts, 'x', one), lax.ppermute(parts, 'x', other))  20.3 us
    ppermute x4, starting transfers between devices, along_z(): lax.ppermute(parts, ('z_hi', 'tensor'), [(z, (z + by) % Z) for z in range...  13.1 us
    ppermute x3, starting transfers between devices, rest_along_x(): lax.ppermute(before[:half], 'x', one)  10.8 us
    ppermute x3, waiting for transfers between devices, rest_along_x(): lax.ppermute(after[half:], 'x', other)  9.36 us
    ppermute x4, waiting for transfers between devices, along_z(): lax.ppermute(parts, ('z_hi', 'tensor'), [(z, (z + by) % Z) for z in range...  8.02 us
    pallas_call x8, Pallas kernels, run_section(): pl.pallas_call(functools.partial(section_kernel, step, last), out_shape=[...  7.67 us
  transfers between devices with their start and end apart: 30, of which 14 were waited for; matrix products, arithmetic and copies ran while one was open for 0% of the time, Pallas kernels for 0%

profile of v3, /device:TPU:6, one launch (start us, length us, event | category | flops | bytes accessed | tf_op | source)
XLA Modules:
  0.0 217.5 jit_solution(13011154758312208699)
XLA Ops:
  4.1 42.2 %all_to_all.5.here_ref = bf16[4,64,640]{2,1,0:T(8,128)(2,1)S(1)} all-to-all(bf16[4,64,640]{2,1,0:T(8,128)(2,1)S(1)} %shard.1), channel_id=1, replica_groups=mesh['x'=4,'z_hi'=4,'core'=2,'pipe'=8,'tensor'=4] {'z_hi'}, dimensions={0} | all-to-all | bytes 655360 | tf_op jit(solution)/shard_map/all_to_all | solution.py:240
  46.3 3.9 %collective-permute-start.2 = (bf16[4,64,640]{2,1,0:T(8,128)(2,1)S(1)}, bf16[4,64,640]{2,1,0:T(8,128)(2,1)S(1)}, u32[]{:S(2)}, u32[]{:S(2)}) collective-permute-start(bf16[4,64,640]{2,1,0:T(8,128)(2,1)S(1)} %all_to_all.5.here_ref), channel_id=1, source_target_pairs={{0,195},{1,0},{2,1},{3,2},{64,3},{65,64},{66,65},{67,66},{128,67},... | collective-permute-start | bytes 983048 | tf_op jit(solution)/shard_map/ppermute | solution.py:238
  52.2 2.7 %collective-permute-start.5 = (bf16[4,64,640]{2,1,0:T(8,128)(2,1)S(1)}, bf16[4,64,640]{2,1,0:T(8,128)(2,1)S(1)}, u32[]{:S(2)}, u32[]{:S(2)}) collective-permute-start(bf16[4,64,640]{2,1,0:T(8,128)(2,1)S(1)} %all_to_all.5.here_ref), channel_id=1, source_target_pairs={{0,768},{256,0},{512,256},{768,512},{1,769},{257,1},{513,257},{769... | collective-permute-start | bytes 983048 | tf_op jit(solution)/shard_map/ppermute | solution.py:218
  54.9 4.3 %collective-permute-start.4 = (bf16[4,64,640]{2,1,0:T(8,128)(2,1)S(1)}, bf16[4,64,640]{2,1,0:T(8,128)(2,1)S(1)}, u32[]{:S(2)}, u32[]{:S(2)}) collective-permute-start(bf16[4,64,640]{2,1,0:T(8,128)(2,1)S(1)} %all_to_all.5.here_ref), channel_id=1, source_target_pairs={{0,256},{256,512},{512,768},{768,0},{1,257},{257,513},{513,769},{7... | collective-permute-start | bytes 983048 | tf_op jit(solution)/shard_map/ppermute | solution.py:218
  64.4 2.4 %collective-permute-start.9 = (bf16[8,64,640]{2,1,0:T(8,128)(2,1)S(1)}, bf16[8,64,640]{2,1,0:T(8,128)(2,1)S(1)}, u32[]{:S(2)}, u32[]{:S(2)}) collective-permute-start(bf16[8,64,640]{2,1,0:T(8,128)(2,1)S(1)} %pad_maximum_fusion.here_ref), channel_id=1, source_target_pairs={{0,768},{256,0},{512,256},{768,512},{1,769},{257,1},{513,257},{769... | collective-permute-start | bytes 1966088 | tf_op jit(solution)/shard_map/ppermute | solution.py:218
  66.8 5.0 %collective-permute-start.8 = (bf16[8,64,640]{2,1,0:T(8,128)(2,1)S(1)}, bf16[8,64,640]{2,1,0:T(8,128)(2,1)S(1)}, u32[]{:S(2)}, u32[]{:S(2)}) collective-permute-start(bf16[8,64,640]{2,1,0:T(8,128)(2,1)S(1)} %pad_maximum_fusion.here_ref), channel_id=1, source_target_pairs={{0,256},{256,512},{512,768},{768,0},{1,257},{257,513},{513,769},{7... | collective-permute-start | bytes 1966088 | tf_op jit(solution)/shard_map/ppermute | solution.py:218
  71.9 4.9 %collective-permute-start.3 = (bf16[2,64,640]{2,1,0:T(8,128)(2,1)S(1)}, bf16[2,64,640]{2,1,0:T(8,128)(2,1)S(1)}, u32[]{:S(2)}, u32[]{:S(2)}) collective-permute-start(bf16[2,64,640]{2,1,0:T(8,128)(2,1)S(1)} %slice.33), channel_id=1, source_target_pairs={{0,195},{1,0},{2,1},{3,2},{64,3},{65,64},{66,65},{67,66},{128,67},... | collective-permute-start | bytes 491528 | tf_op jit(solution)/shard_map/ppermute | solution.py:238
  76.8 2.4 %collective-permute-start.1 = (bf16[2,64,640]{2,1,0:T(8,128)(2,1)S(1)}, bf16[2,64,640]{2,1,0:T(8,128)(2,1)S(1)}, u32[]{:S(2)}, u32[]{:S(2)}) collective-permute-start(bf16[2,64,640]{2,1,0:T(8,128)(2,1)S(1)} %slice.32), channel_id=1, source_target_pairs={{0,1},{1,2},{2,3},{3,64},{64,65},{65,66},{66,67},{67,128},{128,129... | collective-permute-start | bytes 491528 | tf_op jit(solution)/shard_map/ppermute | solution.py:238
  80.5 4.7 %collective-permute-done.1 = bf16[2,64,640]{2,1,0:T(8,128)(2,1)S(1)} collective-permute-done((bf16[2,64,640]{2,1,0:T(8,128)(2,1)S(1)}, bf16[2,64,640]{2,1,0:T(8,128)(2,1)S(1)}, u32[]{:S(2)}, u32[]{:S(2)}) %collective-permute-start.1) | collective-permute-done | bytes 163872 | tf_op jit(solution)/shard_map/ppermute | solution.py:238
  85.3 3.9 %collective-permute-start.10 = (bf16[4,64,640]{2,1,0:T(8,128)(2,1)S(1)}, bf16[4,64,640]{2,1,0:T(8,128)(2,1)S(1)}, u32[]{:S(2)}, u32[]{:S(2)}) collective-permute-start(bf16[4,64,640]{2,1,0:T(8,128)(2,1)S(1)} %slice.28), channel_id=1, source_target_pairs={{0,256},{256,512},{512,768},{768,0},{1,257},{257,513},{513,769},{7... | collective-permute-start | bytes 983048 | tf_op jit(solution)/shard_map/ppermute | solution.py:233
  91.2 3.1 %collective-permute-done.10.half_ref = bf16[4,64,640]{2,1,0:T(8,128)(2,1)S(1)} collective-permute-done((bf16[4,64,640]{2,1,0:T(8,128)(2,1)S(1)}, bf16[4,64,640]{2,1,0:T(8,128)(2,1)S(1)}, u32[]{:S(2)}, u32[]{:S(2)}) %collective-permute-start.10) | collective-permute-done | bytes 327712 | tf_op jit(solution)/shard_map/ppermute | solution.py:233
  94.3 5.1 %collective-permute-done.11.rest_ref = bf16[4,64,640]{2,1,0:T(8,128)(2,1)S(1)} collective-permute-done((bf16[4,64,640]{2,1,0:T(8,128)(2,1)S(1)}, bf16[4,64,640]{2,1,0:T(8,128)(2,1)S(1)}, u32[]{:S(2)}, u32[]{:S(2)}) %collective-permute-start.11) | collective-permute-done | bytes 327712 | tf_op jit(solution)/shard_map/ppermute | solution.py:234
  103.5 3.9 %collective-permute-start.12 = (bf16[4,64,640]{2,1,0:T(8,128)(2,1)S(1)}, bf16[4,64,640]{2,1,0:T(8,128)(2,1)S(1)}, u32[]{:S(2)}, u32[]{:S(2)}) collective-permute-start(bf16[4,64,640]{2,1,0:T(8,128)(2,1)S(1)} %pad_maximum_fusion.1.here_ref), channel_id=1, source_target_pairs={{0,768},{256,0},{512,256},{768,512},{1,769},{257,1},{513,257},{769... | collective-permute-start | bytes 983048 | tf_op jit(solution)/shard_map/ppermute | solution.py:218
  107.5 3.1 %collective-permute-start.6 = (bf16[2,64,640]{2,1,0:T(8,128)(2,1)S(1)}, bf16[2,64,640]{2,1,0:T(8,128)(2,1)S(1)}, u32[]{:S(2)}, u32[]{:S(2)}) collective-permute-start(bf16[2,64,640]{2,1,0:T(8,128)(2,1)S(1)} %slice.26), channel_id=1, source_target_pairs={{0,256},{256,512},{512,768},{768,0},{1,257},{257,513},{513,769},{7... | collective-permute-start | bytes 491528 | tf_op jit(solution)/shard_map/ppermute | solution.py:233
  110.6 2.7 %collective-permute-start.7 = (bf16[2,64,640]{2,1,0:T(8,128)(2,1)S(1)}, bf16[2,64,640]{2,1,0:T(8,128)(2,1)S(1)}, u32[]{:S(2)}, u32[]{:S(2)}) collective-permute-start(bf16[2,64,640]{2,1,0:T(8,128)(2,1)S(1)} %slice.27), channel_id=1, source_target_pairs={{0,768},{256,0},{512,256},{768,512},{1,769},{257,1},{513,257},{769... | collective-permute-start | bytes 491528 | tf_op jit(solution)/shard_map/ppermute | solution.py:234
  114.0 3.7 %collective-permute-start.14 = (bf16[2,64,640]{2,1,0:T(8,128)(2,1)S(1)}, bf16[2,64,640]{2,1,0:T(8,128)(2,1)S(1)}, u32[]{:S(2)}, u32[]{:S(2)}) collective-permute-start(bf16[2,64,640]{2,1,0:T(8,128)(2,1)S(1)} %slice.34), channel_id=1, source_target_pairs={{0,256},{256,512},{512,768},{768,0},{1,257},{257,513},{513,769},{7... | collective-permute-start | bytes 491528 | tf_op jit(solution)/shard_map/ppermute | solution.py:233
  117.7 2.1 collective-permute-start.15
  120.4 2.1 collective-permute-start.16
  122.4 3.9 %collective-permute-done.15.rest_ref = bf16[2,64,640]{2,1,0:T(8,128)(2,1)S(1)} collective-permute-done((bf16[2,64,640]{2,1,0:T(8,128)(2,1)S(1)}, bf16[2,64,640]{2,1,0:T(8,128)(2,1)S(1)}, u32[]{:S(2)}, u32[]{:S(2)}) %collective-permute-start.15) | collective-permute-done | bytes 163872 | tf_op jit(solution)/shard_map/ppermute | solution.py:234
  131.4 3.4 %section.8.held_ref = bf16[32,2048]{1,0:T(8,128)(2,1)S(1)} custom-call(s32[4]{0:T(128)S(1)} %pad_add_fusion.where, bf16[32,2048]{1,0:T(8,128)(2,1)S(1)} %get-tuple-element.16.x_ref, f32[128,32]{1,0:T(8,128)S(1)} %get-tuple-element.17.allowed_ref, bf16[32,2048]{1,0:T(8,128)(2,1)S(1)} %broadcast_in_dim.73.held_ref, ...), custom_call_target="tpu_custom_call", output_to_operand_aliasing={{}: (3, {})} | custom-call | tf_op jit(solution)/shard_map/section/pallas_call | solution.py:147
  136.1 3.3 %collective-permute-done.19.x_ref = bf16[32,2048]{1,0:T(8,128)(2,1)S(1)} collective-permute-done((bf16[32,2048]{1,0:T(8,128)(2,1)S(1)}, bf16[32,2048]{1,0:T(8,128)(2,1)S(1)}, u32[]{:S(2)}, u32[]{:S(2)}) %collective-permute-start.19) | collective-permute-done | bytes 131104 | tf_op jit(solution)/shard_map/ppermute | solution.py:369
  148.5 6.2 %collective-permute-start.27 = (bf16[8,2048]{1,0:T(8,128)(2,1)S(1)}, bf16[8,2048]{1,0:T(8,128)(2,1)S(1)}, u32[]{:S(2)}, u32[]{:S(2)}) collective-permute-start(bf16[8,2048]{1,0:T(8,128)(2,1)S(1)} %get-tuple-element.27), channel_id=1, source_target_pairs={{0,1},{1,2},{2,31},{3,28},{4,5},{5,6},{6,27},{7,24},{8,9},{9,10},{... | collective-permute-start | bytes 98312 | tf_op jit(solution)/shard_map/ppermute | solution.py:336
  154.7 55.4 %collective-permute-start.28 = (bf16[8,2048]{1,0:T(8,128)(2,1)S(1)}, bf16[8,2048]{1,0:T(8,128)(2,1)S(1)}, u32[]{:S(2)}, u32[]{:S(2)}) collective-permute-start(bf16[8,2048]{1,0:T(8,128)(2,1)S(1)} %get-tuple-element.28), channel_id=1, source_target_pairs={{0,2},{1,3},{2,28},{3,29},{4,6},{5,7},{6,24},{7,25},{8,10},{9,11},... | collective-permute-start | bytes 98312 | tf_op jit(solution)/shard_map/ppermute | solution.py:336
  210.2 4.3 %collective-permute-start.29 = (bf16[8,2048]{1,0:T(8,128)(2,1)S(1)}, bf16[8,2048]{1,0:T(8,128)(2,1)S(1)}, u32[]{:S(2)}, u32[]{:S(2)}) collective-permute-start(bf16[8,2048]{1,0:T(8,128)(2,1)S(1)} %get-tuple-element.29), channel_id=1, source_target_pairs={{0,3},{1,0},{2,29},{3,30},{4,7},{5,4},{6,25},{7,26},{8,11},{9,8},{... | collective-permute-start | bytes 98312 | tf_op jit(solution)/shard_map/ppermute | solution.py:336
  (81 shorter events, 37.4 us)
Async XLA Ops:
  46.3 12.9 %collective-permute-start.2 = (bf16[4,64,640]{2,1,0:T(8,128)(2,1)S(1)}, bf16[4,64,640]{2,1,0:T(8,128)(2,1)S(1)}, u32[]{:S(2)}, u32[]{:S(2)}) collective-permute-start(bf16[4,64,640]{2,1,0:T(8,128)(2,1)S(1)} %all_to_all.5.here_ref), channel_id=1, source_target_pairs={{0,195},{1,0},{2,1},{3,2},{64,3},{65,64},{66,65},{67,66},{128,67},... | collective-permute-start | bytes 983048 | tf_op jit(solution)/shard_map/ppermute | solution.py:238
  50.2 11.0 %collective-permute-start = (bf16[4,64,640]{2,1,0:T(8,128)(2,1)S(1)}, bf16[4,64,640]{2,1,0:T(8,128)(2,1)S(1)}, u32[]{:S(2)}, u32[]{:S(2)}) collective-permute-start(bf16[4,64,640]{2,1,0:T(8,128)(2,1)S(1)} %all_to_all.5.here_ref), channel_id=1, source_target_pairs={{0,1},{1,2},{2,3},{3,64},{64,65},{65,66},{66,67},{67,128},{128,129... | collective-permute-start | bytes 983048 | tf_op jit(solution)/shard_map/ppermute | solution.py:238
  52.2 11.0 %collective-permute-start.5 = (bf16[4,64,640]{2,1,0:T(8,128)(2,1)S(1)}, bf16[4,64,640]{2,1,0:T(8,128)(2,1)S(1)}, u32[]{:S(2)}, u32[]{:S(2)}) collective-permute-start(bf16[4,64,640]{2,1,0:T(8,128)(2,1)S(1)} %all_to_all.5.here_ref), channel_id=1, source_target_pairs={{0,768},{256,0},{512,256},{768,512},{1,769},{257,1},{513,257},{769... | collective-permute-start | bytes 983048 | tf_op jit(solution)/shard_map/ppermute | solution.py:218
  54.9 9.5 %collective-permute-start.4 = (bf16[4,64,640]{2,1,0:T(8,128)(2,1)S(1)}, bf16[4,64,640]{2,1,0:T(8,128)(2,1)S(1)}, u32[]{:S(2)}, u32[]{:S(2)}) collective-permute-start(bf16[4,64,640]{2,1,0:T(8,128)(2,1)S(1)} %all_to_all.5.here_ref), channel_id=1, source_target_pairs={{0,256},{256,512},{512,768},{768,0},{1,257},{257,513},{513,769},{7... | collective-permute-start | bytes 983048 | tf_op jit(solution)/shard_map/ppermute | solution.py:218
  64.4 20.8 %collective-permute-start.9 = (bf16[8,64,640]{2,1,0:T(8,128)(2,1)S(1)}, bf16[8,64,640]{2,1,0:T(8,128)(2,1)S(1)}, u32[]{:S(2)}, u32[]{:S(2)}) collective-permute-start(bf16[8,64,640]{2,1,0:T(8,128)(2,1)S(1)} %pad_maximum_fusion.here_ref), channel_id=1, source_target_pairs={{0,768},{256,0},{512,256},{768,512},{1,769},{257,1},{513,257},{769... | collective-permute-start | bytes 1966088 | tf_op jit(solution)/shard_map/ppermute | solution.py:218
  66.8 18.4 %collective-permute-start.8 = (bf16[8,64,640]{2,1,0:T(8,128)(2,1)S(1)}, bf16[8,64,640]{2,1,0:T(8,128)(2,1)S(1)}, u32[]{:S(2)}, u32[]{:S(2)}) collective-permute-start(bf16[8,64,640]{2,1,0:T(8,128)(2,1)S(1)} %pad_maximum_fusion.here_ref), channel_id=1, source_target_pairs={{0,256},{256,512},{512,768},{768,0},{1,257},{257,513},{513,769},{7... | collective-permute-start | bytes 1966088 | tf_op jit(solution)/shard_map/ppermute | solution.py:218
  71.9 8.6 %collective-permute-start.3 = (bf16[2,64,640]{2,1,0:T(8,128)(2,1)S(1)}, bf16[2,64,640]{2,1,0:T(8,128)(2,1)S(1)}, u32[]{:S(2)}, u32[]{:S(2)}) collective-permute-start(bf16[2,64,640]{2,1,0:T(8,128)(2,1)S(1)} %slice.33), channel_id=1, source_target_pairs={{0,195},{1,0},{2,1},{3,2},{64,3},{65,64},{66,65},{67,66},{128,67},... | collective-permute-start | bytes 491528 | tf_op jit(solution)/shard_map/ppermute | solution.py:238
  76.8 8.4 %collective-permute-start.1 = (bf16[2,64,640]{2,1,0:T(8,128)(2,1)S(1)}, bf16[2,64,640]{2,1,0:T(8,128)(2,1)S(1)}, u32[]{:S(2)}, u32[]{:S(2)}) collective-permute-start(bf16[2,64,640]{2,1,0:T(8,128)(2,1)S(1)} %slice.32), channel_id=1, source_target_pairs={{0,1},{1,2},{2,3},{3,64},{64,65},{65,66},{66,67},{67,128},{128,129... | collective-permute-start | bytes 491528 | tf_op jit(solution)/shard_map/ppermute | solution.py:238
  85.3 9.0 %collective-permute-start.10 = (bf16[4,64,640]{2,1,0:T(8,128)(2,1)S(1)}, bf16[4,64,640]{2,1,0:T(8,128)(2,1)S(1)}, u32[]{:S(2)}, u32[]{:S(2)}) collective-permute-start(bf16[4,64,640]{2,1,0:T(8,128)(2,1)S(1)} %slice.28), channel_id=1, source_target_pairs={{0,256},{256,512},{512,768},{768,0},{1,257},{257,513},{513,769},{7... | collective-permute-start | bytes 983048 | tf_op jit(solution)/shard_map/ppermute | solution.py:233
  89.2 10.2 %collective-permute-start.11 = (bf16[4,64,640]{2,1,0:T(8,128)(2,1)S(1)}, bf16[4,64,640]{2,1,0:T(8,128)(2,1)S(1)}, u32[]{:S(2)}, u32[]{:S(2)}) collective-permute-start(bf16[4,64,640]{2,1,0:T(8,128)(2,1)S(1)} %slice.29), channel_id=1, source_target_pairs={{0,768},{256,0},{512,256},{768,512},{1,769},{257,1},{513,257},{769... | collective-permute-start | bytes 983048 | tf_op jit(solution)/shard_map/ppermute | solution.py:234
  99.6 31.7 %collective-permute-start.17 = (bf16[4,8,64,640]{3,2,1,0:T(8,128)(2,1)S(1)}, bf16[4,8,64,640]{3,2,1,0:T(8,128)(2,1)S(1)}, u32[]{:S(2)}, u32[]{:S(2)}) collective-permute-start(bf16[4,8,64,640]{3,2,1,0:T(8,128)(2,1)S(1)} %join.4.refs_6_), channel_id=1, source_target_pairs={{0,32},{32,0},{1,33},{33,1},{2,34},{34,2},{3,35},{35,3},{4,36},{36... | collective-permute-start | bytes 7864328 | tf_op jit(solution)/shard_map/ppermute | solution.py:255
  101.6 12.4 %collective-permute-start.13 = (bf16[4,64,640]{2,1,0:T(8,128)(2,1)S(1)}, bf16[4,64,640]{2,1,0:T(8,128)(2,1)S(1)}, u32[]{:S(2)}, u32[]{:S(2)}) collective-permute-start(bf16[4,64,640]{2,1,0:T(8,128)(2,1)S(1)} %pad_maximum_fusion.1.here_ref), channel_id=1, source_target_pairs={{0,256},{256,512},{512,768},{768,0},{1,257},{257,513},{513,769},{7... | collective-permute-start | bytes 983048 | tf_op jit(solution)/shard_map/ppermute | solution.py:218
  103.5 14.2 %collective-permute-start.12 = (bf16[4,64,640]{2,1,0:T(8,128)(2,1)S(1)}, bf16[4,64,640]{2,1,0:T(8,128)(2,1)S(1)}, u32[]{:S(2)}, u32[]{:S(2)}) collective-permute-start(bf16[4,64,640]{2,1,0:T(8,128)(2,1)S(1)} %pad_maximum_fusion.1.here_ref), channel_id=1, source_target_pairs={{0,768},{256,0},{512,256},{768,512},{1,769},{257,1},{513,257},{769... | collective-permute-start | bytes 983048 | tf_op jit(solution)/shard_map/ppermute | solution.py:218
  107.5 12.4 %collective-permute-start.6 = (bf16[2,64,640]{2,1,0:T(8,128)(2,1)S(1)}, bf16[2,64,640]{2,1,0:T(8,128)(2,1)S(1)}, u32[]{:S(2)}, u32[]{:S(2)}) collective-permute-start(bf16[2,64,640]{2,1,0:T(8,128)(2,1)S(1)} %slice.26), channel_id=1, source_target_pairs={{0,256},{256,512},{512,768},{768,0},{1,257},{257,513},{513,769},{7... | collective-permute-start | bytes 491528 | tf_op jit(solution)/shard_map/ppermute | solution.py:233
  110.6 9.6 %collective-permute-start.7 = (bf16[2,64,640]{2,1,0:T(8,128)(2,1)S(1)}, bf16[2,64,640]{2,1,0:T(8,128)(2,1)S(1)}, u32[]{:S(2)}, u32[]{:S(2)}) collective-permute-start(bf16[2,64,640]{2,1,0:T(8,128)(2,1)S(1)} %slice.27), channel_id=1, source_target_pairs={{0,768},{256,0},{512,256},{768,512},{1,769},{257,1},{513,257},{769... | collective-permute-start | bytes 491528 | tf_op jit(solution)/shard_map/ppermute | solution.py:234
  114.0 8.5 %collective-permute-start.14 = (bf16[2,64,640]{2,1,0:T(8,128)(2,1)S(1)}, bf16[2,64,640]{2,1,0:T(8,128)(2,1)S(1)}, u32[]{:S(2)}, u32[]{:S(2)}) collective-permute-start(bf16[2,64,640]{2,1,0:T(8,128)(2,1)S(1)} %slice.34), channel_id=1, source_target_pairs={{0,256},{256,512},{512,768},{768,0},{1,257},{257,513},{513,769},{7... | collective-permute-start | bytes 491528 | tf_op jit(solution)/shard_map/ppermute | solution.py:233
  117.7 8.6 %collective-permute-start.15 = (bf16[2,64,640]{2,1,0:T(8,128)(2,1)S(1)}, bf16[2,64,640]{2,1,0:T(8,128)(2,1)S(1)}, u32[]{:S(2)}, u32[]{:S(2)}) collective-permute-start(bf16[2,64,640]{2,1,0:T(8,128)(2,1)S(1)} %slice.35), channel_id=1, source_target_pairs={{0,768},{256,0},{512,256},{768,512},{1,769},{257,1},{513,257},{769... | collective-permute-start | bytes 491528 | tf_op jit(solution)/shard_map/ppermute | solution.py:234
  120.4 9.0 %collective-permute-start.16 = (bf16[4,4,64,640]{3,2,1,0:T(8,128)(2,1)S(1)}, bf16[4,4,64,640]{3,2,1,0:T(8,128)(2,1)S(1)}, u32[]{:S(2)}, u32[]{:S(2)}) collective-permute-start(bf16[4,4,64,640]{3,2,1,0:T(8,128)(2,1)S(1)} %join.3.refs_5_), channel_id=1, source_target_pairs={{0,32},{32,0},{1,33},{33,1},{2,34},{34,2},{3,35},{35,3},{4,36},{36... | collective-permute-start | bytes 3932168 | tf_op jit(solution)/shard_map/ppermute | solution.py:255
  126.4 4.9 %collective-permute-start.18 = (bf16[4,4,64,640]{3,2,1,0:T(8,128)(2,1)S(1)}, bf16[4,4,64,640]{3,2,1,0:T(8,128)(2,1)S(1)}, u32[]{:S(2)}, u32[]{:S(2)}) collective-permute-start(bf16[4,4,64,640]{3,2,1,0:T(8,128)(2,1)S(1)} %join.5.refs_7_), channel_id=1, source_target_pairs={{0,32},{32,0},{1,33},{33,1},{2,34},{34,2},{3,35},{35,3},{4,36},{36... | collective-permute-start | bytes 3932168 | tf_op jit(solution)/shard_map/ppermute | solution.py:255
  134.8 4.6 %collective-permute-start.19 = (bf16[32,2048]{1,0:T(8,128)(2,1)S(1)}, bf16[32,2048]{1,0:T(8,128)(2,1)S(1)}, u32[]{:S(2)}, u32[]{:S(2)}) collective-permute-start(bf16[32,2048]{1,0:T(8,128)(2,1)S(1)} %section.8.held_ref), channel_id=1, source_target_pairs={{0,4},{1,5},{2,6},{3,7},{32,36},{33,37},{34,38},{35,39},{64,68},{6... | collective-permute-start | bytes 393224 | tf_op jit(solution)/shard_map/ppermute | solution.py:369
  147.9 66.6 %collective-permute-start.26 = (bf16[8,2048]{1,0:T(8,128)(2,1)S(1)}, bf16[8,2048]{1,0:T(8,128)(2,1)S(1)}, u32[]{:S(2)}, u32[]{:S(2)}) collective-permute-start(bf16[8,2048]{1,0:T(8,128)(2,1)S(1)} %get-tuple-element.26), channel_id=1, source_target_pairs={{0,0},{1,1},{2,30},{3,31},{4,4},{5,5},{6,26},{7,27},{8,8},{9,9},{1... | collective-permute-start | bytes 98312 | tf_op jit(solution)/shard_map/ppermute | solution.py:336
  148.5 65.9 %collective-permute-start.27 = (bf16[8,2048]{1,0:T(8,128)(2,1)S(1)}, bf16[8,2048]{1,0:T(8,128)(2,1)S(1)}, u32[]{:S(2)}, u32[]{:S(2)}) collective-permute-start(bf16[8,2048]{1,0:T(8,128)(2,1)S(1)} %get-tuple-element.27), channel_id=1, source_target_pairs={{0,1},{1,2},{2,31},{3,28},{4,5},{5,6},{6,27},{7,24},{8,9},{9,10},{... | collective-permute-start | bytes 98312 | tf_op jit(solution)/shard_map/ppermute | solution.py:336
  154.7 60.0 %collective-permute-start.28 = (bf16[8,2048]{1,0:T(8,128)(2,1)S(1)}, bf16[8,2048]{1,0:T(8,128)(2,1)S(1)}, u32[]{:S(2)}, u32[]{:S(2)}) collective-permute-start(bf16[8,2048]{1,0:T(8,128)(2,1)S(1)} %get-tuple-element.28), channel_id=1, source_target_pairs={{0,2},{1,3},{2,28},{3,29},{4,6},{5,7},{6,24},{7,25},{8,10},{9,11},... | collective-permute-start | bytes 98312 | tf_op jit(solution)/shard_map/ppermute | solution.py:336
  210.2 5.8 %collective-permute-start.29 = (bf16[8,2048]{1,0:T(8,128)(2,1)S(1)}, bf16[8,2048]{1,0:T(8,128)(2,1)S(1)}, u32[]{:S(2)}, u32[]{:S(2)}) collective-permute-start(bf16[8,2048]{1,0:T(8,128)(2,1)S(1)} %get-tuple-element.29), channel_id=1, source_target_pairs={{0,3},{1,0},{2,29},{3,30},{4,7},{5,4},{6,25},{7,26},{8,11},{9,8},{... | collective-permute-start | bytes 98312 | tf_op jit(solution)/shard_map/ppermute | solution.py:336
  (13 other events, 38.9 us)

commit v4 on v3

--- a/solution.py
+++ b/solution.py
@@ -137,7 +137,7 @@
     if last:
         rows = outputs[0].shape[0]
         for k, chunk_ref in enumerate(outputs[:-1]):
-            place = (where[3] + k) % (SEQ // rows)
+            place = (where[2] + k) % (SEQ // rows)
             chunk_ref[...] = out_ref[pl.ds(pl.multiple_of(place * rows, rows), rows), :].astype(BF16)
 
 
@@ -182,19 +182,36 @@
         shard_ref[z, :, pl.ds(QKV, CTX)] = out_ref[0]
 
 
-def join_kernel(here_ref, after_ref, before_ref, half_ref, rest_ref, out_ref):
-    half = half_ref.shape[0]
-    out_ref[0] = here_ref[...]
-    out_ref[1] = after_ref[...]
-    out_ref[2, pl.ds(0, half)] = half_ref[...]
-    out_ref[2, pl.ds(half, half)] = rest_ref[...]
-    out_ref[3] = before_ref[...]
+def spread_kernel(*refs):
+    *parts, out_ref, done = refs
+    copies = []
+    for x in range(X):
+        first = 0
+        for part_ref in parts:
+            place = out_ref.at[x, pl.ds(first, part_ref.shape[0])]
+            copies.append(pltpu.make_async_copy(part_ref, place, done.at[len(copies)]))
+            first += part_ref.shape[0]
+    for copy in copies:
+        copy.start()
+    for copy in copies:
+        copy.wait()
+
+
+def settle_kernel(*refs):
+    count = len(refs) // 2
+    copies = [
+        pltpu.make_async_copy(refs[i], refs[count + i], refs[-1].at[i]) for i in range(count)
+    ]
+    for copy in copies:
+        copy.start()
+    for copy in copies:
+        copy.wait()
 
 
 def gather_section(where, w_qkv, w_out, norm_gain):
     rows = w_qkv.shape[1]
     shape = (ZH, rows, QKV + CTX)
-    vmem = pl.BlockSpec(memory_space=pltpu.VMEM)
+    anywhere = pl.BlockSpec(memory_space=pl.ANY)
     shards = pl.pallas_call(
         shard_kernel,
         out_shape=jax.ShapeDtypeStruct(shape, BF16),
@@ -208,62 +225,53 @@
             ],
             out_specs=pl.BlockSpec(shape, lambda i, where: (0, 0, 0)),
         ),
-        compiler_params=SMALL,
+        compiler_params=pltpu.CompilerParams(vmem_limit_bytes=48 * 1024 * 1024),
         name="shard",
     )(where, w_qkv, w_out.transpose(0, 2, 1), norm_gain)
 
-    one, other = [(x, (x + 1) % X) for x in range(X)], [(x, (x - 1) % X) for x in range(X)]
-
-    def first_along_x(parts):
-        return lax.ppermute(parts, "x", one), lax.ppermute(parts, "x", other)
-
-    def rest_along_x(parts, before, after):
-        half = parts.shape[0] // 2
-        return pl.pallas_call(
-            join_kernel,
-            out_shape=jax.ShapeDtypeStruct((X, *parts.shape), BF16),
-            in_specs=[vmem] * 5,
-            out_specs=vmem,
-            compiler_params=MEDIUM,
-            name="join",
-        )(
-            parts,
-            after,
-            before,
-            lax.ppermute(before[:half], "x", one),
-            lax.ppermute(after[half:], "x", other),
-        )
+
+    def along_x(*parts):
+        count = sum(part.shape[0] for part in parts)
+        copies = pl.pallas_call(
+            spread_kernel,
+            out_shape=jax.ShapeDtypeStruct((X, count, rows, QKV + CTX), BF16),
+            in_specs=[anywhere] * len(parts),
+            out_specs=anywhere,
+            scratch_shapes=[pltpu.SemaphoreType.DMA((X * len(parts),))],
+            compiler_params=SMALL,
+            name="spread",
+        )(*parts)
+        return lax.all_to_all(copies, "x", 0, 0)
 
     def along_z(parts, by):
         return lax.ppermute(parts, ("z_hi", "tensor"), [(z, (z + by) % Z) for z in range(Z)])
+
+    def swapped(parts):
+        return lax.ppermute(parts, "core", [(0, 1), (1, 0)])
 
     here = lax.all_to_all(shards, "z_hi", 0, 0)
     half = ZH // 2
     ahead, behind = along_z(here, 1), along_z(here, -1)
-    here_x = first_along_x(here)
-    near, *here_x = lax.optimization_barrier((jnp.concatenate([ahead, behind]), *here_x))
-    near_x = first_along_x(near)
-    across = jnp.concatenate([along_z(ahead[:half], 1), along_z(behind[half:], -1)])
-    across, *here_x = lax.optimization_barrier((across, *here_x))
-    across_x = first_along_x(across)
-    _, *near_x = lax.optimization_barrier((across, *near_x))
-    own = [
-        rest_along_x(here, *here_x),
-        rest_along_x(near, *near_x),
-        rest_along_x(across, *across_x),
-    ]
-    return own + [lax.ppermute(part, "core", [(0, 1), (1, 0)]) for part in own]
-
-
-def turned(values, by):
-    result = values
-    for count in range(1, X):
-        result = jnp.where(by == count, pltpu.roll(values, 64 * count, 1), result)
-    return result
+    here_x = along_x(here)
+    across = along_z(ahead[:half], 1), along_z(behind[half:], -1)
+    *near, here_x = lax.optimization_barrier((ahead, behind, here_x))
+    near_x = along_x(*near)
+    *across, near_x = lax.optimization_barrier((*across, near_x))
+    own = [here_x, near_x, along_x(*across)]
+    weights = own + [swapped(part) for part in own]
+    return pl.pallas_call(
+        settle_kernel,
+        out_shape=[jax.ShapeDtypeStruct(part.shape, part.dtype) for part in weights],
+        in_specs=[anywhere] * len(weights),
+        out_specs=[pl.BlockSpec(memory_space=pltpu.VMEM)] * len(weights),
+        scratch_shapes=[pltpu.SemaphoreType.DMA((len(weights),))],
+        compiler_params=MEDIUM,
+        name="settle",
+    )(*weights)
 
 
 def enter_kernel(where, down_ref, up_ref, down_docs_ref, up_docs_ref, out_ref, allowed_ref):
-    member = where[3]
+    member = where[2]
     x_ref = jnp.where(member < 2, down_ref[member % 2], up_ref[member % 2]).astype(F32)
     docs = [docs_ref[...] for docs_ref in (down_docs_ref, up_docs_ref)]
     docs = jnp.where(member < 2, docs[0], docs[1])
@@ -285,9 +293,9 @@
                 else jnp.where(lane < 64, pltpu.roll(a, 64, 1), b)
                 for a, b in (tiles[:2], tiles[2:])
             ]
-            cores.append(turned(jnp.concatenate(pairs, axis=1), (X - where[1]) % X))
+            cores.append(jnp.concatenate(pairs, axis=1))
         for i in range(2):
-            part = jnp.where(where[2] == i, cores[0], cores[1])
+            part = jnp.where(where[1] == i, cores[0], cores[1])
             out_ref[:, pl.ds((i * ZH + zh) * ROWS, ROWS)] = part.astype(BF16)
 
 
@@ -299,10 +307,9 @@
     tiles = {}
     for zh in range(ZH):
         mine, other = (
-            turned(values[:, (i * ZH + zh) * ROWS : (i * ZH + zh + 1) * ROWS], where[1])
-            for i in range(2)
+            values[:, (i * ZH + zh) * ROWS : (i * ZH + zh + 1) * ROWS] for i in range(2)
         )
-        zero, one = jnp.where(where[2] == 0, mine, other), jnp.where(where[2] == 0, other, mine)
+        zero, one = jnp.where(where[1] == 0, mine, other), jnp.where(where[1] == 0, other, mine)
         for pair in range(2):
             a, b = (part[:, pair * 128 : (pair + 1) * 128] for part in (zero, one))
             tiles[2 * pair, zh] = jnp.where(lane < 64, a, pltpu.roll(b, 64, 1))
@@ -311,7 +318,7 @@
         [tiles[x, zh] for x in range(X) for zh in range(ZH)], axis=1
     ).astype(BF16)
     for k in range(len(received)):
-        source = (where[3] + len(received) - k) % len(received)
+        source = (where[2] + len(received) - k) % len(received)
         part = natural[k * rows : (k + 1) * rows]
 
         @pl.when(source < 2)
@@ -347,7 +354,7 @@
 
 
 def on_device(down_in, up_in, w_qkv, w_out, norm_gain, down_docs, up_docs):
-    where = jnp.stack([lax.axis_index(name) for name in ("pipe", "x", "core", "tensor")])
+    where = jnp.stack([lax.axis_index(name) for name in ("pipe", "core", "tensor")])
     sections = lax.axis_size("pipe")
     weights = gather_section(where, w_qkv, w_out, norm_gain)
     rope = rotary_tables()

time: 219 us -> 230 us (1.050)
  starting transfers between devices: 129 us -> 109 us
  waiting for transfers between devices: 31.1 us -> 51.1 us
  Pallas kernels: 11.2 us -> 17.1 us
  local copies, waits for them, and re-layouts: 2.82 us -> 6.73 us
    ppermute x15 -> x3, starting transfers between devices: 43.8 us -> 5.93 us  [swapped(): return lax.ppermute(parts, 'core', [(0, 1), (1, 0)])]
    all_to_all x0 -> x3, waiting for transfers between devices: none -> 30 us  [along_x(): return lax.all_to_all(copies, 'x', 0, 0)]
    all_to_all x0 -> x3, starting transfers between devices: none -> 16 us  [along_x(): return lax.all_to_all(copies, 'x', 0, 0)]
    ppermute x15 -> x3, waiting for transfers between devices: 18.2 us -> 2.33 us  [swapped(): return lax.ppermute(parts, 'core', [(0, 1), (1, 0)])]
    pallas_call x3 -> x4, Pallas kernels: 0.41 us -> 6.64 us  [the longest x3 3.79 us: along_x(): pl.pallas_call(spread_kernel, out_shape=jax.ShapeDtypeStruct((X, count, r...]
    ppermute x4, waiting for transfers between devices: 8.02 us -> 13.9 us  [along_z(): lax.ppermute(parts, ('z_hi', 'tensor'), [(z, (z + by) % Z) for z in range...]
    unnamed x14 -> x22, local copies, waits for them, and re-layouts: 2.65 us -> 6.68 us
  transfers between devices with their start and end apart: 30 -> 21, of which waited for: 14 -> 9; matrix products, arithmetic and copies ran while one was open for 0% -> 0% of each run, Pallas kernels for 0% -> 1%
where the time goes in v4:
time: 230 us; the launch traced here: 227 us
  starting transfers between devices  109 us (47%)
  waiting for transfers between devices  51.1 us (22%)
  blocking collectives  42.2 us (18%)
  Pallas kernels  17.1 us (7%)
  local copies, waits for them, and re-layouts  6.73 us (3%)
    ppermute x4, starting transfers between devices, exchange(): received.append(lax.ppermute(chunk, ('pipe', 'tensor'), pairs))  67.3 us
    all_to_all x1, blocking collectives, gather_section(): here = lax.all_to_all(shards, 'z_hi', 0, 0)  42.2 us
    all_to_all x3, waiting for transfers between devices, along_x(): return lax.all_to_all(copies, 'x', 0, 0)  30 us
    all_to_all x3, starting transfers between devices, along_x(): return lax.all_to_all(copies, 'x', 0, 0)  16 us
    ppermute x4, starting transfers between devices, along_z(): lax.ppermute(parts, ('z_hi', 'tensor'), [(z, (z + by) % Z) for z in range...  14.1 us
    ppermute x4, waiting for transfers between devices, along_z(): lax.ppermute(parts, ('z_hi', 'tensor'), [(z, (z + by) % Z) for z in range...  13.9 us
    pallas_call x8, Pallas kernels, run_section(): pl.pallas_call(functools.partial(section_kernel, step, last), out_shape=[...  7.64 us
    unnamed x22, local copies, waits for them, and re-layouts  6.68 us
  transfers between devices with their start and end apart: 21, of which 9 were waited for; matrix products, arithmetic and copies ran while one was open for 0% of the time, Pallas kernels for 1%

profile of v4, /device:TPU:6, one launch (start us, length us, event | category | flops | bytes accessed | tf_op | source)
XLA Modules:
  0.0 227.0 jit_solution(2232076845294352521)
XLA Ops:
  4.1 42.2 %all_to_all.20.refs_0_ = bf16[4,64,640]{2,1,0:T(8,128)(2,1)S(1)} all-to-all(bf16[4,64,640]{2,1,0:T(8,128)(2,1)S(1)} %shard.1), channel_id=1, replica_groups=mesh['x'=4,'z_hi'=4,'core'=2,'pipe'=8,'tensor'=4] {'z_hi'}, dimensions={0} | all-to-all | bytes 655360 | tf_op jit(solution)/shard_map/all_to_all | solution.py:252
  47.4 4.8 %all-to-all-start.1 = ((bf16[4,4,64,640]{3,2,1,0:T(8,128)(2,1)}), bf16[4,4,64,640]{3,2,1,0:T(8,128)(2,1)S(1)}, u32[]{:S(2)}, u32[]{:S(2)}) async-start(bf16[4,4,64,640]{3,2,1,0:T(8,128)(2,1)} %spread.3), calls=%async_computation.1 | async-start | bytes 2621440 | tf_op jit(solution)/shard_map/all_to_all | solution.py:244
  52.2 3.7 %collective-permute-start = (bf16[4,64,640]{2,1,0:T(8,128)(2,1)S(1)}, bf16[4,64,640]{2,1,0:T(8,128)(2,1)S(1)}, u32[]{:S(2)}, u32[]{:S(2)}) collective-permute-start(bf16[4,64,640]{2,1,0:T(8,128)(2,1)S(1)} %all_to_all.20.refs_0_), channel_id=1, source_target_pairs={{0,1},{1,2},{2,3},{3,64},{64,65},{65,66},{66,67},{67,128},{128,129... | collective-permute-start | bytes 983048 | tf_op jit(solution)/shard_map/ppermute | solution.py:247
  55.9 3.4 %collective-permute-start.1 = (bf16[4,64,640]{2,1,0:T(8,128)(2,1)S(1)}, bf16[4,64,640]{2,1,0:T(8,128)(2,1)S(1)}, u32[]{:S(2)}, u32[]{:S(2)}) collective-permute-start(bf16[4,64,640]{2,1,0:T(8,128)(2,1)S(1)} %all_to_all.20.refs_0_), channel_id=1, source_target_pairs={{0,195},{1,0},{2,1},{3,2},{64,3},{65,64},{66,65},{67,66},{128,67},... | collective-permute-start | bytes 983048 | tf_op jit(solution)/shard_map/ppermute | solution.py:247
  59.3 3.1 %collective-permute-done.refs_0_ = bf16[4,64,640]{2,1,0:T(8,128)(2,1)S(1)} collective-permute-done((bf16[4,64,640]{2,1,0:T(8,128)(2,1)S(1)}, bf16[4,64,640]{2,1,0:T(8,128)(2,1)S(1)}, u32[]{:S(2)}, u32[]{:S(2)}) %collective-permute-start) | collective-permute-done | bytes 327712 | tf_op jit(solution)/shard_map/ppermute | solution.py:247
  62.4 4.6 %collective-permute-done.1.refs_1_ = bf16[4,64,640]{2,1,0:T(8,128)(2,1)S(1)} collective-permute-done((bf16[4,64,640]{2,1,0:T(8,128)(2,1)S(1)}, bf16[4,64,640]{2,1,0:T(8,128)(2,1)S(1)}, u32[]{:S(2)}, u32[]{:S(2)}) %collective-permute-start.1) | collective-permute-done | bytes 327712 | tf_op jit(solution)/shard_map/ppermute | solution.py:247
  69.6 4.8 %all-to-all-start.2 = ((bf16[4,8,64,640]{3,2,1,0:T(8,128)(2,1)}), bf16[4,8,64,640]{3,2,1,0:T(8,128)(2,1)S(1)}, u32[]{:S(2)}, u32[]{:S(2)}) async-start(bf16[4,8,64,640]{3,2,1,0:T(8,128)(2,1)} %copy-done), calls=%async_computation.2 | async-start | bytes 5242880 | tf_op jit(solution)/shard_map/all_to_all | solution.py:244
  74.4 4.1 %collective-permute-start.2 = (bf16[2,64,640]{2,1,0:T(8,128)(2,1)S(1)}, bf16[2,64,640]{2,1,0:T(8,128)(2,1)S(1)}, u32[]{:S(2)}, u32[]{:S(2)}) collective-permute-start(bf16[2,64,640]{2,1,0:T(8,128)(2,1)S(1)} %slice.8), channel_id=1, source_target_pairs={{0,1},{1,2},{2,3},{3,64},{64,65},{65,66},{66,67},{67,128},{128,129... | collective-permute-start | bytes 491528 | tf_op jit(solution)/shard_map/ppermute | solution.py:247
  78.5 3.0 %collective-permute-start.3 = (bf16[2,64,640]{2,1,0:T(8,128)(2,1)S(1)}, bf16[2,64,640]{2,1,0:T(8,128)(2,1)S(1)}, u32[]{:S(2)}, u32[]{:S(2)}) collective-permute-start(bf16[2,64,640]{2,1,0:T(8,128)(2,1)S(1)} %slice.9), channel_id=1, source_target_pairs={{0,195},{1,0},{2,1},{3,2},{64,3},{65,64},{66,65},{67,66},{128,67},... | collective-permute-start | bytes 491528 | tf_op jit(solution)/shard_map/ppermute | solution.py:247
  82.8 4.8 %collective-permute-done.3.refs_1_ = bf16[2,64,640]{2,1,0:T(8,128)(2,1)S(1)} collective-permute-done((bf16[2,64,640]{2,1,0:T(8,128)(2,1)S(1)}, bf16[2,64,640]{2,1,0:T(8,128)(2,1)S(1)}, u32[]{:S(2)}, u32[]{:S(2)}) %collective-permute-start.3) | collective-permute-done | bytes 163872 | tf_op jit(solution)/shard_map/ppermute | solution.py:247
  87.6 15.3 %all-to-all-done.2.refs_1_ = bf16[4,8,64,640]{3,2,1,0:T(8,128)(2,1)S(1)} async-done(((bf16[4,8,64,640]{3,2,1,0:T(8,128)(2,1)}), bf16[4,8,64,640]{3,2,1,0:T(8,128)(2,1)S(1)}, u32[]{:S(2)}, u32[]{:S(2)}) %all-to-all-start.2) | async-done | bytes 2621472 | tf_op jit(solution)/shard_map/all_to_all | solution.py:244
  102.9 1.9 collective-permute-start.5
  104.8 1.8 spread.5
  107.7 6.5 %all-to-all-start.3 = ((bf16[4,4,64,640]{3,2,1,0:T(8,128)(2,1)}), bf16[4,4,64,640]{3,2,1,0:T(8,128)(2,1)}, u32[]{:S(2)}, u32[]{:S(2)}) async-start(bf16[4,4,64,640]{3,2,1,0:T(8,128)(2,1)} %copy-done.3), calls=%async_computation.3 | async-start | bytes 2621440 | tf_op jit(solution)/shard_map/all_to_all | solution.py:244
  114.1 2.1 collective-permute-start.4
  116.3 14.8 %all-to-all-done.3.refs_2_ = bf16[4,4,64,640]{3,2,1,0:T(8,128)(2,1)} async-done(((bf16[4,4,64,640]{3,2,1,0:T(8,128)(2,1)}), bf16[4,4,64,640]{3,2,1,0:T(8,128)(2,1)}, u32[]{:S(2)}, u32[]{:S(2)}) %all-to-all-start.3) | async-done | bytes 1310752 | tf_op jit(solution)/shard_map/all_to_all | solution.py:244
  131.0 1.9 collective-permute-start.6
  133.8 2.3 %collective-permute-done.6.refs_5_ = bf16[4,4,64,640]{3,2,1,0:T(8,128)(2,1)S(1)} collective-permute-done((bf16[4,4,64,640]{3,2,1,0:T(8,128)(2,1)}, bf16[4,4,64,640]{3,2,1,0:T(8,128)(2,1)S(1)}, u32[]{:S(2)}, u32[]{:S(2)}) %collective-permute-start.6) | collective-permute-done | bytes 1310752 | tf_op jit(solution)/shard_map/ppermute | solution.py:250
  137.5 2.9 %settle.1 = (bf16[4,4,64,640]{3,2,1,0:T(8,128)(2,1)S(1)}, bf16[4,8,64,640]{3,2,1,0:T(8,128)(2,1)S(1)}, bf16[4,4,64,640]{3,2,1,0:T(8,128)(2,1)S(1)}, bf16[4,4,64,...) custom-call(bf16[4,4,64,640]{3,2,1,0:T(8,128)(2,1)S(1)} %copy-done.2, ...), custom_call_target="tpu_custom_call" | custom-call | tf_op jit(solution)/shard_map/settle/pallas_call | solution.py:262
  140.3 3.4 %section.8.held_ref = bf16[32,2048]{1,0:T(8,128)(2,1)S(1)} custom-call(s32[3]{0:T(128)S(1)} %pad_add_fusion.where, bf16[32,2048]{1,0:T(8,128)(2,1)S(1)} %get-tuple-element.20.x_ref, f32[128,32]{1,0:T(8,128)S(1)} %get-tuple-element.21.allowed_ref, bf16[32,2048]{1,0:T(8,128)(2,1)S(1)} %broadcast_in_dim.73.held_ref, ...), custom_call_target="tpu_custom_call", output_to_operand_aliasing={{}: (3, {})} | custom-call | tf_op jit(solution)/shard_map/section/pallas_call | solution.py:147
  145.1 3.3 %collective-permute-done.7.x_ref = bf16[32,2048]{1,0:T(8,128)(2,1)S(1)} collective-permute-done((bf16[32,2048]{1,0:T(8,128)(2,1)S(1)}, bf16[32,2048]{1,0:T(8,128)(2,1)S(1)}, u32[]{:S(2)}, u32[]{:S(2)}) %collective-permute-start.7) | collective-permute-done | bytes 131104 | tf_op jit(solution)/shard_map/ppermute | solution.py:376
  157.5 3.4 %collective-permute-start.15 = (bf16[8,2048]{1,0:T(8,128)(2,1)S(1)}, bf16[8,2048]{1,0:T(8,128)(2,1)S(1)}, u32[]{:S(2)}, u32[]{:S(2)}) collective-permute-start(bf16[8,2048]{1,0:T(8,128)(2,1)S(1)} %get-tuple-element.35), channel_id=1, source_target_pairs={{0,1},{1,2},{2,31},{3,28},{4,5},{5,6},{6,27},{7,24},{8,9},{9,10},{... | collective-permute-start | bytes 98312 | tf_op jit(solution)/shard_map/ppermute | solution.py:343
  160.8 59.0 %collective-permute-start.16 = (bf16[8,2048]{1,0:T(8,128)(2,1)S(1)}, bf16[8,2048]{1,0:T(8,128)(2,1)S(1)}, u32[]{:S(2)}, u32[]{:S(2)}) collective-permute-start(bf16[8,2048]{1,0:T(8,128)(2,1)S(1)} %get-tuple-element.36), channel_id=1, source_target_pairs={{0,2},{1,3},{2,28},{3,29},{4,6},{5,7},{6,24},{7,25},{8,10},{9,11},... | collective-permute-start | bytes 98312 | tf_op jit(solution)/shard_map/ppermute | solution.py:343
  219.8 4.3 %collective-permute-start.17 = (bf16[8,2048]{1,0:T(8,128)(2,1)S(1)}, bf16[8,2048]{1,0:T(8,128)(2,1)S(1)}, u32[]{:S(2)}, u32[]{:S(2)}) collective-permute-start(bf16[8,2048]{1,0:T(8,128)(2,1)S(1)} %get-tuple-element.37), channel_id=1, source_target_pairs={{0,3},{1,0},{2,29},{3,30},{4,7},{5,4},{6,25},{7,26},{8,11},{9,8},{... | collective-permute-start | bytes 98312 | tf_op jit(solution)/shard_map/ppermute | solution.py:343
  (64 shorter events, 24.8 us)
Async XLA Ops:
  47.4 19.6 %all-to-all-start.1 = ((bf16[4,4,64,640]{3,2,1,0:T(8,128)(2,1)}), bf16[4,4,64,640]{3,2,1,0:T(8,128)(2,1)S(1)}, u32[]{:S(2)}, u32[]{:S(2)}) async-start(bf16[4,4,64,640]{3,2,1,0:T(8,128)(2,1)} %spread.3), calls=%async_computation.1 | async-start | bytes 2621440 | tf_op jit(solution)/shard_map/all_to_all | solution.py:244
  52.2 10.2 %collective-permute-start = (bf16[4,64,640]{2,1,0:T(8,128)(2,1)S(1)}, bf16[4,64,640]{2,1,0:T(8,128)(2,1)S(1)}, u32[]{:S(2)}, u32[]{:S(2)}) collective-permute-start(bf16[4,64,640]{2,1,0:T(8,128)(2,1)S(1)} %all_to_all.20.refs_0_), channel_id=1, source_target_pairs={{0,1},{1,2},{2,3},{3,64},{64,65},{65,66},{66,67},{67,128},{128,129... | collective-permute-start | bytes 983048 | tf_op jit(solution)/shard_map/ppermute | solution.py:247
  55.9 11.1 %collective-permute-start.1 = (bf16[4,64,640]{2,1,0:T(8,128)(2,1)S(1)}, bf16[4,64,640]{2,1,0:T(8,128)(2,1)S(1)}, u32[]{:S(2)}, u32[]{:S(2)}) collective-permute-start(bf16[4,64,640]{2,1,0:T(8,128)(2,1)S(1)} %all_to_all.20.refs_0_), channel_id=1, source_target_pairs={{0,195},{1,0},{2,1},{3,2},{64,3},{65,64},{66,65},{67,66},{128,67},... | collective-permute-start | bytes 983048 | tf_op jit(solution)/shard_map/ppermute | solution.py:247
  69.6 33.3 %all-to-all-start.2 = ((bf16[4,8,64,640]{3,2,1,0:T(8,128)(2,1)}), bf16[4,8,64,640]{3,2,1,0:T(8,128)(2,1)S(1)}, u32[]{:S(2)}, u32[]{:S(2)}) async-start(bf16[4,8,64,640]{3,2,1,0:T(8,128)(2,1)} %copy-done), calls=%async_computation.2 | async-start | bytes 5242880 | tf_op jit(solution)/shard_map/all_to_all | solution.py:244
  74.4 8.4 %collective-permute-start.2 = (bf16[2,64,640]{2,1,0:T(8,128)(2,1)S(1)}, bf16[2,64,640]{2,1,0:T(8,128)(2,1)S(1)}, u32[]{:S(2)}, u32[]{:S(2)}) collective-permute-start(bf16[2,64,640]{2,1,0:T(8,128)(2,1)S(1)} %slice.8), channel_id=1, source_target_pairs={{0,1},{1,2},{2,3},{3,64},{64,65},{65,66},{66,67},{67,128},{128,129... | collective-permute-start | bytes 491528 | tf_op jit(solution)/shard_map/ppermute | solution.py:247
  78.5 9.1 %collective-permute-start.3 = (bf16[2,64,640]{2,1,0:T(8,128)(2,1)S(1)}, bf16[2,64,640]{2,1,0:T(8,128)(2,1)S(1)}, u32[]{:S(2)}, u32[]{:S(2)}) collective-permute-start(bf16[2,64,640]{2,1,0:T(8,128)(2,1)S(1)} %slice.9), channel_id=1, source_target_pairs={{0,195},{1,0},{2,1},{3,2},{64,3},{65,64},{66,65},{67,66},{128,67},... | collective-permute-start | bytes 491528 | tf_op jit(solution)/shard_map/ppermute | solution.py:247
  102.9 33.3 %collective-permute-start.5 = (bf16[4,8,64,640]{3,2,1,0:T(8,128)(2,1)S(1)}, bf16[4,8,64,640]{3,2,1,0:T(8,128)(2,1)}, u32[]{:S(2)}, u32[]{:S(2)}) collective-permute-start(bf16[4,8,64,640]{3,2,1,0:T(8,128)(2,1)S(1)} %all-to-all-done.2.refs_1_), channel_id=1, source_target_pairs={{0,32},{32,0},{1,33},{33,1},{2,34},{34,2},{3,35},{35,3},{4,36},{36... | collective-permute-start | bytes 7864328 | tf_op jit(solution)/shard_map/ppermute | solution.py:250
  107.7 25.3 %copy-start.7 = (bf16[2,32,2048]{2,1,0:T(8,128)(2,1)S(1)}, bf16[2,32,2048]{2,1,0:T(8,128)(2,1)}, u32[]{:S(2)}) copy-start(bf16[2,32,2048]{2,1,0:T(8,128)(2,1)} %up_ref.1) | copy-start | bytes 786436
  107.7 25.3 %copy-start.9 = (s32[2,32]{1,0:T(2,128)S(1)}, s32[2,32]{1,0:T(2,128)}, u32[]{:S(2)}) copy-start(s32[2,32]{1,0:T(2,128)} %down_docs_ref.1) | copy-start | bytes 772
  107.7 25.3 %copy-start.10 = (s32[2,32]{1,0:T(2,128)S(1)}, s32[2,32]{1,0:T(2,128)}, u32[]{:S(2)}) copy-start(s32[2,32]{1,0:T(2,128)} %up_docs_ref.1) | copy-start | bytes 772
  107.7 23.4 %all-to-all-start.3 = ((bf16[4,4,64,640]{3,2,1,0:T(8,128)(2,1)}), bf16[4,4,64,640]{3,2,1,0:T(8,128)(2,1)}, u32[]{:S(2)}, u32[]{:S(2)}) async-start(bf16[4,4,64,640]{3,2,1,0:T(8,128)(2,1)} %copy-done.3), calls=%async_computation.3 | async-start | bytes 2621440 | tf_op jit(solution)/shard_map/all_to_all | solution.py:244
  114.1 19.7 %collective-permute-start.4 = (bf16[4,4,64,640]{3,2,1,0:T(8,128)(2,1)}, bf16[4,4,64,640]{3,2,1,0:T(8,128)(2,1)}, u32[]{:S(2)}, u32[]{:S(2)}) collective-permute-start(bf16[4,4,64,640]{3,2,1,0:T(8,128)(2,1)} %copy-done.1), channel_id=1, source_target_pairs={{0,32},{32,0},{1,33},{33,1},{2,34},{34,2},{3,35},{35,3},{4,36},{36... | collective-permute-start | bytes 3932168 | tf_op jit(solution)/shard_map/ppermute | solution.py:250
  131.0 5.1 %collective-permute-start.6 = (bf16[4,4,64,640]{3,2,1,0:T(8,128)(2,1)}, bf16[4,4,64,640]{3,2,1,0:T(8,128)(2,1)S(1)}, u32[]{:S(2)}, u32[]{:S(2)}) collective-permute-start(bf16[4,4,64,640]{3,2,1,0:T(8,128)(2,1)} %all-to-all-done.3.refs_2_), channel_id=1, source_target_pairs={{0,32},{32,0},{1,33},{33,1},{2,34},{34,2},{3,35},{35,3},{4,36},{36... | collective-permute-start | bytes 3932168 | tf_op jit(solution)/shard_map/ppermute | solution.py:250
  143.8 4.6 %collective-permute-start.7 = (bf16[32,2048]{1,0:T(8,128)(2,1)S(1)}, bf16[32,2048]{1,0:T(8,128)(2,1)S(1)}, u32[]{:S(2)}, u32[]{:S(2)}) collective-permute-start(bf16[32,2048]{1,0:T(8,128)(2,1)S(1)} %section.8.held_ref), channel_id=1, source_target_pairs={{0,4},{1,5},{2,6},{3,7},{32,36},{33,37},{34,38},{35,39},{64,68},{6... | collective-permute-start | bytes 393224 | tf_op jit(solution)/shard_map/ppermute | solution.py:376
  149.0 0.7 collective-permute-start.8
  150.2 0.7 collective-permute-start.9
  151.5 0.7 collective-permute-start.10
  152.8 0.7 collective-permute-start.11
  154.2 0.7 collective-permute-start.12
  155.5 0.7 collective-permute-start.13
  156.8 67.3 %collective-permute-start.14 = (bf16[8,2048]{1,0:T(8,128)(2,1)S(1)}, bf16[8,2048]{1,0:T(8,128)(2,1)S(1)}, u32[]{:S(2)}, u32[]{:S(2)}) collective-permute-start(bf16[8,2048]{1,0:T(8,128)(2,1)S(1)} %get-tuple-element.34), channel_id=1, source_target_pairs={{0,0},{1,1},{2,30},{3,31},{4,4},{5,5},{6,26},{7,27},{8,8},{9,9},{1... | collective-permute-start | bytes 98312 | tf_op jit(solution)/shard_map/ppermute | solution.py:343
  157.5 66.6 %collective-permute-start.15 = (bf16[8,2048]{1,0:T(8,128)(2,1)S(1)}, bf16[8,2048]{1,0:T(8,128)(2,1)S(1)}, u32[]{:S(2)}, u32[]{:S(2)}) collective-permute-start(bf16[8,2048]{1,0:T(8,128)(2,1)S(1)} %get-tuple-element.35), channel_id=1, source_target_pairs={{0,1},{1,2},{2,31},{3,28},{4,5},{5,6},{6,27},{7,24},{8,9},{9,10},{... | collective-permute-start | bytes 98312 | tf_op jit(solution)/shard_map/ppermute | solution.py:343
  160.8 63.3 %collective-permute-start.16 = (bf16[8,2048]{1,0:T(8,128)(2,1)S(1)}, bf16[8,2048]{1,0:T(8,128)(2,1)S(1)}, u32[]{:S(2)}, u32[]{:S(2)}) collective-permute-start(bf16[8,2048]{1,0:T(8,128)(2,1)S(1)} %get-tuple-element.36), channel_id=1, source_target_pairs={{0,2},{1,3},{2,28},{3,29},{4,6},{5,7},{6,24},{7,25},{8,10},{9,11},... | collective-permute-start | bytes 98312 | tf_op jit(solution)/shard_map/ppermute | solution.py:343
  219.8 5.9 %collective-permute-start.17 = (bf16[8,2048]{1,0:T(8,128)(2,1)S(1)}, bf16[8,2048]{1,0:T(8,128)(2,1)S(1)}, u32[]{:S(2)}, u32[]{:S(2)}) collective-permute-start(bf16[8,2048]{1,0:T(8,128)(2,1)S(1)} %get-tuple-element.37), channel_id=1, source_target_pairs={{0,3},{1,0},{2,29},{3,30},{4,7},{5,4},{6,25},{7,26},{8,11},{9,8},{... | collective-permute-start | bytes 98312 | tf_op jit(solution)/shard_map/ppermute | solution.py:343
  (8 other events, 32.9 us)

commit v5 on v3

--- a/solution.py
+++ b/solution.py
@@ -156,15 +156,24 @@
     )(where, values, allowed, held, *rope, *weights)
 
 
-def shard_kernel(where, qkv_ref, out_ref, gain_ref, shard_ref):
-    rows = qkv_ref.shape[1]
+def shard_kernel(where, qkv_any, out_any, gain_any, shard_ref, qkv_ref, out_ref, gain_ref, done):
+    copies = [
+        pltpu.make_async_copy(qkv_any.at[where[0]], qkv_ref, done.at[0]),
+        pltpu.make_async_copy(out_any.at[where[0]], out_ref, done.at[1]),
+        pltpu.make_async_copy(gain_any, gain_ref, done.at[2]),
+    ]
+    for copy in copies:
+        copy.start()
+    for copy in copies:
+        copy.wait()
+    rows = qkv_ref.shape[0]
     section = lax.broadcasted_iota(jnp.int32, gain_ref.shape, 0)
     gain = jnp.where(section == where[0], gain_ref[...].astype(F32), 0.0)
     gain = jnp.sum(gain, axis=0, keepdims=True)
     row = lax.broadcasted_iota(jnp.int32, (rows, rows), 0)
     column = lax.broadcasted_iota(jnp.int32, (rows, rows), 1)
     gain = jnp.sum(jnp.where(row == column, gain, 0.0), axis=1, keepdims=True)
-    qkv = qkv_ref[0].astype(F32) * gain
+    qkv = qkv_ref[...].astype(F32) * gain
     one, two = qkv[:, :128], qkv[:, 128:256]
     lane = lax.broadcasted_iota(jnp.int32, (rows, 128), 1)
 
@@ -176,10 +185,19 @@
 
     first = lanes([one, pltpu.roll(one, 96, 1), pltpu.roll(two, 64, 1), pltpu.roll(two, 32, 1)])
     second = lanes([pltpu.roll(one, 96, 1), pltpu.roll(one, 64, 1), pltpu.roll(two, 32, 1), two])
-    shard = jnp.concatenate([first, second, qkv[:, 256:]], axis=1).astype(BF16)
-    for z in range(shard_ref.shape[0]):
-        shard_ref[z, :, pl.ds(0, QKV)] = shard
-        shard_ref[z, :, pl.ds(QKV, CTX)] = out_ref[0]
+    shard_ref[:, pl.ds(0, 128)] = first.astype(BF16)
+    shard_ref[:, pl.ds(128, 128)] = second.astype(BF16)
+    shard_ref[:, pl.ds(256, 128)] = qkv[:, 256:].astype(BF16)
+    shard_ref[:, pl.ds(QKV, CTX)] = out_ref[...]
+
+
+def column_kernel(where, own_ref, below_ref, above_ref, half_ref, rest_ref, out_ref):
+    own, half = where[4], half_ref.shape[0]
+    out_ref[own] = own_ref[...]
+    out_ref[(own + ZH - 1) % ZH] = below_ref[...]
+    out_ref[(own + 1) % ZH] = above_ref[...]
+    out_ref[(own + 2) % ZH, pl.ds(0, half)] = half_ref[...]
+    out_ref[(own + 2) % ZH, pl.ds(half, half)] = rest_ref[...]
 
 
 def join_kernel(here_ref, after_ref, before_ref, half_ref, rest_ref, out_ref):
@@ -193,22 +211,19 @@
 
 def gather_section(where, w_qkv, w_out, norm_gain):
     rows = w_qkv.shape[1]
-    shape = (ZH, rows, QKV + CTX)
     vmem = pl.BlockSpec(memory_space=pltpu.VMEM)
-    shards = pl.pallas_call(
+    smem = pl.BlockSpec(memory_space=pltpu.SMEM)
+    shard = pl.pallas_call(
         shard_kernel,
-        out_shape=jax.ShapeDtypeStruct(shape, BF16),
-        grid_spec=pltpu.PrefetchScalarGridSpec(
-            num_scalar_prefetch=1,
-            grid=(1,),
-            in_specs=[
-                pl.BlockSpec((1, rows, QKV), lambda i, where: (where[0], 0, 0)),
-                pl.BlockSpec((1, rows, CTX), lambda i, where: (where[0], 0, 0)),
-                pl.BlockSpec(norm_gain.shape, lambda i, where: (0, 0)),
-            ],
-            out_specs=pl.BlockSpec(shape, lambda i, where: (0, 0, 0)),
-        ),
-        compiler_params=SMALL,
+        out_shape=jax.ShapeDtypeStruct((rows, QKV + CTX), BF16),
+        in_specs=[smem] + [pl.BlockSpec(memory_space=pl.ANY)] * 3,
+        out_specs=vmem,
+        scratch_shapes=[
+            pltpu.VMEM((rows, QKV), BF16),
+            pltpu.VMEM((rows, CTX), BF16),
+            pltpu.VMEM(norm_gain.shape, BF16),
+            pltpu.SemaphoreType.DMA((3,)),
+        ],
         name="shard",
     )(where, w_qkv, w_out.transpose(0, 2, 1), norm_gain)
 
@@ -217,40 +232,54 @@
     def first_along_x(parts):
         return lax.ppermute(parts, "x", one), lax.ppermute(parts, "x", other)
 
-    def rest_along_x(parts, before, after):
-        half = parts.shape[0] // 2
+    def rest_along_x(before, after):
+        half = before.shape[0] // 2
+        return lax.ppermute(before[:half], "x", one), lax.ppermute(after[half:], "x", other)
+
+    def join(here, before, after, half, rest):
         return pl.pallas_call(
             join_kernel,
-            out_shape=jax.ShapeDtypeStruct((X, *parts.shape), BF16),
+            out_shape=jax.ShapeDtypeStruct((X, *here.shape), BF16),
             in_specs=[vmem] * 5,
             out_specs=vmem,
             compiler_params=MEDIUM,
             name="join",
-        )(
-            parts,
-            after,
-            before,
-            lax.ppermute(before[:half], "x", one),
-            lax.ppermute(after[half:], "x", other),
-        )
+        )(here, after, before, half, rest)
 
     def along_z(parts, by):
         return lax.ppermute(parts, ("z_hi", "tensor"), [(z, (z + by) % Z) for z in range(Z)])
 
-    here = lax.all_to_all(shards, "z_hi", 0, 0)
+    here = pl.pallas_call(
+        column_kernel,
+        out_shape=jax.ShapeDtypeStruct((ZH, *shard.shape), BF16),
+        in_specs=[smem] + [vmem] * 5,
+        out_specs=vmem,
+        compiler_params=SMALL,
+        name="column",
+    )(
+        where,
+        shard,
+        along_z(shard, ZL),
+        along_z(shard, -ZL),
+        along_z(shard[: rows // 2], 2 * ZL),
+        along_z(shard[rows // 2 :], -2 * ZL),
+    )
     half = ZH // 2
     ahead, behind = along_z(here, 1), along_z(here, -1)
     here_x = first_along_x(here)
     near, *here_x = lax.optimization_barrier((jnp.concatenate([ahead, behind]), *here_x))
     near_x = first_along_x(near)
     across = jnp.concatenate([along_z(ahead[:half], 1), along_z(behind[half:], -1)])
-    across, *here_x = lax.optimization_barrier((across, *here_x))
+    here_rest = rest_along_x(*here_x)
+    across, *here_rest = lax.optimization_barrier((across, *here_rest))
     across_x = first_along_x(across)
-    _, *near_x = lax.optimization_barrier((across, *near_x))
+    near_rest = rest_along_x(*near_x)
+    *across_x, near_0, near_1 = lax.optimization_barrier((*across_x, *near_rest))
+    across_rest = rest_along_x(*across_x)
     own = [
-        rest_along_x(here, *here_x),
-        rest_along_x(near, *near_x),
-        rest_along_x(across, *across_x),
+        join(here, *here_x, *here_rest),
+        join(near, *near_x, near_0, near_1),
+        join(across, *across_x, *across_rest),
     ]
     return own + [lax.ppermute(part, "core", [(0, 1), (1, 0)]) for part in own]
 
@@ -347,7 +376,7 @@
 
 
 def on_device(down_in, up_in, w_qkv, w_out, norm_gain, down_docs, up_docs):
-    where = jnp.stack([lax.axis_index(name) for name in ("pipe", "x", "core", "tensor")])
+    where = jnp.stack([lax.axis_index(name) for name in ("pipe", "x", "core", "tensor", "z_hi")])
     sections = lax.axis_size("pipe")
     weights = gather_section(where, w_qkv, w_out, norm_gain)
     rope = rotary_tables()

time: 219 us -> 222 us (1.014)
  blocking collectives: 42.2 us -> 0 us
  starting transfers between devices: 129 us -> 165 us
  waiting for transfers between devices: 31.1 us -> 38 us
    all_to_all x1 -> x0, blocking collectives: 42.2 us -> none  [gather_section(): here = lax.all_to_all(shards, 'z_hi', 0, 0)]
    ppermute x4 -> x8, starting transfers between devices: 13.1 us -> 47.5 us  [along_z(): lax.ppermute(parts, ('z_hi', 'tensor'), [(z, (z + by) % Z) for z in range...]
    ppermute x4 -> x8, waiting for transfers between devices: 8.02 us -> 9.38 us  [along_z(): lax.ppermute(parts, ('z_hi', 'tensor'), [(z, (z + by) % Z) for z in range...]
  transfers between devices with their start and end apart: 30 -> 34, of which waited for: 14 -> 14; matrix products, arithmetic and copies ran while one was open for 0% -> 1% of each run, Pallas kernels for 0% -> 0%
where the time goes in v5:
time: 222 us; the launch traced here: 221 us
  starting transfers between devices  165 us (74%)
  waiting for transfers between devices  38 us (17%)
  Pallas kernels  13.3 us (6%)
  local copies, waits for them, and re-layouts  3.25 us (1%)
    ppermute x4, starting transfers between devices, exchange(): received.append(lax.ppermute(chunk, ('pipe', 'tensor'), pairs))  66 us
    ppermute x8, starting transfers between devices, along_z(): lax.ppermute(parts, ('z_hi', 'tensor'), [(z, (z + by) % Z) for z in range...  47.5 us
    ppermute x6, starting transfers between devices, first_along_x(): return (lax.ppermute(parts, 'x', one), lax.ppermute(parts, 'x', other))  21.5 us
    ppermute x3, waiting for transfers between devices, rest_along_x(): lax.ppermute(after[half:], 'x', other)  11.5 us
    ppermute x3, starting transfers between devices, rest_along_x(): lax.ppermute(before[:half], 'x', one)  10.3 us
    ppermute x8, waiting for transfers between devices, along_z(): lax.ppermute(parts, ('z_hi', 'tensor'), [(z, (z + by) % Z) for z in range...  9.38 us
    ppermute x3, starting transfers between devices, rest_along_x(): lax.ppermute(after[half:], 'x', other)  8.43 us
    pallas_call x8, Pallas kernels, run_section(): pl.pallas_call(functools.partial(section_kernel, step, last), out_shape=[...  7.63 us
  transfers between devices with their start and end apart: 34, of which 14 were waited for; matrix products, arithmetic and copies ran while one was open for 1% of the time, Pallas kernels for 0%

profile of v5, /device:TPU:6, one launch (start us, length us, event | category | flops | bytes accessed | tf_op | source)
XLA Modules:
  0.0 221.1 jit_solution(17547137435250952625)
XLA Ops:
  3.6 18.2 %collective-permute-start.1 = (bf16[64,640]{1,0:T(8,128)(2,1)}, bf16[64,640]{1,0:T(8,128)(2,1)S(1)}, u32[]{:S(2)}, u32[]{:S(2)}) collective-permute-start(bf16[64,640]{1,0:T(8,128)(2,1)} %shard.1.own_ref), channel_id=1, source_target_pairs={{0,192},{1,193},{2,194},{3,195},{64,0},{65,1},{66,2},{67,3},{128,6... | collective-permute-start | bytes 245768 | tf_op jit(solution)/shard_map/ppermute | solution.py:250
  24.6 9.0 %collective-permute-start.3 = (bf16[32,640]{1,0:T(8,128)(2,1)S(1)}, bf16[32,640]{1,0:T(8,128)(2,1)S(1)}, u32[]{:S(2)}, u32[]{:S(2)}) collective-permute-start(bf16[32,640]{1,0:T(8,128)(2,1)S(1)} %get-tuple-element.34), channel_id=1, source_target_pairs={{0,128},{1,129},{2,130},{3,131},{64,192},{65,193},{66,194},{67,195... | collective-permute-start | bytes 122888 | tf_op jit(solution)/shard_map/ppermute | solution.py:250
  33.6 5.6 %collective-permute-start.2 = (bf16[32,640]{1,0:T(8,128)(2,1)S(1)}, bf16[32,640]{1,0:T(8,128)(2,1)S(1)}, u32[]{:S(2)}, u32[]{:S(2)}) collective-permute-start(bf16[32,640]{1,0:T(8,128)(2,1)S(1)} %get-tuple-element.35), channel_id=1, source_target_pairs={{0,128},{1,129},{2,130},{3,131},{64,192},{65,193},{66,194},{67,195... | collective-permute-start | bytes 122888 | tf_op jit(solution)/shard_map/ppermute | solution.py:250
  39.2 9.3 %collective-permute-done.2.half_ref = bf16[32,640]{1,0:T(8,128)(2,1)S(1)} collective-permute-done((bf16[32,640]{1,0:T(8,128)(2,1)S(1)}, bf16[32,640]{1,0:T(8,128)(2,1)S(1)}, u32[]{:S(2)}, u32[]{:S(2)}) %collective-permute-start.2) | collective-permute-done | bytes 40992 | tf_op jit(solution)/shard_map/ppermute | solution.py:250
  52.6 3.9 %collective-permute-start.4 = (bf16[4,64,640]{2,1,0:T(8,128)(2,1)S(1)}, bf16[4,64,640]{2,1,0:T(8,128)(2,1)S(1)}, u32[]{:S(2)}, u32[]{:S(2)}) collective-permute-start(bf16[4,64,640]{2,1,0:T(8,128)(2,1)S(1)} %column.1.here_ref), channel_id=1, source_target_pairs={{0,1},{1,2},{2,3},{3,64},{64,65},{65,66},{66,67},{67,128},{128,129... | collective-permute-start | bytes 983048 | tf_op jit(solution)/shard_map/ppermute | solution.py:250
  56.5 2.7 %collective-permute-start.7 = (bf16[4,64,640]{2,1,0:T(8,128)(2,1)S(1)}, bf16[4,64,640]{2,1,0:T(8,128)(2,1)S(1)}, u32[]{:S(2)}, u32[]{:S(2)}) collective-permute-start(bf16[4,64,640]{2,1,0:T(8,128)(2,1)S(1)} %column.1.here_ref), channel_id=1, source_target_pairs={{0,768},{256,0},{512,256},{768,512},{1,769},{257,1},{513,257},{769... | collective-permute-start | bytes 983048 | tf_op jit(solution)/shard_map/ppermute | solution.py:233
  59.2 4.3 %collective-permute-start.6 = (bf16[4,64,640]{2,1,0:T(8,128)(2,1)S(1)}, bf16[4,64,640]{2,1,0:T(8,128)(2,1)S(1)}, u32[]{:S(2)}, u32[]{:S(2)}) collective-permute-start(bf16[4,64,640]{2,1,0:T(8,128)(2,1)S(1)} %column.1.here_ref), channel_id=1, source_target_pairs={{0,256},{256,512},{512,768},{768,0},{1,257},{257,513},{513,769},{7... | collective-permute-start | bytes 983048 | tf_op jit(solution)/shard_map/ppermute | solution.py:233
  63.7 3.3 %collective-permute-done.7.after_ref = bf16[4,64,640]{2,1,0:T(8,128)(2,1)S(1)} collective-permute-done((bf16[4,64,640]{2,1,0:T(8,128)(2,1)S(1)}, bf16[4,64,640]{2,1,0:T(8,128)(2,1)S(1)}, u32[]{:S(2)}, u32[]{:S(2)}) %collective-permute-start.7) | collective-permute-done | bytes 327712 | tf_op jit(solution)/shard_map/ppermute | solution.py:233
  68.2 5.5 %collective-permute-start.13 = (bf16[8,64,640]{2,1,0:T(8,128)(2,1)S(1)}, bf16[8,64,640]{2,1,0:T(8,128)(2,1)S(1)}, u32[]{:S(2)}, u32[]{:S(2)}) collective-permute-start(bf16[8,64,640]{2,1,0:T(8,128)(2,1)S(1)} %pad_maximum_fusion.here_ref), channel_id=1, source_target_pairs={{0,256},{256,512},{512,768},{768,0},{1,257},{257,513},{513,769},{7... | collective-permute-start | bytes 1966088 | tf_op jit(solution)/shard_map/ppermute | solution.py:233
  75.7 3.4 %collective-permute-start.9 = (bf16[2,64,640]{2,1,0:T(8,128)(2,1)S(1)}, bf16[2,64,640]{2,1,0:T(8,128)(2,1)S(1)}, u32[]{:S(2)}, u32[]{:S(2)}) collective-permute-start(bf16[2,64,640]{2,1,0:T(8,128)(2,1)S(1)} %slice.43), channel_id=1, source_target_pairs={{0,195},{1,0},{2,1},{3,2},{64,3},{65,64},{66,65},{67,66},{128,67},... | collective-permute-start | bytes 491528 | tf_op jit(solution)/shard_map/ppermute | solution.py:250
  79.1 3.6 %collective-permute-start.8 = (bf16[2,64,640]{2,1,0:T(8,128)(2,1)S(1)}, bf16[2,64,640]{2,1,0:T(8,128)(2,1)S(1)}, u32[]{:S(2)}, u32[]{:S(2)}) collective-permute-start(bf16[2,64,640]{2,1,0:T(8,128)(2,1)S(1)} %slice.42), channel_id=1, source_target_pairs={{0,1},{1,2},{2,3},{3,64},{64,65},{65,66},{66,67},{67,128},{128,129... | collective-permute-start | bytes 491528 | tf_op jit(solution)/shard_map/ppermute | solution.py:250
  82.8 5.1 %collective-permute-start.10 = (bf16[2,64,640]{2,1,0:T(8,128)(2,1)S(1)}, bf16[2,64,640]{2,1,0:T(8,128)(2,1)S(1)}, u32[]{:S(2)}, u32[]{:S(2)}) collective-permute-start(bf16[2,64,640]{2,1,0:T(8,128)(2,1)S(1)} %slice.34), channel_id=1, source_target_pairs={{0,256},{256,512},{512,768},{768,0},{1,257},{257,513},{513,769},{7... | collective-permute-start | bytes 491528 | tf_op jit(solution)/shard_map/ppermute | solution.py:237
  90.7 5.6 %collective-permute-done.11.rest_ref = bf16[2,64,640]{2,1,0:T(8,128)(2,1)S(1)} collective-permute-done((bf16[2,64,640]{2,1,0:T(8,128)(2,1)S(1)}, bf16[2,64,640]{2,1,0:T(8,128)(2,1)S(1)}, u32[]{:S(2)}, u32[]{:S(2)}) %collective-permute-start.11) | collective-permute-done | bytes 163872 | tf_op jit(solution)/shard_map/ppermute | solution.py:237
  98.3 5.1 %collective-permute-start.14 = (bf16[4,64,640]{2,1,0:T(8,128)(2,1)S(1)}, bf16[4,64,640]{2,1,0:T(8,128)(2,1)S(1)}, u32[]{:S(2)}, u32[]{:S(2)}) collective-permute-start(bf16[4,64,640]{2,1,0:T(8,128)(2,1)S(1)} %pad_maximum_fusion.1.here_ref), channel_id=1, source_target_pairs={{0,256},{256,512},{512,768},{768,0},{1,257},{257,513},{513,769},{7... | collective-permute-start | bytes 983048 | tf_op jit(solution)/shard_map/ppermute | solution.py:233
  105.4 3.9 %collective-permute-start.17 = (bf16[4,64,640]{2,1,0:T(8,128)(2,1)S(1)}, bf16[4,64,640]{2,1,0:T(8,128)(2,1)S(1)}, u32[]{:S(2)}, u32[]{:S(2)}) collective-permute-start(bf16[4,64,640]{2,1,0:T(8,128)(2,1)S(1)} %slice.45), channel_id=1, source_target_pairs={{0,768},{256,0},{512,256},{768,512},{1,769},{257,1},{513,257},{769... | collective-permute-start | bytes 983048 | tf_op jit(solution)/shard_map/ppermute | solution.py:237
  110.4 3.5 %collective-permute-done.16.half_ref = bf16[4,64,640]{2,1,0:T(8,128)(2,1)S(1)} collective-permute-done((bf16[4,64,640]{2,1,0:T(8,128)(2,1)S(1)}, bf16[4,64,640]{2,1,0:T(8,128)(2,1)S(1)}, u32[]{:S(2)}, u32[]{:S(2)}) %collective-permute-start.16) | collective-permute-done | bytes 327712 | tf_op jit(solution)/shard_map/ppermute | solution.py:237
  117.8 3.3 %collective-permute-start.18 = (bf16[2,64,640]{2,1,0:T(8,128)(2,1)S(1)}, bf16[2,64,640]{2,1,0:T(8,128)(2,1)S(1)}, u32[]{:S(2)}, u32[]{:S(2)}) collective-permute-start(bf16[2,64,640]{2,1,0:T(8,128)(2,1)S(1)} %slice.38), channel_id=1, source_target_pairs={{0,256},{256,512},{512,768},{768,0},{1,257},{257,513},{513,769},{7... | collective-permute-start | bytes 491528 | tf_op jit(solution)/shard_map/ppermute | solution.py:237
  121.1 2.6 %collective-permute-start.19 = (bf16[2,64,640]{2,1,0:T(8,128)(2,1)S(1)}, bf16[2,64,640]{2,1,0:T(8,128)(2,1)S(1)}, u32[]{:S(2)}, u32[]{:S(2)}) collective-permute-start(bf16[2,64,640]{2,1,0:T(8,128)(2,1)S(1)} %slice.39), channel_id=1, source_target_pairs={{0,768},{256,0},{512,256},{768,512},{1,769},{257,1},{513,257},{769... | collective-permute-start | bytes 491528 | tf_op jit(solution)/shard_map/ppermute | solution.py:237
  126.3 4.2 %collective-permute-done.19.rest_ref = bf16[2,64,640]{2,1,0:T(8,128)(2,1)S(1)} collective-permute-done((bf16[2,64,640]{2,1,0:T(8,128)(2,1)S(1)}, bf16[2,64,640]{2,1,0:T(8,128)(2,1)S(1)}, u32[]{:S(2)}, u32[]{:S(2)}) %collective-permute-start.19) | collective-permute-done | bytes 163872 | tf_op jit(solution)/shard_map/ppermute | solution.py:237
  135.5 3.4 %section.8.held_ref = bf16[32,2048]{1,0:T(8,128)(2,1)S(1)} custom-call(s32[5]{0:T(128)S(1)} %copy-done.4, bf16[32,2048]{1,0:T(8,128)(2,1)S(1)} %get-tuple-element.18.x_ref, f32[128,32]{1,0:T(8,128)S(1)} %get-tuple-element.19.allowed_ref, bf16[32,2048]{1,0:T(8,128)(2,1)S(1)} %broadcast_in_dim.73.held_ref, ...), custom_call_target="tpu_custom_call", output_to_operand_aliasing={{}: (3, {})} | custom-call | tf_op jit(solution)/shard_map/section/pallas_call | solution.py:147
  140.3 3.3 %collective-permute-done.23.x_ref = bf16[32,2048]{1,0:T(8,128)(2,1)S(1)} collective-permute-done((bf16[32,2048]{1,0:T(8,128)(2,1)S(1)}, bf16[32,2048]{1,0:T(8,128)(2,1)S(1)}, u32[]{:S(2)}, u32[]{:S(2)}) %collective-permute-start.23) | collective-permute-done | bytes 131104 | tf_op jit(solution)/shard_map/ppermute | solution.py:398
  152.6 5.8 %collective-permute-start.31 = (bf16[8,2048]{1,0:T(8,128)(2,1)S(1)}, bf16[8,2048]{1,0:T(8,128)(2,1)S(1)}, u32[]{:S(2)}, u32[]{:S(2)}) collective-permute-start(bf16[8,2048]{1,0:T(8,128)(2,1)S(1)} %get-tuple-element.31), channel_id=1, source_target_pairs={{0,1},{1,2},{2,31},{3,28},{4,5},{5,6},{6,27},{7,24},{8,9},{9,10},{... | collective-permute-start | bytes 98312 | tf_op jit(solution)/shard_map/ppermute | solution.py:365
  158.4 55.3 %collective-permute-start.32 = (bf16[8,2048]{1,0:T(8,128)(2,1)S(1)}, bf16[8,2048]{1,0:T(8,128)(2,1)S(1)}, u32[]{:S(2)}, u32[]{:S(2)}) collective-permute-start(bf16[8,2048]{1,0:T(8,128)(2,1)S(1)} %get-tuple-element.32), channel_id=1, source_target_pairs={{0,2},{1,3},{2,28},{3,29},{4,6},{5,7},{6,24},{7,25},{8,10},{9,11},... | collective-permute-start | bytes 98312 | tf_op jit(solution)/shard_map/ppermute | solution.py:365
  213.7 4.3 %collective-permute-start.33 = (bf16[8,2048]{1,0:T(8,128)(2,1)S(1)}, bf16[8,2048]{1,0:T(8,128)(2,1)S(1)}, u32[]{:S(2)}, u32[]{:S(2)}) collective-permute-start(bf16[8,2048]{1,0:T(8,128)(2,1)S(1)} %get-tuple-element.33), channel_id=1, source_target_pairs={{0,3},{1,0},{2,29},{3,30},{4,7},{5,4},{6,25},{7,26},{8,11},{9,8},{... | collective-permute-start | bytes 98312 | tf_op jit(solution)/shard_map/ppermute | solution.py:365
  (90 shorter events, 45.6 us)
Async XLA Ops:
  3.6 44.9 %collective-permute-start.1 = (bf16[64,640]{1,0:T(8,128)(2,1)}, bf16[64,640]{1,0:T(8,128)(2,1)S(1)}, u32[]{:S(2)}, u32[]{:S(2)}) collective-permute-start(bf16[64,640]{1,0:T(8,128)(2,1)} %shard.1.own_ref), channel_id=1, source_target_pairs={{0,192},{1,193},{2,194},{3,195},{64,0},{65,1},{66,2},{67,3},{128,6... | collective-permute-start | bytes 245768 | tf_op jit(solution)/shard_map/ppermute | solution.py:250
  21.8 26.7 %collective-permute-start = (bf16[64,640]{1,0:T(8,128)(2,1)}, bf16[64,640]{1,0:T(8,128)(2,1)S(1)}, u32[]{:S(2)}, u32[]{:S(2)}) collective-permute-start(bf16[64,640]{1,0:T(8,128)(2,1)} %shard.1.own_ref), channel_id=1, source_target_pairs={{0,64},{1,65},{2,66},{3,67},{64,128},{65,129},{66,130},{67,131},{1... | collective-permute-start | bytes 245768 | tf_op jit(solution)/shard_map/ppermute | solution.py:250
  24.6 14.6 %collective-permute-start.3 = (bf16[32,640]{1,0:T(8,128)(2,1)S(1)}, bf16[32,640]{1,0:T(8,128)(2,1)S(1)}, u32[]{:S(2)}, u32[]{:S(2)}) collective-permute-start(bf16[32,640]{1,0:T(8,128)(2,1)S(1)} %get-tuple-element.34), channel_id=1, source_target_pairs={{0,128},{1,129},{2,130},{3,131},{64,192},{65,193},{66,194},{67,195... | collective-permute-start | bytes 122888 | tf_op jit(solution)/shard_map/ppermute | solution.py:250
  33.6 14.9 %collective-permute-start.2 = (bf16[32,640]{1,0:T(8,128)(2,1)S(1)}, bf16[32,640]{1,0:T(8,128)(2,1)S(1)}, u32[]{:S(2)}, u32[]{:S(2)}) collective-permute-start(bf16[32,640]{1,0:T(8,128)(2,1)S(1)} %get-tuple-element.35), channel_id=1, source_target_pairs={{0,128},{1,129},{2,130},{3,131},{64,192},{65,193},{66,194},{67,195... | collective-permute-start | bytes 122888 | tf_op jit(solution)/shard_map/ppermute | solution.py:250
  50.6 12.9 %collective-permute-start.5 = (bf16[4,64,640]{2,1,0:T(8,128)(2,1)S(1)}, bf16[4,64,640]{2,1,0:T(8,128)(2,1)S(1)}, u32[]{:S(2)}, u32[]{:S(2)}) collective-permute-start(bf16[4,64,640]{2,1,0:T(8,128)(2,1)S(1)} %column.1.here_ref), channel_id=1, source_target_pairs={{0,195},{1,0},{2,1},{3,2},{64,3},{65,64},{66,65},{67,66},{128,67},... | collective-permute-start | bytes 983048 | tf_op jit(solution)/shard_map/ppermute | solution.py:250
  52.6 11.0 %collective-permute-start.4 = (bf16[4,64,640]{2,1,0:T(8,128)(2,1)S(1)}, bf16[4,64,640]{2,1,0:T(8,128)(2,1)S(1)}, u32[]{:S(2)}, u32[]{:S(2)}) collective-permute-start(bf16[4,64,640]{2,1,0:T(8,128)(2,1)S(1)} %column.1.here_ref), channel_id=1, source_target_pairs={{0,1},{1,2},{2,3},{3,64},{64,65},{65,66},{66,67},{67,128},{128,129... | collective-permute-start | bytes 983048 | tf_op jit(solution)/shard_map/ppermute | solution.py:250
  56.5 10.4 %collective-permute-start.7 = (bf16[4,64,640]{2,1,0:T(8,128)(2,1)S(1)}, bf16[4,64,640]{2,1,0:T(8,128)(2,1)S(1)}, u32[]{:S(2)}, u32[]{:S(2)}) collective-permute-start(bf16[4,64,640]{2,1,0:T(8,128)(2,1)S(1)} %column.1.here_ref), channel_id=1, source_target_pairs={{0,768},{256,0},{512,256},{768,512},{1,769},{257,1},{513,257},{769... | collective-permute-start | bytes 983048 | tf_op jit(solution)/shard_map/ppermute | solution.py:233
  59.2 9.0 %collective-permute-start.6 = (bf16[4,64,640]{2,1,0:T(8,128)(2,1)S(1)}, bf16[4,64,640]{2,1,0:T(8,128)(2,1)S(1)}, u32[]{:S(2)}, u32[]{:S(2)}) collective-permute-start(bf16[4,64,640]{2,1,0:T(8,128)(2,1)S(1)} %column.1.here_ref), channel_id=1, source_target_pairs={{0,256},{256,512},{512,768},{768,0},{1,257},{257,513},{513,769},{7... | collective-permute-start | bytes 983048 | tf_op jit(solution)/shard_map/ppermute | solution.py:233
  68.2 35.2 %collective-permute-start.13 = (bf16[8,64,640]{2,1,0:T(8,128)(2,1)S(1)}, bf16[8,64,640]{2,1,0:T(8,128)(2,1)S(1)}, u32[]{:S(2)}, u32[]{:S(2)}) collective-permute-start(bf16[8,64,640]{2,1,0:T(8,128)(2,1)S(1)} %pad_maximum_fusion.here_ref), channel_id=1, source_target_pairs={{0,256},{256,512},{512,768},{768,0},{1,257},{257,513},{513,769},{7... | collective-permute-start | bytes 1966088 | tf_op jit(solution)/shard_map/ppermute | solution.py:233
  73.7 31.6 %collective-permute-start.12 = (bf16[8,64,640]{2,1,0:T(8,128)(2,1)S(1)}, bf16[8,64,640]{2,1,0:T(8,128)(2,1)S(1)}, u32[]{:S(2)}, u32[]{:S(2)}) collective-permute-start(bf16[8,64,640]{2,1,0:T(8,128)(2,1)S(1)} %pad_maximum_fusion.here_ref), channel_id=1, source_target_pairs={{0,768},{256,0},{512,256},{768,512},{1,769},{257,1},{513,257},{769... | collective-permute-start | bytes 1966088 | tf_op jit(solution)/shard_map/ppermute | solution.py:233
  75.7 12.2 %collective-permute-start.9 = (bf16[2,64,640]{2,1,0:T(8,128)(2,1)S(1)}, bf16[2,64,640]{2,1,0:T(8,128)(2,1)S(1)}, u32[]{:S(2)}, u32[]{:S(2)}) collective-permute-start(bf16[2,64,640]{2,1,0:T(8,128)(2,1)S(1)} %slice.43), channel_id=1, source_target_pairs={{0,195},{1,0},{2,1},{3,2},{64,3},{65,64},{66,65},{67,66},{128,67},... | collective-permute-start | bytes 491528 | tf_op jit(solution)/shard_map/ppermute | solution.py:250
  79.1 10.7 %collective-permute-start.8 = (bf16[2,64,640]{2,1,0:T(8,128)(2,1)S(1)}, bf16[2,64,640]{2,1,0:T(8,128)(2,1)S(1)}, u32[]{:S(2)}, u32[]{:S(2)}) collective-permute-start(bf16[2,64,640]{2,1,0:T(8,128)(2,1)S(1)} %slice.42), channel_id=1, source_target_pairs={{0,1},{1,2},{2,3},{3,64},{64,65},{65,66},{66,67},{67,128},{128,129... | collective-permute-start | bytes 491528 | tf_op jit(solution)/shard_map/ppermute | solution.py:250
  87.9 8.4 %collective-permute-start.11 = (bf16[2,64,640]{2,1,0:T(8,128)(2,1)S(1)}, bf16[2,64,640]{2,1,0:T(8,128)(2,1)S(1)}, u32[]{:S(2)}, u32[]{:S(2)}) collective-permute-start(bf16[2,64,640]{2,1,0:T(8,128)(2,1)S(1)} %slice.35), channel_id=1, source_target_pairs={{0,768},{256,0},{512,256},{768,512},{1,769},{257,1},{513,257},{769... | collective-permute-start | bytes 491528 | tf_op jit(solution)/shard_map/ppermute | solution.py:237
  96.3 13.0 %collective-permute-start.15 = (bf16[4,64,640]{2,1,0:T(8,128)(2,1)S(1)}, bf16[4,64,640]{2,1,0:T(8,128)(2,1)S(1)}, u32[]{:S(2)}, u32[]{:S(2)}) collective-permute-start(bf16[4,64,640]{2,1,0:T(8,128)(2,1)S(1)} %pad_maximum_fusion.1.here_ref), channel_id=1, source_target_pairs={{0,768},{256,0},{512,256},{768,512},{1,769},{257,1},{513,257},{769... | collective-permute-start | bytes 983048 | tf_op jit(solution)/shard_map/ppermute | solution.py:233
  98.3 12.1 %collective-permute-start.14 = (bf16[4,64,640]{2,1,0:T(8,128)(2,1)S(1)}, bf16[4,64,640]{2,1,0:T(8,128)(2,1)S(1)}, u32[]{:S(2)}, u32[]{:S(2)}) collective-permute-start(bf16[4,64,640]{2,1,0:T(8,128)(2,1)S(1)} %pad_maximum_fusion.1.here_ref), channel_id=1, source_target_pairs={{0,256},{256,512},{512,768},{768,0},{1,257},{257,513},{513,769},{7... | collective-permute-start | bytes 983048 | tf_op jit(solution)/shard_map/ppermute | solution.py:233
  103.5 10.5 %collective-permute-start.16 = (bf16[4,64,640]{2,1,0:T(8,128)(2,1)S(1)}, bf16[4,64,640]{2,1,0:T(8,128)(2,1)S(1)}, u32[]{:S(2)}, u32[]{:S(2)}) collective-permute-start(bf16[4,64,640]{2,1,0:T(8,128)(2,1)S(1)} %slice.44), channel_id=1, source_target_pairs={{0,256},{256,512},{512,768},{768,0},{1,257},{257,513},{513,769},{7... | collective-permute-start | bytes 983048 | tf_op jit(solution)/shard_map/ppermute | solution.py:237
  105.4 10.2 %collective-permute-start.17 = (bf16[4,64,640]{2,1,0:T(8,128)(2,1)S(1)}, bf16[4,64,640]{2,1,0:T(8,128)(2,1)S(1)}, u32[]{:S(2)}, u32[]{:S(2)}) collective-permute-start(bf16[4,64,640]{2,1,0:T(8,128)(2,1)S(1)} %slice.45), channel_id=1, source_target_pairs={{0,768},{256,0},{512,256},{768,512},{1,769},{257,1},{513,257},{769... | collective-permute-start | bytes 983048 | tf_op jit(solution)/shard_map/ppermute | solution.py:237
  115.8 19.7 %collective-permute-start.21 = (bf16[4,8,64,640]{3,2,1,0:T(8,128)(2,1)S(1)}, bf16[4,8,64,640]{3,2,1,0:T(8,128)(2,1)S(1)}, u32[]{:S(2)}, u32[]{:S(2)}) collective-permute-start(bf16[4,8,64,640]{3,2,1,0:T(8,128)(2,1)S(1)} %join.4.refs_6_), channel_id=1, source_target_pairs={{0,32},{32,0},{1,33},{33,1},{2,34},{34,2},{3,35},{35,3},{4,36},{36... | collective-permute-start | bytes 7864328 | tf_op jit(solution)/shard_map/ppermute | solution.py:284
  117.8 8.5 %collective-permute-start.18 = (bf16[2,64,640]{2,1,0:T(8,128)(2,1)S(1)}, bf16[2,64,640]{2,1,0:T(8,128)(2,1)S(1)}, u32[]{:S(2)}, u32[]{:S(2)}) collective-permute-start(bf16[2,64,640]{2,1,0:T(8,128)(2,1)S(1)} %slice.38), channel_id=1, source_target_pairs={{0,256},{256,512},{512,768},{768,0},{1,257},{257,513},{513,769},{7... | collective-permute-start | bytes 491528 | tf_op jit(solution)/shard_map/ppermute | solution.py:237
  121.1 9.4 %collective-permute-start.19 = (bf16[2,64,640]{2,1,0:T(8,128)(2,1)S(1)}, bf16[2,64,640]{2,1,0:T(8,128)(2,1)S(1)}, u32[]{:S(2)}, u32[]{:S(2)}) collective-permute-start(bf16[2,64,640]{2,1,0:T(8,128)(2,1)S(1)} %slice.39), channel_id=1, source_target_pairs={{0,768},{256,0},{512,256},{768,512},{1,769},{257,1},{513,257},{769... | collective-permute-start | bytes 491528 | tf_op jit(solution)/shard_map/ppermute | solution.py:237
  123.8 9.7 %collective-permute-start.20 = (bf16[4,4,64,640]{3,2,1,0:T(8,128)(2,1)S(1)}, bf16[4,4,64,640]{3,2,1,0:T(8,128)(2,1)S(1)}, u32[]{:S(2)}, u32[]{:S(2)}) collective-permute-start(bf16[4,4,64,640]{3,2,1,0:T(8,128)(2,1)S(1)} %join.3.refs_5_), channel_id=1, source_target_pairs={{0,32},{32,0},{1,33},{33,1},{2,34},{34,2},{3,35},{35,3},{4,36},{36... | collective-permute-start | bytes 3932168 | tf_op jit(solution)/shard_map/ppermute | solution.py:284
  152.0 66.0 %collective-permute-start.30 = (bf16[8,2048]{1,0:T(8,128)(2,1)S(1)}, bf16[8,2048]{1,0:T(8,128)(2,1)S(1)}, u32[]{:S(2)}, u32[]{:S(2)}) collective-permute-start(bf16[8,2048]{1,0:T(8,128)(2,1)S(1)} %get-tuple-element.30), channel_id=1, source_target_pairs={{0,0},{1,1},{2,30},{3,31},{4,4},{5,5},{6,26},{7,27},{8,8},{9,9},{1... | collective-permute-start | bytes 98312 | tf_op jit(solution)/shard_map/ppermute | solution.py:365
  152.6 65.4 %collective-permute-start.31 = (bf16[8,2048]{1,0:T(8,128)(2,1)S(1)}, bf16[8,2048]{1,0:T(8,128)(2,1)S(1)}, u32[]{:S(2)}, u32[]{:S(2)}) collective-permute-start(bf16[8,2048]{1,0:T(8,128)(2,1)S(1)} %get-tuple-element.31), channel_id=1, source_target_pairs={{0,1},{1,2},{2,31},{3,28},{4,5},{5,6},{6,27},{7,24},{8,9},{9,10},{... | collective-permute-start | bytes 98312 | tf_op jit(solution)/shard_map/ppermute | solution.py:365
  158.4 59.6 %collective-permute-start.32 = (bf16[8,2048]{1,0:T(8,128)(2,1)S(1)}, bf16[8,2048]{1,0:T(8,128)(2,1)S(1)}, u32[]{:S(2)}, u32[]{:S(2)}) collective-permute-start(bf16[8,2048]{1,0:T(8,128)(2,1)S(1)} %get-tuple-element.32), channel_id=1, source_target_pairs={{0,2},{1,3},{2,28},{3,29},{4,6},{5,7},{6,24},{7,25},{8,10},{9,11},... | collective-permute-start | bytes 98312 | tf_op jit(solution)/shard_map/ppermute | solution.py:365
  (17 other events, 72.7 us)

commit v6 on v5

--- a/solution.py
+++ b/solution.py
@@ -94,11 +94,15 @@
 
 
 def section_kernel(step, last, where, x_ref, allowed_ref, held_ref, *refs):
-    rope, weights, outputs = refs[:5], (refs[5:8], refs[8:11]), refs[11:]
+    rope, group, weights, outputs = refs[:5], refs[5], (refs[6:8], refs[8:10]), refs[10:]
     out_ref = outputs[-1]
 
     def rows_of(i, zh, t, columns):
-        part, first = ((0, 0), (1, ZH), (2, 0), (1, 0))[t]
+        if t == 0:
+            core = where[2] if i == 0 else 1 - where[2]
+            places = [(((where[1] + x) % X) * ZH + zh) * 2 + core for x in range(X)]
+            return jnp.concatenate([group[place, :, columns] for place in places], axis=0)
+        part, first = ((0, ZH), (1, 0), (0, 0))[t - 1]
         return jnp.concatenate(
             [weights[i][part][x, first + zh, :, columns] for x in range(X)], axis=0
         )
@@ -147,7 +151,7 @@
     return pl.pallas_call(
         functools.partial(section_kernel, step, last),
         out_shape=[chunk] * 4 if last else whole,
-        in_specs=[pl.BlockSpec(memory_space=pltpu.SMEM)] + [vmem] * 14,
+        in_specs=[pl.BlockSpec(memory_space=pltpu.SMEM)] + [vmem] * 13,
         out_specs=[vmem] * 4 if last else vmem,
         scratch_shapes=[pltpu.VMEM((SEQ, D), F32)] if last else [],
         input_output_aliases={} if last else {3: 0},
@@ -156,7 +160,9 @@
     )(where, values, allowed, held, *rope, *weights)
 
 
-def shard_kernel(where, qkv_any, out_any, gain_any, shard_ref, qkv_ref, out_ref, gain_ref, done):
+def shard_kernel(
+    where, qkv_any, out_any, gain_any, shard_ref, copies_ref, qkv_ref, out_ref, gain_ref, done
+):
     copies = [
         pltpu.make_async_copy(qkv_any.at[where[0]], qkv_ref, done.at[0]),
         pltpu.make_async_copy(out_any.at[where[0]], out_ref, done.at[1]),
@@ -189,15 +195,19 @@
     shard_ref[:, pl.ds(128, 128)] = second.astype(BF16)
     shard_ref[:, pl.ds(256, 128)] = qkv[:, 256:].astype(BF16)
     shard_ref[:, pl.ds(QKV, CTX)] = out_ref[...]
-
-
-def column_kernel(where, own_ref, below_ref, above_ref, half_ref, rest_ref, out_ref):
-    own, half = where[4], half_ref.shape[0]
-    out_ref[own] = own_ref[...]
-    out_ref[(own + ZH - 1) % ZH] = below_ref[...]
-    out_ref[(own + 1) % ZH] = above_ref[...]
-    out_ref[(own + 2) % ZH, pl.ds(0, half)] = half_ref[...]
-    out_ref[(own + 2) % ZH, pl.ds(half, half)] = rest_ref[...]
+    for zh in range(copies_ref.shape[0]):
+        copies_ref[zh] = shard_ref[...]
+
+
+def settle_kernel(*refs):
+    count = len(refs) // 2
+    copies = [
+        pltpu.make_async_copy(refs[i], refs[count + i], refs[-1].at[i]) for i in range(count)
+    ]
+    for copy in copies:
+        copy.start()
+    for copy in copies:
+        copy.wait()
 
 
 def join_kernel(here_ref, after_ref, before_ref, half_ref, rest_ref, out_ref):
@@ -213,11 +223,15 @@
     rows = w_qkv.shape[1]
     vmem = pl.BlockSpec(memory_space=pltpu.VMEM)
     smem = pl.BlockSpec(memory_space=pltpu.SMEM)
-    shard = pl.pallas_call(
+    anywhere = pl.BlockSpec(memory_space=pl.ANY)
+    shard, shards = pl.pallas_call(
         shard_kernel,
-        out_shape=jax.ShapeDtypeStruct((rows, QKV + CTX), BF16),
-        in_specs=[smem] + [pl.BlockSpec(memory_space=pl.ANY)] * 3,
-        out_specs=vmem,
+        out_shape=[
+            jax.ShapeDtypeStruct((rows, QKV + CTX), BF16),
+            jax.ShapeDtypeStruct((ZH, rows, QKV + CTX), BF16),
+        ],
+        in_specs=[smem] + [anywhere] * 3,
+        out_specs=[vmem, vmem],
         scratch_shapes=[
             pltpu.VMEM((rows, QKV), BF16),
             pltpu.VMEM((rows, CTX), BF16),
@@ -226,6 +240,7 @@
         ],
         name="shard",
     )(where, w_qkv, w_out.transpose(0, 2, 1), norm_gain)
+    group = lax.all_gather(shard, ("x", "z_hi", "core"))
 
     one, other = [(x, (x + 1) % X) for x in range(X)], [(x, (x - 1) % X) for x in range(X)]
 
@@ -249,39 +264,28 @@
     def along_z(parts, by):
         return lax.ppermute(parts, ("z_hi", "tensor"), [(z, (z + by) % Z) for z in range(Z)])
 
-    here = pl.pallas_call(
-        column_kernel,
-        out_shape=jax.ShapeDtypeStruct((ZH, *shard.shape), BF16),
-        in_specs=[smem] + [vmem] * 5,
-        out_specs=vmem,
-        compiler_params=SMALL,
-        name="column",
-    )(
-        where,
-        shard,
-        along_z(shard, ZL),
-        along_z(shard, -ZL),
-        along_z(shard[: rows // 2], 2 * ZL),
-        along_z(shard[rows // 2 :], -2 * ZL),
-    )
+    here = lax.all_to_all(shards, "z_hi", 0, 0)
     half = ZH // 2
     ahead, behind = along_z(here, 1), along_z(here, -1)
-    here_x = first_along_x(here)
-    near, *here_x = lax.optimization_barrier((jnp.concatenate([ahead, behind]), *here_x))
+    near = jnp.concatenate([ahead, behind])
     near_x = first_along_x(near)
     across = jnp.concatenate([along_z(ahead[:half], 1), along_z(behind[half:], -1)])
-    here_rest = rest_along_x(*here_x)
-    across, *here_rest = lax.optimization_barrier((across, *here_rest))
     across_x = first_along_x(across)
     near_rest = rest_along_x(*near_x)
     *across_x, near_0, near_1 = lax.optimization_barrier((*across_x, *near_rest))
     across_rest = rest_along_x(*across_x)
-    own = [
-        join(here, *here_x, *here_rest),
-        join(near, *near_x, near_0, near_1),
-        join(across, *across_x, *across_rest),
-    ]
-    return own + [lax.ppermute(part, "core", [(0, 1), (1, 0)]) for part in own]
+    own = [join(near, *near_x, near_0, near_1), join(across, *across_x, *across_rest)]
+    other_core = [lax.ppermute(part, "core", [(0, 1), (1, 0)]) for part in own]
+    weights = [group] + own + other_core
+    return pl.pallas_call(
+        settle_kernel,
+        out_shape=[jax.ShapeDtypeStruct(part.shape, BF16) for part in weights],
+        in_specs=[anywhere] * len(weights),
+        out_specs=[vmem] * len(weights),
+        scratch_shapes=[pltpu.SemaphoreType.DMA((len(weights),))],
+        compiler_params=MEDIUM,
+        name="settle",
+    )(*weights)
 
 
 def turned(values, by):
@@ -376,7 +380,7 @@
 
 
 def on_device(down_in, up_in, w_qkv, w_out, norm_gain, down_docs, up_docs):
-    where = jnp.stack([lax.axis_index(name) for name in ("pipe", "x", "core", "tensor", "z_hi")])
+    where = jnp.stack([lax.axis_index(name) for name in ("pipe", "x", "core", "tensor")])
     sections = lax.axis_size("pipe")
     weights = gather_section(where, w_qkv, w_out, norm_gain)
     rope = rotary_tables()

time: 222 us -> 227 us (1.023)
  starting transfers between devices: 165 us -> 130 us
  waiting for transfers between devices: 38 us -> 57 us
  between operations: 1.34 us -> 14.6 us
  local copies, waits for them, and re-layouts: 3.25 us -> 10.1 us
    ppermute x8 -> x4, starting transfers between devices: 47.5 us -> 15.9 us  [along_z(): lax.ppermute(parts, ('z_hi', 'tensor'), [(z, (z + by) % Z) for z in range...]
    all_to_all x0 -> x1, starting transfers between devices: none -> 18.7 us  [gather_section(): here = lax.all_to_all(shards, 'z_hi', 0, 0)]
    all_to_all x0 -> x1, waiting for transfers between devices: none -> 18.7 us  [gather_section(): here = lax.all_to_all(shards, 'z_hi', 0, 0)]
    ppermute x6 -> x4, starting transfers between devices: 21.5 us -> 11.7 us  [first_along_x(): return (lax.ppermute(parts, 'x', one), lax.ppermute(parts, 'x', other))]
    unnamed x14 -> x26, local copies, waits for them, and re-layouts: 1.58 us -> 9.91 us
    ppermute x8 -> x4, waiting for transfers between devices: 9.38 us -> 13.8 us  [along_z(): lax.ppermute(parts, ('z_hi', 'tensor'), [(z, (z + by) % Z) for z in range...]
    ppermute x3 -> x2, waiting for transfers between devices: 11.5 us -> 7.25 us  [rest_along_x(): lax.ppermute(after[half:], 'x', other)]
    ppermute x4, starting transfers between devices: 66 us -> 61.8 us  [exchange(): received.append(lax.ppermute(chunk, ('pipe', 'tensor'), pairs))]
  transfers between devices with their start and end apart: 34 -> 27, of which waited for: 14 -> 15; matrix products, arithmetic and copies ran while one was open for 1% -> 0% of each run, Pallas kernels for 0% -> 1%
where the time goes in v6:
time: 227 us; the launch traced here: 226 us
  starting transfers between devices  130 us (57%)
  waiting for transfers between devices  57 us (25%)
  between operations  14.6 us (6%)
  Pallas kernels  13.5 us (6%)
  local copies, waits for them, and re-layouts  10.1 us (4%)
    ppermute x4, starting transfers between devices, exchange(): received.append(lax.ppermute(chunk, ('pipe', 'tensor'), pairs))  61.8 us
    all_to_all x1, starting transfers between devices, gather_section(): here = lax.all_to_all(shards, 'z_hi', 0, 0)  18.7 us
    all_to_all x1, waiting for transfers between devices, gather_section(): here = lax.all_to_all(shards, 'z_hi', 0, 0)  18.7 us
    ppermute x4, starting transfers between devices, along_z(): lax.ppermute(parts, ('z_hi', 'tensor'), [(z, (z + by) % Z) for z in range...  15.9 us
    ppermute x4, waiting for transfers between devices, along_z(): lax.ppermute(parts, ('z_hi', 'tensor'), [(z, (z + by) % Z) for z in range...  13.8 us
    ppermute x4, starting transfers between devices, first_along_x(): return (lax.ppermute(parts, 'x', one), lax.ppermute(parts, 'x', other))  11.7 us
    unnamed x26, local copies, waits for them, and re-layouts  9.91 us
    pallas_call x8, Pallas kernels, run_section(): pl.pallas_call(functools.partial(section_kernel, step, last), out_shape=[...  7.66 us
  transfers between devices with their start and end apart: 27, of which 15 were waited for; matrix products, arithmetic and copies ran while one was open for 0% of the time, Pallas kernels for 1%

profile of v6, /device:TPU:6, one launch (start us, length us, event | category | flops | bytes accessed | tf_op | source)
XLA Modules:
  0.0 225.9 jit_solution(9353389218138093285)
XLA Ops:
  7.8 2.4 %shard.1 = (bf16[64,640]{1,0:T(8,128)(2,1)}, bf16[4,64,640]{2,1,0:T(8,128)(2,1)}) custom-call(s32[4]{0:T(128)} %pad_add_fusion.where, bf16[8,64,384]{2,1,0:T(8,128)(2,1)} %qkv_any.1, bf16[8,64,256]{2,1,0:T(8,128)(2,1)} %bitcast.7, bf16[8,64]{1,0:T(8,128)(2,1)} %gain_any.1), custom_call_target="tpu_custom_call" | custom-call | tf_op jit(solution)/shard_map/shard/pallas_call | solution.py:227
  10.3 18.7 %all-to-all-start = ((bf16[4,64,640]{2,1,0:T(8,128)(2,1)}), bf16[4,64,640]{2,1,0:T(8,128)(2,1)S(1)}, u32[]{:S(2)}, u32[]{:S(2)}) async-start(bf16[4,64,640]{2,1,0:T(8,128)(2,1)} %get-tuple-element.22), calls=%async_computation | async-start | bytes 655360 | tf_op jit(solution)/shard_map/all_to_all | solution.py:267
  29.7 18.7 %all-to-all-done = bf16[4,64,640]{2,1,0:T(8,128)(2,1)S(1)} async-done(((bf16[4,64,640]{2,1,0:T(8,128)(2,1)}), bf16[4,64,640]{2,1,0:T(8,128)(2,1)S(1)}, u32[]{:S(2)}, u32[]{:S(2)}) %all-to-all-start) | async-done | bytes 327712 | tf_op jit(solution)/shard_map/all_to_all | solution.py:267
  48.4 7.0 %collective-permute-start = (bf16[4,64,640]{2,1,0:T(8,128)(2,1)S(1)}, bf16[4,64,640]{2,1,0:T(8,128)(2,1)S(1)}, u32[]{:S(2)}, u32[]{:S(2)}) collective-permute-start(bf16[4,64,640]{2,1,0:T(8,128)(2,1)S(1)} %all-to-all-done), channel_id=1, source_target_pairs={{0,1},{1,2},{2,3},{3,64},{64,65},{65,66},{66,67},{67,128},{128,129... | collective-permute-start | bytes 983048 | tf_op jit(solution)/shard_map/ppermute | solution.py:265
  57.3 5.8 %collective-permute-done = bf16[4,64,640]{2,1,0:T(8,128)(2,1)S(1)} collective-permute-done((bf16[4,64,640]{2,1,0:T(8,128)(2,1)S(1)}, bf16[4,64,640]{2,1,0:T(8,128)(2,1)S(1)}, u32[]{:S(2)}, u32[]{:S(2)}) %collective-permute-start) | collective-permute-done | bytes 327712 | tf_op jit(solution)/shard_map/ppermute | solution.py:265
  63.1 3.9 %collective-permute-done.1 = bf16[4,64,640]{2,1,0:T(8,128)(2,1)S(1)} collective-permute-done((bf16[4,64,640]{2,1,0:T(8,128)(2,1)S(1)}, bf16[4,64,640]{2,1,0:T(8,128)(2,1)S(1)}, u32[]{:S(2)}, u32[]{:S(2)}) %collective-permute-start.1) | collective-permute-done | bytes 327712 | tf_op jit(solution)/shard_map/ppermute | solution.py:265
  67.1 2.4 %collective-permute-start.3 = (bf16[8,64,640]{2,1,0:T(8,128)(2,1)S(1)}, bf16[8,64,640]{2,1,0:T(8,128)(2,1)S(1)}, u32[]{:S(2)}, u32[]{:S(2)}) collective-permute-start(bf16[8,64,640]{2,1,0:T(8,128)(2,1)S(1)} %constant_dynamic-update-slice_fusion.here_ref), channel_id=1, source_target_pairs={{0,256},{256,512},{512,768},{768,0},{1,257},{257,513},{513,769},{7... | collective-permute-start | bytes 1966088 | tf_op jit(solution)/shard_map/ppermute | solution.py:248
  69.5 3.5 %collective-permute-start.2 = (bf16[8,64,640]{2,1,0:T(8,128)(2,1)S(1)}, bf16[8,64,640]{2,1,0:T(8,128)(2,1)S(1)}, u32[]{:S(2)}, u32[]{:S(2)}) collective-permute-start(bf16[8,64,640]{2,1,0:T(8,128)(2,1)S(1)} %constant_dynamic-update-slice_fusion.here_ref), channel_id=1, source_target_pairs={{0,768},{256,0},{512,256},{768,512},{1,769},{257,1},{513,257},{769... | collective-permute-start | bytes 1966088 | tf_op jit(solution)/shard_map/ppermute | solution.py:248
  73.0 3.9 %collective-permute-start.4 = (bf16[2,64,640]{2,1,0:T(8,128)(2,1)S(1)}, bf16[2,64,640]{2,1,0:T(8,128)(2,1)S(1)}, u32[]{:S(2)}, u32[]{:S(2)}) collective-permute-start(bf16[2,64,640]{2,1,0:T(8,128)(2,1)S(1)} %slice.24), channel_id=1, source_target_pairs={{0,1},{1,2},{2,3},{3,64},{64,65},{65,66},{66,67},{67,128},{128,129... | collective-permute-start | bytes 491528 | tf_op jit(solution)/shard_map/ppermute | solution.py:265
  76.9 3.1 %collective-permute-start.5 = (bf16[2,64,640]{2,1,0:T(8,128)(2,1)S(1)}, bf16[2,64,640]{2,1,0:T(8,128)(2,1)S(1)}, u32[]{:S(2)}, u32[]{:S(2)}) collective-permute-start(bf16[2,64,640]{2,1,0:T(8,128)(2,1)S(1)} %slice.25), channel_id=1, source_target_pairs={{0,195},{1,0},{2,1},{3,2},{64,3},{65,64},{66,65},{67,66},{128,67},... | collective-permute-start | bytes 491528 | tf_op jit(solution)/shard_map/ppermute | solution.py:265
  81.4 2.7 %collective-permute-done.5 = bf16[2,64,640]{2,1,0:T(8,128)(2,1)S(1)} collective-permute-done((bf16[2,64,640]{2,1,0:T(8,128)(2,1)S(1)}, bf16[2,64,640]{2,1,0:T(8,128)(2,1)S(1)}, u32[]{:S(2)}, u32[]{:S(2)}) %collective-permute-start.5) | collective-permute-done | bytes 163872 | tf_op jit(solution)/shard_map/ppermute | solution.py:265
  84.2 3.5 %collective-permute-start.6 = (bf16[4,64,640]{2,1,0:T(8,128)(2,1)S(1)}, bf16[4,64,640]{2,1,0:T(8,128)(2,1)S(1)}, u32[]{:S(2)}, u32[]{:S(2)}) collective-permute-start(bf16[4,64,640]{2,1,0:T(8,128)(2,1)S(1)} %constant_dynamic-update-slice_fusion.2.here_ref), channel_id=1, source_target_pairs={{0,256},{256,512},{512,768},{768,0},{1,257},{257,513},{513,769},{7... | collective-permute-start | bytes 983048 | tf_op jit(solution)/shard_map/ppermute | solution.py:248
  87.7 2.3 %collective-permute-start.7 = (bf16[4,64,640]{2,1,0:T(8,128)(2,1)S(1)}, bf16[4,64,640]{2,1,0:T(8,128)(2,1)S(1)}, u32[]{:S(2)}, u32[]{:S(2)}) collective-permute-start(bf16[4,64,640]{2,1,0:T(8,128)(2,1)S(1)} %constant_dynamic-update-slice_fusion.2.here_ref), channel_id=1, source_target_pairs={{0,768},{256,0},{512,256},{768,512},{1,769},{257,1},{513,257},{769... | collective-permute-start | bytes 983048 | tf_op jit(solution)/shard_map/ppermute | solution.py:248
  90.1 4.8 %collective-permute-start.8 = (bf16[4,64,640]{2,1,0:T(8,128)(2,1)S(1)}, bf16[4,64,640]{2,1,0:T(8,128)(2,1)S(1)}, u32[]{:S(2)}, u32[]{:S(2)}) collective-permute-start(bf16[4,64,640]{2,1,0:T(8,128)(2,1)S(1)} %slice.26), channel_id=1, source_target_pairs={{0,256},{256,512},{512,768},{768,0},{1,257},{257,513},{513,769},{7... | collective-permute-start | bytes 983048 | tf_op jit(solution)/shard_map/ppermute | solution.py:252
  98.2 3.9 %collective-permute-done.7.after_ref = bf16[4,64,640]{2,1,0:T(8,128)(2,1)S(1)} collective-permute-done((bf16[4,64,640]{2,1,0:T(8,128)(2,1)S(1)}, bf16[4,64,640]{2,1,0:T(8,128)(2,1)S(1)}, u32[]{:S(2)}, u32[]{:S(2)}) %collective-permute-start.7) | collective-permute-done | bytes 327712 | tf_op jit(solution)/shard_map/ppermute | solution.py:248
  102.9 4.5 %collective-permute-done.9.rest_ref = bf16[4,64,640]{2,1,0:T(8,128)(2,1)S(1)} collective-permute-done((bf16[4,64,640]{2,1,0:T(8,128)(2,1)S(1)}, bf16[4,64,640]{2,1,0:T(8,128)(2,1)S(1)}, u32[]{:S(2)}, u32[]{:S(2)}) %collective-permute-start.9) | collective-permute-done | bytes 327712 | tf_op jit(solution)/shard_map/ppermute | solution.py:252
  107.7 2.1 collective-permute-start.12
  111.8 3.9 %collective-permute-start.11 = (bf16[2,64,640]{2,1,0:T(8,128)(2,1)S(1)}, bf16[2,64,640]{2,1,0:T(8,128)(2,1)S(1)}, u32[]{:S(2)}, u32[]{:S(2)}) collective-permute-start(bf16[2,64,640]{2,1,0:T(8,128)(2,1)S(1)} %slice.23), channel_id=1, source_target_pairs={{0,768},{256,0},{512,256},{768,512},{1,769},{257,1},{513,257},{769... | collective-permute-start | bytes 491528 | tf_op jit(solution)/shard_map/ppermute | solution.py:252
  115.7 3.2 %collective-permute-done.10.half_ref = bf16[2,64,640]{2,1,0:T(8,128)(2,1)S(1)} collective-permute-done((bf16[2,64,640]{2,1,0:T(8,128)(2,1)S(1)}, bf16[2,64,640]{2,1,0:T(8,128)(2,1)S(1)}, u32[]{:S(2)}, u32[]{:S(2)}) %collective-permute-start.10) | collective-permute-done | bytes 163872 | tf_op jit(solution)/shard_map/ppermute | solution.py:252
  118.9 2.7 %collective-permute-done.11.rest_ref = bf16[2,64,640]{2,1,0:T(8,128)(2,1)S(1)} collective-permute-done((bf16[2,64,640]{2,1,0:T(8,128)(2,1)S(1)}, bf16[2,64,640]{2,1,0:T(8,128)(2,1)S(1)}, u32[]{:S(2)}, u32[]{:S(2)}) %collective-permute-start.11) | collective-permute-done | bytes 163872 | tf_op jit(solution)/shard_map/ppermute | solution.py:252
  136.2 3.4 %section.8.held_ref = bf16[32,2048]{1,0:T(8,128)(2,1)S(1)} custom-call(s32[4]{0:T(128)S(1)} %copy-done.9, bf16[32,2048]{1,0:T(8,128)(2,1)S(1)} %get-tuple-element.19.x_ref, f32[128,32]{1,0:T(8,128)S(1)} %get-tuple-element.20.allowed_ref, bf16[32,2048]{1,0:T(8,128)(2,1)S(1)} %broadcast_in_dim.73.held_ref, ...), custom_call_target="tpu_custom_call", output_to_operand_aliasing={{}: (3, {})} | custom-call | tf_op jit(solution)/shard_map/section/pallas_call | solution.py:151
  140.9 3.4 %collective-permute-done.14.x_ref = bf16[32,2048]{1,0:T(8,128)(2,1)S(1)} collective-permute-done((bf16[32,2048]{1,0:T(8,128)(2,1)S(1)}, bf16[32,2048]{1,0:T(8,128)(2,1)S(1)}, u32[]{:S(2)}, u32[]{:S(2)}) %collective-permute-start.14) | collective-permute-done | bytes 131104 | tf_op jit(solution)/shard_map/ppermute | solution.py:402
  155.3 56.4 %collective-permute-start.23 = (bf16[8,2048]{1,0:T(8,128)(2,1)S(1)}, bf16[8,2048]{1,0:T(8,128)(2,1)S(1)}, u32[]{:S(2)}, u32[]{:S(2)}) collective-permute-start(bf16[8,2048]{1,0:T(8,128)(2,1)S(1)} %get-tuple-element.34), channel_id=1, source_target_pairs={{0,2},{1,3},{2,28},{3,29},{4,6},{5,7},{6,24},{7,25},{8,10},{9,11},... | collective-permute-start | bytes 98312 | tf_op jit(solution)/shard_map/ppermute | solution.py:369
  211.7 2.8 %collective-permute-start.24 = (bf16[8,2048]{1,0:T(8,128)(2,1)S(1)}, bf16[8,2048]{1,0:T(8,128)(2,1)S(1)}, u32[]{:S(2)}, u32[]{:S(2)}) collective-permute-start(bf16[8,2048]{1,0:T(8,128)(2,1)S(1)} %get-tuple-element.35), channel_id=1, source_target_pairs={{0,3},{1,0},{2,29},{3,30},{4,7},{5,4},{6,25},{7,26},{8,11},{9,8},{... | collective-permute-start | bytes 98312 | tf_op jit(solution)/shard_map/ppermute | solution.py:369
  (85 shorter events, 42.2 us)
Async XLA Ops:
  10.3 38.1 %all-to-all-start = ((bf16[4,64,640]{2,1,0:T(8,128)(2,1)}), bf16[4,64,640]{2,1,0:T(8,128)(2,1)S(1)}, u32[]{:S(2)}, u32[]{:S(2)}) async-start(bf16[4,64,640]{2,1,0:T(8,128)(2,1)} %get-tuple-element.22), calls=%async_computation | async-start | bytes 655360 | tf_op jit(solution)/shard_map/all_to_all | solution.py:267
  29.0 100.3 %all-gather.3.cloned.1.call-start = ((), (), s32[]{:S(2)}) async-start(), calls=%async_computation.1 | async-start | bytes 2703360 | tf_op jit(solution)/shard_map/all_gather | solution.py:243
  48.4 14.7 %collective-permute-start = (bf16[4,64,640]{2,1,0:T(8,128)(2,1)S(1)}, bf16[4,64,640]{2,1,0:T(8,128)(2,1)S(1)}, u32[]{:S(2)}, u32[]{:S(2)}) collective-permute-start(bf16[4,64,640]{2,1,0:T(8,128)(2,1)S(1)} %all-to-all-done), channel_id=1, source_target_pairs={{0,1},{1,2},{2,3},{3,64},{64,65},{65,66},{66,67},{67,128},{128,129... | collective-permute-start | bytes 983048 | tf_op jit(solution)/shard_map/ppermute | solution.py:265
  55.4 11.7 %collective-permute-start.1 = (bf16[4,64,640]{2,1,0:T(8,128)(2,1)S(1)}, bf16[4,64,640]{2,1,0:T(8,128)(2,1)S(1)}, u32[]{:S(2)}, u32[]{:S(2)}) collective-permute-start(bf16[4,64,640]{2,1,0:T(8,128)(2,1)S(1)} %all-to-all-done), channel_id=1, source_target_pairs={{0,195},{1,0},{2,1},{3,2},{64,3},{65,64},{66,65},{67,66},{128,67},... | collective-permute-start | bytes 983048 | tf_op jit(solution)/shard_map/ppermute | solution.py:265
  67.1 22.9 %collective-permute-start.3 = (bf16[8,64,640]{2,1,0:T(8,128)(2,1)S(1)}, bf16[8,64,640]{2,1,0:T(8,128)(2,1)S(1)}, u32[]{:S(2)}, u32[]{:S(2)}) collective-permute-start(bf16[8,64,640]{2,1,0:T(8,128)(2,1)S(1)} %constant_dynamic-update-slice_fusion.here_ref), channel_id=1, source_target_pairs={{0,256},{256,512},{512,768},{768,0},{1,257},{257,513},{513,769},{7... | collective-permute-start | bytes 1966088 | tf_op jit(solution)/shard_map/ppermute | solution.py:248
  69.5 25.3 %collective-permute-start.2 = (bf16[8,64,640]{2,1,0:T(8,128)(2,1)S(1)}, bf16[8,64,640]{2,1,0:T(8,128)(2,1)S(1)}, u32[]{:S(2)}, u32[]{:S(2)}) collective-permute-start(bf16[8,64,640]{2,1,0:T(8,128)(2,1)S(1)} %constant_dynamic-update-slice_fusion.here_ref), channel_id=1, source_target_pairs={{0,768},{256,0},{512,256},{768,512},{1,769},{257,1},{513,257},{769... | collective-permute-start | bytes 1966088 | tf_op jit(solution)/shard_map/ppermute | solution.py:248
  73.0 8.4 %collective-permute-start.4 = (bf16[2,64,640]{2,1,0:T(8,128)(2,1)S(1)}, bf16[2,64,640]{2,1,0:T(8,128)(2,1)S(1)}, u32[]{:S(2)}, u32[]{:S(2)}) collective-permute-start(bf16[2,64,640]{2,1,0:T(8,128)(2,1)S(1)} %slice.24), channel_id=1, source_target_pairs={{0,1},{1,2},{2,3},{3,64},{64,65},{65,66},{66,67},{67,128},{128,129... | collective-permute-start | bytes 491528 | tf_op jit(solution)/shard_map/ppermute | solution.py:265
  76.9 7.2 %collective-permute-start.5 = (bf16[2,64,640]{2,1,0:T(8,128)(2,1)S(1)}, bf16[2,64,640]{2,1,0:T(8,128)(2,1)S(1)}, u32[]{:S(2)}, u32[]{:S(2)}) collective-permute-start(bf16[2,64,640]{2,1,0:T(8,128)(2,1)S(1)} %slice.25), channel_id=1, source_target_pairs={{0,195},{1,0},{2,1},{3,2},{64,3},{65,64},{66,65},{67,66},{128,67},... | collective-permute-start | bytes 491528 | tf_op jit(solution)/shard_map/ppermute | solution.py:265
  84.2 14.1 %collective-permute-start.6 = (bf16[4,64,640]{2,1,0:T(8,128)(2,1)S(1)}, bf16[4,64,640]{2,1,0:T(8,128)(2,1)S(1)}, u32[]{:S(2)}, u32[]{:S(2)}) collective-permute-start(bf16[4,64,640]{2,1,0:T(8,128)(2,1)S(1)} %constant_dynamic-update-slice_fusion.2.here_ref), channel_id=1, source_target_pairs={{0,256},{256,512},{512,768},{768,0},{1,257},{257,513},{513,769},{7... | collective-permute-start | bytes 983048 | tf_op jit(solution)/shard_map/ppermute | solution.py:248
  87.7 14.4 %collective-permute-start.7 = (bf16[4,64,640]{2,1,0:T(8,128)(2,1)S(1)}, bf16[4,64,640]{2,1,0:T(8,128)(2,1)S(1)}, u32[]{:S(2)}, u32[]{:S(2)}) collective-permute-start(bf16[4,64,640]{2,1,0:T(8,128)(2,1)S(1)} %constant_dynamic-update-slice_fusion.2.here_ref), channel_id=1, source_target_pairs={{0,768},{256,0},{512,256},{768,512},{1,769},{257,1},{513,257},{769... | collective-permute-start | bytes 983048 | tf_op jit(solution)/shard_map/ppermute | solution.py:248
  90.1 12.9 %collective-permute-start.8 = (bf16[4,64,640]{2,1,0:T(8,128)(2,1)S(1)}, bf16[4,64,640]{2,1,0:T(8,128)(2,1)S(1)}, u32[]{:S(2)}, u32[]{:S(2)}) collective-permute-start(bf16[4,64,640]{2,1,0:T(8,128)(2,1)S(1)} %slice.26), channel_id=1, source_target_pairs={{0,256},{256,512},{512,768},{768,0},{1,257},{257,513},{513,769},{7... | collective-permute-start | bytes 983048 | tf_op jit(solution)/shard_map/ppermute | solution.py:252
  94.9 12.6 %collective-permute-start.9 = (bf16[4,64,640]{2,1,0:T(8,128)(2,1)S(1)}, bf16[4,64,640]{2,1,0:T(8,128)(2,1)S(1)}, u32[]{:S(2)}, u32[]{:S(2)}) collective-permute-start(bf16[4,64,640]{2,1,0:T(8,128)(2,1)S(1)} %slice.27), channel_id=1, source_target_pairs={{0,768},{256,0},{512,256},{768,512},{1,769},{257,1},{513,257},{769... | collective-permute-start | bytes 983048 | tf_op jit(solution)/shard_map/ppermute | solution.py:252
  107.7 20.0 %collective-permute-start.12 = (bf16[4,8,64,640]{3,2,1,0:T(8,128)(2,1)S(1)}, bf16[4,8,64,640]{3,2,1,0:T(8,128)(2,1)S(1)}, u32[]{:S(2)}, u32[]{:S(2)}) collective-permute-start(bf16[4,8,64,640]{3,2,1,0:T(8,128)(2,1)S(1)} %join.2.refs_1_), channel_id=1, source_target_pairs={{0,32},{32,0},{1,33},{33,1},{2,34},{34,2},{3,35},{35,3},{4,36},{36... | collective-permute-start | bytes 7864328 | tf_op jit(solution)/shard_map/ppermute | solution.py:278
  109.8 9.1 %collective-permute-start.10 = (bf16[2,64,640]{2,1,0:T(8,128)(2,1)S(1)}, bf16[2,64,640]{2,1,0:T(8,128)(2,1)S(1)}, u32[]{:S(2)}, u32[]{:S(2)}) collective-permute-start(bf16[2,64,640]{2,1,0:T(8,128)(2,1)S(1)} %slice.22), channel_id=1, source_target_pairs={{0,256},{256,512},{512,768},{768,0},{1,257},{257,513},{513,769},{7... | collective-permute-start | bytes 491528 | tf_op jit(solution)/shard_map/ppermute | solution.py:252
  111.8 9.8 %collective-permute-start.11 = (bf16[2,64,640]{2,1,0:T(8,128)(2,1)S(1)}, bf16[2,64,640]{2,1,0:T(8,128)(2,1)S(1)}, u32[]{:S(2)}, u32[]{:S(2)}) collective-permute-start(bf16[2,64,640]{2,1,0:T(8,128)(2,1)S(1)} %slice.23), channel_id=1, source_target_pairs={{0,768},{256,0},{512,256},{768,512},{1,769},{257,1},{513,257},{769... | collective-permute-start | bytes 491528 | tf_op jit(solution)/shard_map/ppermute | solution.py:252
  121.7 4.9 %collective-permute-start.13 = (bf16[4,4,64,640]{3,2,1,0:T(8,128)(2,1)S(1)}, bf16[4,4,64,640]{3,2,1,0:T(8,128)(2,1)S(1)}, u32[]{:S(2)}, u32[]{:S(2)}) collective-permute-start(bf16[4,4,64,640]{3,2,1,0:T(8,128)(2,1)S(1)} %join.3.refs_2_), channel_id=1, source_target_pairs={{0,32},{32,0},{1,33},{33,1},{2,34},{34,2},{3,35},{35,3},{4,36},{36... | collective-permute-start | bytes 3932168 | tf_op jit(solution)/shard_map/ppermute | solution.py:278
  139.6 4.7 %collective-permute-start.14 = (bf16[32,2048]{1,0:T(8,128)(2,1)S(1)}, bf16[32,2048]{1,0:T(8,128)(2,1)S(1)}, u32[]{:S(2)}, u32[]{:S(2)}) collective-permute-start(bf16[32,2048]{1,0:T(8,128)(2,1)S(1)} %section.8.held_ref), channel_id=1, source_target_pairs={{0,4},{1,5},{2,6},{3,7},{32,36},{33,37},{34,38},{35,39},{64,68},{6... | collective-permute-start | bytes 393224 | tf_op jit(solution)/shard_map/ppermute | solution.py:402
  144.9 0.7 collective-permute-start.15
  147.4 0.7 collective-permute-start.17
  148.9 0.7 collective-permute-start.18
  152.7 61.8 %collective-permute-start.21 = (bf16[8,2048]{1,0:T(8,128)(2,1)S(1)}, bf16[8,2048]{1,0:T(8,128)(2,1)S(1)}, u32[]{:S(2)}, u32[]{:S(2)}) collective-permute-start(bf16[8,2048]{1,0:T(8,128)(2,1)S(1)} %get-tuple-element.32), channel_id=1, source_target_pairs={{0,0},{1,1},{2,30},{3,31},{4,4},{5,5},{6,26},{7,27},{8,8},{9,9},{1... | collective-permute-start | bytes 98312 | tf_op jit(solution)/shard_map/ppermute | solution.py:369
  153.4 61.1 %collective-permute-start.22 = (bf16[8,2048]{1,0:T(8,128)(2,1)S(1)}, bf16[8,2048]{1,0:T(8,128)(2,1)S(1)}, u32[]{:S(2)}, u32[]{:S(2)}) collective-permute-start(bf16[8,2048]{1,0:T(8,128)(2,1)S(1)} %get-tuple-element.33), channel_id=1, source_target_pairs={{0,1},{1,2},{2,31},{3,28},{4,5},{5,6},{6,27},{7,24},{8,9},{9,10},{... | collective-permute-start | bytes 98312 | tf_op jit(solution)/shard_map/ppermute | solution.py:369
  155.3 61.0 %collective-permute-start.23 = (bf16[8,2048]{1,0:T(8,128)(2,1)S(1)}, bf16[8,2048]{1,0:T(8,128)(2,1)S(1)}, u32[]{:S(2)}, u32[]{:S(2)}) collective-permute-start(bf16[8,2048]{1,0:T(8,128)(2,1)S(1)} %get-tuple-element.34), channel_id=1, source_target_pairs={{0,2},{1,3},{2,28},{3,29},{4,6},{5,7},{6,24},{7,25},{8,10},{9,11},... | collective-permute-start | bytes 98312 | tf_op jit(solution)/shard_map/ppermute | solution.py:369
  211.7 5.8 %collective-permute-start.24 = (bf16[8,2048]{1,0:T(8,128)(2,1)S(1)}, bf16[8,2048]{1,0:T(8,128)(2,1)S(1)}, u32[]{:S(2)}, u32[]{:S(2)}) collective-permute-start(bf16[8,2048]{1,0:T(8,128)(2,1)S(1)} %get-tuple-element.35), channel_id=1, source_target_pairs={{0,3},{1,0},{2,29},{3,30},{4,7},{5,4},{6,25},{7,26},{8,11},{9,8},{... | collective-permute-start | bytes 98312 | tf_op jit(solution)/shard_map/ppermute | solution.py:369
  (15 other events, 97.2 us)
Sparse Core Ops, SparseCore 0:
  34.1 91.2 all-gather.2

commit v7 on v5

--- a/solution.py
+++ b/solution.py
@@ -22,6 +22,7 @@
 ZH = 4
 ZL = 4
 Z = ZH * ZL
+HALF = SEQ // 2
 ROWS = 256
 
 F32, BF16 = jnp.float32, jnp.bfloat16
@@ -45,9 +46,10 @@
     ]
 
 
-def attention(projected, rope, allowed):
-    lane = lax.broadcasted_iota(jnp.int32, (SEQ, 128), 1)
-    lane2 = lax.broadcasted_iota(jnp.int32, (SEQ, 256), 1)
+def attention(projected, rope, allowed, earlier):
+    rows = projected[0].shape[0]
+    lane = lax.broadcasted_iota(jnp.int32, (rows, 128), 1)
+    lane2 = lax.broadcasted_iota(jnp.int32, (rows, 256), 1)
     head_of = (lane2 % 128) // 32
     zero = jnp.zeros((), BF16)
     cos, sin, kcos, ksin_a, ksin_b = rope
@@ -71,41 +73,52 @@
         key_b = key_b + pltpu.roll(key_b, 64, 1)
         keys.append(jnp.concatenate([key_a, key_b], axis=-1).astype(BF16))
         values.append(kv.astype(BF16))
+    all_keys, all_values = keys, values
+    if earlier is not None:
+        all_keys = [jnp.concatenate(pair, axis=0) for pair in zip(earlier[0], keys)]
+        all_values = [jnp.concatenate(pair, axis=0) for pair in zip(earlier[1], values)]
     scores = [
         lax.dot_general(q, k, (((1,), (1,)), ((), ())), preferred_element_type=F32)
-        for q, k in zip(queries, keys)
+        for q, k in zip(queries, all_keys)
     ]
     scores = [jnp.where(allowed, s * HEAD_DIM ** (-0.5), -1e30) for s in scores]
     scores = [jnp.exp(s - jnp.max(s, axis=-1, keepdims=True)) for s in scores]
     weights = [(s * (1.0 / jnp.sum(s, axis=-1, keepdims=True))).astype(BF16) for s in scores]
     contexts = []
-    for weight, value in zip(weights, values):
+    for weight, value in zip(weights, all_values):
         mixed = jnp.dot(weight, value, preferred_element_type=F32)
-        rows = [mixed[h * SEQ : (h + 1) * SEQ] for h in range(GROUP_HEADS)]
+        heads = [mixed[h * rows : (h + 1) * rows] for h in range(GROUP_HEADS)]
         context = jnp.concatenate(
             [
-                jnp.where(lane < 64, pltpu.roll(rows[0], 64, 1), rows[1]),
-                jnp.where(lane < 64, pltpu.roll(rows[2], 64, 1), rows[3]),
+                jnp.where(lane < 64, pltpu.roll(heads[0], 64, 1), heads[1]),
+                jnp.where(lane < 64, pltpu.roll(heads[2], 64, 1), heads[3]),
             ],
             axis=-1,
         )
         contexts.append(context.astype(BF16))
-    return contexts
-
-
-def section_kernel(step, last, where, x_ref, allowed_ref, held_ref, *refs):
-    rope, weights, outputs = refs[:5], (refs[5:8], refs[8:11]), refs[11:]
-    out_ref = outputs[-1]
+    return contexts, keys, values
+
+
+def section_kernel(step, half, last, where, x_ref, allowed_ref, held_ref, *refs):
+    rope, weights, refs = refs[:5], (refs[5:8], refs[8:11]), refs[11:]
+    first = half * HALF
+    if half == 0:
+        out_ref, keys_ref, values_ref = refs
+    elif last:
+        keys_ref, values_ref, before_ref, *chunks, out_ref = refs
+    else:
+        keys_ref, values_ref, out_ref = refs
+    out_rows = pl.ds(first if last and half else 0, HALF)
 
     def rows_of(i, zh, t, columns):
-        part, first = ((0, 0), (1, ZH), (2, 0), (1, 0))[t]
+        part, start = ((0, 0), (1, ZH), (2, 0), (1, 0))[t]
         return jnp.concatenate(
-            [weights[i][part][x, first + zh, :, columns] for x in range(X)], axis=0
+            [weights[i][part][x, start + zh, :, columns] for x in range(X)], axis=0
         )
 
     @pl.when(where[0] != step)
     def _():
-        out_ref[...] = held_ref[...].astype(out_ref.dtype)
+        out_ref[out_rows, :] = held_ref[...].astype(out_ref.dtype)
 
     @pl.when(where[0] == step)
     def _():
@@ -120,40 +133,58 @@
                 for part, (i, zh) in zip(parts, places)
             ]
             projected.append(functools.reduce(jnp.add, terms) * scale)
-        contexts = attention(projected, [part[...] for part in rope], allowed_ref[...] > 0.5)
+        allowed = allowed_ref[pl.ds(first, HALF), pl.ds(0, first + HALF)] > 0.5
+        allowed = jnp.concatenate([allowed] * GROUP_HEADS, axis=0)
+        earlier = None
+        if half:
+            earlier = [[ref[t] for t in range(GROUPS)] for ref in (keys_ref, values_ref)]
+        contexts, keys, values = attention(
+            projected, [part[pl.ds(first, HALF), :] for part in rope], allowed, earlier
+        )
+        if not half:
+            for t in range(GROUPS):
+                keys_ref[t] = keys[t]
+                values_ref[t] = values[t]
         for j, (i, zh) in enumerate(places):
             terms = [
-                lax.dot_general(
-                    contexts[t],
-                    rows_of(i, zh, t, pl.ds(QKV, CTX)),
-                    (((1,), (1,)), ((), ())),
-                    preferred_element_type=F32,
+                jnp.dot(
+                    contexts[t], rows_of(i, zh, t, pl.ds(QKV, CTX)), preferred_element_type=F32
                 )
                 for t in range(GROUPS)
             ]
             total = x_ref[:, pl.ds(j * ROWS, ROWS)].astype(F32) + functools.reduce(jnp.add, terms)
-            out_ref[:, pl.ds(j * ROWS, ROWS)] = total.astype(out_ref.dtype)
-
-    if last:
-        rows = outputs[0].shape[0]
-        for k, chunk_ref in enumerate(outputs[:-1]):
+            out_ref[out_rows, pl.ds(j * ROWS, ROWS)] = total.astype(out_ref.dtype)
+
+    if last and half:
+        out_ref[pl.ds(0, HALF), :] = before_ref[...].astype(F32)
+        rows = chunks[0].shape[0]
+        for k, chunk_ref in enumerate(chunks):
             place = (where[3] + k) % (SEQ // rows)
             chunk_ref[...] = out_ref[pl.ds(pl.multiple_of(place * rows, rows), rows), :].astype(BF16)
 
 
-def run_section(step, last, where, values, allowed, held, rope, weights):
+def run_section(step, half, last, where, values, allowed, held, rope, weights, *more):
     vmem = pl.BlockSpec(memory_space=pltpu.VMEM)
-    whole, chunk = (jax.ShapeDtypeStruct((rows, D), BF16) for rows in (SEQ, SEQ // 4))
+    part = jax.ShapeDtypeStruct((HALF, D), BF16)
+    split = bool(last and half)
+    if half == 0:
+        shapes = [
+            part,
+            jax.ShapeDtypeStruct((GROUPS, HALF, 256), BF16),
+            jax.ShapeDtypeStruct((GROUPS, HALF, 128), BF16),
+        ]
+    else:
+        shapes = [jax.ShapeDtypeStruct((SEQ // 4, D), BF16)] * 4 if split else [part]
     return pl.pallas_call(
-        functools.partial(section_kernel, step, last),
-        out_shape=[chunk] * 4 if last else whole,
-        in_specs=[pl.BlockSpec(memory_space=pltpu.SMEM)] + [vmem] * 14,
-        out_specs=[vmem] * 4 if last else vmem,
-        scratch_shapes=[pltpu.VMEM((SEQ, D), F32)] if last else [],
-        input_output_aliases={} if last else {3: 0},
+        functools.partial(section_kernel, step, half, last),
+        out_shape=shapes,
+        in_specs=[pl.BlockSpec(memory_space=pltpu.SMEM)] + [vmem] * (14 + len(more)),
+        out_specs=[vmem] * len(shapes),
+        scratch_shapes=[pltpu.VMEM((SEQ, D), F32)] if split else [],
+        input_output_aliases={} if split else {3: 0},
         compiler_params=MEDIUM,
         name="section",
-    )(where, values, allowed, held, *rope, *weights)
+    )(where, values, allowed, held, *rope, *weights, *more)
 
 
 def shard_kernel(where, qkv_any, out_any, gain_any, shard_ref, qkv_ref, out_ref, gain_ref, done):
@@ -185,37 +216,33 @@
 
     first = lanes([one, pltpu.roll(one, 96, 1), pltpu.roll(two, 64, 1), pltpu.roll(two, 32, 1)])
     second = lanes([pltpu.roll(one, 96, 1), pltpu.roll(one, 64, 1), pltpu.roll(two, 32, 1), two])
-    shard_ref[:, pl.ds(0, 128)] = first.astype(BF16)
-    shard_ref[:, pl.ds(128, 128)] = second.astype(BF16)
-    shard_ref[:, pl.ds(256, 128)] = qkv[:, 256:].astype(BF16)
-    shard_ref[:, pl.ds(QKV, CTX)] = out_ref[...]
-
-
-def column_kernel(where, own_ref, below_ref, above_ref, half_ref, rest_ref, out_ref):
-    own, half = where[4], half_ref.shape[0]
-    out_ref[own] = own_ref[...]
-    out_ref[(own + ZH - 1) % ZH] = below_ref[...]
-    out_ref[(own + 1) % ZH] = above_ref[...]
-    out_ref[(own + 2) % ZH, pl.ds(0, half)] = half_ref[...]
-    out_ref[(own + 2) % ZH, pl.ds(half, half)] = rest_ref[...]
+    for zh in range(shard_ref.shape[0]):
+        shard_ref[zh, :, pl.ds(0, 128)] = first.astype(BF16)
+        shard_ref[zh, :, pl.ds(128, 128)] = second.astype(BF16)
+        shard_ref[zh, :, pl.ds(256, 128)] = qkv[:, 256:].astype(BF16)
+        shard_ref[zh, :, pl.ds(QKV, CTX)] = out_ref[...]
 
 
 def join_kernel(here_ref, after_ref, before_ref, half_ref, rest_ref, out_ref):
     half = half_ref.shape[0]
-    out_ref[0] = here_ref[...]
-    out_ref[1] = after_ref[...]
-    out_ref[2, pl.ds(0, half)] = half_ref[...]
-    out_ref[2, pl.ds(half, half)] = rest_ref[...]
-    out_ref[3] = before_ref[...]
+    for i in range(out_ref.shape[1]):
+        middle = half_ref.at[i] if i < half else rest_ref.at[i - half]
+        parts = [here_ref.at[i], after_ref.at[i], middle, before_ref.at[i]]
+        for x, part in enumerate(parts):
+            out_ref[x, i, :, pl.ds(0, QKV)] = part[:, pl.ds(0, QKV)]
+        columns = jnp.concatenate([part[:, pl.ds(QKV, CTX)] for part in parts], axis=0)
+        turned_columns = columns.astype(F32).T.astype(BF16)
+        for x in range(X):
+            out_ref[x, i, :, pl.ds(QKV, CTX)] = turned_columns[x * 64 : (x + 1) * 64]
 
 
 def gather_section(where, w_qkv, w_out, norm_gain):
     rows = w_qkv.shape[1]
     vmem = pl.BlockSpec(memory_space=pltpu.VMEM)
     smem = pl.BlockSpec(memory_space=pltpu.SMEM)
-    shard = pl.pallas_call(
+    shards = pl.pallas_call(
         shard_kernel,
-        out_shape=jax.ShapeDtypeStruct((rows, QKV + CTX), BF16),
+        out_shape=jax.ShapeDtypeStruct((ZH, rows, QKV + CTX), BF16),
         in_specs=[smem] + [pl.BlockSpec(memory_space=pl.ANY)] * 3,
         out_specs=vmem,
         scratch_shapes=[
@@ -249,21 +276,7 @@
     def along_z(parts, by):
         return lax.ppermute(parts, ("z_hi", "tensor"), [(z, (z + by) % Z) for z in range(Z)])
 
-    here = pl.pallas_call(
-        column_kernel,
-        out_shape=jax.ShapeDtypeStruct((ZH, *shard.shape), BF16),
-        in_specs=[smem] + [vmem] * 5,
-        out_specs=vmem,
-        compiler_params=SMALL,
-        name="column",
-    )(
-        where,
-        shard,
-        along_z(shard, ZL),
-        along_z(shard, -ZL),
-        along_z(shard[: rows // 2], 2 * ZL),
-        along_z(shard[rows // 2 :], -2 * ZL),
-    )
+    here = lax.all_to_all(shards, "z_hi", 0, 0)
     half = ZH // 2
     ahead, behind = along_z(here, 1), along_z(here, -1)
     here_x = first_along_x(here)
@@ -291,7 +304,9 @@
     return result
 
 
-def enter_kernel(where, down_ref, up_ref, down_docs_ref, up_docs_ref, out_ref, allowed_ref):
+def enter_kernel(
+    where, down_ref, up_ref, down_docs_ref, up_docs_ref, first_ref, second_ref, allowed_ref
+):
     member = where[3]
     x_ref = jnp.where(member < 2, down_ref[member % 2], up_ref[member % 2]).astype(F32)
     docs = [docs_ref[...] for docs_ref in (down_docs_ref, up_docs_ref)]
@@ -301,8 +316,7 @@
     column = lax.broadcasted_iota(jnp.int32, (SEQ, SEQ), 1)
     own_docs = jnp.sum(jnp.where(row == column, docs, 0), axis=1, keepdims=True)
     allowed = jnp.where((row >= column) & (own_docs == docs), 1.0, 0.0)
-    for h in range(GROUP_HEADS):
-        allowed_ref[pl.ds(h * SEQ, SEQ), :] = allowed
+    allowed_ref[...] = allowed
     lane = lax.broadcasted_iota(jnp.int32, (SEQ, 128), 1)
     for zh in range(ZH):
         tiles = [x_ref[:, x * 512 + zh * 128 : x * 512 + zh * 128 + 128] for x in range(X)]
@@ -317,7 +331,9 @@
             cores.append(turned(jnp.concatenate(pairs, axis=1), (X - where[1]) % X))
         for i in range(2):
             part = jnp.where(where[2] == i, cores[0], cores[1])
-            out_ref[:, pl.ds((i * ZH + zh) * ROWS, ROWS)] = part.astype(BF16)
+            columns = pl.ds((i * ZH + zh) * ROWS, ROWS)
+            first_ref[:, columns] = part[:HALF].astype(BF16)
+            second_ref[:, columns] = part[HALF:].astype(BF16)
 
 
 def order_kernel(where, *refs):
@@ -376,28 +392,38 @@
 
 
 def on_device(down_in, up_in, w_qkv, w_out, norm_gain, down_docs, up_docs):
-    where = jnp.stack([lax.axis_index(name) for name in ("pipe", "x", "core", "tensor", "z_hi")])
+    where = jnp.stack([lax.axis_index(name) for name in ("pipe", "x", "core", "tensor")])
     sections = lax.axis_size("pipe")
     weights = gather_section(where, w_qkv, w_out, norm_gain)
     rope = rotary_tables()
     vmem = pl.BlockSpec(memory_space=pltpu.VMEM)
-    values, allowed = pl.pallas_call(
+    part = jax.ShapeDtypeStruct((HALF, D), BF16)
+    *values, allowed = pl.pallas_call(
         enter_kernel,
-        out_shape=[
-            jax.ShapeDtypeStruct((SEQ, D), BF16),
-            jax.ShapeDtypeStruct((GROUP_HEADS * SEQ, SEQ), F32),
-        ],
+        out_shape=[part, part, jax.ShapeDtypeStruct((SEQ, SEQ), F32)],
         in_specs=[pl.BlockSpec(memory_space=pltpu.SMEM)] + [vmem] * 4,
-        out_specs=[vmem, vmem],
+        out_specs=[vmem] * 3,
         compiler_params=SMALL,
         name="enter",
     )(where, down_in, up_in, down_docs, up_docs)
-    held = jnp.zeros((SEQ, D), BF16)
-    for step in range(sections - 1):
-        held = run_section(step, False, where, values, allowed, held, rope, weights)
-        values = lax.ppermute(held, "pipe", [(step, step + 1)])
-    chunks = run_section(sections - 1, True, where, values, allowed, held, rope, weights)
-    return exchange(chunks, where)
+    held = [jnp.zeros((HALF, D), BF16)] * 2
+    for step in range(sections):
+        last = step + 1 == sections
+
+        def run(half, *more):
+            return run_section(
+                step, half, last, where, values[half], allowed, held[half], rope, weights, *more
+            )
+
+        def next_plane(part):
+            return lax.ppermute(part, "pipe", [(step, step + 1)])
+
+        one, *state = run(0)
+        if last:
+            return exchange(run(1, *state, one), where)
+        (two,) = run(1, *state)
+        held = [one, two]
+        values = [next_plane(one), next_plane(two)]
 
 
 def solution(mesh):

time: 222 us -> 212 us (0.955)
  starting transfers between devices: 165 us -> 120 us
  blocking collectives: 0 us -> 42.4 us
  waiting for transfers between devices: 38 us -> 26.6 us
  Pallas kernels: 13.3 us -> 19.5 us
  local copies, waits for them, and re-layouts: 3.25 us -> 0.2 us
    all_to_all x0 -> x1, blocking collectives: none -> 42.4 us  [gather_section(): here = lax.all_to_all(shards, 'z_hi', 0, 0)]
    ppermute x8 -> x4, starting transfers between devices: 47.5 us -> 13.1 us  [along_z(): lax.ppermute(parts, ('z_hi', 'tensor'), [(z, (z + by) % Z) for z in range...]
    ppermute x4, starting transfers between devices: 66 us -> 50 us  [exchange(): received.append(lax.ppermute(chunk, ('pipe', 'tensor'), pairs))]
    ppermute x8 -> x4, waiting for transfers between devices: 9.38 us -> 1.99 us  [along_z(): lax.ppermute(parts, ('z_hi', 'tensor'), [(z, (z + by) % Z) for z in range...]
    pallas_call x11 -> x18, Pallas kernels: 11.4 us -> 17.1 us  [the longest x16 13.9 us: run_section(): pl.pallas_call(functools.partial(section_kernel, step, half, last), out_s...]
    ppermute x7 -> x14, starting transfers between devices: 5.31 us -> 10.6 us  [next_plane(): return lax.ppermute(part, 'pipe', [(step, step + 1)])]
    ppermute x7 -> x14, waiting for transfers between devices: 3.33 us -> 0.66 us  [next_plane(): return lax.ppermute(part, 'pipe', [(step, step + 1)])]
  transfers between devices with their start and end apart: 34 -> 37, of which waited for: 14 -> 14; matrix products, arithmetic and copies ran while one was open for 1% -> 0% of each run, Pallas kernels for 0% -> 6%
where the time goes in v7:
time: 212 us; the launch traced here: 211 us
  starting transfers between devices  120 us (57%)
  blocking collectives  42.4 us (20%)
  waiting for transfers between devices  26.6 us (13%)
  Pallas kernels  19.5 us (9%)
    ppermute x4, starting transfers between devices, exchange(): received.append(lax.ppermute(chunk, ('pipe', 'tensor'), pairs))  50 us
    all_to_all x1, blocking collectives, gather_section(): here = lax.all_to_all(shards, 'z_hi', 0, 0)  42.4 us
    ppermute x6, starting transfers between devices, first_along_x(): return (lax.ppermute(parts, 'x', one), lax.ppermute(parts, 'x', other))  21.5 us
    pallas_call x16, Pallas kernels, run_section(): pl.pallas_call(functools.partial(section_kernel, step, half, last), out_s...  13.9 us
    ppermute x4, starting transfers between devices, along_z(): lax.ppermute(parts, ('z_hi', 'tensor'), [(z, (z + by) % Z) for z in range...  13.1 us
    ppermute x3, waiting for transfers between devices, rest_along_x(): lax.ppermute(after[half:], 'x', other)  11.5 us
    ppermute x14, starting transfers between devices, next_plane(): return lax.ppermute(part, 'pipe', [(step, step + 1)])  10.6 us
    ppermute x3, starting transfers between devices, rest_along_x(): lax.ppermute(before[:half], 'x', one)  10.5 us
  transfers between devices with their start and end apart: 37, of which 14 were waited for; matrix products, arithmetic and copies ran while one was open for 0% of the time, Pallas kernels for 6%

profile of v7, /device:TPU:6, one launch (start us, length us, event | category | flops | bytes accessed | tf_op | source)
XLA Modules:
  0.0 210.9 jit_solution(9557150806012430018)
XLA Ops:
  1.3 2.4 %shard.1 = bf16[4,64,640]{2,1,0:T(8,128)(2,1)} custom-call(s32[4]{0:T(128)} %pad_add_fusion.where, bf16[8,64,384]{2,1,0:T(8,128)(2,1)} %qkv_any.1, bf16[8,64,256]{2,1,0:T(8,128)(2,1)} %bitcast.5, bf16[8,64]{1,0:T(8,128)(2,1)} %gain_any.1), custom_call_target="tpu_custom_call" | custom-call | tf_op jit(solution)/shard_map/shard/pallas_call | solution.py:243
  3.7 42.4 %all_to_all.5.here_ref = bf16[4,64,640]{2,1,0:T(8,128)(2,1)S(1)} all-to-all(bf16[4,64,640]{2,1,0:T(8,128)(2,1)} %shard.1), channel_id=1, replica_groups=mesh['x'=4,'z_hi'=4,'core'=2,'pipe'=8,'tensor'=4] {'z_hi'}, dimensions={0} | all-to-all | bytes 655360 | tf_op jit(solution)/shard_map/all_to_all | solution.py:279
  46.1 3.9 %collective-permute-start.1 = (bf16[4,64,640]{2,1,0:T(8,128)(2,1)S(1)}, bf16[4,64,640]{2,1,0:T(8,128)(2,1)S(1)}, u32[]{:S(2)}, u32[]{:S(2)}) collective-permute-start(bf16[4,64,640]{2,1,0:T(8,128)(2,1)S(1)} %all_to_all.5.here_ref), channel_id=1, source_target_pairs={{0,195},{1,0},{2,1},{3,2},{64,3},{65,64},{66,65},{67,66},{128,67},... | collective-permute-start | bytes 983048 | tf_op jit(solution)/shard_map/ppermute | solution.py:277
  50.0 2.0 collective-permute-start
  51.9 2.7 %collective-permute-start.3 = (bf16[4,64,640]{2,1,0:T(8,128)(2,1)S(1)}, bf16[4,64,640]{2,1,0:T(8,128)(2,1)S(1)}, u32[]{:S(2)}, u32[]{:S(2)}) collective-permute-start(bf16[4,64,640]{2,1,0:T(8,128)(2,1)S(1)} %all_to_all.5.here_ref), channel_id=1, source_target_pairs={{0,768},{256,0},{512,256},{768,512},{1,769},{257,1},{513,257},{769... | collective-permute-start | bytes 983048 | tf_op jit(solution)/shard_map/ppermute | solution.py:260
  54.7 4.3 %collective-permute-start.2 = (bf16[4,64,640]{2,1,0:T(8,128)(2,1)S(1)}, bf16[4,64,640]{2,1,0:T(8,128)(2,1)S(1)}, u32[]{:S(2)}, u32[]{:S(2)}) collective-permute-start(bf16[4,64,640]{2,1,0:T(8,128)(2,1)S(1)} %all_to_all.5.here_ref), channel_id=1, source_target_pairs={{0,256},{256,512},{512,768},{768,0},{1,257},{257,513},{513,769},{7... | collective-permute-start | bytes 983048 | tf_op jit(solution)/shard_map/ppermute | solution.py:260
  59.0 2.0 collective-permute-done
  64.2 5.5 %collective-permute-start.9 = (bf16[8,64,640]{2,1,0:T(8,128)(2,1)S(1)}, bf16[8,64,640]{2,1,0:T(8,128)(2,1)S(1)}, u32[]{:S(2)}, u32[]{:S(2)}) collective-permute-start(bf16[8,64,640]{2,1,0:T(8,128)(2,1)S(1)} %pad_maximum_fusion.here_ref), channel_id=1, source_target_pairs={{0,256},{256,512},{512,768},{768,0},{1,257},{257,513},{513,769},{7... | collective-permute-start | bytes 1966088 | tf_op jit(solution)/shard_map/ppermute | solution.py:260
  71.7 4.9 %collective-permute-start.5 = (bf16[2,64,640]{2,1,0:T(8,128)(2,1)S(1)}, bf16[2,64,640]{2,1,0:T(8,128)(2,1)S(1)}, u32[]{:S(2)}, u32[]{:S(2)}) collective-permute-start(bf16[2,64,640]{2,1,0:T(8,128)(2,1)S(1)} %slice.33), channel_id=1, source_target_pairs={{0,195},{1,0},{2,1},{3,2},{64,3},{65,64},{66,65},{67,66},{128,67},... | collective-permute-start | bytes 491528 | tf_op jit(solution)/shard_map/ppermute | solution.py:277
  76.6 2.4 %collective-permute-start.4 = (bf16[2,64,640]{2,1,0:T(8,128)(2,1)S(1)}, bf16[2,64,640]{2,1,0:T(8,128)(2,1)S(1)}, u32[]{:S(2)}, u32[]{:S(2)}) collective-permute-start(bf16[2,64,640]{2,1,0:T(8,128)(2,1)S(1)} %slice.32), channel_id=1, source_target_pairs={{0,1},{1,2},{2,3},{3,64},{64,65},{65,66},{66,67},{67,128},{128,129... | collective-permute-start | bytes 491528 | tf_op jit(solution)/shard_map/ppermute | solution.py:277
  79.0 5.1 %collective-permute-start.6 = (bf16[2,64,640]{2,1,0:T(8,128)(2,1)S(1)}, bf16[2,64,640]{2,1,0:T(8,128)(2,1)S(1)}, u32[]{:S(2)}, u32[]{:S(2)}) collective-permute-start(bf16[2,64,640]{2,1,0:T(8,128)(2,1)S(1)} %slice.26), channel_id=1, source_target_pairs={{0,256},{256,512},{512,768},{768,0},{1,257},{257,513},{513,769},{7... | collective-permute-start | bytes 491528 | tf_op jit(solution)/shard_map/ppermute | solution.py:264
  86.9 5.6 %collective-permute-done.7.rest_ref = bf16[2,64,640]{2,1,0:T(8,128)(2,1)S(1)} collective-permute-done((bf16[2,64,640]{2,1,0:T(8,128)(2,1)S(1)}, bf16[2,64,640]{2,1,0:T(8,128)(2,1)S(1)}, u32[]{:S(2)}, u32[]{:S(2)}) %collective-permute-start.7) | collective-permute-done | bytes 163872 | tf_op jit(solution)/shard_map/ppermute | solution.py:264
  94.5 5.1 %collective-permute-start.10 = (bf16[4,64,640]{2,1,0:T(8,128)(2,1)S(1)}, bf16[4,64,640]{2,1,0:T(8,128)(2,1)S(1)}, u32[]{:S(2)}, u32[]{:S(2)}) collective-permute-start(bf16[4,64,640]{2,1,0:T(8,128)(2,1)S(1)} %pad_maximum_fusion.1.here_ref), channel_id=1, source_target_pairs={{0,256},{256,512},{512,768},{768,0},{1,257},{257,513},{513,769},{7... | collective-permute-start | bytes 983048 | tf_op jit(solution)/shard_map/ppermute | solution.py:260
  101.6 3.9 %collective-permute-start.13 = (bf16[4,64,640]{2,1,0:T(8,128)(2,1)S(1)}, bf16[4,64,640]{2,1,0:T(8,128)(2,1)S(1)}, u32[]{:S(2)}, u32[]{:S(2)}) collective-permute-start(bf16[4,64,640]{2,1,0:T(8,128)(2,1)S(1)} %slice.35), channel_id=1, source_target_pairs={{0,768},{256,0},{512,256},{768,512},{1,769},{257,1},{513,257},{769... | collective-permute-start | bytes 983048 | tf_op jit(solution)/shard_map/ppermute | solution.py:264
  106.8 3.5 %collective-permute-done.12.half_ref = bf16[4,64,640]{2,1,0:T(8,128)(2,1)S(1)} collective-permute-done((bf16[4,64,640]{2,1,0:T(8,128)(2,1)S(1)}, bf16[4,64,640]{2,1,0:T(8,128)(2,1)S(1)}, u32[]{:S(2)}, u32[]{:S(2)}) %collective-permute-start.12) | collective-permute-done | bytes 327712 | tf_op jit(solution)/shard_map/ppermute | solution.py:264
  114.2 3.4 %collective-permute-start.14 = (bf16[2,64,640]{2,1,0:T(8,128)(2,1)S(1)}, bf16[2,64,640]{2,1,0:T(8,128)(2,1)S(1)}, u32[]{:S(2)}, u32[]{:S(2)}) collective-permute-start(bf16[2,64,640]{2,1,0:T(8,128)(2,1)S(1)} %slice.30), channel_id=1, source_target_pairs={{0,256},{256,512},{512,768},{768,0},{1,257},{257,513},{513,769},{7... | collective-permute-start | bytes 491528 | tf_op jit(solution)/shard_map/ppermute | solution.py:264
  117.7 2.4 %collective-permute-start.15 = (bf16[2,64,640]{2,1,0:T(8,128)(2,1)S(1)}, bf16[2,64,640]{2,1,0:T(8,128)(2,1)S(1)}, u32[]{:S(2)}, u32[]{:S(2)}) collective-permute-start(bf16[2,64,640]{2,1,0:T(8,128)(2,1)S(1)} %slice.31), channel_id=1, source_target_pairs={{0,768},{256,0},{512,256},{768,512},{1,769},{257,1},{513,257},{769... | collective-permute-start | bytes 491528 | tf_op jit(solution)/shard_map/ppermute | solution.py:264
  120.4 2.1 collective-permute-start.16
  122.7 4.4 %collective-permute-done.15.rest_ref = bf16[2,64,640]{2,1,0:T(8,128)(2,1)S(1)} collective-permute-done((bf16[2,64,640]{2,1,0:T(8,128)(2,1)S(1)}, bf16[2,64,640]{2,1,0:T(8,128)(2,1)S(1)}, u32[]{:S(2)}, u32[]{:S(2)}) %collective-permute-start.15) | collective-permute-done | bytes 163872 | tf_op jit(solution)/shard_map/ppermute | solution.py:264
  132.3 2.7 %section.16 = (bf16[16,2048]{1,0:T(8,128)(2,1)S(1)}, bf16[4,16,256]{2,1,0:T(8,128)(2,1)S(1)}, bf16[4,16,128]{2,1,0:T(8,128)(2,1)S(1)}) custom-call(s32[4]{0:T(128)S(1)} %copy-done.2, bf16[16,2048]{1,0:T(8,128)(2,1)S(1)} %get-tuple-element.55.x_ref, f32[32,32]{1,0:T(8,128)S(1)} %get-tuple-element.44.allowed_ref, ...), custom_call_target="tpu_custom_call", output_to_operand_aliasing={{0}: (3, {})} | custom-call | tf_op jit(solution)/shard_map/section/pallas_call | solution.py:178
  136.3 2.7 %section.17.held_ref = bf16[16,2048]{1,0:T(8,128)(2,1)S(1)} custom-call(s32[4]{0:T(128)S(1)} %copy-done.2, bf16[16,2048]{1,0:T(8,128)(2,1)S(1)} %get-tuple-element.43.x_ref, f32[32,32]{1,0:T(8,128)S(1)} %get-tuple-element.44.allowed_ref, bf16[16,2048]{1,0:T(8,128)(2,1)S(1)} %broadcast_in_dim.121.held_ref, ...), custom_call_target="tpu_custom_call", output_to_operand_aliasing={{}: (3, {})} | custom-call | tf_op jit(solution)/shard_map/section/pallas_call | solution.py:178
  158.4 5.8 %collective-permute-start.34 = (bf16[8,2048]{1,0:T(8,128)(2,1)S(1)}, bf16[8,2048]{1,0:T(8,128)(2,1)S(1)}, u32[]{:S(2)}, u32[]{:S(2)}) collective-permute-start(bf16[8,2048]{1,0:T(8,128)(2,1)S(1)} %get-tuple-element.81), channel_id=1, source_target_pairs={{0,1},{1,2},{2,31},{3,28},{4,5},{5,6},{6,27},{7,24},{8,9},{9,10},{... | collective-permute-start | bytes 98312 | tf_op jit(solution)/shard_map/ppermute | solution.py:381
  164.1 39.4 %collective-permute-start.35 = (bf16[8,2048]{1,0:T(8,128)(2,1)S(1)}, bf16[8,2048]{1,0:T(8,128)(2,1)S(1)}, u32[]{:S(2)}, u32[]{:S(2)}) collective-permute-start(bf16[8,2048]{1,0:T(8,128)(2,1)S(1)} %get-tuple-element.82), channel_id=1, source_target_pairs={{0,2},{1,3},{2,28},{3,29},{4,6},{5,7},{6,24},{7,25},{8,10},{9,11},... | collective-permute-start | bytes 98312 | tf_op jit(solution)/shard_map/ppermute | solution.py:381
  203.5 4.2 %collective-permute-start.36 = (bf16[8,2048]{1,0:T(8,128)(2,1)S(1)}, bf16[8,2048]{1,0:T(8,128)(2,1)S(1)}, u32[]{:S(2)}, u32[]{:S(2)}) collective-permute-start(bf16[8,2048]{1,0:T(8,128)(2,1)S(1)} %get-tuple-element.83), channel_id=1, source_target_pairs={{0,3},{1,0},{2,29},{3,30},{4,7},{5,4},{6,25},{7,26},{8,11},{9,8},{... | collective-permute-start | bytes 98312 | tf_op jit(solution)/shard_map/ppermute | solution.py:381
  (100 shorter events, 46.6 us)
Async XLA Ops:
  46.1 12.9 %collective-permute-start.1 = (bf16[4,64,640]{2,1,0:T(8,128)(2,1)S(1)}, bf16[4,64,640]{2,1,0:T(8,128)(2,1)S(1)}, u32[]{:S(2)}, u32[]{:S(2)}) collective-permute-start(bf16[4,64,640]{2,1,0:T(8,128)(2,1)S(1)} %all_to_all.5.here_ref), channel_id=1, source_target_pairs={{0,195},{1,0},{2,1},{3,2},{64,3},{65,64},{66,65},{67,66},{128,67},... | collective-permute-start | bytes 983048 | tf_op jit(solution)/shard_map/ppermute | solution.py:277
  50.0 11.0 %collective-permute-start = (bf16[4,64,640]{2,1,0:T(8,128)(2,1)S(1)}, bf16[4,64,640]{2,1,0:T(8,128)(2,1)S(1)}, u32[]{:S(2)}, u32[]{:S(2)}) collective-permute-start(bf16[4,64,640]{2,1,0:T(8,128)(2,1)S(1)} %all_to_all.5.here_ref), channel_id=1, source_target_pairs={{0,1},{1,2},{2,3},{3,64},{64,65},{65,66},{66,67},{67,128},{128,129... | collective-permute-start | bytes 983048 | tf_op jit(solution)/shard_map/ppermute | solution.py:277
  51.9 11.0 %collective-permute-start.3 = (bf16[4,64,640]{2,1,0:T(8,128)(2,1)S(1)}, bf16[4,64,640]{2,1,0:T(8,128)(2,1)S(1)}, u32[]{:S(2)}, u32[]{:S(2)}) collective-permute-start(bf16[4,64,640]{2,1,0:T(8,128)(2,1)S(1)} %all_to_all.5.here_ref), channel_id=1, source_target_pairs={{0,768},{256,0},{512,256},{768,512},{1,769},{257,1},{513,257},{769... | collective-permute-start | bytes 983048 | tf_op jit(solution)/shard_map/ppermute | solution.py:260
  54.7 9.5 %collective-permute-start.2 = (bf16[4,64,640]{2,1,0:T(8,128)(2,1)S(1)}, bf16[4,64,640]{2,1,0:T(8,128)(2,1)S(1)}, u32[]{:S(2)}, u32[]{:S(2)}) collective-permute-start(bf16[4,64,640]{2,1,0:T(8,128)(2,1)S(1)} %all_to_all.5.here_ref), channel_id=1, source_target_pairs={{0,256},{256,512},{512,768},{768,0},{1,257},{257,513},{513,769},{7... | collective-permute-start | bytes 983048 | tf_op jit(solution)/shard_map/ppermute | solution.py:260
  64.2 35.4 %collective-permute-start.9 = (bf16[8,64,640]{2,1,0:T(8,128)(2,1)S(1)}, bf16[8,64,640]{2,1,0:T(8,128)(2,1)S(1)}, u32[]{:S(2)}, u32[]{:S(2)}) collective-permute-start(bf16[8,64,640]{2,1,0:T(8,128)(2,1)S(1)} %pad_maximum_fusion.here_ref), channel_id=1, source_target_pairs={{0,256},{256,512},{512,768},{768,0},{1,257},{257,513},{513,769},{7... | collective-permute-start | bytes 1966088 | tf_op jit(solution)/shard_map/ppermute | solution.py:260
  69.7 31.9 %collective-permute-start.8 = (bf16[8,64,640]{2,1,0:T(8,128)(2,1)S(1)}, bf16[8,64,640]{2,1,0:T(8,128)(2,1)S(1)}, u32[]{:S(2)}, u32[]{:S(2)}) collective-permute-start(bf16[8,64,640]{2,1,0:T(8,128)(2,1)S(1)} %pad_maximum_fusion.here_ref), channel_id=1, source_target_pairs={{0,768},{256,0},{512,256},{768,512},{1,769},{257,1},{513,257},{769... | collective-permute-start | bytes 1966088 | tf_op jit(solution)/shard_map/ppermute | solution.py:260
  71.7 12.5 %collective-permute-start.5 = (bf16[2,64,640]{2,1,0:T(8,128)(2,1)S(1)}, bf16[2,64,640]{2,1,0:T(8,128)(2,1)S(1)}, u32[]{:S(2)}, u32[]{:S(2)}) collective-permute-start(bf16[2,64,640]{2,1,0:T(8,128)(2,1)S(1)} %slice.33), channel_id=1, source_target_pairs={{0,195},{1,0},{2,1},{3,2},{64,3},{65,64},{66,65},{67,66},{128,67},... | collective-permute-start | bytes 491528 | tf_op jit(solution)/shard_map/ppermute | solution.py:277
  76.6 9.5 %collective-permute-start.4 = (bf16[2,64,640]{2,1,0:T(8,128)(2,1)S(1)}, bf16[2,64,640]{2,1,0:T(8,128)(2,1)S(1)}, u32[]{:S(2)}, u32[]{:S(2)}) collective-permute-start(bf16[2,64,640]{2,1,0:T(8,128)(2,1)S(1)} %slice.32), channel_id=1, source_target_pairs={{0,1},{1,2},{2,3},{3,64},{64,65},{65,66},{66,67},{67,128},{128,129... | collective-permute-start | bytes 491528 | tf_op jit(solution)/shard_map/ppermute | solution.py:277
  79.0 8.0 %collective-permute-start.6 = (bf16[2,64,640]{2,1,0:T(8,128)(2,1)S(1)}, bf16[2,64,640]{2,1,0:T(8,128)(2,1)S(1)}, u32[]{:S(2)}, u32[]{:S(2)}) collective-permute-start(bf16[2,64,640]{2,1,0:T(8,128)(2,1)S(1)} %slice.26), channel_id=1, source_target_pairs={{0,256},{256,512},{512,768},{768,0},{1,257},{257,513},{513,769},{7... | collective-permute-start | bytes 491528 | tf_op jit(solution)/shard_map/ppermute | solution.py:264
  84.1 8.4 %collective-permute-start.7 = (bf16[2,64,640]{2,1,0:T(8,128)(2,1)S(1)}, bf16[2,64,640]{2,1,0:T(8,128)(2,1)S(1)}, u32[]{:S(2)}, u32[]{:S(2)}) collective-permute-start(bf16[2,64,640]{2,1,0:T(8,128)(2,1)S(1)} %slice.27), channel_id=1, source_target_pairs={{0,768},{256,0},{512,256},{768,512},{1,769},{257,1},{513,257},{769... | collective-permute-start | bytes 491528 | tf_op jit(solution)/shard_map/ppermute | solution.py:264
  92.6 13.0 %collective-permute-start.11 = (bf16[4,64,640]{2,1,0:T(8,128)(2,1)S(1)}, bf16[4,64,640]{2,1,0:T(8,128)(2,1)S(1)}, u32[]{:S(2)}, u32[]{:S(2)}) collective-permute-start(bf16[4,64,640]{2,1,0:T(8,128)(2,1)S(1)} %pad_maximum_fusion.1.here_ref), channel_id=1, source_target_pairs={{0,768},{256,0},{512,256},{768,512},{1,769},{257,1},{513,257},{769... | collective-permute-start | bytes 983048 | tf_op jit(solution)/shard_map/ppermute | solution.py:260
  94.5 12.3 %collective-permute-start.10 = (bf16[4,64,640]{2,1,0:T(8,128)(2,1)S(1)}, bf16[4,64,640]{2,1,0:T(8,128)(2,1)S(1)}, u32[]{:S(2)}, u32[]{:S(2)}) collective-permute-start(bf16[4,64,640]{2,1,0:T(8,128)(2,1)S(1)} %pad_maximum_fusion.1.here_ref), channel_id=1, source_target_pairs={{0,256},{256,512},{512,768},{768,0},{1,257},{257,513},{513,769},{7... | collective-permute-start | bytes 983048 | tf_op jit(solution)/shard_map/ppermute | solution.py:260
  99.7 10.6 %collective-permute-start.12 = (bf16[4,64,640]{2,1,0:T(8,128)(2,1)S(1)}, bf16[4,64,640]{2,1,0:T(8,128)(2,1)S(1)}, u32[]{:S(2)}, u32[]{:S(2)}) collective-permute-start(bf16[4,64,640]{2,1,0:T(8,128)(2,1)S(1)} %slice.34), channel_id=1, source_target_pairs={{0,256},{256,512},{512,768},{768,0},{1,257},{257,513},{513,769},{7... | collective-permute-start | bytes 983048 | tf_op jit(solution)/shard_map/ppermute | solution.py:264
  101.6 10.2 %collective-permute-start.13 = (bf16[4,64,640]{2,1,0:T(8,128)(2,1)S(1)}, bf16[4,64,640]{2,1,0:T(8,128)(2,1)S(1)}, u32[]{:S(2)}, u32[]{:S(2)}) collective-permute-start(bf16[4,64,640]{2,1,0:T(8,128)(2,1)S(1)} %slice.35), channel_id=1, source_target_pairs={{0,768},{256,0},{512,256},{768,512},{1,769},{257,1},{513,257},{769... | collective-permute-start | bytes 983048 | tf_op jit(solution)/shard_map/ppermute | solution.py:264
  112.2 20.0 %collective-permute-start.17 = (bf16[4,8,64,640]{3,2,1,0:T(8,128)(2,1)S(1)}, bf16[4,8,64,640]{3,2,1,0:T(8,128)(2,1)S(1)}, u32[]{:S(2)}, u32[]{:S(2)}) collective-permute-start(bf16[4,8,64,640]{3,2,1,0:T(8,128)(2,1)S(1)} %join.4.refs_6_), channel_id=1, source_target_pairs={{0,32},{32,0},{1,33},{33,1},{2,34},{34,2},{3,35},{35,3},{4,36},{36... | collective-permute-start | bytes 7864328 | tf_op jit(solution)/shard_map/ppermute | solution.py:297
  114.2 8.5 %collective-permute-start.14 = (bf16[2,64,640]{2,1,0:T(8,128)(2,1)S(1)}, bf16[2,64,640]{2,1,0:T(8,128)(2,1)S(1)}, u32[]{:S(2)}, u32[]{:S(2)}) collective-permute-start(bf16[2,64,640]{2,1,0:T(8,128)(2,1)S(1)} %slice.30), channel_id=1, source_target_pairs={{0,256},{256,512},{512,768},{768,0},{1,257},{257,513},{513,769},{7... | collective-permute-start | bytes 491528 | tf_op jit(solution)/shard_map/ppermute | solution.py:264
  117.7 9.4 %collective-permute-start.15 = (bf16[2,64,640]{2,1,0:T(8,128)(2,1)S(1)}, bf16[2,64,640]{2,1,0:T(8,128)(2,1)S(1)}, u32[]{:S(2)}, u32[]{:S(2)}) collective-permute-start(bf16[2,64,640]{2,1,0:T(8,128)(2,1)S(1)} %slice.31), channel_id=1, source_target_pairs={{0,768},{256,0},{512,256},{768,512},{1,769},{257,1},{513,257},{769... | collective-permute-start | bytes 491528 | tf_op jit(solution)/shard_map/ppermute | solution.py:264
  120.4 9.9 %collective-permute-start.16 = (bf16[4,4,64,640]{3,2,1,0:T(8,128)(2,1)S(1)}, bf16[4,4,64,640]{3,2,1,0:T(8,128)(2,1)S(1)}, u32[]{:S(2)}, u32[]{:S(2)}) collective-permute-start(bf16[4,4,64,640]{3,2,1,0:T(8,128)(2,1)S(1)} %join.3.refs_5_), channel_id=1, source_target_pairs={{0,32},{32,0},{1,33},{33,1},{2,34},{34,2},{3,35},{35,3},{4,36},{36... | collective-permute-start | bytes 3932168 | tf_op jit(solution)/shard_map/ppermute | solution.py:297
  127.3 4.9 %collective-permute-start.18 = (bf16[4,4,64,640]{3,2,1,0:T(8,128)(2,1)S(1)}, bf16[4,4,64,640]{3,2,1,0:T(8,128)(2,1)S(1)}, u32[]{:S(2)}, u32[]{:S(2)}) collective-permute-start(bf16[4,4,64,640]{3,2,1,0:T(8,128)(2,1)S(1)} %join.5.refs_7_), channel_id=1, source_target_pairs={{0,32},{32,0},{1,33},{33,1},{2,34},{34,2},{3,35},{35,3},{4,36},{36... | collective-permute-start | bytes 3932168 | tf_op jit(solution)/shard_map/ppermute | solution.py:297
  135.0 5.4 %collective-permute-start.20 = (bf16[16,2048]{1,0:T(8,128)(2,1)S(1)}, bf16[16,2048]{1,0:T(8,128)(2,1)S(1)}, u32[]{:S(2)}, u32[]{:S(2)}) collective-permute-start(bf16[16,2048]{1,0:T(8,128)(2,1)S(1)} %get-tuple-element.58.held_ref), channel_id=1, source_target_pairs={{0,4},{1,5},{2,6},{3,7},{32,36},{33,37},{34,38},{35,39},{64,68},{6... | collective-permute-start | bytes 196616 | tf_op jit(solution)/shard_map/ppermute | solution.py:419
  157.7 50.1 %collective-permute-start.33 = (bf16[8,2048]{1,0:T(8,128)(2,1)S(1)}, bf16[8,2048]{1,0:T(8,128)(2,1)S(1)}, u32[]{:S(2)}, u32[]{:S(2)}) collective-permute-start(bf16[8,2048]{1,0:T(8,128)(2,1)S(1)} %get-tuple-element.80), channel_id=1, source_target_pairs={{0,0},{1,1},{2,30},{3,31},{4,4},{5,5},{6,26},{7,27},{8,8},{9,9},{1... | collective-permute-start | bytes 98312 | tf_op jit(solution)/shard_map/ppermute | solution.py:381
  158.4 49.4 %collective-permute-start.34 = (bf16[8,2048]{1,0:T(8,128)(2,1)S(1)}, bf16[8,2048]{1,0:T(8,128)(2,1)S(1)}, u32[]{:S(2)}, u32[]{:S(2)}) collective-permute-start(bf16[8,2048]{1,0:T(8,128)(2,1)S(1)} %get-tuple-element.81), channel_id=1, source_target_pairs={{0,1},{1,2},{2,31},{3,28},{4,5},{5,6},{6,27},{7,24},{8,9},{9,10},{... | collective-permute-start | bytes 98312 | tf_op jit(solution)/shard_map/ppermute | solution.py:381
  164.1 43.9 %collective-permute-start.35 = (bf16[8,2048]{1,0:T(8,128)(2,1)S(1)}, bf16[8,2048]{1,0:T(8,128)(2,1)S(1)}, u32[]{:S(2)}, u32[]{:S(2)}) collective-permute-start(bf16[8,2048]{1,0:T(8,128)(2,1)S(1)} %get-tuple-element.82), channel_id=1, source_target_pairs={{0,2},{1,3},{2,28},{3,29},{4,6},{5,7},{6,24},{7,25},{8,10},{9,11},... | collective-permute-start | bytes 98312 | tf_op jit(solution)/shard_map/ppermute | solution.py:381
  203.5 5.8 %collective-permute-start.36 = (bf16[8,2048]{1,0:T(8,128)(2,1)S(1)}, bf16[8,2048]{1,0:T(8,128)(2,1)S(1)}, u32[]{:S(2)}, u32[]{:S(2)}) collective-permute-start(bf16[8,2048]{1,0:T(8,128)(2,1)S(1)} %get-tuple-element.83), channel_id=1, source_target_pairs={{0,3},{1,0},{2,29},{3,30},{4,7},{5,4},{6,25},{7,26},{8,11},{9,8},{... | collective-permute-start | bytes 98312 | tf_op jit(solution)/shard_map/ppermute | solution.py:381
  (18 other events, 71.4 us)

commit v8 on v7

--- a/solution.py
+++ b/solution.py
@@ -105,7 +105,7 @@
     if half == 0:
         out_ref, keys_ref, values_ref = refs
     elif last:
-        keys_ref, values_ref, before_ref, *chunks, out_ref = refs
+        keys_ref, values_ref, before_ref, chunks_ref, out_ref = refs
     else:
         keys_ref, values_ref, out_ref = refs
     out_rows = pl.ds(first if last and half else 0, HALF)
@@ -157,10 +157,9 @@
 
     if last and half:
         out_ref[pl.ds(0, HALF), :] = before_ref[...].astype(F32)
-        rows = chunks[0].shape[0]
-        for k, chunk_ref in enumerate(chunks):
-            place = (where[3] + k) % (SEQ // rows)
-            chunk_ref[...] = out_ref[pl.ds(pl.multiple_of(place * rows, rows), rows), :].astype(BF16)
+        for k in range(chunks_ref.shape[0]):
+            place = k % GROUPS * (SEQ // GROUPS)
+            chunks_ref[k] = out_ref[pl.ds(place, SEQ // GROUPS), :].astype(BF16)
 
 
 def run_section(step, half, last, where, values, allowed, held, rope, weights, *more):
@@ -174,7 +173,7 @@
             jax.ShapeDtypeStruct((GROUPS, HALF, 128), BF16),
         ]
     else:
-        shapes = [jax.ShapeDtypeStruct((SEQ // 4, D), BF16)] * 4 if split else [part]
+        shapes = [jax.ShapeDtypeStruct((8, SEQ // 4, D), BF16) if split else part]
     return pl.pallas_call(
         functools.partial(section_kernel, step, half, last),
         out_shape=shapes,
@@ -336,12 +335,12 @@
             second_ref[:, columns] = part[HALF:].astype(BF16)
 
 
-def order_kernel(where, *refs):
-    *received, down_ref, up_ref = refs
-    rows = received[0].shape[0]
-    values = jnp.concatenate([part[...] for part in received], axis=0).astype(F32)
+def order_kernel(where, received_ref, down_ref, up_ref):
+    plane = where[0] // 4
+    rows = received_ref.shape[1]
+    parts = [received_ref[(plane if t < 2 else 1 - plane) * 4 + t] for t in range(4)]
+    values = jnp.concatenate([part.astype(F32) for part in parts], axis=0)
     lane = lax.broadcasted_iota(jnp.int32, (values.shape[0], 128), 1)
-    tiles = {}
     for zh in range(ZH):
         mine, other = (
             turned(values[:, (i * ZH + zh) * ROWS : (i * ZH + zh + 1) * ROWS], where[1])
@@ -350,45 +349,33 @@
         zero, one = jnp.where(where[2] == 0, mine, other), jnp.where(where[2] == 0, other, mine)
         for pair in range(2):
             a, b = (part[:, pair * 128 : (pair + 1) * 128] for part in (zero, one))
-            tiles[2 * pair, zh] = jnp.where(lane < 64, a, pltpu.roll(b, 64, 1))
-            tiles[2 * pair + 1, zh] = jnp.where(lane < 64, pltpu.roll(a, 64, 1), b)
-    natural = jnp.concatenate(
-        [tiles[x, zh] for x in range(X) for zh in range(ZH)], axis=1
-    ).astype(BF16)
-    for k in range(len(received)):
-        source = (where[3] + len(received) - k) % len(received)
-        part = natural[k * rows : (k + 1) * rows]
-
-        @pl.when(source < 2)
-        def _():
-            down_ref[0, source] = part
-
-        @pl.when(source >= 2)
-        def _():
-            up_ref[0, source - 2] = part
+            even = jnp.where(lane < 64, a, pltpu.roll(b, 64, 1)).astype(BF16)
+            odd = jnp.where(lane < 64, pltpu.roll(a, 64, 1), b).astype(BF16)
+            for x, tile in ((2 * pair, even), (2 * pair + 1, odd)):
+                columns = pl.ds(x * 512 + zh * 128, 128)
+                for t in range(4):
+                    out_ref = down_ref if t < 2 else up_ref
+                    out_ref[0, t % 2, :, columns] = tile[t * rows : (t + 1) * rows]
 
 
 def exchange(chunks, where):
     planes, members = lax.axis_size("pipe"), lax.axis_size("tensor")
     rows = SEQ // members
-    received = []
-    for k, chunk in enumerate(chunks):
-        pairs = [
-            (y * members + t, (y if t < 2 else planes - 1 - y) * members + (t + k) % members)
-            for y in range(planes)
-            for t in range(members)
-        ]
-        received.append(lax.ppermute(chunk, ("pipe", "tensor"), pairs))
+    groups = [
+        [plane * members + t for plane in (y, planes - 1 - y) for t in range(members)]
+        for y in range(planes // 2)
+    ]
+    received = lax.all_to_all(chunks, ("pipe", "tensor"), 0, 0, axis_index_groups=groups)
     vmem = pl.BlockSpec(memory_space=pltpu.VMEM)
     shape = jax.ShapeDtypeStruct((1, members // 2, rows, D), BF16)
     return pl.pallas_call(
         order_kernel,
         out_shape=[shape, shape],
-        in_specs=[pl.BlockSpec(memory_space=pltpu.SMEM)] + [vmem] * members,
+        in_specs=[pl.BlockSpec(memory_space=pltpu.SMEM), vmem],
         out_specs=[vmem, vmem],
         compiler_params=SMALL,
         name="order",
-    )(where, *received)
+    )(where, received)
 
 
 def on_device(down_in, up_in, w_qkv, w_out, norm_gain, down_docs, up_docs):
@@ -420,7 +407,7 @@
 
         one, *state = run(0)
         if last:
-            return exchange(run(1, *state, one), where)
+            return exchange(run(1, *state, one)[0], where)
         (two,) = run(1, *state)
         held = [one, two]
         values = [next_plane(one), next_plane(two)]

time: 212 us -> 211 us (level)
  blocking collectives: 42.4 us -> 92.8 us
  starting transfers between devices: 120 us -> 69.8 us
    all_to_all x0 -> x1, blocking collectives: none -> 50.4 us  [exchange(): lax.all_to_all(chunks, ('pipe', 'tensor'), 0, 0, axis_index_groups=groups)]
    ppermute x4 -> x0, starting transfers between devices: 50 us -> none  [exchange(): received.append(lax.ppermute(chunk, ('pipe', 'tensor'), pairs))]
  transfers between devices with their start and end apart: 37 -> 33, of which waited for: 14 -> 12; matrix products, arithmetic and copies ran while one was open for 0% -> 0% of each run, Pallas kernels for 6% -> 6%
where the time goes in v8:
time: 211 us; the launch traced here: 210 us
  blocking collectives  92.8 us (44%)
  starting transfers between devices  69.8 us (33%)
  waiting for transfers between devices  25.1 us (12%)
  Pallas kernels  19.4 us (9%)
    all_to_all x1, blocking collectives, exchange(): lax.all_to_all(chunks, ('pipe', 'tensor'), 0, 0, axis_index_groups=groups)  50.4 us
    all_to_all x1, blocking collectives, gather_section(): here = lax.all_to_all(shards, 'z_hi', 0, 0)  42.4 us
    ppermute x6, starting transfers between devices, first_along_x(): return (lax.ppermute(parts, 'x', one), lax.ppermute(parts, 'x', other))  21.5 us
    pallas_call x16, Pallas kernels, run_section(): pl.pallas_call(functools.partial(section_kernel, step, half, last), out_s...  13.8 us
    ppermute x4, starting transfers between devices, along_z(): lax.ppermute(parts, ('z_hi', 'tensor'), [(z, (z + by) % Z) for z in range...  13.1 us
    ppermute x3, waiting for transfers between devices, rest_along_x(): lax.ppermute(after[half:], 'x', other)  11.5 us
    ppermute x14, starting transfers between devices, next_plane(): return lax.ppermute(part, 'pipe', [(step, step + 1)])  10.6 us
    ppermute x3, starting transfers between devices, rest_along_x(): lax.ppermute(before[:half], 'x', one)  10.5 us
  transfers between devices with their start and end apart: 33, of which 12 were waited for; matrix products, arithmetic and copies ran while one was open for 0% of the time, Pallas kernels for 6%

profile of v8, /device:TPU:6, one launch (start us, length us, event | category | flops | bytes accessed | tf_op | source)
XLA Modules:
  0.0 209.6 jit_solution(13466204121545961066)
XLA Ops:
  1.3 2.4 %shard.1 = bf16[4,64,640]{2,1,0:T(8,128)(2,1)} custom-call(s32[4]{0:T(128)} %pad_add_fusion.where, bf16[8,64,384]{2,1,0:T(8,128)(2,1)} %qkv_any.1, bf16[8,64,256]{2,1,0:T(8,128)(2,1)} %bitcast.5, bf16[8,64]{1,0:T(8,128)(2,1)} %gain_any.1), custom_call_target="tpu_custom_call" | custom-call | tf_op jit(solution)/shard_map/shard/pallas_call | solution.py:242
  3.7 42.4 %all_to_all.10.here_ref = bf16[4,64,640]{2,1,0:T(8,128)(2,1)S(1)} all-to-all(bf16[4,64,640]{2,1,0:T(8,128)(2,1)} %shard.1), channel_id=1, replica_groups=mesh['x'=4,'z_hi'=4,'core'=2,'pipe'=8,'tensor'=4] {'z_hi'}, dimensions={0} | all-to-all | bytes 655360 | tf_op jit(solution)/shard_map/all_to_all | solution.py:278
  46.1 3.9 %collective-permute-start.1 = (bf16[4,64,640]{2,1,0:T(8,128)(2,1)S(1)}, bf16[4,64,640]{2,1,0:T(8,128)(2,1)S(1)}, u32[]{:S(2)}, u32[]{:S(2)}) collective-permute-start(bf16[4,64,640]{2,1,0:T(8,128)(2,1)S(1)} %all_to_all.10.here_ref), channel_id=1, source_target_pairs={{0,195},{1,0},{2,1},{3,2},{64,3},{65,64},{66,65},{67,66},{128,67},... | collective-permute-start | bytes 983048 | tf_op jit(solution)/shard_map/ppermute | solution.py:276
  50.0 2.0 collective-permute-start
  52.0 2.7 %collective-permute-start.3 = (bf16[4,64,640]{2,1,0:T(8,128)(2,1)S(1)}, bf16[4,64,640]{2,1,0:T(8,128)(2,1)S(1)}, u32[]{:S(2)}, u32[]{:S(2)}) collective-permute-start(bf16[4,64,640]{2,1,0:T(8,128)(2,1)S(1)} %all_to_all.10.here_ref), channel_id=1, source_target_pairs={{0,768},{256,0},{512,256},{768,512},{1,769},{257,1},{513,257},{769... | collective-permute-start | bytes 983048 | tf_op jit(solution)/shard_map/ppermute | solution.py:259
  54.7 4.3 %collective-permute-start.2 = (bf16[4,64,640]{2,1,0:T(8,128)(2,1)S(1)}, bf16[4,64,640]{2,1,0:T(8,128)(2,1)S(1)}, u32[]{:S(2)}, u32[]{:S(2)}) collective-permute-start(bf16[4,64,640]{2,1,0:T(8,128)(2,1)S(1)} %all_to_all.10.here_ref), channel_id=1, source_target_pairs={{0,256},{256,512},{512,768},{768,0},{1,257},{257,513},{513,769},{7... | collective-permute-start | bytes 983048 | tf_op jit(solution)/shard_map/ppermute | solution.py:259
  59.1 2.0 collective-permute-done
  64.2 5.5 %collective-permute-start.9 = (bf16[8,64,640]{2,1,0:T(8,128)(2,1)S(1)}, bf16[8,64,640]{2,1,0:T(8,128)(2,1)S(1)}, u32[]{:S(2)}, u32[]{:S(2)}) collective-permute-start(bf16[8,64,640]{2,1,0:T(8,128)(2,1)S(1)} %pad_maximum_fusion.here_ref), channel_id=1, source_target_pairs={{0,256},{256,512},{512,768},{768,0},{1,257},{257,513},{513,769},{7... | collective-permute-start | bytes 1966088 | tf_op jit(solution)/shard_map/ppermute | solution.py:259
  71.7 4.9 %collective-permute-start.5 = (bf16[2,64,640]{2,1,0:T(8,128)(2,1)S(1)}, bf16[2,64,640]{2,1,0:T(8,128)(2,1)S(1)}, u32[]{:S(2)}, u32[]{:S(2)}) collective-permute-start(bf16[2,64,640]{2,1,0:T(8,128)(2,1)S(1)} %slice.33), channel_id=1, source_target_pairs={{0,195},{1,0},{2,1},{3,2},{64,3},{65,64},{66,65},{67,66},{128,67},... | collective-permute-start | bytes 491528 | tf_op jit(solution)/shard_map/ppermute | solution.py:276
  76.6 2.4 %collective-permute-start.4 = (bf16[2,64,640]{2,1,0:T(8,128)(2,1)S(1)}, bf16[2,64,640]{2,1,0:T(8,128)(2,1)S(1)}, u32[]{:S(2)}, u32[]{:S(2)}) collective-permute-start(bf16[2,64,640]{2,1,0:T(8,128)(2,1)S(1)} %slice.32), channel_id=1, source_target_pairs={{0,1},{1,2},{2,3},{3,64},{64,65},{65,66},{66,67},{67,128},{128,129... | collective-permute-start | bytes 491528 | tf_op jit(solution)/shard_map/ppermute | solution.py:276
  79.0 5.1 %collective-permute-start.6 = (bf16[2,64,640]{2,1,0:T(8,128)(2,1)S(1)}, bf16[2,64,640]{2,1,0:T(8,128)(2,1)S(1)}, u32[]{:S(2)}, u32[]{:S(2)}) collective-permute-start(bf16[2,64,640]{2,1,0:T(8,128)(2,1)S(1)} %slice.26), channel_id=1, source_target_pairs={{0,256},{256,512},{512,768},{768,0},{1,257},{257,513},{513,769},{7... | collective-permute-start | bytes 491528 | tf_op jit(solution)/shard_map/ppermute | solution.py:263
  87.0 5.6 %collective-permute-done.7.rest_ref = bf16[2,64,640]{2,1,0:T(8,128)(2,1)S(1)} collective-permute-done((bf16[2,64,640]{2,1,0:T(8,128)(2,1)S(1)}, bf16[2,64,640]{2,1,0:T(8,128)(2,1)S(1)}, u32[]{:S(2)}, u32[]{:S(2)}) %collective-permute-start.7) | collective-permute-done | bytes 163872 | tf_op jit(solution)/shard_map/ppermute | solution.py:263
  94.5 5.1 %collective-permute-start.10 = (bf16[4,64,640]{2,1,0:T(8,128)(2,1)S(1)}, bf16[4,64,640]{2,1,0:T(8,128)(2,1)S(1)}, u32[]{:S(2)}, u32[]{:S(2)}) collective-permute-start(bf16[4,64,640]{2,1,0:T(8,128)(2,1)S(1)} %pad_maximum_fusion.1.here_ref), channel_id=1, source_target_pairs={{0,256},{256,512},{512,768},{768,0},{1,257},{257,513},{513,769},{7... | collective-permute-start | bytes 983048 | tf_op jit(solution)/shard_map/ppermute | solution.py:259
  101.7 3.9 %collective-permute-start.13 = (bf16[4,64,640]{2,1,0:T(8,128)(2,1)S(1)}, bf16[4,64,640]{2,1,0:T(8,128)(2,1)S(1)}, u32[]{:S(2)}, u32[]{:S(2)}) collective-permute-start(bf16[4,64,640]{2,1,0:T(8,128)(2,1)S(1)} %slice.35), channel_id=1, source_target_pairs={{0,768},{256,0},{512,256},{768,512},{1,769},{257,1},{513,257},{769... | collective-permute-start | bytes 983048 | tf_op jit(solution)/shard_map/ppermute | solution.py:263
  106.8 3.5 %collective-permute-done.12.half_ref = bf16[4,64,640]{2,1,0:T(8,128)(2,1)S(1)} collective-permute-done((bf16[4,64,640]{2,1,0:T(8,128)(2,1)S(1)}, bf16[4,64,640]{2,1,0:T(8,128)(2,1)S(1)}, u32[]{:S(2)}, u32[]{:S(2)}) %collective-permute-start.12) | collective-permute-done | bytes 327712 | tf_op jit(solution)/shard_map/ppermute | solution.py:263
  114.3 3.4 %collective-permute-start.14 = (bf16[2,64,640]{2,1,0:T(8,128)(2,1)S(1)}, bf16[2,64,640]{2,1,0:T(8,128)(2,1)S(1)}, u32[]{:S(2)}, u32[]{:S(2)}) collective-permute-start(bf16[2,64,640]{2,1,0:T(8,128)(2,1)S(1)} %slice.30), channel_id=1, source_target_pairs={{0,256},{256,512},{512,768},{768,0},{1,257},{257,513},{513,769},{7... | collective-permute-start | bytes 491528 | tf_op jit(solution)/shard_map/ppermute | solution.py:263
  117.7 2.4 %collective-permute-start.15 = (bf16[2,64,640]{2,1,0:T(8,128)(2,1)S(1)}, bf16[2,64,640]{2,1,0:T(8,128)(2,1)S(1)}, u32[]{:S(2)}, u32[]{:S(2)}) collective-permute-start(bf16[2,64,640]{2,1,0:T(8,128)(2,1)S(1)} %slice.31), channel_id=1, source_target_pairs={{0,768},{256,0},{512,256},{768,512},{1,769},{257,1},{513,257},{769... | collective-permute-start | bytes 491528 | tf_op jit(solution)/shard_map/ppermute | solution.py:263
  120.4 2.1 collective-permute-start.16
  122.8 4.4 %collective-permute-done.15.rest_ref = bf16[2,64,640]{2,1,0:T(8,128)(2,1)S(1)} collective-permute-done((bf16[2,64,640]{2,1,0:T(8,128)(2,1)S(1)}, bf16[2,64,640]{2,1,0:T(8,128)(2,1)S(1)}, u32[]{:S(2)}, u32[]{:S(2)}) %collective-permute-start.15) | collective-permute-done | bytes 163872 | tf_op jit(solution)/shard_map/ppermute | solution.py:263
  127.4 1.9 collective-permute-start.18
  130.3 1.9 collective-permute-done.18.refs_10_
  132.3 2.7 %section.16 = (bf16[16,2048]{1,0:T(8,128)(2,1)S(1)}, bf16[4,16,256]{2,1,0:T(8,128)(2,1)S(1)}, bf16[4,16,128]{2,1,0:T(8,128)(2,1)S(1)}) custom-call(s32[4]{0:T(128)S(1)} %copy-done.2, bf16[16,2048]{1,0:T(8,128)(2,1)S(1)} %get-tuple-element.51.x_ref, f32[32,32]{1,0:T(8,128)S(1)} %get-tuple-element.40.allowed_ref, ...), custom_call_target="tpu_custom_call", output_to_operand_aliasing={{0}: (3, {})} | custom-call | tf_op jit(solution)/shard_map/section/pallas_call | solution.py:177
  136.4 2.7 %section.17.held_ref = bf16[16,2048]{1,0:T(8,128)(2,1)S(1)} custom-call(s32[4]{0:T(128)S(1)} %copy-done.2, bf16[16,2048]{1,0:T(8,128)(2,1)S(1)} %get-tuple-element.39.x_ref, f32[32,32]{1,0:T(8,128)S(1)} %get-tuple-element.40.allowed_ref, bf16[16,2048]{1,0:T(8,128)(2,1)S(1)} %broadcast_in_dim.121.held_ref, ...), custom_call_target="tpu_custom_call", output_to_operand_aliasing={{}: (3, {})} | custom-call | tf_op jit(solution)/shard_map/section/pallas_call | solution.py:177
  157.7 50.4 %all_to_all.11.received_ref = bf16[8,8,2048]{2,1,0:T(8,128)(2,1)S(1)} all-to-all(bf16[8,8,2048]{2,1,0:T(8,128)(2,1)S(1)} %section.31), channel_id=1, replica_groups={{0,1,2,3,28,29,30,31},{4,5,6,7,24,25,26,27},{8,9,10,11,20,21,22,23},{12..., dimensions={0} | all-to-all | bytes 524288 | tf_op jit(solution)/shard_map/all_to_all | solution.py:368
  (93 shorter events, 40.5 us)
Async XLA Ops:
  46.1 12.9 %collective-permute-start.1 = (bf16[4,64,640]{2,1,0:T(8,128)(2,1)S(1)}, bf16[4,64,640]{2,1,0:T(8,128)(2,1)S(1)}, u32[]{:S(2)}, u32[]{:S(2)}) collective-permute-start(bf16[4,64,640]{2,1,0:T(8,128)(2,1)S(1)} %all_to_all.10.here_ref), channel_id=1, source_target_pairs={{0,195},{1,0},{2,1},{3,2},{64,3},{65,64},{66,65},{67,66},{128,67},... | collective-permute-start | bytes 983048 | tf_op jit(solution)/shard_map/ppermute | solution.py:276
  50.0 11.0 %collective-permute-start = (bf16[4,64,640]{2,1,0:T(8,128)(2,1)S(1)}, bf16[4,64,640]{2,1,0:T(8,128)(2,1)S(1)}, u32[]{:S(2)}, u32[]{:S(2)}) collective-permute-start(bf16[4,64,640]{2,1,0:T(8,128)(2,1)S(1)} %all_to_all.10.here_ref), channel_id=1, source_target_pairs={{0,1},{1,2},{2,3},{3,64},{64,65},{65,66},{66,67},{67,128},{128,129... | collective-permute-start | bytes 983048 | tf_op jit(solution)/shard_map/ppermute | solution.py:276
  52.0 11.0 %collective-permute-start.3 = (bf16[4,64,640]{2,1,0:T(8,128)(2,1)S(1)}, bf16[4,64,640]{2,1,0:T(8,128)(2,1)S(1)}, u32[]{:S(2)}, u32[]{:S(2)}) collective-permute-start(bf16[4,64,640]{2,1,0:T(8,128)(2,1)S(1)} %all_to_all.10.here_ref), channel_id=1, source_target_pairs={{0,768},{256,0},{512,256},{768,512},{1,769},{257,1},{513,257},{769... | collective-permute-start | bytes 983048 | tf_op jit(solution)/shard_map/ppermute | solution.py:259
  54.7 9.5 %collective-permute-start.2 = (bf16[4,64,640]{2,1,0:T(8,128)(2,1)S(1)}, bf16[4,64,640]{2,1,0:T(8,128)(2,1)S(1)}, u32[]{:S(2)}, u32[]{:S(2)}) collective-permute-start(bf16[4,64,640]{2,1,0:T(8,128)(2,1)S(1)} %all_to_all.10.here_ref), channel_id=1, source_target_pairs={{0,256},{256,512},{512,768},{768,0},{1,257},{257,513},{513,769},{7... | collective-permute-start | bytes 983048 | tf_op jit(solution)/shard_map/ppermute | solution.py:259
  64.2 35.4 %collective-permute-start.9 = (bf16[8,64,640]{2,1,0:T(8,128)(2,1)S(1)}, bf16[8,64,640]{2,1,0:T(8,128)(2,1)S(1)}, u32[]{:S(2)}, u32[]{:S(2)}) collective-permute-start(bf16[8,64,640]{2,1,0:T(8,128)(2,1)S(1)} %pad_maximum_fusion.here_ref), channel_id=1, source_target_pairs={{0,256},{256,512},{512,768},{768,0},{1,257},{257,513},{513,769},{7... | collective-permute-start | bytes 1966088 | tf_op jit(solution)/shard_map/ppermute | solution.py:259
  69.8 31.9 %collective-permute-start.8 = (bf16[8,64,640]{2,1,0:T(8,128)(2,1)S(1)}, bf16[8,64,640]{2,1,0:T(8,128)(2,1)S(1)}, u32[]{:S(2)}, u32[]{:S(2)}) collective-permute-start(bf16[8,64,640]{2,1,0:T(8,128)(2,1)S(1)} %pad_maximum_fusion.here_ref), channel_id=1, source_target_pairs={{0,768},{256,0},{512,256},{768,512},{1,769},{257,1},{513,257},{769... | collective-permute-start | bytes 1966088 | tf_op jit(solution)/shard_map/ppermute | solution.py:259
  71.7 12.5 %collective-permute-start.5 = (bf16[2,64,640]{2,1,0:T(8,128)(2,1)S(1)}, bf16[2,64,640]{2,1,0:T(8,128)(2,1)S(1)}, u32[]{:S(2)}, u32[]{:S(2)}) collective-permute-start(bf16[2,64,640]{2,1,0:T(8,128)(2,1)S(1)} %slice.33), channel_id=1, source_target_pairs={{0,195},{1,0},{2,1},{3,2},{64,3},{65,64},{66,65},{67,66},{128,67},... | collective-permute-start | bytes 491528 | tf_op jit(solution)/shard_map/ppermute | solution.py:276
  76.6 9.5 %collective-permute-start.4 = (bf16[2,64,640]{2,1,0:T(8,128)(2,1)S(1)}, bf16[2,64,640]{2,1,0:T(8,128)(2,1)S(1)}, u32[]{:S(2)}, u32[]{:S(2)}) collective-permute-start(bf16[2,64,640]{2,1,0:T(8,128)(2,1)S(1)} %slice.32), channel_id=1, source_target_pairs={{0,1},{1,2},{2,3},{3,64},{64,65},{65,66},{66,67},{67,128},{128,129... | collective-permute-start | bytes 491528 | tf_op jit(solution)/shard_map/ppermute | solution.py:276
  79.0 8.0 %collective-permute-start.6 = (bf16[2,64,640]{2,1,0:T(8,128)(2,1)S(1)}, bf16[2,64,640]{2,1,0:T(8,128)(2,1)S(1)}, u32[]{:S(2)}, u32[]{:S(2)}) collective-permute-start(bf16[2,64,640]{2,1,0:T(8,128)(2,1)S(1)} %slice.26), channel_id=1, source_target_pairs={{0,256},{256,512},{512,768},{768,0},{1,257},{257,513},{513,769},{7... | collective-permute-start | bytes 491528 | tf_op jit(solution)/shard_map/ppermute | solution.py:263
  84.2 8.4 %collective-permute-start.7 = (bf16[2,64,640]{2,1,0:T(8,128)(2,1)S(1)}, bf16[2,64,640]{2,1,0:T(8,128)(2,1)S(1)}, u32[]{:S(2)}, u32[]{:S(2)}) collective-permute-start(bf16[2,64,640]{2,1,0:T(8,128)(2,1)S(1)} %slice.27), channel_id=1, source_target_pairs={{0,768},{256,0},{512,256},{768,512},{1,769},{257,1},{513,257},{769... | collective-permute-start | bytes 491528 | tf_op jit(solution)/shard_map/ppermute | solution.py:263
  92.6 13.0 %collective-permute-start.11 = (bf16[4,64,640]{2,1,0:T(8,128)(2,1)S(1)}, bf16[4,64,640]{2,1,0:T(8,128)(2,1)S(1)}, u32[]{:S(2)}, u32[]{:S(2)}) collective-permute-start(bf16[4,64,640]{2,1,0:T(8,128)(2,1)S(1)} %pad_maximum_fusion.1.here_ref), channel_id=1, source_target_pairs={{0,768},{256,0},{512,256},{768,512},{1,769},{257,1},{513,257},{769... | collective-permute-start | bytes 983048 | tf_op jit(solution)/shard_map/ppermute | solution.py:259
  94.5 12.3 %collective-permute-start.10 = (bf16[4,64,640]{2,1,0:T(8,128)(2,1)S(1)}, bf16[4,64,640]{2,1,0:T(8,128)(2,1)S(1)}, u32[]{:S(2)}, u32[]{:S(2)}) collective-permute-start(bf16[4,64,640]{2,1,0:T(8,128)(2,1)S(1)} %pad_maximum_fusion.1.here_ref), channel_id=1, source_target_pairs={{0,256},{256,512},{512,768},{768,0},{1,257},{257,513},{513,769},{7... | collective-permute-start | bytes 983048 | tf_op jit(solution)/shard_map/ppermute | solution.py:259
  99.7 10.6 %collective-permute-start.12 = (bf16[4,64,640]{2,1,0:T(8,128)(2,1)S(1)}, bf16[4,64,640]{2,1,0:T(8,128)(2,1)S(1)}, u32[]{:S(2)}, u32[]{:S(2)}) collective-permute-start(bf16[4,64,640]{2,1,0:T(8,128)(2,1)S(1)} %slice.34), channel_id=1, source_target_pairs={{0,256},{256,512},{512,768},{768,0},{1,257},{257,513},{513,769},{7... | collective-permute-start | bytes 983048 | tf_op jit(solution)/shard_map/ppermute | solution.py:263
  101.7 10.2 %collective-permute-start.13 = (bf16[4,64,640]{2,1,0:T(8,128)(2,1)S(1)}, bf16[4,64,640]{2,1,0:T(8,128)(2,1)S(1)}, u32[]{:S(2)}, u32[]{:S(2)}) collective-permute-start(bf16[4,64,640]{2,1,0:T(8,128)(2,1)S(1)} %slice.35), channel_id=1, source_target_pairs={{0,768},{256,0},{512,256},{768,512},{1,769},{257,1},{513,257},{769... | collective-permute-start | bytes 983048 | tf_op jit(solution)/shard_map/ppermute | solution.py:263
  112.3 20.0 %collective-permute-start.17 = (bf16[4,8,64,640]{3,2,1,0:T(8,128)(2,1)S(1)}, bf16[4,8,64,640]{3,2,1,0:T(8,128)(2,1)S(1)}, u32[]{:S(2)}, u32[]{:S(2)}) collective-permute-start(bf16[4,8,64,640]{3,2,1,0:T(8,128)(2,1)S(1)} %join.4.refs_6_), channel_id=1, source_target_pairs={{0,32},{32,0},{1,33},{33,1},{2,34},{34,2},{3,35},{35,3},{4,36},{36... | collective-permute-start | bytes 7864328 | tf_op jit(solution)/shard_map/ppermute | solution.py:296
  114.3 8.5 %collective-permute-start.14 = (bf16[2,64,640]{2,1,0:T(8,128)(2,1)S(1)}, bf16[2,64,640]{2,1,0:T(8,128)(2,1)S(1)}, u32[]{:S(2)}, u32[]{:S(2)}) collective-permute-start(bf16[2,64,640]{2,1,0:T(8,128)(2,1)S(1)} %slice.30), channel_id=1, source_target_pairs={{0,256},{256,512},{512,768},{768,0},{1,257},{257,513},{513,769},{7... | collective-permute-start | bytes 491528 | tf_op jit(solution)/shard_map/ppermute | solution.py:263
  117.7 9.4 %collective-permute-start.15 = (bf16[2,64,640]{2,1,0:T(8,128)(2,1)S(1)}, bf16[2,64,640]{2,1,0:T(8,128)(2,1)S(1)}, u32[]{:S(2)}, u32[]{:S(2)}) collective-permute-start(bf16[2,64,640]{2,1,0:T(8,128)(2,1)S(1)} %slice.31), channel_id=1, source_target_pairs={{0,768},{256,0},{512,256},{768,512},{1,769},{257,1},{513,257},{769... | collective-permute-start | bytes 491528 | tf_op jit(solution)/shard_map/ppermute | solution.py:263
  120.4 9.9 %collective-permute-start.16 = (bf16[4,4,64,640]{3,2,1,0:T(8,128)(2,1)S(1)}, bf16[4,4,64,640]{3,2,1,0:T(8,128)(2,1)S(1)}, u32[]{:S(2)}, u32[]{:S(2)}) collective-permute-start(bf16[4,4,64,640]{3,2,1,0:T(8,128)(2,1)S(1)} %join.3.refs_5_), channel_id=1, source_target_pairs={{0,32},{32,0},{1,33},{33,1},{2,34},{34,2},{3,35},{35,3},{4,36},{36... | collective-permute-start | bytes 3932168 | tf_op jit(solution)/shard_map/ppermute | solution.py:296
  127.4 4.9 %collective-permute-start.18 = (bf16[4,4,64,640]{3,2,1,0:T(8,128)(2,1)S(1)}, bf16[4,4,64,640]{3,2,1,0:T(8,128)(2,1)S(1)}, u32[]{:S(2)}, u32[]{:S(2)}) collective-permute-start(bf16[4,4,64,640]{3,2,1,0:T(8,128)(2,1)S(1)} %join.5.refs_7_), channel_id=1, source_target_pairs={{0,32},{32,0},{1,33},{33,1},{2,34},{34,2},{3,35},{35,3},{4,36},{36... | collective-permute-start | bytes 3932168 | tf_op jit(solution)/shard_map/ppermute | solution.py:296
  135.0 5.4 %collective-permute-start.20 = (bf16[16,2048]{1,0:T(8,128)(2,1)S(1)}, bf16[16,2048]{1,0:T(8,128)(2,1)S(1)}, u32[]{:S(2)}, u32[]{:S(2)}) collective-permute-start(bf16[16,2048]{1,0:T(8,128)(2,1)S(1)} %get-tuple-element.54.held_ref), channel_id=1, source_target_pairs={{0,4},{1,5},{2,6},{3,7},{32,36},{33,37},{34,38},{35,39},{64,68},{6... | collective-permute-start | bytes 196616 | tf_op jit(solution)/shard_map/ppermute | solution.py:406
  139.1 3.2 %collective-permute-start.19 = (bf16[16,2048]{1,0:T(8,128)(2,1)S(1)}, bf16[16,2048]{1,0:T(8,128)(2,1)S(1)}, u32[]{:S(2)}, u32[]{:S(2)}) collective-permute-start(bf16[16,2048]{1,0:T(8,128)(2,1)S(1)} %section.17.held_ref), channel_id=1, source_target_pairs={{0,4},{1,5},{2,6},{3,7},{32,36},{33,37},{34,38},{35,39},{64,68},{6... | collective-permute-start | bytes 196616 | tf_op jit(solution)/shard_map/ppermute | solution.py:406
  141.0 2.5 %collective-permute-start.22 = (bf16[16,2048]{1,0:T(8,128)(2,1)S(1)}, bf16[16,2048]{1,0:T(8,128)(2,1)S(1)}, u32[]{:S(2)}, u32[]{:S(2)}) collective-permute-start(bf16[16,2048]{1,0:T(8,128)(2,1)S(1)} %get-tuple-element.57.held_ref), channel_id=1, source_target_pairs={{4,8},{5,9},{6,10},{7,11},{36,40},{37,41},{38,42},{39,43},{68,72},... | collective-permute-start | bytes 196616 | tf_op jit(solution)/shard_map/ppermute | solution.py:406
  142.9 2.1 %collective-permute-start.21 = (bf16[16,2048]{1,0:T(8,128)(2,1)S(1)}, bf16[16,2048]{1,0:T(8,128)(2,1)S(1)}, u32[]{:S(2)}, u32[]{:S(2)}) collective-permute-start(bf16[16,2048]{1,0:T(8,128)(2,1)S(1)} %section.19.held_ref), channel_id=1, source_target_pairs={{4,8},{5,9},{6,10},{7,11},{36,40},{37,41},{38,42},{39,43},{68,72},... | collective-permute-start | bytes 196616 | tf_op jit(solution)/shard_map/ppermute | solution.py:406
  151.9 2.2 %collective-permute-start.30 = (bf16[16,2048]{1,0:T(8,128)(2,1)S(1)}, bf16[16,2048]{1,0:T(8,128)(2,1)S(1)}, u32[]{:S(2)}, u32[]{:S(2)}) collective-permute-start(bf16[16,2048]{1,0:T(8,128)(2,1)S(1)} %get-tuple-element.69.held_ref), channel_id=1, source_target_pairs={{20,24},{21,25},{22,26},{23,27},{52,56},{53,57},{54,58},{55,59},{8... | collective-permute-start | bytes 196616 | tf_op jit(solution)/shard_map/ppermute | solution.py:406
  (14 other events, 61.4 us)

commit v9 on v8

--- a/solution.py
+++ b/solution.py
@@ -100,7 +100,7 @@
 
 
 def section_kernel(step, half, last, where, x_ref, allowed_ref, held_ref, *refs):
-    rope, weights, refs = refs[:5], (refs[5:8], refs[8:11]), refs[11:]
+    rope, weights, refs = refs[:5], (refs[5:7], refs[7:9]), refs[9:]
     first = half * HALF
     if half == 0:
         out_ref, keys_ref, values_ref = refs
@@ -111,7 +111,7 @@
     out_rows = pl.ds(first if last and half else 0, HALF)
 
     def rows_of(i, zh, t, columns):
-        part, start = ((0, 0), (1, ZH), (2, 0), (1, 0))[t]
+        part, start = ((0, 0), (0, 2 * ZH), (1, 0), (0, ZH))[t]
         return jnp.concatenate(
             [weights[i][part][x, start + zh, :, columns] for x in range(X)], axis=0
         )
@@ -177,7 +177,7 @@
     return pl.pallas_call(
         functools.partial(section_kernel, step, half, last),
         out_shape=shapes,
-        in_specs=[pl.BlockSpec(memory_space=pltpu.SMEM)] + [vmem] * (14 + len(more)),
+        in_specs=[pl.BlockSpec(memory_space=pltpu.SMEM)] + [vmem] * (12 + len(more)),
         out_specs=[vmem] * len(shapes),
         scratch_shapes=[pltpu.VMEM((SEQ, D), F32)] if split else [],
         input_output_aliases={} if split else {3: 0},
@@ -278,21 +278,13 @@
     here = lax.all_to_all(shards, "z_hi", 0, 0)
     half = ZH // 2
     ahead, behind = along_z(here, 1), along_z(here, -1)
-    here_x = first_along_x(here)
-    near, *here_x = lax.optimization_barrier((jnp.concatenate([ahead, behind]), *here_x))
+    near = jnp.concatenate([here, ahead, behind])
     near_x = first_along_x(near)
     across = jnp.concatenate([along_z(ahead[:half], 1), along_z(behind[half:], -1)])
-    here_rest = rest_along_x(*here_x)
-    across, *here_rest = lax.optimization_barrier((across, *here_rest))
     across_x = first_along_x(across)
-    near_rest = rest_along_x(*near_x)
-    *across_x, near_0, near_1 = lax.optimization_barrier((*across_x, *near_rest))
-    across_rest = rest_along_x(*across_x)
-    own = [
-        join(here, *here_x, *here_rest),
-        join(near, *near_x, near_0, near_1),
-        join(across, *across_x, *across_rest),
-    ]
+    rest = rest_along_x(*near_x) + rest_along_x(*across_x)
+    rest = lax.optimization_barrier(rest)
+    own = [join(near, *near_x, *rest[:2]), join(across, *across_x, *rest[2:])]
     return own + [lax.ppermute(part, "core", [(0, 1), (1, 0)]) for part in own]
 
 

time: 211 us -> 197 us (0.934)
  starting transfers between devices: 69.8 us -> 54.9 us
  waiting for transfers between devices: 25.1 us -> 29.6 us
  blocking collectives: 92.8 us -> 89.5 us
    ppermute x4, waiting for transfers between devices: 1.99 us -> 12 us  [along_z(): lax.ppermute(parts, ('z_hi', 'tensor'), [(z, (z + by) % Z) for z in range...]
    ppermute x6 -> x4, starting transfers between devices: 21.5 us -> 12.9 us  [first_along_x(): return (lax.ppermute(parts, 'x', one), lax.ppermute(parts, 'x', other))]
    ppermute x3 -> x2, waiting for transfers between devices: 11.5 us -> 4.49 us  [rest_along_x(): lax.ppermute(after[half:], 'x', other)]
    ppermute x3 -> x2, waiting for transfers between devices: 4.63 us -> 0.01 us  [rest_along_x(): lax.ppermute(before[:half], 'x', one)]
    ppermute x3 -> x2, starting transfers between devices: 8.25 us -> 4.55 us  [rest_along_x(): lax.ppermute(after[half:], 'x', other)]
    all_to_all x1, blocking collectives: 50.4 us -> 47.1 us  [exchange(): lax.all_to_all(chunks, ('pipe', 'tensor'), 0, 0, axis_index_groups=groups)]
    ppermute x6 -> x4, waiting for transfers between devices: 4.32 us -> 7.48 us  [first_along_x(): return (lax.ppermute(parts, 'x', one), lax.ppermute(parts, 'x', other))]
    ppermute x3 -> x2, waiting for transfers between devices: 1.95 us -> 4.95 us  [gather_section(): return own + [lax.ppermute(part, 'core', [(0, 1), (1, 0)]) for part in own]]
  transfers between devices with their start and end apart: 33 -> 28, of which waited for: 12 -> 10; matrix products, arithmetic and copies ran while one was open for 0% -> 0% of each run, Pallas kernels for 6% -> 6%
where the time goes in v9:
time: 197 us; the launch traced here: 196 us
  blocking collectives  89.5 us (45%)
  starting transfers between devices  54.9 us (28%)
  waiting for transfers between devices  29.6 us (15%)
  Pallas kernels  19.3 us (10%)
    all_to_all x1, blocking collectives, exchange(): lax.all_to_all(chunks, ('pipe', 'tensor'), 0, 0, axis_index_groups=groups)  47.1 us
    all_to_all x1, blocking collectives, gather_section(): here = lax.all_to_all(shards, 'z_hi', 0, 0)  42.4 us
    ppermute x4, starting transfers between devices, along_z(): lax.ppermute(parts, ('z_hi', 'tensor'), [(z, (z + by) % Z) for z in range...  14.1 us
    pallas_call x16, Pallas kernels, run_section(): pl.pallas_call(functools.partial(section_kernel, step, half, last), out_s...  13.8 us
    ppermute x4, starting transfers between devices, first_along_x(): return (lax.ppermute(parts, 'x', one), lax.ppermute(parts, 'x', other))  12.9 us
    ppermute x4, waiting for transfers between devices, along_z(): lax.ppermute(parts, ('z_hi', 'tensor'), [(z, (z + by) % Z) for z in range...  12 us
    ppermute x14, starting transfers between devices, next_plane(): return lax.ppermute(part, 'pipe', [(step, step + 1)])  10.6 us
    ppermute x2, starting transfers between devices, rest_along_x(): lax.ppermute(before[:half], 'x', one)  8.39 us
  transfers between devices with their start and end apart: 28, of which 10 were waited for; matrix products, arithmetic and copies ran while one was open for 0% of the time, Pallas kernels for 6%

profile of v9, /device:TPU:6, one launch (start us, length us, event | category | flops | bytes accessed | tf_op | source)
XLA Modules:
  0.0 195.7 jit_solution(16015833707765702597)
XLA Ops:
  1.3 2.4 %shard.1 = bf16[4,64,640]{2,1,0:T(8,128)(2,1)} custom-call(s32[4]{0:T(128)} %pad_add_fusion.where, bf16[8,64,384]{2,1,0:T(8,128)(2,1)} %qkv_any.1, bf16[8,64,256]{2,1,0:T(8,128)(2,1)} %bitcast.5, bf16[8,64]{1,0:T(8,128)(2,1)} %gain_any.1), custom_call_target="tpu_custom_call" | custom-call | tf_op jit(solution)/shard_map/shard/pallas_call | solution.py:242
  3.7 42.4 %all_to_all.10 = bf16[4,64,640]{2,1,0:T(8,128)(2,1)S(1)} all-to-all(bf16[4,64,640]{2,1,0:T(8,128)(2,1)} %shard.1), channel_id=1, replica_groups=mesh['x'=4,'z_hi'=4,'core'=2,'pipe'=8,'tensor'=4] {'z_hi'}, dimensions={0} | all-to-all | bytes 655360 | tf_op jit(solution)/shard_map/all_to_all | solution.py:278
  46.2 3.7 %collective-permute-start = (bf16[4,64,640]{2,1,0:T(8,128)(2,1)S(1)}, bf16[4,64,640]{2,1,0:T(8,128)(2,1)S(1)}, u32[]{:S(2)}, u32[]{:S(2)}) collective-permute-start(bf16[4,64,640]{2,1,0:T(8,128)(2,1)S(1)} %all_to_all.10), channel_id=1, source_target_pairs={{0,1},{1,2},{2,3},{3,64},{64,65},{65,66},{66,67},{67,128},{128,129... | collective-permute-start | bytes 983048 | tf_op jit(solution)/shard_map/ppermute | solution.py:276
  49.8 3.4 %collective-permute-start.1 = (bf16[4,64,640]{2,1,0:T(8,128)(2,1)S(1)}, bf16[4,64,640]{2,1,0:T(8,128)(2,1)S(1)}, u32[]{:S(2)}, u32[]{:S(2)}) collective-permute-start(bf16[4,64,640]{2,1,0:T(8,128)(2,1)S(1)} %all_to_all.10), channel_id=1, source_target_pairs={{0,195},{1,0},{2,1},{3,2},{64,3},{65,64},{66,65},{67,66},{128,67},... | collective-permute-start | bytes 983048 | tf_op jit(solution)/shard_map/ppermute | solution.py:276
  53.3 3.2 %collective-permute-done = bf16[4,64,640]{2,1,0:T(8,128)(2,1)S(1)} collective-permute-done((bf16[4,64,640]{2,1,0:T(8,128)(2,1)S(1)}, bf16[4,64,640]{2,1,0:T(8,128)(2,1)S(1)}, u32[]{:S(2)}, u32[]{:S(2)}) %collective-permute-start) | collective-permute-done | bytes 327712 | tf_op jit(solution)/shard_map/ppermute | solution.py:276
  56.5 5.0 %collective-permute-done.1 = bf16[4,64,640]{2,1,0:T(8,128)(2,1)S(1)} collective-permute-done((bf16[4,64,640]{2,1,0:T(8,128)(2,1)S(1)}, bf16[4,64,640]{2,1,0:T(8,128)(2,1)S(1)}, u32[]{:S(2)}, u32[]{:S(2)}) %collective-permute-start.1) | collective-permute-done | bytes 327712 | tf_op jit(solution)/shard_map/ppermute | solution.py:276
  61.6 2.4 %collective-permute-start.3 = (bf16[12,64,640]{2,1,0:T(8,128)(2,1)S(1)}, bf16[12,64,640]{2,1,0:T(8,128)(2,1)S(1)}, u32[]{:S(2)}, u32[]{:S(2)}) collective-permute-start(bf16[12,64,640]{2,1,0:T(8,128)(2,1)S(1)} %constant_dynamic-update-slice_fusion.here_ref), channel_id=1, source_target_pairs={{0,256},{256,512},{512,768},{768,0},{1,257},{257,513},{513,769},{7... | collective-permute-start | bytes 2949128 | tf_op jit(solution)/shard_map/ppermute | solution.py:259
  64.0 3.5 %collective-permute-start.2 = (bf16[12,64,640]{2,1,0:T(8,128)(2,1)S(1)}, bf16[12,64,640]{2,1,0:T(8,128)(2,1)S(1)}, u32[]{:S(2)}, u32[]{:S(2)}) collective-permute-start(bf16[12,64,640]{2,1,0:T(8,128)(2,1)S(1)} %constant_dynamic-update-slice_fusion.here_ref), channel_id=1, source_target_pairs={{0,768},{256,0},{512,256},{768,512},{1,769},{257,1},{513,257},{769... | collective-permute-start | bytes 2949128 | tf_op jit(solution)/shard_map/ppermute | solution.py:259
  67.5 3.6 %collective-permute-start.6 = (bf16[2,64,640]{2,1,0:T(8,128)(2,1)S(1)}, bf16[2,64,640]{2,1,0:T(8,128)(2,1)S(1)}, u32[]{:S(2)}, u32[]{:S(2)}) collective-permute-start(bf16[2,64,640]{2,1,0:T(8,128)(2,1)S(1)} %slice.26), channel_id=1, source_target_pairs={{0,1},{1,2},{2,3},{3,64},{64,65},{65,66},{66,67},{67,128},{128,129... | collective-permute-start | bytes 491528 | tf_op jit(solution)/shard_map/ppermute | solution.py:276
  71.1 3.4 %collective-permute-start.7 = (bf16[2,64,640]{2,1,0:T(8,128)(2,1)S(1)}, bf16[2,64,640]{2,1,0:T(8,128)(2,1)S(1)}, u32[]{:S(2)}, u32[]{:S(2)}) collective-permute-start(bf16[2,64,640]{2,1,0:T(8,128)(2,1)S(1)} %slice.27), channel_id=1, source_target_pairs={{0,195},{1,0},{2,1},{3,2},{64,3},{65,64},{66,65},{67,66},{128,67},... | collective-permute-start | bytes 491528 | tf_op jit(solution)/shard_map/ppermute | solution.py:276
  75.9 2.4 %collective-permute-done.7 = bf16[2,64,640]{2,1,0:T(8,128)(2,1)S(1)} collective-permute-done((bf16[2,64,640]{2,1,0:T(8,128)(2,1)S(1)}, bf16[2,64,640]{2,1,0:T(8,128)(2,1)S(1)}, u32[]{:S(2)}, u32[]{:S(2)}) %collective-permute-start.7) | collective-permute-done | bytes 163872 | tf_op jit(solution)/shard_map/ppermute | solution.py:276
  78.4 2.7 %collective-permute-start.10 = (bf16[4,64,640]{2,1,0:T(8,128)(2,1)S(1)}, bf16[4,64,640]{2,1,0:T(8,128)(2,1)S(1)}, u32[]{:S(2)}, u32[]{:S(2)}) collective-permute-start(bf16[4,64,640]{2,1,0:T(8,128)(2,1)S(1)} %constant_dynamic-update-slice_fusion.3.here_ref), channel_id=1, source_target_pairs={{0,768},{256,0},{512,256},{768,512},{1,769},{257,1},{513,257},{769... | collective-permute-start | bytes 983048 | tf_op jit(solution)/shard_map/ppermute | solution.py:259
  81.1 4.3 %collective-permute-start.8 = (bf16[4,64,640]{2,1,0:T(8,128)(2,1)S(1)}, bf16[4,64,640]{2,1,0:T(8,128)(2,1)S(1)}, u32[]{:S(2)}, u32[]{:S(2)}) collective-permute-start(bf16[4,64,640]{2,1,0:T(8,128)(2,1)S(1)} %constant_dynamic-update-slice_fusion.3.here_ref), channel_id=1, source_target_pairs={{0,256},{256,512},{512,768},{768,0},{1,257},{257,513},{513,769},{7... | collective-permute-start | bytes 983048 | tf_op jit(solution)/shard_map/ppermute | solution.py:259
  85.4 2.7 %collective-permute-done.3.before_ref = bf16[12,64,640]{2,1,0:T(8,128)(2,1)S(1)} collective-permute-done((bf16[12,64,640]{2,1,0:T(8,128)(2,1)S(1)}, bf16[12,64,640]{2,1,0:T(8,128)(2,1)S(1)}, u32[]{:S(2)}, u32[]{:S(2)}) %collective-permute-start.3) | collective-permute-done | bytes 983072 | tf_op jit(solution)/shard_map/ppermute | solution.py:259
  88.2 3.5 %collective-permute-start.4 = (bf16[6,64,640]{2,1,0:T(8,128)(2,1)S(1)}, bf16[6,64,640]{2,1,0:T(8,128)(2,1)S(1)}, u32[]{:S(2)}, u32[]{:S(2)}) collective-permute-start(bf16[6,64,640]{2,1,0:T(8,128)(2,1)S(1)} %slice.24), channel_id=1, source_target_pairs={{0,256},{256,512},{512,768},{768,0},{1,257},{257,513},{513,769},{7... | collective-permute-start | bytes 1474568 | tf_op jit(solution)/shard_map/ppermute | solution.py:263
  91.8 2.3 %collective-permute-start.5 = (bf16[6,64,640]{2,1,0:T(8,128)(2,1)S(1)}, bf16[6,64,640]{2,1,0:T(8,128)(2,1)S(1)}, u32[]{:S(2)}, u32[]{:S(2)}) collective-permute-start(bf16[6,64,640]{2,1,0:T(8,128)(2,1)S(1)} %slice.25), channel_id=1, source_target_pairs={{0,768},{256,0},{512,256},{768,512},{1,769},{257,1},{513,257},{769... | collective-permute-start | bytes 1474568 | tf_op jit(solution)/shard_map/ppermute | solution.py:263
  94.1 4.7 %collective-permute-done.10.after_ref = bf16[4,64,640]{2,1,0:T(8,128)(2,1)S(1)} collective-permute-done((bf16[4,64,640]{2,1,0:T(8,128)(2,1)S(1)}, bf16[4,64,640]{2,1,0:T(8,128)(2,1)S(1)}, u32[]{:S(2)}, u32[]{:S(2)}) %collective-permute-start.10) | collective-permute-done | bytes 327712 | tf_op jit(solution)/shard_map/ppermute | solution.py:259
  101.2 4.9 %collective-permute-start.9 = (bf16[2,64,640]{2,1,0:T(8,128)(2,1)S(1)}, bf16[2,64,640]{2,1,0:T(8,128)(2,1)S(1)}, u32[]{:S(2)}, u32[]{:S(2)}) collective-permute-start(bf16[2,64,640]{2,1,0:T(8,128)(2,1)S(1)} %slice.28), channel_id=1, source_target_pairs={{0,256},{256,512},{512,768},{768,0},{1,257},{257,513},{513,769},{7... | collective-permute-start | bytes 491528 | tf_op jit(solution)/shard_map/ppermute | solution.py:263
  106.1 4.5 %collective-permute-done.11.rest_ref = bf16[2,64,640]{2,1,0:T(8,128)(2,1)S(1)} collective-permute-done((bf16[2,64,640]{2,1,0:T(8,128)(2,1)S(1)}, bf16[2,64,640]{2,1,0:T(8,128)(2,1)S(1)}, u32[]{:S(2)}, u32[]{:S(2)}) %collective-permute-start.11) | collective-permute-done | bytes 163872 | tf_op jit(solution)/shard_map/ppermute | solution.py:263
  113.4 2.4 %collective-permute-start.13 = (bf16[4,4,64,640]{3,2,1,0:T(8,128)(2,1)S(1)}, bf16[4,4,64,640]{3,2,1,0:T(8,128)(2,1)S(1)}, u32[]{:S(2)}, u32[]{:S(2)}) collective-permute-start(bf16[4,4,64,640]{3,2,1,0:T(8,128)(2,1)S(1)} %join.3.refs_6_), channel_id=1, source_target_pairs={{0,32},{32,0},{1,33},{33,1},{2,34},{34,2},{3,35},{35,3},{4,36},{36... | collective-permute-start | bytes 3932168 | tf_op jit(solution)/shard_map/ppermute | solution.py:288
  116.8 4.9 %collective-permute-done.13.refs_8_ = bf16[4,4,64,640]{3,2,1,0:T(8,128)(2,1)S(1)} collective-permute-done((bf16[4,4,64,640]{3,2,1,0:T(8,128)(2,1)S(1)}, bf16[4,4,64,640]{3,2,1,0:T(8,128)(2,1)S(1)}, u32[]{:S(2)}, u32[]{:S(2)}) %collective-permute-start.13) | collective-permute-done | bytes 1310752 | tf_op jit(solution)/shard_map/ppermute | solution.py:288
  121.8 2.7 %section.16 = (bf16[16,2048]{1,0:T(8,128)(2,1)S(1)}, bf16[4,16,256]{2,1,0:T(8,128)(2,1)S(1)}, bf16[4,16,128]{2,1,0:T(8,128)(2,1)S(1)}) custom-call(s32[4]{0:T(128)S(1)} %copy-done.2, bf16[16,2048]{1,0:T(8,128)(2,1)S(1)} %get-tuple-element.39.x_ref, f32[32,32]{1,0:T(8,128)S(1)} %get-tuple-element.34.allowed_ref, ...), custom_call_target="tpu_custom_call", output_to_operand_aliasing={{0}: (3, {})} | custom-call | tf_op jit(solution)/shard_map/section/pallas_call | solution.py:177
  125.9 2.7 %section.17.held_ref = bf16[16,2048]{1,0:T(8,128)(2,1)S(1)} custom-call(s32[4]{0:T(128)S(1)} %copy-done.2, bf16[16,2048]{1,0:T(8,128)(2,1)S(1)} %get-tuple-element.33.x_ref, f32[32,32]{1,0:T(8,128)S(1)} %get-tuple-element.34.allowed_ref, bf16[16,2048]{1,0:T(8,128)(2,1)S(1)} %broadcast_in_dim.121.held_ref, ...), custom_call_target="tpu_custom_call", output_to_operand_aliasing={{}: (3, {})} | custom-call | tf_op jit(solution)/shard_map/section/pallas_call | solution.py:177
  147.2 47.1 %all_to_all.11.received_ref = bf16[8,8,2048]{2,1,0:T(8,128)(2,1)S(1)} all-to-all(bf16[8,8,2048]{2,1,0:T(8,128)(2,1)S(1)} %section.31), channel_id=1, replica_groups={{0,1,2,3,28,29,30,31},{4,5,6,7,24,25,26,27},{8,9,10,11,20,21,22,23},{12..., dimensions={0} | all-to-all | bytes 524288 | tf_op jit(solution)/shard_map/all_to_all | solution.py:360
  (83 shorter events, 29.5 us)
Async XLA Ops:
  46.2 10.3 %collective-permute-start = (bf16[4,64,640]{2,1,0:T(8,128)(2,1)S(1)}, bf16[4,64,640]{2,1,0:T(8,128)(2,1)S(1)}, u32[]{:S(2)}, u32[]{:S(2)}) collective-permute-start(bf16[4,64,640]{2,1,0:T(8,128)(2,1)S(1)} %all_to_all.10), channel_id=1, source_target_pairs={{0,1},{1,2},{2,3},{3,64},{64,65},{65,66},{66,67},{67,128},{128,129... | collective-permute-start | bytes 983048 | tf_op jit(solution)/shard_map/ppermute | solution.py:276
  49.8 11.7 %collective-permute-start.1 = (bf16[4,64,640]{2,1,0:T(8,128)(2,1)S(1)}, bf16[4,64,640]{2,1,0:T(8,128)(2,1)S(1)}, u32[]{:S(2)}, u32[]{:S(2)}) collective-permute-start(bf16[4,64,640]{2,1,0:T(8,128)(2,1)S(1)} %all_to_all.10), channel_id=1, source_target_pairs={{0,195},{1,0},{2,1},{3,2},{64,3},{65,64},{66,65},{67,66},{128,67},... | collective-permute-start | bytes 983048 | tf_op jit(solution)/shard_map/ppermute | solution.py:276
  61.6 26.6 %collective-permute-start.3 = (bf16[12,64,640]{2,1,0:T(8,128)(2,1)S(1)}, bf16[12,64,640]{2,1,0:T(8,128)(2,1)S(1)}, u32[]{:S(2)}, u32[]{:S(2)}) collective-permute-start(bf16[12,64,640]{2,1,0:T(8,128)(2,1)S(1)} %constant_dynamic-update-slice_fusion.here_ref), channel_id=1, source_target_pairs={{0,256},{256,512},{512,768},{768,0},{1,257},{257,513},{513,769},{7... | collective-permute-start | bytes 2949128 | tf_op jit(solution)/shard_map/ppermute | solution.py:259
  64.0 27.8 %collective-permute-start.2 = (bf16[12,64,640]{2,1,0:T(8,128)(2,1)S(1)}, bf16[12,64,640]{2,1,0:T(8,128)(2,1)S(1)}, u32[]{:S(2)}, u32[]{:S(2)}) collective-permute-start(bf16[12,64,640]{2,1,0:T(8,128)(2,1)S(1)} %constant_dynamic-update-slice_fusion.here_ref), channel_id=1, source_target_pairs={{0,768},{256,0},{512,256},{768,512},{1,769},{257,1},{513,257},{769... | collective-permute-start | bytes 2949128 | tf_op jit(solution)/shard_map/ppermute | solution.py:259
  67.5 8.4 %collective-permute-start.6 = (bf16[2,64,640]{2,1,0:T(8,128)(2,1)S(1)}, bf16[2,64,640]{2,1,0:T(8,128)(2,1)S(1)}, u32[]{:S(2)}, u32[]{:S(2)}) collective-permute-start(bf16[2,64,640]{2,1,0:T(8,128)(2,1)S(1)} %slice.26), channel_id=1, source_target_pairs={{0,1},{1,2},{2,3},{3,64},{64,65},{65,66},{66,67},{67,128},{128,129... | collective-permute-start | bytes 491528 | tf_op jit(solution)/shard_map/ppermute | solution.py:276
  71.1 7.2 %collective-permute-start.7 = (bf16[2,64,640]{2,1,0:T(8,128)(2,1)S(1)}, bf16[2,64,640]{2,1,0:T(8,128)(2,1)S(1)}, u32[]{:S(2)}, u32[]{:S(2)}) collective-permute-start(bf16[2,64,640]{2,1,0:T(8,128)(2,1)S(1)} %slice.27), channel_id=1, source_target_pairs={{0,195},{1,0},{2,1},{3,2},{64,3},{65,64},{66,65},{67,66},{128,67},... | collective-permute-start | bytes 491528 | tf_op jit(solution)/shard_map/ppermute | solution.py:276
  78.4 20.4 %collective-permute-start.10 = (bf16[4,64,640]{2,1,0:T(8,128)(2,1)S(1)}, bf16[4,64,640]{2,1,0:T(8,128)(2,1)S(1)}, u32[]{:S(2)}, u32[]{:S(2)}) collective-permute-start(bf16[4,64,640]{2,1,0:T(8,128)(2,1)S(1)} %constant_dynamic-update-slice_fusion.3.here_ref), channel_id=1, source_target_pairs={{0,768},{256,0},{512,256},{768,512},{1,769},{257,1},{513,257},{769... | collective-permute-start | bytes 983048 | tf_op jit(solution)/shard_map/ppermute | solution.py:259
  81.1 19.9 %collective-permute-start.8 = (bf16[4,64,640]{2,1,0:T(8,128)(2,1)S(1)}, bf16[4,64,640]{2,1,0:T(8,128)(2,1)S(1)}, u32[]{:S(2)}, u32[]{:S(2)}) collective-permute-start(bf16[4,64,640]{2,1,0:T(8,128)(2,1)S(1)} %constant_dynamic-update-slice_fusion.3.here_ref), channel_id=1, source_target_pairs={{0,256},{256,512},{512,768},{768,0},{1,257},{257,513},{513,769},{7... | collective-permute-start | bytes 983048 | tf_op jit(solution)/shard_map/ppermute | solution.py:259
  88.2 22.4 %collective-permute-start.4 = (bf16[6,64,640]{2,1,0:T(8,128)(2,1)S(1)}, bf16[6,64,640]{2,1,0:T(8,128)(2,1)S(1)}, u32[]{:S(2)}, u32[]{:S(2)}) collective-permute-start(bf16[6,64,640]{2,1,0:T(8,128)(2,1)S(1)} %slice.24), channel_id=1, source_target_pairs={{0,256},{256,512},{512,768},{768,0},{1,257},{257,513},{513,769},{7... | collective-permute-start | bytes 1474568 | tf_op jit(solution)/shard_map/ppermute | solution.py:263
  91.8 18.8 %collective-permute-start.5 = (bf16[6,64,640]{2,1,0:T(8,128)(2,1)S(1)}, bf16[6,64,640]{2,1,0:T(8,128)(2,1)S(1)}, u32[]{:S(2)}, u32[]{:S(2)}) collective-permute-start(bf16[6,64,640]{2,1,0:T(8,128)(2,1)S(1)} %slice.25), channel_id=1, source_target_pairs={{0,768},{256,0},{512,256},{768,512},{1,769},{257,1},{513,257},{769... | collective-permute-start | bytes 1474568 | tf_op jit(solution)/shard_map/ppermute | solution.py:263
  98.8 11.8 %collective-permute-start.11 = (bf16[2,64,640]{2,1,0:T(8,128)(2,1)S(1)}, bf16[2,64,640]{2,1,0:T(8,128)(2,1)S(1)}, u32[]{:S(2)}, u32[]{:S(2)}) collective-permute-start(bf16[2,64,640]{2,1,0:T(8,128)(2,1)S(1)} %slice.29), channel_id=1, source_target_pairs={{0,768},{256,0},{512,256},{768,512},{1,769},{257,1},{513,257},{769... | collective-permute-start | bytes 491528 | tf_op jit(solution)/shard_map/ppermute | solution.py:263
  101.2 9.4 %collective-permute-start.9 = (bf16[2,64,640]{2,1,0:T(8,128)(2,1)S(1)}, bf16[2,64,640]{2,1,0:T(8,128)(2,1)S(1)}, u32[]{:S(2)}, u32[]{:S(2)}) collective-permute-start(bf16[2,64,640]{2,1,0:T(8,128)(2,1)S(1)} %slice.28), channel_id=1, source_target_pairs={{0,256},{256,512},{512,768},{768,0},{1,257},{257,513},{513,769},{7... | collective-permute-start | bytes 491528 | tf_op jit(solution)/shard_map/ppermute | solution.py:263
  111.2 10.6 %collective-permute-start.12 = (bf16[4,12,64,640]{3,2,1,0:T(8,128)(2,1)S(1)}, bf16[4,12,64,640]{3,2,1,0:T(8,128)(2,1)S(1)}, u32[]{:S(2)}, u32[]{:S(2)}) collective-permute-start(bf16[4,12,64,640]{3,2,1,0:T(8,128)(2,1)S(1)} %join.2.refs_5_), channel_id=1, source_target_pairs={{0,32},{32,0},{1,33},{33,1},{2,34},{34,2},{3,35},{35,3},{4,36},{36... | collective-permute-start | bytes 11796488 | tf_op jit(solution)/shard_map/ppermute | solution.py:288
  113.4 8.4 %collective-permute-start.13 = (bf16[4,4,64,640]{3,2,1,0:T(8,128)(2,1)S(1)}, bf16[4,4,64,640]{3,2,1,0:T(8,128)(2,1)S(1)}, u32[]{:S(2)}, u32[]{:S(2)}) collective-permute-start(bf16[4,4,64,640]{3,2,1,0:T(8,128)(2,1)S(1)} %join.3.refs_6_), channel_id=1, source_target_pairs={{0,32},{32,0},{1,33},{33,1},{2,34},{34,2},{3,35},{35,3},{4,36},{36... | collective-permute-start | bytes 3932168 | tf_op jit(solution)/shard_map/ppermute | solution.py:288
  124.5 5.4 %collective-permute-start.15 = (bf16[16,2048]{1,0:T(8,128)(2,1)S(1)}, bf16[16,2048]{1,0:T(8,128)(2,1)S(1)}, u32[]{:S(2)}, u32[]{:S(2)}) collective-permute-start(bf16[16,2048]{1,0:T(8,128)(2,1)S(1)} %get-tuple-element.42.held_ref), channel_id=1, source_target_pairs={{0,4},{1,5},{2,6},{3,7},{32,36},{33,37},{34,38},{35,39},{64,68},{6... | collective-permute-start | bytes 196616 | tf_op jit(solution)/shard_map/ppermute | solution.py:398
  128.6 3.2 %collective-permute-start.14 = (bf16[16,2048]{1,0:T(8,128)(2,1)S(1)}, bf16[16,2048]{1,0:T(8,128)(2,1)S(1)}, u32[]{:S(2)}, u32[]{:S(2)}) collective-permute-start(bf16[16,2048]{1,0:T(8,128)(2,1)S(1)} %section.17.held_ref), channel_id=1, source_target_pairs={{0,4},{1,5},{2,6},{3,7},{32,36},{33,37},{34,38},{35,39},{64,68},{6... | collective-permute-start | bytes 196616 | tf_op jit(solution)/shard_map/ppermute | solution.py:398
  130.5 2.5 %collective-permute-start.17 = (bf16[16,2048]{1,0:T(8,128)(2,1)S(1)}, bf16[16,2048]{1,0:T(8,128)(2,1)S(1)}, u32[]{:S(2)}, u32[]{:S(2)}) collective-permute-start(bf16[16,2048]{1,0:T(8,128)(2,1)S(1)} %get-tuple-element.45.held_ref), channel_id=1, source_target_pairs={{4,8},{5,9},{6,10},{7,11},{36,40},{37,41},{38,42},{39,43},{68,72},... | collective-permute-start | bytes 196616 | tf_op jit(solution)/shard_map/ppermute | solution.py:398
  132.3 2.1 %collective-permute-start.16 = (bf16[16,2048]{1,0:T(8,128)(2,1)S(1)}, bf16[16,2048]{1,0:T(8,128)(2,1)S(1)}, u32[]{:S(2)}, u32[]{:S(2)}) collective-permute-start(bf16[16,2048]{1,0:T(8,128)(2,1)S(1)} %section.19.held_ref), channel_id=1, source_target_pairs={{4,8},{5,9},{6,10},{7,11},{36,40},{37,41},{38,42},{39,43},{68,72},... | collective-permute-start | bytes 196616 | tf_op jit(solution)/shard_map/ppermute | solution.py:398
  133.8 1.9 collective-permute-start.19
  135.0 1.9 collective-permute-start.18
  136.3 1.9 collective-permute-start.21
  137.6 1.9 collective-permute-start.20
  140.1 1.9 collective-permute-start.22
  141.3 2.2 %collective-permute-start.25 = (bf16[16,2048]{1,0:T(8,128)(2,1)S(1)}, bf16[16,2048]{1,0:T(8,128)(2,1)S(1)}, u32[]{:S(2)}, u32[]{:S(2)}) collective-permute-start(bf16[16,2048]{1,0:T(8,128)(2,1)S(1)} %get-tuple-element.57.held_ref), channel_id=1, source_target_pairs={{20,24},{21,25},{22,26},{23,27},{52,56},{53,57},{54,58},{55,59},{8... | collective-permute-start | bytes 196616 | tf_op jit(solution)/shard_map/ppermute | solution.py:398
  (9 other events, 80.5 us)

commit v10 on v9

--- a/solution.py
+++ b/solution.py
@@ -29,6 +29,10 @@
 
 SMALL = pltpu.CompilerParams(vmem_limit_bytes=4 * 1024 * 1024)
 MEDIUM = pltpu.CompilerParams(vmem_limit_bytes=20 * 1024 * 1024)
+
+
+def device_place():
+    return [lax.axis_index(name) for name in ("pipe", "x", "core", "tensor")]
 
 
 def rotary_tables():
@@ -99,7 +103,8 @@
     return contexts, keys, values
 
 
-def section_kernel(step, half, last, where, x_ref, allowed_ref, held_ref, *refs):
+def section_kernel(step, half, last, x_ref, allowed_ref, held_ref, *refs):
+    where = device_place()
     rope, weights, refs = refs[:5], (refs[5:7], refs[7:9]), refs[9:]
     first = half * HALF
     if half == 0:
@@ -162,7 +167,7 @@
             chunks_ref[k] = out_ref[pl.ds(place, SEQ // GROUPS), :].astype(BF16)
 
 
-def run_section(step, half, last, where, values, allowed, held, rope, weights, *more):
+def run_section(step, half, last, values, allowed, held, rope, weights, *more):
     vmem = pl.BlockSpec(memory_space=pltpu.VMEM)
     part = jax.ShapeDtypeStruct((HALF, D), BF16)
     split = bool(last and half)
@@ -177,16 +182,17 @@
     return pl.pallas_call(
         functools.partial(section_kernel, step, half, last),
         out_shape=shapes,
-        in_specs=[pl.BlockSpec(memory_space=pltpu.SMEM)] + [vmem] * (12 + len(more)),
+        in_specs=[vmem] * (12 + len(more)),
         out_specs=[vmem] * len(shapes),
         scratch_shapes=[pltpu.VMEM((SEQ, D), F32)] if split else [],
-        input_output_aliases={} if split else {3: 0},
+        input_output_aliases={} if split else {2: 0},
         compiler_params=MEDIUM,
         name="section",
-    )(where, values, allowed, held, *rope, *weights, *more)
-
-
-def shard_kernel(where, qkv_any, out_any, gain_any, shard_ref, qkv_ref, out_ref, gain_ref, done):
+    )(values, allowed, held, *rope, *weights, *more)
+
+
+def shard_kernel(qkv_any, out_any, gain_any, shard_ref, qkv_ref, out_ref, gain_ref, done):
+    where = device_place()
     copies = [
         pltpu.make_async_copy(qkv_any.at[where[0]], qkv_ref, done.at[0]),
         pltpu.make_async_copy(out_any.at[where[0]], out_ref, done.at[1]),
@@ -235,14 +241,13 @@
             out_ref[x, i, :, pl.ds(QKV, CTX)] = turned_columns[x * 64 : (x + 1) * 64]
 
 
-def gather_section(where, w_qkv, w_out, norm_gain):
+def gather_section(w_qkv, w_out, norm_gain):
     rows = w_qkv.shape[1]
     vmem = pl.BlockSpec(memory_space=pltpu.VMEM)
-    smem = pl.BlockSpec(memory_space=pltpu.SMEM)
     shards = pl.pallas_call(
         shard_kernel,
         out_shape=jax.ShapeDtypeStruct((ZH, rows, QKV + CTX), BF16),
-        in_specs=[smem] + [pl.BlockSpec(memory_space=pl.ANY)] * 3,
+        in_specs=[pl.BlockSpec(memory_space=pl.ANY)] * 3,
         out_specs=vmem,
         scratch_shapes=[
             pltpu.VMEM((rows, QKV), BF16),
@@ -251,7 +256,7 @@
             pltpu.SemaphoreType.DMA((3,)),
         ],
         name="shard",
-    )(where, w_qkv, w_out.transpose(0, 2, 1), norm_gain)
+    )(w_qkv, w_out.transpose(0, 2, 1), norm_gain)
 
     one, other = [(x, (x + 1) % X) for x in range(X)], [(x, (x - 1) % X) for x in range(X)]
 
@@ -296,8 +301,9 @@
 
 
 def enter_kernel(
-    where, down_ref, up_ref, down_docs_ref, up_docs_ref, first_ref, second_ref, allowed_ref
+    down_ref, up_ref, down_docs_ref, up_docs_ref, first_ref, second_ref, allowed_ref
 ):
+    where = device_place()
     member = where[3]
     x_ref = jnp.where(member < 2, down_ref[member % 2], up_ref[member % 2]).astype(F32)
     docs = [docs_ref[...] for docs_ref in (down_docs_ref, up_docs_ref)]
@@ -327,7 +333,8 @@
             second_ref[:, columns] = part[HALF:].astype(BF16)
 
 
-def order_kernel(where, received_ref, down_ref, up_ref):
+def order_kernel(received_ref, down_ref, up_ref):
+    where = device_place()
     plane = where[0] // 4
     rows = received_ref.shape[1]
     parts = [received_ref[(plane if t < 2 else 1 - plane) * 4 + t] for t in range(4)]
@@ -350,7 +357,7 @@
                     out_ref[0, t % 2, :, columns] = tile[t * rows : (t + 1) * rows]
 
 
-def exchange(chunks, where):
+def exchange(chunks):
     planes, members = lax.axis_size("pipe"), lax.axis_size("tensor")
     rows = SEQ // members
     groups = [
@@ -363,35 +370,34 @@
     return pl.pallas_call(
         order_kernel,
         out_shape=[shape, shape],
-        in_specs=[pl.BlockSpec(memory_space=pltpu.SMEM), vmem],
+        in_specs=[vmem],
         out_specs=[vmem, vmem],
         compiler_params=SMALL,
         name="order",
-    )(where, received)
+    )(received)
 
 
 def on_device(down_in, up_in, w_qkv, w_out, norm_gain, down_docs, up_docs):
-    where = jnp.stack([lax.axis_index(name) for name in ("pipe", "x", "core", "tensor")])
     sections = lax.axis_size("pipe")
-    weights = gather_section(where, w_qkv, w_out, norm_gain)
+    weights = gather_section(w_qkv, w_out, norm_gain)
     rope = rotary_tables()
     vmem = pl.BlockSpec(memory_space=pltpu.VMEM)
     part = jax.ShapeDtypeStruct((HALF, D), BF16)
     *values, allowed = pl.pallas_call(
         enter_kernel,
         out_shape=[part, part, jax.ShapeDtypeStruct((SEQ, SEQ), F32)],
-        in_specs=[pl.BlockSpec(memory_space=pltpu.SMEM)] + [vmem] * 4,
+        in_specs=[vmem] * 4,
         out_specs=[vmem] * 3,
         compiler_params=SMALL,
         name="enter",
-    )(where, down_in, up_in, down_docs, up_docs)
+    )(down_in, up_in, down_docs, up_docs)
     held = [jnp.zeros((HALF, D), BF16)] * 2
     for step in range(sections):
         last = step + 1 == sections
 
         def run(half, *more):
             return run_section(
-                step, half, last, where, values[half], allowed, held[half], rope, weights, *more
+                step, half, last, values[half], allowed, held[half], rope, weights, *more
             )
 
         def next_plane(part):
@@ -399,7 +405,7 @@
 
         one, *state = run(0)
         if last:
-            return exchange(run(1, *state, one)[0], where)
+            return exchange(run(1, *state, one)[0])
         (two,) = run(1, *state)
         held = [one, two]
         values = [next_plane(one), next_plane(two)]

time: 197 us -> 190 us (0.964)
  Pallas kernels: 19.3 us -> 8.95 us
  blocking collectives: 89.5 us -> 92.4 us
    pallas_call x16, Pallas kernels: 13.8 us -> 5.14 us  [run_section(): pl.pallas_call(functools.partial(section_kernel, step, half, last), out_s...]
    all_to_all x1, blocking collectives: 47.1 us -> 50 us  [exchange(): lax.all_to_all(chunks, ('pipe', 'tensor'), 0, 0, axis_index_groups=groups)]
  transfers between devices with their start and end apart: 28 -> 28, of which waited for: 10 -> 10; matrix products, arithmetic and copies ran while one was open for 0% -> 0% of each run, Pallas kernels for 6% -> 2%
where the time goes in v10:
time: 190 us; the launch traced here: 189 us
  blocking collectives  92.4 us (49%)
  starting transfers between devices  54.9 us (29%)
  waiting for transfers between devices  30.7 us (16%)
  Pallas kernels  8.95 us (5%)
    all_to_all x1, blocking collectives, exchange(): lax.all_to_all(chunks, ('pipe', 'tensor'), 0, 0, axis_index_groups=groups)  50 us
    all_to_all x1, blocking collectives, gather_section(): here = lax.all_to_all(shards, 'z_hi', 0, 0)  42.4 us
    ppermute x4, starting transfers between devices, along_z(): lax.ppermute(parts, ('z_hi', 'tensor'), [(z, (z + by) % Z) for z in range...  14.1 us
    ppermute x4, starting transfers between devices, first_along_x(): return (lax.ppermute(parts, 'x', one), lax.ppermute(parts, 'x', other))  12.9 us
    ppermute x4, waiting for transfers between devices, along_z(): lax.ppermute(parts, ('z_hi', 'tensor'), [(z, (z + by) % Z) for z in range...  12 us
    ppermute x14, starting transfers between devices, next_plane(): return lax.ppermute(part, 'pipe', [(step, step + 1)])  10.6 us
    ppermute x2, starting transfers between devices, rest_along_x(): lax.ppermute(before[:half], 'x', one)  8.39 us
    ppermute x4, waiting for transfers between devices, first_along_x(): return (lax.ppermute(parts, 'x', one), lax.ppermute(parts, 'x', other))  7.48 us
  transfers between devices with their start and end apart: 28, of which 10 were waited for; matrix products, arithmetic and copies ran while one was open for 0% of the time, Pallas kernels for 2%

profile of v10, /device:TPU:6, one launch (start us, length us, event | category | flops | bytes accessed | tf_op | source)
XLA Modules:
  0.0 188.6 jit_solution(9934932893109363962)
XLA Ops:
  2.4 42.4 %all_to_all.10 = bf16[4,64,640]{2,1,0:T(8,128)(2,1)S(1)} all-to-all(bf16[4,64,640]{2,1,0:T(8,128)(2,1)} %shard.1), channel_id=1, replica_groups=mesh['x'=4,'z_hi'=4,'core'=2,'pipe'=8,'tensor'=4] {'z_hi'}, dimensions={0} | all-to-all | bytes 655360 | tf_op jit(solution)/shard_map/all_to_all | solution.py:283
  44.9 3.7 %collective-permute-start = (bf16[4,64,640]{2,1,0:T(8,128)(2,1)S(1)}, bf16[4,64,640]{2,1,0:T(8,128)(2,1)S(1)}, u32[]{:S(2)}, u32[]{:S(2)}) collective-permute-start(bf16[4,64,640]{2,1,0:T(8,128)(2,1)S(1)} %all_to_all.10), channel_id=1, source_target_pairs={{0,1},{1,2},{2,3},{3,64},{64,65},{65,66},{66,67},{67,128},{128,129... | collective-permute-start | bytes 983048 | tf_op jit(solution)/shard_map/ppermute | solution.py:281
  48.5 3.4 %collective-permute-start.1 = (bf16[4,64,640]{2,1,0:T(8,128)(2,1)S(1)}, bf16[4,64,640]{2,1,0:T(8,128)(2,1)S(1)}, u32[]{:S(2)}, u32[]{:S(2)}) collective-permute-start(bf16[4,64,640]{2,1,0:T(8,128)(2,1)S(1)} %all_to_all.10), channel_id=1, source_target_pairs={{0,195},{1,0},{2,1},{3,2},{64,3},{65,64},{66,65},{67,66},{128,67},... | collective-permute-start | bytes 983048 | tf_op jit(solution)/shard_map/ppermute | solution.py:281
  51.9 3.2 %collective-permute-done = bf16[4,64,640]{2,1,0:T(8,128)(2,1)S(1)} collective-permute-done((bf16[4,64,640]{2,1,0:T(8,128)(2,1)S(1)}, bf16[4,64,640]{2,1,0:T(8,128)(2,1)S(1)}, u32[]{:S(2)}, u32[]{:S(2)}) %collective-permute-start) | collective-permute-done | bytes 327712 | tf_op jit(solution)/shard_map/ppermute | solution.py:281
  55.2 5.0 %collective-permute-done.1 = bf16[4,64,640]{2,1,0:T(8,128)(2,1)S(1)} collective-permute-done((bf16[4,64,640]{2,1,0:T(8,128)(2,1)S(1)}, bf16[4,64,640]{2,1,0:T(8,128)(2,1)S(1)}, u32[]{:S(2)}, u32[]{:S(2)}) %collective-permute-start.1) | collective-permute-done | bytes 327712 | tf_op jit(solution)/shard_map/ppermute | solution.py:281
  60.3 2.4 %collective-permute-start.3 = (bf16[12,64,640]{2,1,0:T(8,128)(2,1)S(1)}, bf16[12,64,640]{2,1,0:T(8,128)(2,1)S(1)}, u32[]{:S(2)}, u32[]{:S(2)}) collective-permute-start(bf16[12,64,640]{2,1,0:T(8,128)(2,1)S(1)} %constant_dynamic-update-slice_fusion.here_ref), channel_id=1, source_target_pairs={{0,256},{256,512},{512,768},{768,0},{1,257},{257,513},{513,769},{7... | collective-permute-start | bytes 2949128 | tf_op jit(solution)/shard_map/ppermute | solution.py:264
  62.7 3.5 %collective-permute-start.2 = (bf16[12,64,640]{2,1,0:T(8,128)(2,1)S(1)}, bf16[12,64,640]{2,1,0:T(8,128)(2,1)S(1)}, u32[]{:S(2)}, u32[]{:S(2)}) collective-permute-start(bf16[12,64,640]{2,1,0:T(8,128)(2,1)S(1)} %constant_dynamic-update-slice_fusion.here_ref), channel_id=1, source_target_pairs={{0,768},{256,0},{512,256},{768,512},{1,769},{257,1},{513,257},{769... | collective-permute-start | bytes 2949128 | tf_op jit(solution)/shard_map/ppermute | solution.py:264
  66.1 3.6 %collective-permute-start.6 = (bf16[2,64,640]{2,1,0:T(8,128)(2,1)S(1)}, bf16[2,64,640]{2,1,0:T(8,128)(2,1)S(1)}, u32[]{:S(2)}, u32[]{:S(2)}) collective-permute-start(bf16[2,64,640]{2,1,0:T(8,128)(2,1)S(1)} %slice.26), channel_id=1, source_target_pairs={{0,1},{1,2},{2,3},{3,64},{64,65},{65,66},{66,67},{67,128},{128,129... | collective-permute-start | bytes 491528 | tf_op jit(solution)/shard_map/ppermute | solution.py:281
  69.8 3.4 %collective-permute-start.7 = (bf16[2,64,640]{2,1,0:T(8,128)(2,1)S(1)}, bf16[2,64,640]{2,1,0:T(8,128)(2,1)S(1)}, u32[]{:S(2)}, u32[]{:S(2)}) collective-permute-start(bf16[2,64,640]{2,1,0:T(8,128)(2,1)S(1)} %slice.27), channel_id=1, source_target_pairs={{0,195},{1,0},{2,1},{3,2},{64,3},{65,64},{66,65},{67,66},{128,67},... | collective-permute-start | bytes 491528 | tf_op jit(solution)/shard_map/ppermute | solution.py:281
  74.6 2.4 %collective-permute-done.7 = bf16[2,64,640]{2,1,0:T(8,128)(2,1)S(1)} collective-permute-done((bf16[2,64,640]{2,1,0:T(8,128)(2,1)S(1)}, bf16[2,64,640]{2,1,0:T(8,128)(2,1)S(1)}, u32[]{:S(2)}, u32[]{:S(2)}) %collective-permute-start.7) | collective-permute-done | bytes 163872 | tf_op jit(solution)/shard_map/ppermute | solution.py:281
  77.1 2.7 %collective-permute-start.10 = (bf16[4,64,640]{2,1,0:T(8,128)(2,1)S(1)}, bf16[4,64,640]{2,1,0:T(8,128)(2,1)S(1)}, u32[]{:S(2)}, u32[]{:S(2)}) collective-permute-start(bf16[4,64,640]{2,1,0:T(8,128)(2,1)S(1)} %constant_dynamic-update-slice_fusion.3.here_ref), channel_id=1, source_target_pairs={{0,768},{256,0},{512,256},{768,512},{1,769},{257,1},{513,257},{769... | collective-permute-start | bytes 983048 | tf_op jit(solution)/shard_map/ppermute | solution.py:264
  79.8 4.3 %collective-permute-start.8 = (bf16[4,64,640]{2,1,0:T(8,128)(2,1)S(1)}, bf16[4,64,640]{2,1,0:T(8,128)(2,1)S(1)}, u32[]{:S(2)}, u32[]{:S(2)}) collective-permute-start(bf16[4,64,640]{2,1,0:T(8,128)(2,1)S(1)} %constant_dynamic-update-slice_fusion.3.here_ref), channel_id=1, source_target_pairs={{0,256},{256,512},{512,768},{768,0},{1,257},{257,513},{513,769},{7... | collective-permute-start | bytes 983048 | tf_op jit(solution)/shard_map/ppermute | solution.py:264
  84.1 2.7 %collective-permute-done.3.before_ref = bf16[12,64,640]{2,1,0:T(8,128)(2,1)S(1)} collective-permute-done((bf16[12,64,640]{2,1,0:T(8,128)(2,1)S(1)}, bf16[12,64,640]{2,1,0:T(8,128)(2,1)S(1)}, u32[]{:S(2)}, u32[]{:S(2)}) %collective-permute-start.3) | collective-permute-done | bytes 983072 | tf_op jit(solution)/shard_map/ppermute | solution.py:264
  86.9 3.5 %collective-permute-start.4 = (bf16[6,64,640]{2,1,0:T(8,128)(2,1)S(1)}, bf16[6,64,640]{2,1,0:T(8,128)(2,1)S(1)}, u32[]{:S(2)}, u32[]{:S(2)}) collective-permute-start(bf16[6,64,640]{2,1,0:T(8,128)(2,1)S(1)} %slice.24), channel_id=1, source_target_pairs={{0,256},{256,512},{512,768},{768,0},{1,257},{257,513},{513,769},{7... | collective-permute-start | bytes 1474568 | tf_op jit(solution)/shard_map/ppermute | solution.py:268
  90.5 2.3 %collective-permute-start.5 = (bf16[6,64,640]{2,1,0:T(8,128)(2,1)S(1)}, bf16[6,64,640]{2,1,0:T(8,128)(2,1)S(1)}, u32[]{:S(2)}, u32[]{:S(2)}) collective-permute-start(bf16[6,64,640]{2,1,0:T(8,128)(2,1)S(1)} %slice.25), channel_id=1, source_target_pairs={{0,768},{256,0},{512,256},{768,512},{1,769},{257,1},{513,257},{769... | collective-permute-start | bytes 1474568 | tf_op jit(solution)/shard_map/ppermute | solution.py:268
  92.8 4.7 %collective-permute-done.10.after_ref = bf16[4,64,640]{2,1,0:T(8,128)(2,1)S(1)} collective-permute-done((bf16[4,64,640]{2,1,0:T(8,128)(2,1)S(1)}, bf16[4,64,640]{2,1,0:T(8,128)(2,1)S(1)}, u32[]{:S(2)}, u32[]{:S(2)}) %collective-permute-start.10) | collective-permute-done | bytes 327712 | tf_op jit(solution)/shard_map/ppermute | solution.py:264
  97.5 2.2 %collective-permute-start.11 = (bf16[2,64,640]{2,1,0:T(8,128)(2,1)S(1)}, bf16[2,64,640]{2,1,0:T(8,128)(2,1)S(1)}, u32[]{:S(2)}, u32[]{:S(2)}) collective-permute-start(bf16[2,64,640]{2,1,0:T(8,128)(2,1)S(1)} %slice.29), channel_id=1, source_target_pairs={{0,768},{256,0},{512,256},{768,512},{1,769},{257,1},{513,257},{769... | collective-permute-start | bytes 491528 | tf_op jit(solution)/shard_map/ppermute | solution.py:268
  99.8 4.9 %collective-permute-start.9 = (bf16[2,64,640]{2,1,0:T(8,128)(2,1)S(1)}, bf16[2,64,640]{2,1,0:T(8,128)(2,1)S(1)}, u32[]{:S(2)}, u32[]{:S(2)}) collective-permute-start(bf16[2,64,640]{2,1,0:T(8,128)(2,1)S(1)} %slice.28), channel_id=1, source_target_pairs={{0,256},{256,512},{512,768},{768,0},{1,257},{257,513},{513,769},{7... | collective-permute-start | bytes 491528 | tf_op jit(solution)/shard_map/ppermute | solution.py:268
  104.8 4.5 %collective-permute-done.11.rest_ref = bf16[2,64,640]{2,1,0:T(8,128)(2,1)S(1)} collective-permute-done((bf16[2,64,640]{2,1,0:T(8,128)(2,1)S(1)}, bf16[2,64,640]{2,1,0:T(8,128)(2,1)S(1)}, u32[]{:S(2)}, u32[]{:S(2)}) %collective-permute-start.11) | collective-permute-done | bytes 163872 | tf_op jit(solution)/shard_map/ppermute | solution.py:268
  112.1 2.4 %collective-permute-start.13 = (bf16[4,4,64,640]{3,2,1,0:T(8,128)(2,1)S(1)}, bf16[4,4,64,640]{3,2,1,0:T(8,128)(2,1)S(1)}, u32[]{:S(2)}, u32[]{:S(2)}) collective-permute-start(bf16[4,4,64,640]{3,2,1,0:T(8,128)(2,1)S(1)} %join.3.refs_6_), channel_id=1, source_target_pairs={{0,32},{32,0},{1,33},{33,1},{2,34},{34,2},{3,35},{35,3},{4,36},{36... | collective-permute-start | bytes 3932168 | tf_op jit(solution)/shard_map/ppermute | solution.py:293
  115.0 5.5 %collective-permute-done.13.refs_8_ = bf16[4,4,64,640]{3,2,1,0:T(8,128)(2,1)S(1)} collective-permute-done((bf16[4,4,64,640]{3,2,1,0:T(8,128)(2,1)S(1)}, bf16[4,4,64,640]{3,2,1,0:T(8,128)(2,1)S(1)}, u32[]{:S(2)}, u32[]{:S(2)}) %collective-permute-start.13) | collective-permute-done | bytes 1310752 | tf_op jit(solution)/shard_map/ppermute | solution.py:293
  120.5 2.2 %section.16 = (bf16[16,2048]{1,0:T(8,128)(2,1)S(1)}, bf16[4,16,256]{2,1,0:T(8,128)(2,1)S(1)}, bf16[4,16,128]{2,1,0:T(8,128)(2,1)S(1)}) custom-call(bf16[16,2048]{1,0:T(8,128)(2,1)S(1)} %get-tuple-element.39.x_ref, f32[32,32]{1,0:T(8,128)S(1)} %get-tuple-element.34.allowed_ref, ...), custom_call_target="tpu_custom_call", output_to_operand_aliasing={{0}: (2, {})} | custom-call | tf_op jit(solution)/shard_map/section/pallas_call | solution.py:182
  124.0 2.2 %section.17.held_ref = bf16[16,2048]{1,0:T(8,128)(2,1)S(1)} custom-call(bf16[16,2048]{1,0:T(8,128)(2,1)S(1)} %get-tuple-element.33.x_ref, f32[32,32]{1,0:T(8,128)S(1)} %get-tuple-element.34.allowed_ref, bf16[16,2048]{1,0:T(8,128)(2,1)S(1)} %broadcast_in_dim.121.held_ref, f32[32,128]{1,0:T(8,128)S(1)} %get-tuple-element.68.refs_0_, ...), custom_call_target="tpu_custom_call", output_to_operand_aliasing={{}: (2, {})} | custom-call | tf_op jit(solution)/shard_map/section/pallas_call | solution.py:182
  137.8 50.0 %all_to_all.11.received_ref = bf16[8,8,2048]{2,1,0:T(8,128)(2,1)S(1)} all-to-all(bf16[8,8,2048]{2,1,0:T(8,128)(2,1)S(1)} %section.31), channel_id=1, replica_groups={{0,1,2,3,28,29,30,31},{4,5,6,7,24,25,26,27},{8,9,10,11,20,21,22,23},{12..., dimensions={0} | all-to-all | bytes 524288 | tf_op jit(solution)/shard_map/all_to_all | solution.py:367
  (80 shorter events, 20.2 us)
Async XLA Ops:
  44.9 10.3 %collective-permute-start = (bf16[4,64,640]{2,1,0:T(8,128)(2,1)S(1)}, bf16[4,64,640]{2,1,0:T(8,128)(2,1)S(1)}, u32[]{:S(2)}, u32[]{:S(2)}) collective-permute-start(bf16[4,64,640]{2,1,0:T(8,128)(2,1)S(1)} %all_to_all.10), channel_id=1, source_target_pairs={{0,1},{1,2},{2,3},{3,64},{64,65},{65,66},{66,67},{67,128},{128,129... | collective-permute-start | bytes 983048 | tf_op jit(solution)/shard_map/ppermute | solution.py:281
  48.5 11.7 %collective-permute-start.1 = (bf16[4,64,640]{2,1,0:T(8,128)(2,1)S(1)}, bf16[4,64,640]{2,1,0:T(8,128)(2,1)S(1)}, u32[]{:S(2)}, u32[]{:S(2)}) collective-permute-start(bf16[4,64,640]{2,1,0:T(8,128)(2,1)S(1)} %all_to_all.10), channel_id=1, source_target_pairs={{0,195},{1,0},{2,1},{3,2},{64,3},{65,64},{66,65},{67,66},{128,67},... | collective-permute-start | bytes 983048 | tf_op jit(solution)/shard_map/ppermute | solution.py:281
  60.3 26.6 %collective-permute-start.3 = (bf16[12,64,640]{2,1,0:T(8,128)(2,1)S(1)}, bf16[12,64,640]{2,1,0:T(8,128)(2,1)S(1)}, u32[]{:S(2)}, u32[]{:S(2)}) collective-permute-start(bf16[12,64,640]{2,1,0:T(8,128)(2,1)S(1)} %constant_dynamic-update-slice_fusion.here_ref), channel_id=1, source_target_pairs={{0,256},{256,512},{512,768},{768,0},{1,257},{257,513},{513,769},{7... | collective-permute-start | bytes 2949128 | tf_op jit(solution)/shard_map/ppermute | solution.py:264
  62.7 27.8 %collective-permute-start.2 = (bf16[12,64,640]{2,1,0:T(8,128)(2,1)S(1)}, bf16[12,64,640]{2,1,0:T(8,128)(2,1)S(1)}, u32[]{:S(2)}, u32[]{:S(2)}) collective-permute-start(bf16[12,64,640]{2,1,0:T(8,128)(2,1)S(1)} %constant_dynamic-update-slice_fusion.here_ref), channel_id=1, source_target_pairs={{0,768},{256,0},{512,256},{768,512},{1,769},{257,1},{513,257},{769... | collective-permute-start | bytes 2949128 | tf_op jit(solution)/shard_map/ppermute | solution.py:264
  66.1 8.4 %collective-permute-start.6 = (bf16[2,64,640]{2,1,0:T(8,128)(2,1)S(1)}, bf16[2,64,640]{2,1,0:T(8,128)(2,1)S(1)}, u32[]{:S(2)}, u32[]{:S(2)}) collective-permute-start(bf16[2,64,640]{2,1,0:T(8,128)(2,1)S(1)} %slice.26), channel_id=1, source_target_pairs={{0,1},{1,2},{2,3},{3,64},{64,65},{65,66},{66,67},{67,128},{128,129... | collective-permute-start | bytes 491528 | tf_op jit(solution)/shard_map/ppermute | solution.py:281
  69.8 7.2 %collective-permute-start.7 = (bf16[2,64,640]{2,1,0:T(8,128)(2,1)S(1)}, bf16[2,64,640]{2,1,0:T(8,128)(2,1)S(1)}, u32[]{:S(2)}, u32[]{:S(2)}) collective-permute-start(bf16[2,64,640]{2,1,0:T(8,128)(2,1)S(1)} %slice.27), channel_id=1, source_target_pairs={{0,195},{1,0},{2,1},{3,2},{64,3},{65,64},{66,65},{67,66},{128,67},... | collective-permute-start | bytes 491528 | tf_op jit(solution)/shard_map/ppermute | solution.py:281
  77.1 20.4 %collective-permute-start.10 = (bf16[4,64,640]{2,1,0:T(8,128)(2,1)S(1)}, bf16[4,64,640]{2,1,0:T(8,128)(2,1)S(1)}, u32[]{:S(2)}, u32[]{:S(2)}) collective-permute-start(bf16[4,64,640]{2,1,0:T(8,128)(2,1)S(1)} %constant_dynamic-update-slice_fusion.3.here_ref), channel_id=1, source_target_pairs={{0,768},{256,0},{512,256},{768,512},{1,769},{257,1},{513,257},{769... | collective-permute-start | bytes 983048 | tf_op jit(solution)/shard_map/ppermute | solution.py:264
  79.8 19.9 %collective-permute-start.8 = (bf16[4,64,640]{2,1,0:T(8,128)(2,1)S(1)}, bf16[4,64,640]{2,1,0:T(8,128)(2,1)S(1)}, u32[]{:S(2)}, u32[]{:S(2)}) collective-permute-start(bf16[4,64,640]{2,1,0:T(8,128)(2,1)S(1)} %constant_dynamic-update-slice_fusion.3.here_ref), channel_id=1, source_target_pairs={{0,256},{256,512},{512,768},{768,0},{1,257},{257,513},{513,769},{7... | collective-permute-start | bytes 983048 | tf_op jit(solution)/shard_map/ppermute | solution.py:264
  86.9 22.4 %collective-permute-start.4 = (bf16[6,64,640]{2,1,0:T(8,128)(2,1)S(1)}, bf16[6,64,640]{2,1,0:T(8,128)(2,1)S(1)}, u32[]{:S(2)}, u32[]{:S(2)}) collective-permute-start(bf16[6,64,640]{2,1,0:T(8,128)(2,1)S(1)} %slice.24), channel_id=1, source_target_pairs={{0,256},{256,512},{512,768},{768,0},{1,257},{257,513},{513,769},{7... | collective-permute-start | bytes 1474568 | tf_op jit(solution)/shard_map/ppermute | solution.py:268
  90.5 18.8 %collective-permute-start.5 = (bf16[6,64,640]{2,1,0:T(8,128)(2,1)S(1)}, bf16[6,64,640]{2,1,0:T(8,128)(2,1)S(1)}, u32[]{:S(2)}, u32[]{:S(2)}) collective-permute-start(bf16[6,64,640]{2,1,0:T(8,128)(2,1)S(1)} %slice.25), channel_id=1, source_target_pairs={{0,768},{256,0},{512,256},{768,512},{1,769},{257,1},{513,257},{769... | collective-permute-start | bytes 1474568 | tf_op jit(solution)/shard_map/ppermute | solution.py:268
  97.5 11.8 %collective-permute-start.11 = (bf16[2,64,640]{2,1,0:T(8,128)(2,1)S(1)}, bf16[2,64,640]{2,1,0:T(8,128)(2,1)S(1)}, u32[]{:S(2)}, u32[]{:S(2)}) collective-permute-start(bf16[2,64,640]{2,1,0:T(8,128)(2,1)S(1)} %slice.29), channel_id=1, source_target_pairs={{0,768},{256,0},{512,256},{768,512},{1,769},{257,1},{513,257},{769... | collective-permute-start | bytes 491528 | tf_op jit(solution)/shard_map/ppermute | solution.py:268
  99.8 9.4 %collective-permute-start.9 = (bf16[2,64,640]{2,1,0:T(8,128)(2,1)S(1)}, bf16[2,64,640]{2,1,0:T(8,128)(2,1)S(1)}, u32[]{:S(2)}, u32[]{:S(2)}) collective-permute-start(bf16[2,64,640]{2,1,0:T(8,128)(2,1)S(1)} %slice.28), channel_id=1, source_target_pairs={{0,256},{256,512},{512,768},{768,0},{1,257},{257,513},{513,769},{7... | collective-permute-start | bytes 491528 | tf_op jit(solution)/shard_map/ppermute | solution.py:268
  109.9 10.6 %collective-permute-start.12 = (bf16[4,12,64,640]{3,2,1,0:T(8,128)(2,1)S(1)}, bf16[4,12,64,640]{3,2,1,0:T(8,128)(2,1)S(1)}, u32[]{:S(2)}, u32[]{:S(2)}) collective-permute-start(bf16[4,12,64,640]{3,2,1,0:T(8,128)(2,1)S(1)} %join.2.refs_5_), channel_id=1, source_target_pairs={{0,32},{32,0},{1,33},{33,1},{2,34},{34,2},{3,35},{35,3},{4,36},{36... | collective-permute-start | bytes 11796488 | tf_op jit(solution)/shard_map/ppermute | solution.py:293
  112.1 8.4 %collective-permute-start.13 = (bf16[4,4,64,640]{3,2,1,0:T(8,128)(2,1)S(1)}, bf16[4,4,64,640]{3,2,1,0:T(8,128)(2,1)S(1)}, u32[]{:S(2)}, u32[]{:S(2)}) collective-permute-start(bf16[4,4,64,640]{3,2,1,0:T(8,128)(2,1)S(1)} %join.3.refs_6_), channel_id=1, source_target_pairs={{0,32},{32,0},{1,33},{33,1},{2,34},{34,2},{3,35},{35,3},{4,36},{36... | collective-permute-start | bytes 3932168 | tf_op jit(solution)/shard_map/ppermute | solution.py:293
  122.6 4.8 %collective-permute-start.15 = (bf16[16,2048]{1,0:T(8,128)(2,1)S(1)}, bf16[16,2048]{1,0:T(8,128)(2,1)S(1)}, u32[]{:S(2)}, u32[]{:S(2)}) collective-permute-start(bf16[16,2048]{1,0:T(8,128)(2,1)S(1)} %get-tuple-element.42.held_ref), channel_id=1, source_target_pairs={{0,4},{1,5},{2,6},{3,7},{32,36},{33,37},{34,38},{35,39},{64,68},{6... | collective-permute-start | bytes 196616 | tf_op jit(solution)/shard_map/ppermute | solution.py:404
  126.2 3.2 %collective-permute-start.14 = (bf16[16,2048]{1,0:T(8,128)(2,1)S(1)}, bf16[16,2048]{1,0:T(8,128)(2,1)S(1)}, u32[]{:S(2)}, u32[]{:S(2)}) collective-permute-start(bf16[16,2048]{1,0:T(8,128)(2,1)S(1)} %section.17.held_ref), channel_id=1, source_target_pairs={{0,4},{1,5},{2,6},{3,7},{32,36},{33,37},{34,38},{35,39},{64,68},{6... | collective-permute-start | bytes 196616 | tf_op jit(solution)/shard_map/ppermute | solution.py:404
  127.5 2.5 %collective-permute-start.17 = (bf16[16,2048]{1,0:T(8,128)(2,1)S(1)}, bf16[16,2048]{1,0:T(8,128)(2,1)S(1)}, u32[]{:S(2)}, u32[]{:S(2)}) collective-permute-start(bf16[16,2048]{1,0:T(8,128)(2,1)S(1)} %get-tuple-element.45.held_ref), channel_id=1, source_target_pairs={{4,8},{5,9},{6,10},{7,11},{36,40},{37,41},{38,42},{39,43},{68,72},... | collective-permute-start | bytes 196616 | tf_op jit(solution)/shard_map/ppermute | solution.py:404
  129.4 1.6 collective-permute-start.16
  130.3 1.4 collective-permute-start.19
  131.0 1.4 collective-permute-start.18
  131.7 1.4 collective-permute-start.21
  132.4 1.4 collective-permute-start.20
  133.2 1.4 collective-permute-start.23
  134.6 1.6 collective-permute-start.25
  (8 other events, 63.7 us)

commit v11 on v10

--- a/solution.py
+++ b/solution.py
@@ -228,17 +228,36 @@
         shard_ref[zh, :, pl.ds(QKV, CTX)] = out_ref[...]
 
 
-def join_kernel(here_ref, after_ref, before_ref, half_ref, rest_ref, out_ref):
-    half = half_ref.shape[0]
+def join_parts(parts_of, out_ref):
     for i in range(out_ref.shape[1]):
-        middle = half_ref.at[i] if i < half else rest_ref.at[i - half]
-        parts = [here_ref.at[i], after_ref.at[i], middle, before_ref.at[i]]
+        parts = parts_of(i)
         for x, part in enumerate(parts):
             out_ref[x, i, :, pl.ds(0, QKV)] = part[:, pl.ds(0, QKV)]
         columns = jnp.concatenate([part[:, pl.ds(QKV, CTX)] for part in parts], axis=0)
         turned_columns = columns.astype(F32).T.astype(BF16)
         for x in range(X):
             out_ref[x, i, :, pl.ds(QKV, CTX)] = turned_columns[x * 64 : (x + 1) * 64]
+
+
+def join_kernel(here_ref, after_ref, before_ref, half_ref, rest_ref, out_ref):
+    half = half_ref.shape[0]
+
+    def parts_of(i):
+        middle = half_ref.at[i] if i < half else rest_ref.at[i - half]
+        return [here_ref.at[i], after_ref.at[i], middle, before_ref.at[i]]
+
+    join_parts(parts_of, out_ref)
+
+
+def join_across_kernel(low_ref, high_ref, low_middle_ref, high_middle_ref, out_ref):
+    half = low_middle_ref.shape[0]
+
+    def parts_of(i):
+        part, middle = (low_ref, low_middle_ref) if i < half else (high_ref, high_middle_ref)
+        i = i % half
+        return [part.at[i], part.at[half + i], middle.at[i], part.at[2 * half + i]]
+
+    join_parts(parts_of, out_ref)
 
 
 def gather_section(w_qkv, w_out, norm_gain):
@@ -284,12 +303,28 @@
     half = ZH // 2
     ahead, behind = along_z(here, 1), along_z(here, -1)
     near = jnp.concatenate([here, ahead, behind])
-    near_x = first_along_x(near)
-    across = jnp.concatenate([along_z(ahead[:half], 1), along_z(behind[half:], -1)])
-    across_x = first_along_x(across)
-    rest = rest_along_x(*near_x) + rest_along_x(*across_x)
-    rest = lax.optimization_barrier(rest)
-    own = [join(near, *near_x, *rest[:2]), join(across, *across_x, *rest[2:])]
+    before, after = first_along_x(near)
+    near_rest = rest_along_x(before, after)
+
+    def pieces(first):
+        return jnp.concatenate([part[first : first + half] for part in (near, after, before)])
+
+    across = [
+        along_z(pieces(ZH), 1),
+        along_z(pieces(2 * ZH + half), -1),
+        along_z(near_rest[0][ZH : ZH + half], 1),
+        along_z(near_rest[1][ZH : ZH + half], -1),
+    ]
+    near_0, near_1, *across = lax.optimization_barrier((*near_rest, *across))
+    across = pl.pallas_call(
+        join_across_kernel,
+        out_shape=jax.ShapeDtypeStruct((X, *here.shape), BF16),
+        in_specs=[vmem] * 4,
+        out_specs=vmem,
+        compiler_params=MEDIUM,
+        name="join_across",
+    )(*across)
+    own = [join(near, before, after, near_0, near_1), across]
     return own + [lax.ppermute(part, "core", [(0, 1), (1, 0)]) for part in own]
 
 

time: 190 us -> 191 us (level)
  waiting for transfers between devices: 30.7 us -> 39.9 us
  starting transfers between devices: 54.9 us -> 46.4 us
    ppermute x4 -> x2, waiting for transfers between devices: 7.48 us -> 18.7 us  [first_along_x(): return (lax.ppermute(parts, 'x', one), lax.ppermute(parts, 'x', other))]
    ppermute x4 -> x2, starting transfers between devices: 12.9 us -> 5.84 us  [first_along_x(): return (lax.ppermute(parts, 'x', one), lax.ppermute(parts, 'x', other))]
    ppermute x4 -> x6, starting transfers between devices: 14.1 us -> 19.7 us  [along_z(): lax.ppermute(parts, ('z_hi', 'tensor'), [(z, (z + by) % Z) for z in range...]
    ppermute x2 -> x1, starting transfers between devices: 8.39 us -> 3.6 us  [rest_along_x(): lax.ppermute(before[:half], 'x', one)]
    ppermute x2 -> x1, waiting for transfers between devices: 4.5 us -> 1.57 us  [rest_along_x(): lax.ppermute(after[half:], 'x', other)]
    ppermute x2 -> x1, starting transfers between devices: 4.55 us -> 2.25 us  [rest_along_x(): lax.ppermute(after[half:], 'x', other)]
    ppermute x4 -> x6, waiting for transfers between devices: 12 us -> 12.9 us  [along_z(): lax.ppermute(parts, ('z_hi', 'tensor'), [(z, (z + by) % Z) for z in range...]
  transfers between devices with their start and end apart: 28 -> 26, of which waited for: 10 -> 10; matrix products, arithmetic and copies ran while one was open for 0% -> 0% of each run, Pallas kernels for 2% -> 2%
where the time goes in v11:
time: 191 us; the launch traced here: 190 us
  blocking collectives  92.6 us (48%)
  starting transfers between devices  46.4 us (24%)
  waiting for transfers between devices  39.9 us (21%)
  Pallas kernels  8.95 us (5%)
    all_to_all x1, blocking collectives, exchange(): lax.all_to_all(chunks, ('pipe', 'tensor'), 0, 0, axis_index_groups=groups)  50.1 us
    all_to_all x1, blocking collectives, gather_section(): here = lax.all_to_all(shards, 'z_hi', 0, 0)  42.4 us
    ppermute x6, starting transfers between devices, along_z(): lax.ppermute(parts, ('z_hi', 'tensor'), [(z, (z + by) % Z) for z in range...  19.7 us
    ppermute x2, waiting for transfers between devices, first_along_x(): return (lax.ppermute(parts, 'x', one), lax.ppermute(parts, 'x', other))  18.7 us
    ppermute x6, waiting for transfers between devices, along_z(): lax.ppermute(parts, ('z_hi', 'tensor'), [(z, (z + by) % Z) for z in range...  12.9 us
    ppermute x14, starting transfers between devices, next_plane(): return lax.ppermute(part, 'pipe', [(step, step + 1)])  10.6 us
    ppermute x2, starting transfers between devices, first_along_x(): return (lax.ppermute(parts, 'x', one), lax.ppermute(parts, 'x', other))  5.84 us
    ppermute x2, waiting for transfers between devices, gather_section(): return own + [lax.ppermute(part, 'core', [(0, 1), (1, 0)]) for part in own]  5.51 us
  transfers between devices with their start and end apart: 26, of which 10 were waited for; matrix products, arithmetic and copies ran while one was open for 0% of the time, Pallas kernels for 2%

profile of v11, /device:TPU:6, one launch (start us, length us, event | category | flops | bytes accessed | tf_op | source)
XLA Modules:
  0.0 189.7 jit_solution(12552909236797991038)
XLA Ops:
  0.6 1.8 shard.1
  2.4 42.4 %all_to_all.10 = bf16[4,64,640]{2,1,0:T(8,128)(2,1)S(1)} all-to-all(bf16[4,64,640]{2,1,0:T(8,128)(2,1)} %shard.1), channel_id=1, replica_groups=mesh['x'=4,'z_hi'=4,'core'=2,'pipe'=8,'tensor'=4] {'z_hi'}, dimensions={0} | all-to-all | bytes 655360 | tf_op jit(solution)/shard_map/all_to_all | solution.py:302
  44.9 3.7 %collective-permute-start = (bf16[4,64,640]{2,1,0:T(8,128)(2,1)S(1)}, bf16[4,64,640]{2,1,0:T(8,128)(2,1)S(1)}, u32[]{:S(2)}, u32[]{:S(2)}) collective-permute-start(bf16[4,64,640]{2,1,0:T(8,128)(2,1)S(1)} %all_to_all.10), channel_id=1, source_target_pairs={{0,1},{1,2},{2,3},{3,64},{64,65},{65,66},{66,67},{67,128},{128,129... | collective-permute-start | bytes 983048 | tf_op jit(solution)/shard_map/ppermute | solution.py:300
  48.5 3.4 %collective-permute-start.1 = (bf16[4,64,640]{2,1,0:T(8,128)(2,1)S(1)}, bf16[4,64,640]{2,1,0:T(8,128)(2,1)S(1)}, u32[]{:S(2)}, u32[]{:S(2)}) collective-permute-start(bf16[4,64,640]{2,1,0:T(8,128)(2,1)S(1)} %all_to_all.10), channel_id=1, source_target_pairs={{0,195},{1,0},{2,1},{3,2},{64,3},{65,64},{66,65},{67,66},{128,67},... | collective-permute-start | bytes 983048 | tf_op jit(solution)/shard_map/ppermute | solution.py:300
  51.9 3.2 %collective-permute-done = bf16[4,64,640]{2,1,0:T(8,128)(2,1)S(1)} collective-permute-done((bf16[4,64,640]{2,1,0:T(8,128)(2,1)S(1)}, bf16[4,64,640]{2,1,0:T(8,128)(2,1)S(1)}, u32[]{:S(2)}, u32[]{:S(2)}) %collective-permute-start) | collective-permute-done | bytes 327712 | tf_op jit(solution)/shard_map/ppermute | solution.py:300
  55.2 5.0 %collective-permute-done.1 = bf16[4,64,640]{2,1,0:T(8,128)(2,1)S(1)} collective-permute-done((bf16[4,64,640]{2,1,0:T(8,128)(2,1)S(1)}, bf16[4,64,640]{2,1,0:T(8,128)(2,1)S(1)}, u32[]{:S(2)}, u32[]{:S(2)}) %collective-permute-start.1) | collective-permute-done | bytes 327712 | tf_op jit(solution)/shard_map/ppermute | solution.py:300
  60.3 2.4 %collective-permute-start.3 = (bf16[12,64,640]{2,1,0:T(8,128)(2,1)S(1)}, bf16[12,64,640]{2,1,0:T(8,128)(2,1)S(1)}, u32[]{:S(2)}, u32[]{:S(2)}) collective-permute-start(bf16[12,64,640]{2,1,0:T(8,128)(2,1)S(1)} %constant_dynamic-update-slice_fusion.here_ref), channel_id=1, source_target_pairs={{0,256},{256,512},{512,768},{768,0},{1,257},{257,513},{513,769},{7... | collective-permute-start | bytes 2949128 | tf_op jit(solution)/shard_map/ppermute | solution.py:283
  62.7 3.5 %collective-permute-start.2 = (bf16[12,64,640]{2,1,0:T(8,128)(2,1)S(1)}, bf16[12,64,640]{2,1,0:T(8,128)(2,1)S(1)}, u32[]{:S(2)}, u32[]{:S(2)}) collective-permute-start(bf16[12,64,640]{2,1,0:T(8,128)(2,1)S(1)} %constant_dynamic-update-slice_fusion.here_ref), channel_id=1, source_target_pairs={{0,768},{256,0},{512,256},{768,512},{1,769},{257,1},{513,257},{769... | collective-permute-start | bytes 2949128 | tf_op jit(solution)/shard_map/ppermute | solution.py:283
  66.2 18.7 %collective-permute-done.3.before_ref = bf16[12,64,640]{2,1,0:T(8,128)(2,1)S(1)} collective-permute-done((bf16[12,64,640]{2,1,0:T(8,128)(2,1)S(1)}, bf16[12,64,640]{2,1,0:T(8,128)(2,1)S(1)}, u32[]{:S(2)}, u32[]{:S(2)}) %collective-permute-start.3) | collective-permute-done | bytes 983072 | tf_op jit(solution)/shard_map/ppermute | solution.py:283
  84.9 3.6 %collective-permute-start.4 = (bf16[6,64,640]{2,1,0:T(8,128)(2,1)S(1)}, bf16[6,64,640]{2,1,0:T(8,128)(2,1)S(1)}, u32[]{:S(2)}, u32[]{:S(2)}) collective-permute-start(bf16[6,64,640]{2,1,0:T(8,128)(2,1)S(1)} %slice.40), channel_id=1, source_target_pairs={{0,256},{256,512},{512,768},{768,0},{1,257},{257,513},{513,769},{7... | collective-permute-start | bytes 1474568 | tf_op jit(solution)/shard_map/ppermute | solution.py:287
  88.6 2.2 %collective-permute-start.5 = (bf16[6,64,640]{2,1,0:T(8,128)(2,1)S(1)}, bf16[6,64,640]{2,1,0:T(8,128)(2,1)S(1)}, u32[]{:S(2)}, u32[]{:S(2)}) collective-permute-start(bf16[6,64,640]{2,1,0:T(8,128)(2,1)S(1)} %slice.41), channel_id=1, source_target_pairs={{0,768},{256,0},{512,256},{768,512},{1,769},{257,1},{513,257},{769... | collective-permute-start | bytes 1474568 | tf_op jit(solution)/shard_map/ppermute | solution.py:287
  91.0 3.3 %collective-permute-start.6 = (bf16[6,64,640]{2,1,0:T(8,128)(2,1)S(1)}, bf16[6,64,640]{2,1,0:T(8,128)(2,1)S(1)}, u32[]{:S(2)}, u32[]{:S(2)}) collective-permute-start(bf16[6,64,640]{2,1,0:T(8,128)(2,1)S(1)} %pad_maximum_fusion), channel_id=1, source_target_pairs={{0,1},{1,2},{2,3},{3,64},{64,65},{65,66},{66,67},{67,128},{128,129... | collective-permute-start | bytes 1474568 | tf_op jit(solution)/shard_map/ppermute | solution.py:300
  94.4 3.7 %collective-permute-start.7 = (bf16[6,64,640]{2,1,0:T(8,128)(2,1)S(1)}, bf16[6,64,640]{2,1,0:T(8,128)(2,1)S(1)}, u32[]{:S(2)}, u32[]{:S(2)}) collective-permute-start(bf16[6,64,640]{2,1,0:T(8,128)(2,1)S(1)} %pad_maximum_fusion.1), channel_id=1, source_target_pairs={{0,195},{1,0},{2,1},{3,2},{64,3},{65,64},{66,65},{67,66},{128,67},... | collective-permute-start | bytes 1474568 | tf_op jit(solution)/shard_map/ppermute | solution.py:300
  98.2 2.9 %collective-permute-start.8 = (bf16[2,64,640]{2,1,0:T(8,128)(2,1)S(1)}, bf16[2,64,640]{2,1,0:T(8,128)(2,1)S(1)}, u32[]{:S(2)}, u32[]{:S(2)}) collective-permute-start(bf16[2,64,640]{2,1,0:T(8,128)(2,1)S(1)} %slice.48), channel_id=1, source_target_pairs={{0,1},{1,2},{2,3},{3,64},{64,65},{65,66},{66,67},{67,128},{128,129... | collective-permute-start | bytes 491528 | tf_op jit(solution)/shard_map/ppermute | solution.py:300
  101.1 1.6 collective-permute-done.5.rest_ref
  102.8 2.7 %collective-permute-start.9 = (bf16[2,64,640]{2,1,0:T(8,128)(2,1)S(1)}, bf16[2,64,640]{2,1,0:T(8,128)(2,1)S(1)}, u32[]{:S(2)}, u32[]{:S(2)}) collective-permute-start(bf16[2,64,640]{2,1,0:T(8,128)(2,1)S(1)} %slice.49), channel_id=1, source_target_pairs={{0,195},{1,0},{2,1},{3,2},{64,3},{65,64},{66,65},{67,66},{128,67},... | collective-permute-start | bytes 491528 | tf_op jit(solution)/shard_map/ppermute | solution.py:300
  106.6 1.6 collective-permute-done.7.high_ref
  108.3 1.8 collective-permute-done.9.high_middle_ref
  110.7 1.9 %collective-permute-start.10 = (bf16[4,12,64,640]{3,2,1,0:T(8,128)(2,1)S(1)}, bf16[4,12,64,640]{3,2,1,0:T(8,128)(2,1)S(1)}, u32[]{:S(2)}, u32[]{:S(2)}) collective-permute-start(bf16[4,12,64,640]{3,2,1,0:T(8,128)(2,1)S(1)} %join.1.refs_5_), channel_id=1, source_target_pairs={{0,32},{32,0},{1,33},{33,1},{2,34},{34,2},{3,35},{35,3},{4,36},{36... | collective-permute-start | bytes 11796488 | tf_op jit(solution)/shard_map/ppermute | solution.py:328
  112.9 2.4 %collective-permute-start.11 = (bf16[4,4,64,640]{3,2,1,0:T(8,128)(2,1)S(1)}, bf16[4,4,64,640]{3,2,1,0:T(8,128)(2,1)S(1)}, u32[]{:S(2)}, u32[]{:S(2)}) collective-permute-start(bf16[4,4,64,640]{3,2,1,0:T(8,128)(2,1)S(1)} %join_across.1.refs_6_), channel_id=1, source_target_pairs={{0,32},{32,0},{1,33},{33,1},{2,34},{34,2},{3,35},{35,3},{4,36},{36... | collective-permute-start | bytes 3932168 | tf_op jit(solution)/shard_map/ppermute | solution.py:328
  115.8 5.5 %collective-permute-done.11.refs_8_ = bf16[4,4,64,640]{3,2,1,0:T(8,128)(2,1)S(1)} collective-permute-done((bf16[4,4,64,640]{3,2,1,0:T(8,128)(2,1)S(1)}, bf16[4,4,64,640]{3,2,1,0:T(8,128)(2,1)S(1)}, u32[]{:S(2)}, u32[]{:S(2)}) %collective-permute-start.11) | collective-permute-done | bytes 1310752 | tf_op jit(solution)/shard_map/ppermute | solution.py:328
  121.3 2.2 %section.16 = (bf16[16,2048]{1,0:T(8,128)(2,1)S(1)}, bf16[4,16,256]{2,1,0:T(8,128)(2,1)S(1)}, bf16[4,16,128]{2,1,0:T(8,128)(2,1)S(1)}) custom-call(bf16[16,2048]{1,0:T(8,128)(2,1)S(1)} %get-tuple-element.43.x_ref, f32[32,32]{1,0:T(8,128)S(1)} %get-tuple-element.36.allowed_ref, ...), custom_call_target="tpu_custom_call", output_to_operand_aliasing={{0}: (2, {})} | custom-call | tf_op jit(solution)/shard_map/section/pallas_call | solution.py:182
  124.8 2.2 %section.17.held_ref = bf16[16,2048]{1,0:T(8,128)(2,1)S(1)} custom-call(bf16[16,2048]{1,0:T(8,128)(2,1)S(1)} %get-tuple-element.35.x_ref, f32[32,32]{1,0:T(8,128)S(1)} %get-tuple-element.36.allowed_ref, bf16[16,2048]{1,0:T(8,128)(2,1)S(1)} %broadcast_in_dim.121.held_ref, f32[32,128]{1,0:T(8,128)S(1)} %get-tuple-element.76.refs_0_, ...), custom_call_target="tpu_custom_call", output_to_operand_aliasing={{}: (2, {})} | custom-call | tf_op jit(solution)/shard_map/section/pallas_call | solution.py:182
  138.6 50.1 %all_to_all.11.received_ref = bf16[8,8,2048]{2,1,0:T(8,128)(2,1)S(1)} all-to-all(bf16[8,8,2048]{2,1,0:T(8,128)(2,1)S(1)} %section.31), channel_id=1, replica_groups={{0,1,2,3,28,29,30,31},{4,5,6,7,24,25,26,27},{8,9,10,11,20,21,22,23},{12..., dimensions={0} | all-to-all | bytes 524288 | tf_op jit(solution)/shard_map/all_to_all | solution.py:402
  (78 shorter events, 16.6 us)
Async XLA Ops:
  44.9 10.3 %collective-permute-start = (bf16[4,64,640]{2,1,0:T(8,128)(2,1)S(1)}, bf16[4,64,640]{2,1,0:T(8,128)(2,1)S(1)}, u32[]{:S(2)}, u32[]{:S(2)}) collective-permute-start(bf16[4,64,640]{2,1,0:T(8,128)(2,1)S(1)} %all_to_all.10), channel_id=1, source_target_pairs={{0,1},{1,2},{2,3},{3,64},{64,65},{65,66},{66,67},{67,128},{128,129... | collective-permute-start | bytes 983048 | tf_op jit(solution)/shard_map/ppermute | solution.py:300
  48.5 11.7 %collective-permute-start.1 = (bf16[4,64,640]{2,1,0:T(8,128)(2,1)S(1)}, bf16[4,64,640]{2,1,0:T(8,128)(2,1)S(1)}, u32[]{:S(2)}, u32[]{:S(2)}) collective-permute-start(bf16[4,64,640]{2,1,0:T(8,128)(2,1)S(1)} %all_to_all.10), channel_id=1, source_target_pairs={{0,195},{1,0},{2,1},{3,2},{64,3},{65,64},{66,65},{67,66},{128,67},... | collective-permute-start | bytes 983048 | tf_op jit(solution)/shard_map/ppermute | solution.py:300
  60.3 24.6 %collective-permute-start.3 = (bf16[12,64,640]{2,1,0:T(8,128)(2,1)S(1)}, bf16[12,64,640]{2,1,0:T(8,128)(2,1)S(1)}, u32[]{:S(2)}, u32[]{:S(2)}) collective-permute-start(bf16[12,64,640]{2,1,0:T(8,128)(2,1)S(1)} %constant_dynamic-update-slice_fusion.here_ref), channel_id=1, source_target_pairs={{0,256},{256,512},{512,768},{768,0},{1,257},{257,513},{513,769},{7... | collective-permute-start | bytes 2949128 | tf_op jit(solution)/shard_map/ppermute | solution.py:283
  62.7 25.9 %collective-permute-start.2 = (bf16[12,64,640]{2,1,0:T(8,128)(2,1)S(1)}, bf16[12,64,640]{2,1,0:T(8,128)(2,1)S(1)}, u32[]{:S(2)}, u32[]{:S(2)}) collective-permute-start(bf16[12,64,640]{2,1,0:T(8,128)(2,1)S(1)} %constant_dynamic-update-slice_fusion.here_ref), channel_id=1, source_target_pairs={{0,768},{256,0},{512,256},{768,512},{1,769},{257,1},{513,257},{769... | collective-permute-start | bytes 2949128 | tf_op jit(solution)/shard_map/ppermute | solution.py:283
  84.9 13.2 %collective-permute-start.4 = (bf16[6,64,640]{2,1,0:T(8,128)(2,1)S(1)}, bf16[6,64,640]{2,1,0:T(8,128)(2,1)S(1)}, u32[]{:S(2)}, u32[]{:S(2)}) collective-permute-start(bf16[6,64,640]{2,1,0:T(8,128)(2,1)S(1)} %slice.40), channel_id=1, source_target_pairs={{0,256},{256,512},{512,768},{768,0},{1,257},{257,513},{513,769},{7... | collective-permute-start | bytes 1474568 | tf_op jit(solution)/shard_map/ppermute | solution.py:287
  88.6 14.1 %collective-permute-start.5 = (bf16[6,64,640]{2,1,0:T(8,128)(2,1)S(1)}, bf16[6,64,640]{2,1,0:T(8,128)(2,1)S(1)}, u32[]{:S(2)}, u32[]{:S(2)}) collective-permute-start(bf16[6,64,640]{2,1,0:T(8,128)(2,1)S(1)} %slice.41), channel_id=1, source_target_pairs={{0,768},{256,0},{512,256},{768,512},{1,769},{257,1},{513,257},{769... | collective-permute-start | bytes 1474568 | tf_op jit(solution)/shard_map/ppermute | solution.py:287
  91.0 15.6 %collective-permute-start.6 = (bf16[6,64,640]{2,1,0:T(8,128)(2,1)S(1)}, bf16[6,64,640]{2,1,0:T(8,128)(2,1)S(1)}, u32[]{:S(2)}, u32[]{:S(2)}) collective-permute-start(bf16[6,64,640]{2,1,0:T(8,128)(2,1)S(1)} %pad_maximum_fusion), channel_id=1, source_target_pairs={{0,1},{1,2},{2,3},{3,64},{64,65},{65,66},{66,67},{67,128},{128,129... | collective-permute-start | bytes 1474568 | tf_op jit(solution)/shard_map/ppermute | solution.py:300
  94.4 13.8 %collective-permute-start.7 = (bf16[6,64,640]{2,1,0:T(8,128)(2,1)S(1)}, bf16[6,64,640]{2,1,0:T(8,128)(2,1)S(1)}, u32[]{:S(2)}, u32[]{:S(2)}) collective-permute-start(bf16[6,64,640]{2,1,0:T(8,128)(2,1)S(1)} %pad_maximum_fusion.1), channel_id=1, source_target_pairs={{0,195},{1,0},{2,1},{3,2},{64,3},{65,64},{66,65},{67,66},{128,67},... | collective-permute-start | bytes 1474568 | tf_op jit(solution)/shard_map/ppermute | solution.py:300
  98.2 10.2 %collective-permute-start.8 = (bf16[2,64,640]{2,1,0:T(8,128)(2,1)S(1)}, bf16[2,64,640]{2,1,0:T(8,128)(2,1)S(1)}, u32[]{:S(2)}, u32[]{:S(2)}) collective-permute-start(bf16[2,64,640]{2,1,0:T(8,128)(2,1)S(1)} %slice.48), channel_id=1, source_target_pairs={{0,1},{1,2},{2,3},{3,64},{64,65},{65,66},{66,67},{67,128},{128,129... | collective-permute-start | bytes 491528 | tf_op jit(solution)/shard_map/ppermute | solution.py:300
  102.8 7.3 %collective-permute-start.9 = (bf16[2,64,640]{2,1,0:T(8,128)(2,1)S(1)}, bf16[2,64,640]{2,1,0:T(8,128)(2,1)S(1)}, u32[]{:S(2)}, u32[]{:S(2)}) collective-permute-start(bf16[2,64,640]{2,1,0:T(8,128)(2,1)S(1)} %slice.49), channel_id=1, source_target_pairs={{0,195},{1,0},{2,1},{3,2},{64,3},{65,64},{66,65},{67,66},{128,67},... | collective-permute-start | bytes 491528 | tf_op jit(solution)/shard_map/ppermute | solution.py:300
  110.7 10.6 %collective-permute-start.10 = (bf16[4,12,64,640]{3,2,1,0:T(8,128)(2,1)S(1)}, bf16[4,12,64,640]{3,2,1,0:T(8,128)(2,1)S(1)}, u32[]{:S(2)}, u32[]{:S(2)}) collective-permute-start(bf16[4,12,64,640]{3,2,1,0:T(8,128)(2,1)S(1)} %join.1.refs_5_), channel_id=1, source_target_pairs={{0,32},{32,0},{1,33},{33,1},{2,34},{34,2},{3,35},{35,3},{4,36},{36... | collective-permute-start | bytes 11796488 | tf_op jit(solution)/shard_map/ppermute | solution.py:328
  112.9 8.4 %collective-permute-start.11 = (bf16[4,4,64,640]{3,2,1,0:T(8,128)(2,1)S(1)}, bf16[4,4,64,640]{3,2,1,0:T(8,128)(2,1)S(1)}, u32[]{:S(2)}, u32[]{:S(2)}) collective-permute-start(bf16[4,4,64,640]{3,2,1,0:T(8,128)(2,1)S(1)} %join_across.1.refs_6_), channel_id=1, source_target_pairs={{0,32},{32,0},{1,33},{33,1},{2,34},{34,2},{3,35},{35,3},{4,36},{36... | collective-permute-start | bytes 3932168 | tf_op jit(solution)/shard_map/ppermute | solution.py:328
  123.5 4.8 %collective-permute-start.13 = (bf16[16,2048]{1,0:T(8,128)(2,1)S(1)}, bf16[16,2048]{1,0:T(8,128)(2,1)S(1)}, u32[]{:S(2)}, u32[]{:S(2)}) collective-permute-start(bf16[16,2048]{1,0:T(8,128)(2,1)S(1)} %get-tuple-element.46.held_ref), channel_id=1, source_target_pairs={{0,4},{1,5},{2,6},{3,7},{32,36},{33,37},{34,38},{35,39},{64,68},{6... | collective-permute-start | bytes 196616 | tf_op jit(solution)/shard_map/ppermute | solution.py:439
  127.0 3.2 %collective-permute-start.12 = (bf16[16,2048]{1,0:T(8,128)(2,1)S(1)}, bf16[16,2048]{1,0:T(8,128)(2,1)S(1)}, u32[]{:S(2)}, u32[]{:S(2)}) collective-permute-start(bf16[16,2048]{1,0:T(8,128)(2,1)S(1)} %section.17.held_ref), channel_id=1, source_target_pairs={{0,4},{1,5},{2,6},{3,7},{32,36},{33,37},{34,38},{35,39},{64,68},{6... | collective-permute-start | bytes 196616 | tf_op jit(solution)/shard_map/ppermute | solution.py:439
  128.4 2.5 %collective-permute-start.15 = (bf16[16,2048]{1,0:T(8,128)(2,1)S(1)}, bf16[16,2048]{1,0:T(8,128)(2,1)S(1)}, u32[]{:S(2)}, u32[]{:S(2)}) collective-permute-start(bf16[16,2048]{1,0:T(8,128)(2,1)S(1)} %get-tuple-element.49.held_ref), channel_id=1, source_target_pairs={{4,8},{5,9},{6,10},{7,11},{36,40},{37,41},{38,42},{39,43},{68,72},... | collective-permute-start | bytes 196616 | tf_op jit(solution)/shard_map/ppermute | solution.py:439
  130.2 1.6 collective-permute-start.14
  131.1 1.4 collective-permute-start.17
  131.8 1.4 collective-permute-start.16
  132.5 1.4 collective-permute-start.19
  133.3 1.4 collective-permute-start.18
  134.0 1.4 collective-permute-start.21
  134.7 1.4 collective-permute-start.20
  135.4 1.6 collective-permute-start.23
  137.1 1.4 collective-permute-start.25
  (6 other events, 52.4 us)
